TPU v7x, 32 devices: a whole 2x2x4 slice. The times are simulated.
32 devices in a mesh: blk: 8 (over z, x), uly: 4 (over y, core).
Axes of the slice: x: 2, y: 2, z: 4, core: 2. Of those that a mesh axis runs over, the one named last changes fastest.
Arguments:
- tokens: bfloat16 [2048, 2, 1536], P(('blk', 'uly')), may hold values from -6 to 6
- span_order: int32 [2, 16], replicated, may hold values from 0 to 15, as said below
- attn_gain: bfloat16 [1536], P(('blk', 'uly')), may hold values from 0.5 to 1.5
- qkv_weight: bfloat16 [1536, 2048], P(('blk', 'uly')), may hold values from -0.21875 to 0.21875
- qkv_bias: bfloat16 [2048], P(('blk', 'uly')), may hold values from -1.1953125 to 1.1953125
- out_weight: bfloat16 [1536, 1536], P(('blk', 'uly')), may hold values from -1 to 1
- ffn_gain: bfloat16 [1536], P('blk'), may hold values from 0.5 to 1.5
- gate_weight: bfloat16 [1536, 8960], P('blk', 'uly'), may hold values from -0.15625 to 0.15625
- up_weight: bfloat16 [1536, 8960], P('blk', 'uly'), may hold values from -0.15625 to 0.15625
- down_weight: bfloat16 [8960, 1536], P('uly', 'blk'), may hold values from -0.09375 to 0.09375
- cotangent: bfloat16 [2048, 2, 1536], P(('blk', 'uly')), may hold values from -6 to 6
Outputs:
- output: bfloat16 [2048, 2, 1536], P(('blk', 'uly'))
- grad_tokens: float32 [2048, 2, 1536], P(('blk', 'uly'))
- grad_attn_gain: float32 [1536], P(('blk', 'uly'))
- grad_qkv: float32 [1536, 2048], P(('blk', 'uly'))
- grad_bias: float32 [2048], P(('blk', 'uly'))
- grad_out_proj: float32 [1536, 1536], P(('blk', 'uly'))
- grad_ffn_gain: float32 [1536], P(('blk', 'uly'))
- grad_gate: float32 [1536, 8960], P('blk', 'uly')
- grad_up: float32 [1536, 8960], P('blk', 'uly')
- grad_down: float32 [8960, 1536], P('uly', 'blk')
Inputs may be any that keep to these rules, and one draw needn't show every extreme that they name: Each row is a permutation: slot j of sequence s (its rows j * 128 to (j + 1) * 128 - 1) holds the tokens at positions span_order[s, j] * 128 onward, in order.
All inputs are finite; a program needn't handle non-finite values.
Results may differ from a plain program's by a relative error of at most 0.033.
Values may be sent and summed in bfloat16 or wider, within the bound.
No kernel may reach another device: no remote copies, remote signals or barrier semaphores. Data moves between devices by JAX's collectives and lax.ppermute only.
A program may use at most 512 MiB of HBM per device.

v0:
```python
from functools import reduce
import math

import jax
import jax.numpy as jnp
from jax import lax
from jax.sharding import PartitionSpec as P

HEADS = 12
KV_HEADS = 2
HEAD_DIM = 128
SPAN = 128


EPS = 1e-06
THETA = 1000000.0
FLOOR = -1e30


def norm_rows(rows):
    factor = lax.rsqrt(jnp.mean(rows * rows, axis=-1, keepdims=True) + EPS)
    return (rows * factor, factor)


def norm_back(grad_normed, unit, factor, gain):
    gain_grad = jnp.sum(grad_normed * unit, axis=0)
    scaled = grad_normed * gain
    return (factor * (scaled - unit * jnp.mean(scaled * unit, axis=-1, keepdims=True)), gain_grad)


def matmul(left, right):
    return jnp.dot(left, right, preferred_element_type=jnp.float32)


def contract_rows(left, right):
    return lax.dot_general(
        left, right, (((0,), (0,)), ((), ())), preferred_element_type=jnp.float32
    )


def contract_cols(left, right):
    return lax.dot_general(
        left, right, (((1,), (1,)), ((), ())), preferred_element_type=jnp.float32
    )


def positions(order, rows):
    table = jnp.arange(order.shape[1], dtype=jnp.int32)
    slots = rows // SPAN
    picked = jnp.where(slots[None, :, None] == table[None, None, :], order[:, None, :], 0)
    return jnp.sum(picked, axis=-1) * SPAN + (rows % SPAN)[None, :]


def rope_tables(places):
    index = jnp.arange(HEAD_DIM // 2).astype(jnp.float32)
    freq = THETA ** (-2.0 * index / HEAD_DIM)
    angle = places.astype(jnp.float32)[..., None] * freq
    angle = jnp.concatenate([angle, angle], axis=-1)
    return (jnp.cos(angle), jnp.sin(angle))


def rotate(field, cosine, sine):
    half = field.shape[-1] // 2
    turned = jnp.concatenate([-field[..., half:], field[..., :half]], axis=-1)
    return field * cosine + turned * sine


def unrotate(grad, cosine, sine):
    half = grad.shape[-1] // 2
    moved = grad * sine
    return grad * cosine + jnp.concatenate([moved[..., half:], -moved[..., :half]], axis=-1)


def per_device(
    tokens,
    span_order,
    attn_gain,
    qkv_weight,
    qkv_bias,
    out_weight,
    ffn_gain,
    gate_weight,
    up_weight,
    down_weight,
    cotangent,
):
    local_rows, seqs = (tokens.shape[0], tokens.shape[1])
    uly_size = lax.axis_size("uly")
    cycle_rows = local_rows * uly_size
    group = HEADS // uly_size
    factor = 1.0 / math.sqrt(HEAD_DIM)
    width = HEADS * HEAD_DIM
    side = KV_HEADS * HEAD_DIM
    slot_heads = [u * group // (HEADS // KV_HEADS) for u in range(uly_size)]
    cycle_start = lax.axis_index("blk") * cycle_rows
    token_rows = (
        cycle_start + lax.axis_index("uly") * local_rows + jnp.arange(local_rows, dtype=jnp.int32)
    )
    head_rows = cycle_start + jnp.arange(cycle_rows, dtype=jnp.int32)
    query_places = positions(span_order, head_rows)
    gain_one, qkv_full, bias_full, out_full = (
        lax.all_gather(attn_gain, ("blk", "uly"), axis=0, tiled=True),
        lax.all_gather(qkv_weight, ("blk", "uly"), axis=0, tiled=True),
        lax.all_gather(qkv_bias, ("blk", "uly"), axis=0, tiled=True),
        lax.all_gather(out_weight, ("blk", "uly"), axis=0, tiled=True),
    )
    rows = tokens.astype(jnp.float32).reshape(local_rows * seqs, -1)
    unit_one, factor_one = norm_rows(rows)
    normed = (unit_one * gain_one.astype(jnp.float32)).astype(jnp.bfloat16)
    mixed = (matmul(normed, qkv_full) + bias_full.astype(jnp.float32)).reshape(local_rows, seqs, -1)
    cosine, sine = rope_tables(positions(span_order, token_rows).T)
    cosine = cosine[:, :, None, :]
    sine = sine[:, :, None, :]
    query = rotate(
        mixed[..., :width].reshape(local_rows, seqs, HEADS, HEAD_DIM), cosine, sine
    ).astype(jnp.bfloat16)
    keys = rotate(
        mixed[..., width : width + side].reshape(local_rows, seqs, KV_HEADS, HEAD_DIM), cosine, sine
    ).astype(jnp.bfloat16)
    values = (
        mixed[..., width + side :]
        .reshape(local_rows, seqs, KV_HEADS, HEAD_DIM)
        .astype(jnp.bfloat16)
    )
    paired = jnp.stack([keys, values], axis=3)
    slotted = jnp.stack([paired[:, :, head] for head in slot_heads], axis=2)
    query_heads, pair_heads = (
        lax.all_to_all(query, "uly", split_axis=2, concat_axis=0, tiled=True),
        lax.all_to_all(slotted, "uly", split_axis=2, concat_axis=0, tiled=True),
    )
    pair_heads = pair_heads[:, :, 0]
    query_t = jnp.transpose(query_heads, (1, 2, 0, 3))
    pairs_all = lax.all_gather(pair_heads, "blk", axis=0, tiled=True)
    total_rows = pairs_all.shape[0]
    size = math.gcd(total_rows, 4 * SPAN)

    def forward_step(state, index):
        summed, peak, weight_sum = state
        offset = index * size
        block = lax.dynamic_slice_in_dim(pairs_all, offset, size, 0)
        key_places = positions(span_order, offset + jnp.arange(size, dtype=jnp.int32))
        scores = (
            jnp.einsum(
                "shrd,ksd->shrk", query_t, block[:, :, 0], preferred_element_type=jnp.float32
            )
            * factor
        )
        allowed = key_places[:, None, None, :] <= query_places[:, None, :, None]
        scores = jnp.where(allowed, scores, FLOOR)
        new_peak = jnp.maximum(peak, jnp.max(scores, axis=-1))
        weights = jnp.where(allowed, jnp.exp(scores - new_peak[..., None]), 0.0)
        fade = jnp.exp(peak - new_peak)
        weight_sum = weight_sum * fade + jnp.sum(weights, axis=-1)
        summed = summed * fade[..., None] + jnp.einsum(
            "shrk,ksd->shrd",
            weights.astype(jnp.bfloat16),
            block[:, :, 1],
            preferred_element_type=jnp.float32,
        )
        return ((summed, new_peak, weight_sum), None)

    initial = (
        jnp.zeros((seqs, group, cycle_rows, HEAD_DIM), jnp.float32),
        jnp.full((seqs, group, cycle_rows), FLOOR, jnp.float32),
        jnp.zeros((seqs, group, cycle_rows), jnp.float32),
    )
    (summed, peak, weight_sum), unused = lax.scan(
        forward_step, initial, jnp.arange(total_rows // size, dtype=jnp.int32)
    )
    log_total = peak + jnp.log(weight_sum)
    result_t = (summed / weight_sum[..., None]).astype(jnp.bfloat16)
    result_heads = jnp.transpose(result_t, (2, 0, 1, 3))
    attended = lax.all_to_all(result_heads, "uly", split_axis=0, concat_axis=2, tiled=True).reshape(
        local_rows * seqs, width
    )
    hidden = rows + matmul(attended, out_full)
    gain_two, gate_part, upper_part, down_part = (
        lax.all_gather(ffn_gain, "blk", axis=0, tiled=True),
        lax.all_gather(gate_weight, "blk", axis=0, tiled=True),
        lax.all_gather(up_weight, "blk", axis=0, tiled=True),
        lax.all_gather(down_weight, "blk", axis=1, tiled=True),
    )
    unit_two, factor_two = norm_rows(hidden)
    normed_mid = (unit_two * gain_two.astype(jnp.float32)).astype(jnp.bfloat16)
    grad_rows = cotangent.astype(jnp.float32).reshape(local_rows * seqs, -1)
    branch_two = grad_rows.astype(jnp.bfloat16)
    gate_used, upper_used, down_used = (
        lax.all_gather(gate_part, "uly", axis=1, tiled=True),
        lax.all_gather(upper_part, "uly", axis=1, tiled=True),
        lax.all_gather(down_part, "uly", axis=0, tiled=True),
    )
    mid_rows, cot_rows = (normed_mid, branch_two)
    gate = matmul(mid_rows, gate_used)
    upper = matmul(mid_rows, upper_used)
    sigmoid = jax.nn.sigmoid(gate)
    active = (gate * sigmoid * upper).astype(jnp.bfloat16)
    branch_out = matmul(active, down_used)
    grad_down = contract_rows(active, cot_rows)
    active_grad = contract_cols(cot_rows, down_used)
    gate_grad = (active_grad * upper * sigmoid * (1.0 + gate * (1.0 - sigmoid))).astype(
        jnp.bfloat16
    )
    upper_grad = (active_grad * gate * sigmoid).astype(jnp.bfloat16)
    grad_gate = contract_rows(mid_rows, gate_grad)
    grad_upper = contract_rows(mid_rows, upper_grad)
    mid_grad = contract_cols(gate_grad, gate_used) + contract_cols(upper_grad, upper_used)
    grad_gate, grad_upper, grad_down = (
        lax.psum_scatter(
            grad_gate.astype(jnp.bfloat16), "uly", scatter_dimension=1, tiled=True
        ).astype(jnp.float32),
        lax.psum_scatter(
            grad_upper.astype(jnp.bfloat16), "uly", scatter_dimension=1, tiled=True
        ).astype(jnp.float32),
        lax.psum_scatter(
            grad_down.astype(jnp.bfloat16), "uly", scatter_dimension=0, tiled=True
        ).astype(jnp.float32),
    )
    result = hidden + branch_out
    output = result.astype(jnp.bfloat16).reshape(local_rows, seqs, -1)
    hidden_part, grad_gain_two = norm_back(
        mid_grad, unit_two, factor_two, gain_two.astype(jnp.float32)
    )
    hidden_grad = grad_rows + hidden_part
    ffn_shares = (
        lax.psum_scatter(
            grad_gate.astype(jnp.bfloat16), "blk", scatter_dimension=0, tiled=True
        ).astype(jnp.float32),
        lax.psum_scatter(
            grad_upper.astype(jnp.bfloat16), "blk", scatter_dimension=0, tiled=True
        ).astype(jnp.float32),
        lax.psum_scatter(
            grad_down.astype(jnp.bfloat16), "blk", scatter_dimension=1, tiled=True
        ).astype(jnp.float32),
    )
    branch_one = hidden_grad.astype(jnp.bfloat16)
    grad_out_w = contract_rows(attended, branch_one)
    attended_grad = (
        contract_cols(branch_one, out_full)
        .astype(jnp.bfloat16)
        .reshape(local_rows, seqs, HEADS, HEAD_DIM)
    )
    grad_heads = lax.all_to_all(attended_grad, "uly", split_axis=2, concat_axis=0, tiled=True)
    grad_t = jnp.transpose(grad_heads, (1, 2, 0, 3))
    delta = jnp.sum(grad_t.astype(jnp.float32) * result_t.astype(jnp.float32), axis=-1)

    def backward_step(query_grad, index):
        offset = index * size
        block = lax.dynamic_slice_in_dim(pairs_all, offset, size, 0)
        key_places = positions(span_order, offset + jnp.arange(size, dtype=jnp.int32))
        scores = (
            jnp.einsum(
                "shrd,ksd->shrk", query_t, block[:, :, 0], preferred_element_type=jnp.float32
            )
            * factor
        )
        allowed = key_places[:, None, None, :] <= query_places[:, None, :, None]
        probs = jnp.where(allowed, jnp.exp(scores - log_total[..., None]), 0.0)
        prob_grad = jnp.einsum(
            "shrd,ksd->shrk", grad_t, block[:, :, 1], preferred_element_type=jnp.float32
        )
        score_grad = (probs * (prob_grad - delta[..., None])).astype(jnp.bfloat16)
        query_grad = (
            query_grad
            + jnp.einsum(
                "shrk,ksd->shrd", score_grad, block[:, :, 0], preferred_element_type=jnp.float32
            )
            * factor
        )
        key_grad = (
            jnp.einsum("shrk,shrd->ksd", score_grad, query_t, preferred_element_type=jnp.float32)
            * factor
        )
        value_grad = jnp.einsum(
            "shrk,shrd->ksd", probs.astype(jnp.bfloat16), grad_t, preferred_element_type=jnp.float32
        )
        return (query_grad, jnp.stack([key_grad, value_grad], axis=2))

    query_grad_t, terms = lax.scan(
        backward_step,
        jnp.zeros((seqs, group, cycle_rows, HEAD_DIM), jnp.float32),
        jnp.arange(total_rows // size, dtype=jnp.int32),
    )
    terms = terms.reshape(total_rows, seqs, 2, HEAD_DIM)
    pair_grads = lax.psum_scatter(
        terms.astype(jnp.bfloat16), "blk", scatter_dimension=0, tiled=True
    )
    query_grad_heads = jnp.transpose(query_grad_t, (2, 0, 1, 3)).astype(jnp.bfloat16)
    pair_grad_heads = pair_grads[:, :, None]
    query_back, slot_back = (
        lax.all_to_all(query_grad_heads, "uly", split_axis=0, concat_axis=2, tiled=True),
        lax.all_to_all(pair_grad_heads, "uly", split_axis=0, concat_axis=2, tiled=True),
    )
    slot_float = slot_back.astype(jnp.float32)
    merged = []
    for head in range(KV_HEADS):
        chosen = [slot_float[:, :, u] for u in range(uly_size) if slot_heads[u] == head]
        merged.append(reduce(jnp.add, chosen))
    paired_grad = jnp.stack(merged, axis=2)
    keys_grad = unrotate(paired_grad[:, :, :, 0], cosine, sine)
    values_grad = paired_grad[:, :, :, 1]
    query_grad = unrotate(query_back.astype(jnp.float32), cosine, sine)
    mixed_grad = jnp.concatenate(
        [
            query_grad.reshape(local_rows, seqs, width),
            keys_grad.reshape(local_rows, seqs, side),
            values_grad.reshape(local_rows, seqs, side),
        ],
        axis=-1,
    )
    mixed_grad = mixed_grad.reshape(local_rows * seqs, -1).astype(jnp.bfloat16)
    grad_bias = jnp.sum(mixed_grad.astype(jnp.float32), axis=0)
    grad_qkv = contract_rows(normed, mixed_grad)
    normed_grad = contract_cols(mixed_grad, qkv_full)
    rows_part, grad_gain_one = norm_back(
        normed_grad, unit_one, factor_one, gain_one.astype(jnp.float32)
    )
    grad_tokens = (hidden_grad + rows_part).reshape(local_rows, seqs, -1)
    attn_shares = (
        lax.psum_scatter(grad_gain_one, ("blk", "uly"), scatter_dimension=0, tiled=True),
        lax.psum_scatter(grad_qkv, ("blk", "uly"), scatter_dimension=0, tiled=True),
        lax.psum_scatter(grad_bias, ("blk", "uly"), scatter_dimension=0, tiled=True),
        lax.psum_scatter(grad_out_w, ("blk", "uly"), scatter_dimension=0, tiled=True),
        lax.psum_scatter(grad_gain_two, ("blk", "uly"), scatter_dimension=0, tiled=True),
    )
    return (
        output,
        grad_tokens,
        attn_shares[0],
        attn_shares[1],
        attn_shares[2],
        attn_shares[3],
        attn_shares[4],
        ffn_shares[0],
        ffn_shares[1],
        ffn_shares[2],
    )


def solution(mesh):
    in_specs = (
        P(("blk", "uly"), None, None),
        P(),
        P(("blk", "uly")),
        P(("blk", "uly"), None),
        P(("blk", "uly")),
        P(("blk", "uly"), None),
        P("blk"),
        P("blk", "uly"),
        P("blk", "uly"),
        P("uly", "blk"),
        P(("blk", "uly"), None, None),
    )
    out_specs = (
        P(("blk", "uly"), None, None),
        P(("blk", "uly"), None, None),
        P(("blk", "uly")),
        P(("blk", "uly"), None),
        P(("blk", "uly")),
        P(("blk", "uly"), None),
        P(("blk", "uly")),
        P("blk", "uly"),
        P("blk", "uly"),
        P("uly", "blk"),
    )
    return jax.shard_map(
        per_device, mesh=mesh, in_specs=in_specs, out_specs=out_specs, check_vma=False
    )
```

profile of v0, /device:TPU:0, one launch (start us, length us, event | category | flops | bytes accessed | tf_op | source)
XLA Modules:
  0.0 2442.0 jit_solution(13567965745597081703)
XLA Ops:
  11.7 42.6 %all-reduce.7 = (bf16[2048]{0:T(1024)(128)(2,1)S(1)}, bf16[1536]{0:T(1024)(128)(2,1)S(1)}) all-reduce(bf16[2048]{0:T(1024)(128)(2,1)S(1)} %dynamic-update-slice.1, bf16[1536]{0:T(1024)(128)(2,1)S(1)} %dynamic-update-slice), channel_id=1, replica_groups=mesh['blk'=8,'uly'=4] {'blk','uly'}, use_global_device_ids=true, to_apply=%add.1 | all-reduce | flops 3584 | bytes 14336
  56.2 27.1 %all-gather.10.cloned.1.call-done = bf16[1536,2048]{1,0:T(8,128)(2,1)} async-done(((bf16[48,2048]{1,0:T(8,128)(2,1)}), bf16[1536,2048]{1,0:T(8,128)(2,1)}) %all-gather.10.cloned.1.call-update) | async-done | bytes 6291472 | tf_op jit(solution)/shard_map/all_gather | solution.py:103
  83.4 3.8 convolution_add_fusion.3
  89.3 8.6 all_to_all.84
  99.2 93.7 %all-gather.16.cloned.1.call-done = bf16[1536,2240]{1,0:T(8,128)(2,1)} async-done(((bf16[192,2240]{1,0:T(8,128)(2,1)}), bf16[1536,2240]{1,0:T(8,128)(2,1)}) %all-gather.16.cloned.1.call-update) | async-done | bytes 6881296 | tf_op jit(solution)/shard_map/all_gather | solution.py:179
  192.9 10.3 copy.201
  203.3 98.8 %all-gather.20.cloned.1.call-done = bf16[1536,2240]{1,0:T(8,128)(2,1)} async-done(((bf16[192,2240]{1,0:T(8,128)(2,1)}), bf16[1536,2240]{1,0:T(8,128)(2,1)}) %all-gather.20.cloned.1.call-update) | async-done | bytes 6881296 | tf_op jit(solution)/shard_map/all_gather | solution.py:180
  302.1 10.3 copy.202
  312.5 98.6 %all-gather.24.cloned.1.call-done = bf16[2240,1536]{0,1:T(8,128)(2,1)} async-done(((bf16[2240,192]{0,1:T(8,128)(2,1)}), bf16[2240,1536]{0,1:T(8,128)(2,1)}) %all-gather.24.cloned.1.call-update) | async-done | bytes 6881296 | tf_op jit(solution)/shard_map/all_gather | solution.py:181
  411.1 10.2 copy.203
  424.3 3.7 all-to-all-start.1
  428.6 6.8 all-to-all-done.1
  435.4 25.8 %all-gather.12.cloned.1.call-done = bf16[2048,2,2,128]{3,0,2,1:T(8,128)(2,1)} async-done(((bf16[256,2,2,128]{3,0,2,1:T(8,128)(2,1)}), bf16[2048,2,2,128]{3,0,2,1:T(8,128)(2,1)}) %all-gather.12.cloned.1.call-update) | async-done | bytes 2097168 | tf_op jit(solution)/shard_map/all_gather | solution.py:133
  461.2 3.1 copy.198
  464.8 54.1 %while.32 = (s32[]{:T(128)}, f32[2,3,256,128]{3,2,1,0:T(8,128)}, f32[2,3,256]{2,1,0:T(4,128)S(1)}, f32[2,3,256]{2,1,0:T(4,128)}, s32[4]{0:T(128)}, /*index=5*/s3...) while((s32[]{:T(128)}, f32[2,3,256,128]{3,2,1,0:T(8,128)}, ...), condition=%wide.region_7.8_spmd.clone, body=%wide.region_3.7_spmd.clone.sunk | while | flops 413788672 | bytes 13119855 | solution.py:167
  488.0 3.4 fusion.122
  501.8 3.4 fusion.122
  515.5 3.4 fusion.122
  521.5 3.5 all-to-all-start.2
  527.8 18.9 all-reduce.2
  549.2 3.8 multiply_reduce_fusion.5
  553.1 141.3 %all-gather.18.cloned.1.call-done = bf16[1536,8960]{0,1:T(8,128)(2,1)} async-done(((bf16[1536,2240]{0,1:T(8,128)(2,1)}), bf16[1536,8960]{0,1:T(8,128)(2,1)}) %all-gather.18.cloned.1.call-update) | async-done | bytes 27525136 | tf_op jit(solution)/shard_map/all_gather | solution.py:188
  694.4 17.4 fusion.65
  711.8 152.1 %all-gather.22.cloned.1.call-done = bf16[1536,8960]{0,1:T(8,128)(2,1)} async-done(((bf16[1536,2240]{0,1:T(8,128)(2,1)}), bf16[1536,8960]{0,1:T(8,128)(2,1)}) %all-gather.22.cloned.1.call-update) | async-done | bytes 27525136 | tf_op jit(solution)/shard_map/all_gather | solution.py:189
  863.9 16.7 fusion.66
  880.6 152.8 %all-gather.26.cloned.1.call-done = bf16[8960,1536]{1,0:T(8,128)(2,1)} async-done(((bf16[2240,1536]{1,0:T(8,128)(2,1)}), bf16[8960,1536]{1,0:T(8,128)(2,1)}) %all-gather.26.cloned.1.call-update) | async-done | bytes 27525136 | tf_op jit(solution)/shard_map/all_gather | solution.py:190
  1033.4 17.5 multiply_convert_fusion
  1050.9 15.0 convolution_convert_fusion.2
  1066.0 20.2 convolution_convert_fusion.1
  1086.3 18.1 convolution_convert_fusion
  1104.4 12.8 fusion.67
  1117.2 12.1 multiply_reduce_fusion
  1134.3 3.5 all-to-all-start.3
  1138.4 11.3 all-to-all-done.3
  1152.5 64.8 %while.33 = (s32[]{:T(128)}, f32[2,3,256,128]{3,2,1,0:T(8,128)S(1)}, bf16[4,512,2,2,128]{4,1,0,3,2:T(8,128)(2,1)}, s32[4]{0:T(128)}, s32[2,16]{1,0:T(2,128)}, /*...) while((s32[]{:T(128)}, ...), condition=%wide.region_13.14_spmd.clone, body=%wide.region_11.13_spmd.clone.sunk | while | flops 1015925760 | bytes 34165208 | solution.py:278
  1154.6 3.3 fusion.130
  1160.3 3.2 fusion.131
  1171.0 3.3 fusion.130
  1176.7 3.1 fusion.131
  1187.0 3.3 fusion.130
  1192.7 3.2 fusion.131
  1203.1 3.3 fusion.130
  1208.8 3.2 fusion.131
  1217.4 48.8 %reduce-scatter.22.cloned.1.call-done = bf16[1536,2240]{0,1:T(8,128)(2,1)} async-done(((bf16[1536,8960]{0,1:T(8,128)(2,1)}), bf16[1536,2240]{0,1:T(8,128)(2,1)}) %reduce-scatter.22.cloned.1.call-update) | async-done | bytes 6881296 | tf_op jit(solution)/shard_map/reduce_scatter | solution.py:208
  1266.1 9.7 copy.235
  1275.9 188.9 %reduce-scatter.24.cloned.1.call-done = bf16[1536,2240]{0,1:T(8,128)(2,1)} async-done(((bf16[1536,8960]{0,1:T(8,128)(2,1)}), bf16[1536,2240]{0,1:T(8,128)(2,1)}) %reduce-scatter.24.cloned.1.call-update) | async-done | bytes 6881296 | tf_op jit(solution)/shard_map/reduce_scatter | solution.py:211
  1464.8 10.4 copy.237
  1475.2 187.9 %reduce-scatter.26.cloned.1.call-done = bf16[2240,1536]{1,0:T(8,128)(2,1)} async-done(((bf16[8960,1536]{1,0:T(8,128)(2,1)}), bf16[2240,1536]{1,0:T(8,128)(2,1)}) %reduce-scatter.26.cloned.1.call-update) | async-done | bytes 6881296 | tf_op jit(solution)/shard_map/reduce_scatter | solution.py:214
  1663.1 9.7 copy.239
  1674.0 4.9 fusion.47
  1680.2 3.6 all-to-all-start.4
  1683.8 7.3 all-to-all-done.4
  1695.7 39.6 %reduce-scatter.16.cloned.1.call-done = bf16[256,2,2,128]{3,0,2,1:T(8,128)(2,1)} async-done(((bf16[2048,2,2,128]{3,0,2,1:T(8,128)(2,1)}), bf16[256,2,2,128]{3,0,2,1:T(8,128)(2,1)}) %reduce-scatter.16.cloned.1.call-update) | async-done | bytes 262160 | tf_op jit(solution)/shard_map/reduce_scatter | solution.py:284
  1737.1 3.4 all-to-all-start.5
  1742.7 3.9 all-to-all-done.5
  1747.4 6.4 fusion.59
  1753.8 13.4 fusion.39
  1768.2 5.1 multiply_reduce_fusion.1
  1775.1 41.0 %all-reduce.6 = (f32[1536]{0:T(1024)S(1)}, f32[2048]{0:T(1024)S(1)}, f32[1536]{0:T(1024)S(1)}) all-reduce(f32[1536]{0:T(1024)S(1)} %get-tuple-element.472, f32[2048]{0:T(1024)S(1)} %convert_reduce_fusion, f32[1536]{0:T(1024)S(1)} %copy-done.27), channel_id=3, replica_groups=mesh['blk'=8,'uly'=4] {'blk','uly'}, use_global_device_ids=true, to_apply=%region_17.18.clone | all-reduce | flops 5120 | bytes 40960
  1817.9 50.2 %reduce-scatter.28.cloned.1.call-done = bf16[192,2240]{1,0:T(8,128)(2,1)} async-done(((bf16[1536,2240]{1,0:T(8,128)(2,1)}), bf16[192,2240]{1,0:T(8,128)(2,1)}) %reduce-scatter.28.cloned.1.call-update) | async-done | bytes 860176
  1871.5 128.3 %reduce-scatter.30.cloned.1.call-done = bf16[192,2240]{1,0:T(8,128)(2,1)} async-done(((bf16[1536,2240]{1,0:T(8,128)(2,1)}), bf16[192,2240]{1,0:T(8,128)(2,1)}) %reduce-scatter.30.cloned.1.call-update) | async-done | bytes 860176
  2003.1 128.7 %reduce-scatter.32.cloned.1.call-done = bf16[192,2240]{1,0:T(8,128)(2,1)} async-done(((bf16[1536,2240]{1,0:T(8,128)(2,1)}), bf16[192,2240]{1,0:T(8,128)(2,1)}) %reduce-scatter.32.cloned.1.call-update) | async-done | bytes 860176
  2135.2 137.4 %reduce-scatter.20.cloned.1.call-done = f32[48,1536]{1,0:T(8,128)} async-done(((f32[1536,1536]{1,0:T(8,128)}), f32[48,1536]{1,0:T(8,128)}) %reduce-scatter.20.cloned.1.call-update) | async-done | bytes 294928 | tf_op jit(solution)/shard_map/reduce_scatter | solution.py:322
  2272.6 162.1 %reduce-scatter.18.cloned.1.call-done = f32[48,2048]{1,0:T(8,128)} async-done(((f32[1536,2048]{1,0:T(8,128)}), f32[48,2048]{1,0:T(8,128)}) %reduce-scatter.18.cloned.1.call-update) | async-done | bytes 393232 | tf_op jit(solution)/shard_map/reduce_scatter | solution.py:320
  (323 shorter events, 133.2 us)
Async XLA Ops:
  7.2 47.1 %copy-start.17 = (bf16[64,2,1536]{2,1,0:T(2,128)(2,1)S(1)}, bf16[64,2,1536]{2,1,0:T(2,128)(2,1)}, u32[]{:S(2)}) copy-start(bf16[64,2,1536]{2,1,0:T(2,128)(2,1)} %param.15) | copy-start | bytes 1179652
  7.2 4.0 copy-start.31
  7.2 4.3 copy-start.32
  7.2 76.1 %all-gather.10.cloned.1.call-start = ((), (), s32[]{:S(2)}) async-start(), calls=%async_computation.15 | async-start | bytes 6488064 | tf_op jit(solution)/shard_map/all_gather | solution.py:103
  7.9 184.9 %all-gather.16.cloned.1.call-start = ((), (), s32[]{:S(2)}) async-start(), calls=%async_computation.18 | async-start | bytes 7962624 | tf_op jit(solution)/shard_map/all_gather | solution.py:179
  8.7 293.4 %all-gather.20.cloned.1.call-start = ((), (), s32[]{:S(2)}) async-start(), calls=%async_computation.20 | async-start | bytes 7962624 | tf_op jit(solution)/shard_map/all_gather | solution.py:180
  9.4 401.7 %all-gather.24.cloned.1.call-start = ((), (), s32[]{:S(2)}) async-start(), calls=%async_computation.22 | async-start | bytes 7962624 | tf_op jit(solution)/shard_map/all_gather | solution.py:181
  10.0 451.2 %all-gather.12.cloned.1.call-start = ((), (), s32[]{:S(2)}) async-start(), calls=%async_computation.16 | async-start | bytes 2359296 | tf_op jit(solution)/shard_map/all_gather | solution.py:133
  11.2 76.0 %copy-start.1 = (f32[128,1536]{1,0:T(8,128)}, f32[128,1536]{1,0:T(8,128)S(1)}, u32[]{:S(2)}) copy-start(f32[128,1536]{1,0:T(8,128)S(1)} %reshape.493) | copy-start | bytes 2359300
  54.3 29.1 %copy-start.25 = (f32[1536]{0:T(1024)}, f32[1536]{0:T(1024)S(1)}, u32[]{:S(2)}) copy-start(f32[1536]{0:T(1024)S(1)} %convert_element_type.178) | copy-start | bytes 18436
  54.9 28.4 %copy-start.28 = (f32[128]{0:T(128)}, f32[128]{0:T(128)S(1)}, u32[]{:S(2)}) copy-start(f32[128]{0:T(128)S(1)} %rsqrt.20) | copy-start | bytes 1540
  56.2 366.7 %copy-start.15 = (f32[64,2,128]{2,0,1:T(8,128)}, f32[64,2,128]{2,0,1:T(8,128)S(1)}, u32[]{:S(2)}) copy-start(f32[64,2,128]{2,0,1:T(8,128)S(1)} %get-tuple-element.543) | copy-start | bytes 196612
  56.2 366.7 %copy-start.22 = (f32[64,2,128]{2,0,1:T(8,128)}, f32[64,2,128]{2,0,1:T(8,128)S(1)}, u32[]{:S(2)}) copy-start(f32[64,2,128]{2,0,1:T(8,128)S(1)} %get-tuple-element.542) | copy-start | bytes 196612
  98.6 450.6 %all-gather.14.cloned.1.call-start = ((), (), s32[]{:S(2)}) async-start(), calls=%async_computation.17 | async-start | bytes 4866048 | tf_op jit(solution)/shard_map/all_gather | solution.py:105
  99.2 595.3 %all-gather.18.cloned.1.call-start = ((), (), s32[]{:S(2)}) async-start(), calls=%async_computation.19 | async-start | bytes 34406400 | tf_op jit(solution)/shard_map/all_gather | solution.py:188
  203.2 660.7 %all-gather.22.cloned.1.call-start = ((), (), s32[]{:S(2)}) async-start(), calls=%async_computation.21 | async-start | bytes 34406400 | tf_op jit(solution)/shard_map/all_gather | solution.py:189
  312.4 720.9 %all-gather.26.cloned.1.call-start = ((), (), s32[]{:S(2)}) async-start(), calls=%async_computation.23 | async-start | bytes 34406400 | tf_op jit(solution)/shard_map/all_gather | solution.py:190
  424.3 11.1 all-to-all-start.1
  518.9 30.3 %copy-start.2 = (f32[128,1536]{1,0:T(8,128)S(1)}, f32[128,1536]{1,0:T(8,128)}, u32[]{:S(2)}) copy-start(f32[128,1536]{1,0:T(8,128)} %copy-done.1) | copy-start | bytes 2359300
  521.5 27.1 %all-to-all-start.2 = ((bf16[256,2,3,128]{3,1,2,0:T(2,128)(2,1)}), bf16[256,2,3,128]{3,1,2,0:T(2,128)(2,1)S(1)}, u32[]{:S(2)}, u32[]{:S(2)}) async-start(bf16[256,2,3,128]{3,1,2,0:T(2,128)(2,1)} %copy.199), calls=%async_computation.2 | async-start | bytes 786432 | tf_op jit(solution)/shard_map/all_to_all | solution.py:173
  525.0 741.1 %reduce-scatter.22.cloned.1.call-start = ((), (), s32[]{:S(2)}) async-start(), calls=%async_computation.27 | async-start | bytes 34406400 | tf_op jit(solution)/shard_map/reduce_scatter | solution.py:208
  549.2 3.8 copy-start.10
  553.1 310.8 %copy-start.7 = (bf16[128,1536]{1,0:T(8,128)(2,1)}, bf16[128,1536]{1,0:T(8,128)(2,1)S(1)}, u32[]{:S(2)}) copy-start(bf16[128,1536]{1,0:T(8,128)(2,1)S(1)} %multiply_convert_fusion.3) | copy-start | bytes 1179652
  1050.9 35.3 %copy-start.4 = (bf16[128,8960]{1,0:T(8,128)(2,1)}, bf16[128,8960]{1,0:T(8,128)(2,1)S(1)}, u32[]{:S(2)}) copy-start(bf16[128,8960]{1,0:T(8,128)(2,1)S(1)} %get-tuple-element.531) | copy-start | bytes 6881284
  1065.9 398.9 %reduce-scatter.24.cloned.1.call-start = ((), (), s32[]{:S(2)}) async-start(), calls=%async_computation.28 | async-start | bytes 34406400 | tf_op jit(solution)/shard_map/reduce_scatter | solution.py:211
  1086.2 576.9 %reduce-scatter.26.cloned.1.call-start = ((), (), s32[]{:S(2)}) async-start(), calls=%async_computation.29 | async-start | bytes 34406400 | tf_op jit(solution)/shard_map/reduce_scatter | solution.py:214
  1104.3 12.8 copy-start.8
  1104.4 25.2 %slice-start = ((s8[4718592]{0:T(1024)(128)(4,1)}), s8[4194304]{0:T(1024)(128)(4,1)S(1)}, s32[]{:S(2)}) async-start(s8[4718592]{0:T(1024)(128)(4,1)} %bitcast.253), calls=%async_computation.33 | async-start | bytes 8388608
  1117.1 12.1 copy-start.13
  1117.2 12.4 slice-start.1
  1129.5 3.8 copy-start.5
  1129.5 8.3 copy-start.24
  1132.0 18.5 copy-start.14
  1134.3 15.4 all-to-all-start.3
  1137.7 597.5 %reduce-scatter.16.cloned.1.call-start = ((), (), s32[]{:S(2)}) async-start(), calls=%async_computation.24 | async-start | bytes 2359296 | tf_op jit(solution)/shard_map/reduce_scatter | solution.py:284
  1152.7 7.6 copy-start.30
  1163.5 2.3 copy-start
  1163.5 2.3 copy-start.9
  1169.1 7.6 copy-start.30
  1179.8 2.0 copy-start
  1179.8 2.0 copy-start.9
  1185.1 7.6 copy-start.30
  1195.9 2.0 copy-start
  1195.9 2.0 copy-start.9
  1201.2 7.6 copy-start.30
  1212.0 2.0 copy-start
  1212.0 2.0 copy-start.9
  1217.3 650.8 %reduce-scatter.28.cloned.1.call-start = ((), (), s32[]{:S(2)}) async-start(), calls=%async_computation.30 | async-start | bytes 7962624
  1275.9 723.9 %reduce-scatter.30.cloned.1.call-start = ((), (), s32[]{:S(2)}) async-start(), calls=%async_computation.31 | async-start | bytes 7962624
  1475.2 656.6 %reduce-scatter.32.cloned.1.call-start = ((), (), s32[]{:S(2)}) async-start(), calls=%async_computation.32 | async-start | bytes 7962624
  1672.8 599.8 %reduce-scatter.20.cloned.1.call-start = ((), (), s32[]{:S(2)}) async-start(), calls=%async_computation.26 | async-start | bytes 9732096 | tf_op jit(solution)/shard_map/reduce_scatter | solution.py:322
  1678.9 4.8 copy-start.23
  1680.2 12.7 copy-start.16
  1680.2 11.0 all-to-all-start.4
  1737.1 9.4 all-to-all-start.5
  1740.6 694.1 %reduce-scatter.18.cloned.1.call-start = ((), (), s32[]{:S(2)}) async-start(), calls=%async_computation.25 | async-start | bytes 12976128 | tf_op jit(solution)/shard_map/reduce_scatter | solution.py:320
  1742.7 4.7 copy-start.3
  1742.7 4.7 copy-start.26
  1742.7 4.7 copy-start.29
  1746.8 21.4 copy-start.20
  1747.4 20.8 copy-start.18
  1773.3 1.6 copy-start.19
  1773.4 1.6 copy-start.21
  1773.4 1.7 copy-start.27
  (3 other events, 3.8 us)
Sparse Core Ops, SparseCore 0:
  10.9 72.3 all-gather.9
  85.5 107.2 all-gather.15
  195.1 106.9 all-gather.19
  304.1 106.9 all-gather.23
  413.7 47.4 all-gather.11
  464.0 62.0 all-gather.13
  527.7 166.7 all-gather.17
  696.0 167.8 all-gather.21
  865.5 167.8 all-gather.25
  1066.0 200.0 reduce-scatter.21
  1268.9 195.8 reduce-scatter.23
  1467.2 195.8 reduce-scatter.25
  1667.1 68.1 reduce-scatter.15
  1739.2 128.8 reduce-scatter.27
  1871.6 128.0 reduce-scatter.29
  2003.7 128.0 reduce-scatter.31
  2138.1 134.4 reduce-scatter.19
  2280.1 154.5 reduce-scatter.17
where the time goes:
time: 2450 us; the launch traced here: 2440 us
  waiting for transfers between devices  1890 us (77%)
  matrix products  235 us (10%)
  local copies, waits for them, and re-layouts  111 us (5%)
  blocking collectives  111 us (5%)
  other arithmetic  49.8 us (2%)
    unnamed x21, waiting for transfers between devices  310 us
    reduce_scatter x1, waiting for transfers between devices, per_device(): lax.psum_scatter(grad_upper.astype(jnp.bfloat16), 'uly', scatter_dimensio...  189 us
    reduce_scatter x1, waiting for transfers between devices, per_device(): lax.psum_scatter(grad_down.astype(jnp.bfloat16), 'uly', scatter_dimension...  188 us
    reduce_scatter x1, waiting for transfers between devices, per_device(): lax.psum_scatter(grad_qkv, ('blk', 'uly'), scatter_dimension=0, tiled=True)  162 us
    all_gather x1, waiting for transfers between devices, per_device(): lax.all_gather(down_part, 'uly', axis=0, tiled=True)  153 us
    all_gather x1, waiting for transfers between devices, per_device(): lax.all_gather(upper_part, 'uly', axis=1, tiled=True)  152 us
    all_gather x1, waiting for transfers between devices, per_device(): lax.all_gather(gate_part, 'uly', axis=1, tiled=True)  141 us
    reduce_scatter x1, waiting for transfers between devices, per_device(): lax.psum_scatter(grad_out_w, ('blk', 'uly'), scatter_dimension=0, tiled=T...  137 us
  transfers between devices with their start and end apart: 23, of which 21 were waited for; matrix products, arithmetic and copies ran while one was open for 15% of the time, Pallas kernels for 0%

commit v1 on v0

v1 whole, which is shorter than its diff:
```python
import math

import jax
import jax.numpy as jnp
from jax import lax
from jax.sharding import PartitionSpec as P

HEADS = 12
KV_HEADS = 2
HEAD_DIM = 128
SPAN = 128
PAIR = 2


EPS = 1e-06
THETA = 1000000.0
FLOOR = -1e30
BF16 = jnp.bfloat16
F32 = jnp.float32


def norm_rows(rows):
    factor = lax.rsqrt(jnp.mean(rows * rows, axis=-1, keepdims=True) + EPS)
    return (rows * factor, factor)


def norm_back(scaled, unit, factor):
    return factor * (scaled - unit * jnp.mean(scaled * unit, axis=-1, keepdims=True))


def matmul(left, right):
    return jnp.dot(left, right, preferred_element_type=F32)


def contract_rows(left, right):
    return lax.dot_general(left, right, (((0,), (0,)), ((), ())), preferred_element_type=F32)


def contract_cols(left, right):
    return lax.dot_general(left, right, (((1,), (1,)), ((), ())), preferred_element_type=F32)


def positions(order, rows):
    table = jnp.arange(order.shape[1], dtype=jnp.int32)
    slots = rows // SPAN
    picked = jnp.where(slots[None, :, None] == table[None, None, :], order[:, None, :], 0)
    return jnp.sum(picked, axis=-1) * SPAN + (rows % SPAN)[None, :]


def rope_tables(places):
    index = jnp.arange(HEAD_DIM // 2).astype(F32)
    freq = THETA ** (-2.0 * index / HEAD_DIM)
    angle = places.astype(F32)[..., None] * freq
    angle = jnp.concatenate([angle, angle], axis=-1)
    return (jnp.cos(angle), jnp.sin(angle))


def rotate(field, cosine, sine):
    half = field.shape[-1] // 2
    turned = jnp.concatenate([-field[..., half:], field[..., :half]], axis=-1)
    return field * cosine + turned * sine


def unrotate(grad, cosine, sine):
    half = grad.shape[-1] // 2
    moved = grad * sine
    return grad * cosine + jnp.concatenate([moved[..., half:], -moved[..., :half]], axis=-1)


class Grid:
    def __init__(self):
        self.blocks = lax.axis_size("blk")
        self.ulys = lax.axis_size("uly")
        self.depth = self.blocks // PAIR
        self.b = lax.axis_index("blk")
        self.u = lax.axis_index("uly")
        self.z = self.b // PAIR
        self.x = self.b % PAIR
        self.y = self.u // 2
        self.c = self.u % 2

    def to_z(self, value, step):
        pairs = [
            (z * PAIR + x, ((z + step) % self.depth) * PAIR + x)
            for z in range(self.depth)
            for x in range(PAIR)
        ]
        return lax.ppermute(value, "blk", pairs)

    def swap_x(self, value):
        return lax.ppermute(value, "blk", [(i, i ^ 1) for i in range(self.blocks)])

    def swap_y(self, value):
        return lax.ppermute(value, "uly", [(i, i ^ 2) for i in range(self.ulys)])

    def swap_core(self, value):
        return lax.ppermute(value, "uly", [(i, i ^ 1) for i in range(self.ulys)])


def paired(bit, mine, other, axis):
    low = jnp.where(bit == 0, mine, other)
    high = jnp.where(bit == 0, other, mine)
    return jnp.stack([low, high], axis=axis)


def pick(bit, array, axis):
    low = lax.index_in_dim(array, 0, axis, keepdims=False)
    high = lax.index_in_dim(array, 1, axis, keepdims=False)
    return jnp.where(bit == 0, low, high), jnp.where(bit == 0, high, low)


def order_z(grid, pieces):
    stacked = jnp.stack(pieces[::-1] + pieces[::-1][:-1])
    start = (grid.depth - 1 - grid.z) % grid.depth
    return lax.dynamic_slice_in_dim(stacked, start, grid.depth, 0)


def gather_uly(grid, value):
    both = paired(grid.y, value, grid.swap_y(value), 0)
    every = paired(grid.c, both, grid.swap_core(both), 1)
    return every.reshape((grid.ulys,) + value.shape)


def scatter_uly(grid, parts, kind=BF16):
    parts = parts.reshape((2, 2) + parts.shape[1:])
    keep, send = pick(grid.c, parts, 1)
    both = keep.astype(F32) + grid.swap_core(send.astype(kind)).astype(F32)
    keep, send = pick(grid.y, both, 0)
    return keep + grid.swap_y(send.astype(kind)).astype(F32)


def gather_blk(grid, value):
    pieces = [value] + [grid.to_z(value, d) for d in range(1, grid.depth)]
    pairs = [paired(grid.x, piece, grid.swap_x(piece), 0) for piece in pieces]
    return order_z(grid, pairs)


def exchange_z(grid, parts):
    pieces = [lax.dynamic_index_in_dim(parts, grid.z, 0, keepdims=False)]
    for d in range(1, grid.depth):
        there = (grid.z + d) % grid.depth
        pieces.append(grid.to_z(lax.dynamic_index_in_dim(parts, there, 0, keepdims=False), d))
    return pieces


def scatter_blk(grid, parts):
    keep, send = pick(grid.x, parts, 1)
    both = keep.astype(F32) + grid.swap_x(send.astype(BF16)).astype(F32)
    pieces = exchange_z(grid, both.astype(BF16))
    return sum(piece.astype(F32) for piece in pieces)


def exchange_uly(parts):
    return lax.all_to_all(parts, "uly", split_axis=0, concat_axis=0, tiled=True)


def per_device(
    tokens,
    span_order,
    attn_gain,
    qkv_weight,
    qkv_bias,
    out_weight,
    ffn_gain,
    gate_weight,
    up_weight,
    down_weight,
    cotangent,
):
    grid = Grid()
    local_rows, seqs, model = tokens.shape
    count = local_rows * seqs
    ulys = grid.ulys
    depth = grid.depth
    cycle_rows = local_rows * ulys
    group = HEADS // ulys
    factor = 1.0 / math.sqrt(HEAD_DIM)
    width = group * HEAD_DIM
    columns = width + HEAD_DIM
    shard = qkv_weight.shape[0]
    cycle_start = grid.b * cycle_rows
    head_rows = cycle_start + jnp.arange(cycle_rows, dtype=jnp.int32)
    query_places = positions(span_order, head_rows)

    gain_one = attn_gain.astype(F32)[:, None]
    scaled = (qkv_weight.astype(F32) * gain_one).astype(BF16)
    side = HEADS * HEAD_DIM

    def by_uly(array):
        lead = array.shape[0]
        heads = array[:, :side].reshape(lead, ulys, width)
        kinds = array[:, side:].reshape(lead, 2, KV_HEADS, HEAD_DIM)
        kinds = jnp.transpose(kinds, (0, 2, 1, 3)).reshape(lead, ulys, HEAD_DIM)
        return jnp.transpose(jnp.concatenate([heads, kinds], axis=-1), (1, 0, 2))

    def from_uly(array):
        lead = array.shape[1]
        heads = jnp.transpose(array[..., :width], (1, 0, 2)).reshape(lead, side)
        kinds = array[..., width:].reshape(KV_HEADS, 2, lead, HEAD_DIM)
        kinds = jnp.transpose(kinds, (2, 1, 0, 3)).reshape(lead, 2 * KV_HEADS * HEAD_DIM)
        return jnp.concatenate([heads, kinds], axis=-1)

    block_rows = exchange_uly(by_uly(scaled)).reshape(ulys * shard, columns)
    qkv_part = gather_blk(grid, block_rows).reshape(model, columns)
    bias_full = lax.all_gather(qkv_bias, ("blk", "uly"), axis=0, tiled=True)
    bias = lax.dynamic_index_in_dim(by_uly(bias_full[None]), grid.u, 0, keepdims=False)

    rows = tokens.astype(F32).reshape(count, model)
    unit_one, factor_one = norm_rows(rows)
    units = gather_uly(grid, unit_one.astype(BF16)).reshape(ulys * count, model)
    mixed = (matmul(units, qkv_part) + bias.astype(F32)).reshape(cycle_rows, seqs, columns)

    cosine, sine = rope_tables(query_places.T)
    cosine = cosine[:, :, None, :]
    sine = sine[:, :, None, :]
    query = rotate(
        mixed[..., :width].reshape(cycle_rows, seqs, group, HEAD_DIM), cosine, sine
    ).astype(BF16)
    is_key = grid.c == 0
    kind_cosine = jnp.where(is_key, cosine, 1.0)
    kind_sine = jnp.where(is_key, sine, 0.0)
    kind = rotate(mixed[:, :, None, width:], kind_cosine, kind_sine)[:, :, 0].astype(BF16)
    kinds = gather_blk(grid, kind).reshape(grid.blocks * cycle_rows, seqs, HEAD_DIM)
    pairs_all = paired(grid.c, kinds, grid.swap_core(kinds), 2)
    query_t = jnp.transpose(query, (1, 2, 0, 3))
    total_rows = pairs_all.shape[0]
    size = math.gcd(total_rows, 4 * SPAN)

    out_rows = gather_blk(grid, out_weight).reshape(ulys, grid.blocks // ulys, shard, model)
    out_part = jnp.transpose(exchange_uly(out_rows), (1, 0, 2, 3)).reshape(width, model)

    gain_two = ffn_gain.astype(F32)[:, None]
    hidden_units = gate_weight.shape[1] // depth

    def by_z(array):
        return jnp.transpose(array.reshape(array.shape[0], depth, hidden_units), (1, 0, 2))

    tiles = jnp.stack(
        [
            by_z((gate_weight.astype(F32) * gain_two).astype(BF16)),
            by_z((up_weight.astype(F32) * gain_two).astype(BF16)),
            by_z(down_weight.T),
        ],
        axis=1,
    )
    tile_pieces = exchange_z(grid, tiles)
    tile_pairs = [paired(grid.x, piece, grid.swap_x(piece), 0) for piece in tile_pieces]
    ffn_weights = order_z(grid, tile_pairs)
    ffn_weights = jnp.transpose(ffn_weights, (2, 0, 1, 3, 4)).reshape(3, model, hidden_units)
    gate_used, upper_used, down_used = ffn_weights[0], ffn_weights[1], ffn_weights[2]

    def spread(value):
        chunks = []
        for d in range(depth):
            piece = value if d == 0 else grid.to_z(value, d)
            both = jnp.concatenate([piece, grid.swap_y(piece)], axis=0)
            chunks.append(jnp.concatenate([both, grid.swap_core(both)], axis=0))
        return chunks

    def collect(chunks):
        total = None
        for d, chunk in enumerate(chunks):
            chunk = chunk.reshape(2, 2, count, model)
            both = chunk[0].astype(F32) + grid.swap_core(chunk[1].astype(BF16)).astype(F32)
            part = both[0] + grid.swap_y(both[1].astype(BF16)).astype(F32)
            if d > 0:
                part = grid.to_z(part.astype(BF16), -d).astype(F32)
            total = part if total is None else total + part
        return total

    cot_flat = cotangent.reshape(count, model)
    cot_chunks = spread(cot_flat)

    def forward_step(state, index):
        summed, peak, weight_sum = state
        offset = index * size
        block = lax.dynamic_slice_in_dim(pairs_all, offset, size, 0)
        key_places = positions(span_order, offset + jnp.arange(size, dtype=jnp.int32))
        scores = (
            jnp.einsum("shrd,ksd->shrk", query_t, block[:, :, 0], preferred_element_type=F32)
            * factor
        )
        allowed = key_places[:, None, None, :] <= query_places[:, None, :, None]
        scores = jnp.where(allowed, scores, FLOOR)
        new_peak = jnp.maximum(peak, jnp.max(scores, axis=-1))
        weights = jnp.where(allowed, jnp.exp(scores - new_peak[..., None]), 0.0)
        fade = jnp.exp(peak - new_peak)
        weight_sum = weight_sum * fade + jnp.sum(weights, axis=-1)
        summed = summed * fade[..., None] + jnp.einsum(
            "shrk,ksd->shrd",
            weights.astype(BF16),
            block[:, :, 1],
            preferred_element_type=F32,
        )
        return ((summed, new_peak, weight_sum), None)

    initial = (
        jnp.zeros((seqs, group, cycle_rows, HEAD_DIM), F32),
        jnp.full((seqs, group, cycle_rows), FLOOR, F32),
        jnp.zeros((seqs, group, cycle_rows), F32),
    )
    (summed, peak, weight_sum), unused = lax.scan(
        forward_step, initial, jnp.arange(total_rows // size, dtype=jnp.int32)
    )
    log_total = peak + jnp.log(weight_sum)
    result_t = (summed / weight_sum[..., None]).astype(BF16)
    attended = jnp.transpose(result_t, (2, 0, 1, 3)).reshape(cycle_rows * seqs, width)
    projected = matmul(attended, out_part).reshape(ulys, count, model)
    hidden = rows + scatter_uly(grid, projected)

    unit_two, factor_two = norm_rows(hidden)
    grad_rows = cotangent.astype(F32).reshape(count, model)
    mid_chunks = spread(unit_two.astype(BF16))

    actives, gate_grads, upper_grads, back_chunks = [], [], [], []
    for mid, cot in zip(mid_chunks, cot_chunks):
        gate = matmul(mid, gate_used)
        upper = matmul(mid, upper_used)
        sigmoid = jax.nn.sigmoid(gate)
        active_grad = matmul(cot, down_used)
        actives.append((gate * sigmoid * upper).astype(BF16))
        gate_grad = (active_grad * upper * sigmoid * (1.0 + gate * (1.0 - sigmoid))).astype(BF16)
        upper_grad = (active_grad * gate * sigmoid).astype(BF16)
        gate_grads.append(gate_grad)
        upper_grads.append(upper_grad)
        back_chunks.append(contract_cols(gate_grad, gate_used) + contract_cols(upper_grad, upper_used))
    mid_grad = collect(back_chunks)
    out_chunks = [contract_cols(active, down_used) for active in actives]
    result = hidden + collect(out_chunks)
    output = result.astype(BF16).reshape(local_rows, seqs, model)

    mid_all = jnp.concatenate(mid_chunks)
    cot_all = jnp.concatenate(cot_chunks)
    shares = jnp.stack(
        [
            contract_rows(mid_all, jnp.concatenate(gate_grads)).astype(BF16),
            contract_rows(mid_all, jnp.concatenate(upper_grads)).astype(BF16),
            contract_rows(cot_all, jnp.concatenate(actives)).astype(BF16),
        ]
    ).reshape(3, depth, PAIR, model // grid.blocks, hidden_units)
    keep, send = pick(grid.x, shares, 2)
    both = keep.astype(F32) + grid.swap_x(send).astype(F32)
    both = jnp.transpose(both, (1, 0, 2, 3)).astype(BF16)
    owned = order_z(grid, exchange_z(grid, both)).astype(F32)
    owned = jnp.transpose(owned, (1, 2, 0, 3)).reshape(3, model // grid.blocks, -1)
    grad_gate = owned[0] * gain_two
    grad_upper = owned[1] * gain_two
    grad_down = owned[2].T
    gain_part = jnp.sum(
        owned[0] * gate_weight.astype(F32) + owned[1] * up_weight.astype(F32), axis=-1
    )
    grad_gain_two = scatter_uly(grid, gain_part.reshape(ulys, -1), F32)

    hidden_grad = grad_rows + norm_back(mid_grad, unit_two, factor_two)
    branch_one = gather_uly(grid, hidden_grad.astype(BF16)).reshape(ulys * count, model)
    grad_heads = (
        contract_cols(branch_one, out_part)
        .astype(BF16)
        .reshape(cycle_rows, seqs, group, HEAD_DIM)
    )
    out_share = contract_rows(attended, branch_one).astype(BF16)
    out_share = out_share.reshape(grid.blocks // ulys, ulys, shard, model)
    out_share = exchange_uly(jnp.transpose(out_share, (1, 0, 2, 3)))
    grad_out = scatter_blk(grid, out_share.reshape(depth, PAIR, shard, model))

    grad_t = jnp.transpose(grad_heads, (1, 2, 0, 3))
    delta = jnp.sum(grad_t.astype(F32) * result_t.astype(F32), axis=-1)

    def backward_step(query_grad, index):
        offset = index * size
        block = lax.dynamic_slice_in_dim(pairs_all, offset, size, 0)
        key_places = positions(span_order, offset + jnp.arange(size, dtype=jnp.int32))
        scores = (
            jnp.einsum("shrd,ksd->shrk", query_t, block[:, :, 0], preferred_element_type=F32)
            * factor
        )
        allowed = key_places[:, None, None, :] <= query_places[:, None, :, None]
        probs = jnp.where(allowed, jnp.exp(scores - log_total[..., None]), 0.0)
        prob_grad = jnp.einsum(
            "shrd,ksd->shrk", grad_t, block[:, :, 1], preferred_element_type=F32
        )
        score_grad = (probs * (prob_grad - delta[..., None])).astype(BF16)
        query_grad = (
            query_grad
            + jnp.einsum("shrk,ksd->shrd", score_grad, block[:, :, 0], preferred_element_type=F32)
            * factor
        )
        key_grad = (
            jnp.einsum("shrk,shrd->ksd", score_grad, query_t, preferred_element_type=F32) * factor
        )
        value_grad = jnp.einsum(
            "shrk,shrd->ksd", probs.astype(BF16), grad_t, preferred_element_type=F32
        )
        return (query_grad, jnp.stack([key_grad, value_grad], axis=0))

    query_grad_t, terms = lax.scan(
        backward_step,
        jnp.zeros((seqs, group, cycle_rows, HEAD_DIM), F32),
        jnp.arange(total_rows // size, dtype=jnp.int32),
    )
    terms = jnp.transpose(terms, (1, 0, 2, 3, 4)).reshape(2, total_rows, seqs, HEAD_DIM)
    keep, send = pick(grid.c, terms, 0)
    kind_terms = keep + grid.swap_core(send.astype(BF16)).astype(F32)
    kind_terms = kind_terms.astype(BF16).reshape(depth, PAIR, cycle_rows, seqs, HEAD_DIM)
    kind_grad = scatter_blk(grid, kind_terms)
    kind_grad = unrotate(kind_grad[:, :, None, :], kind_cosine, kind_sine)
    query_grad = jnp.transpose(query_grad_t, (2, 0, 1, 3)).astype(BF16).astype(F32)
    query_grad = unrotate(query_grad, cosine, sine)
    mixed_grad = jnp.concatenate([query_grad, kind_grad], axis=2)
    mixed_grad = mixed_grad.reshape(cycle_rows * seqs, columns).astype(BF16)
    bias_part = lax.psum(jnp.sum(mixed_grad.astype(F32), axis=0), "blk")
    bias_all = lax.all_gather(bias_part, "uly", axis=0)
    bias_all = from_uly(bias_all[:, None, :])[0]
    owned_columns = qkv_bias.shape[0]
    grad_bias = lax.dynamic_slice_in_dim(
        bias_all, (grid.b * ulys + grid.u) * owned_columns, owned_columns, 0
    )
    normed_grad = contract_cols(mixed_grad, qkv_part).reshape(ulys, count, model)
    rows_part = norm_back(scatter_uly(grid, normed_grad), unit_one, factor_one)
    grad_tokens = (hidden_grad + rows_part).reshape(local_rows, seqs, model)
    qkv_share = contract_rows(units, mixed_grad).astype(BF16)
    qkv_share = scatter_blk(grid, qkv_share.reshape(depth, PAIR, ulys * shard, columns))
    qkv_share = exchange_uly(qkv_share.astype(BF16).reshape(ulys, shard, columns))
    qkv_share = from_uly(qkv_share).astype(F32)
    grad_qkv = qkv_share * gain_one
    grad_gain_one = jnp.sum(qkv_share * qkv_weight.astype(F32), axis=-1)
    return (
        output,
        grad_tokens,
        grad_gain_one,
        grad_qkv,
        grad_bias,
        grad_out,
        grad_gain_two.reshape(-1),
        grad_gate,
        grad_upper,
        grad_down,
    )


def solution(mesh):
    in_specs = (
        P(("blk", "uly"), None, None),
        P(),
        P(("blk", "uly")),
        P(("blk", "uly"), None),
        P(("blk", "uly")),
        P(("blk", "uly"), None),
        P("blk"),
        P("blk", "uly"),
        P("blk", "uly"),
        P("uly", "blk"),
        P(("blk", "uly"), None, None),
    )
    out_specs = (
        P(("blk", "uly"), None, None),
        P(("blk", "uly"), None, None),
        P(("blk", "uly")),
        P(("blk", "uly"), None),
        P(("blk", "uly")),
        P(("blk", "uly"), None),
        P(("blk", "uly")),
        P("blk", "uly"),
        P("blk", "uly"),
        P("uly", "blk"),
    )
    return jax.shard_map(
        per_device, mesh=mesh, in_specs=in_specs, out_specs=out_specs, check_vma=False
    )
```

time: 2450 us -> 935 us (0.38)
  waiting for transfers between devices: 1890 us -> 305 us
  starting transfers between devices: 18.6 us -> 139 us
  matrix products: 235 us -> 127 us
  other arithmetic: 49.8 us -> 136 us
  blocking collectives: 111 us -> 72.6 us
    all_gather x9 -> x0, waiting for transfers between devices: 790 us -> none  [the longest x1 153 us: per_device(): lax.all_gather(down_part, 'uly', axis=0, tiled=True)]
    reduce_scatter x6 -> x0, waiting for transfers between devices: 765 us -> none  [the longest x1 189 us: per_device(): lax.psum_scatter(grad_upper.astype(jnp.bfloat16), 'uly', scatter_dimensio...]
    unnamed x21 -> x0, waiting for transfers between devices: 310 us -> none
    ppermute x0 -> x100, waiting for transfers between devices: none -> 304 us  [the longest x36 140 us: to_z(): return lax.ppermute(value, 'blk', pairs)]
    ppermute x0 -> x100, starting transfers between devices: none -> 124 us  [the longest x36 77.1 us: to_z(): return lax.ppermute(value, 'blk', pairs)]
    unnamed x3 -> x1, blocking collectives: 102 us -> 40.2 us
    dot_general x5, matrix products: 64.6 us -> 23.5 us  [contract_rows(): lax.dot_general(left, right, (((0,), (0,)), ((), ())), preferred_element_...]
    dot_general x13 -> x22, matrix products: 75.4 us -> 39 us  [the longest x14 22.6 us: matmul(): return jnp.dot(left, right, preferred_element_type=F32)]
  transfers between devices with their start and end apart: 23 -> 104, of which waited for: 21 -> 36; matrix products, arithmetic and copies ran while one was open for 15% -> 41% of each run, Pallas kernels for 0% -> 0%
where the time goes in v1:
time: 935 us; the launch traced here: 921 us
  waiting for transfers between devices  305 us (33%)
  starting transfers between devices  139 us (15%)
  other arithmetic  136 us (15%)
  local copies, waits for them, and re-layouts  131 us (14%)
  matrix products  127 us (14%)
  blocking collectives  72.6 us (8%)
    ppermute x36, waiting for transfers between devices, to_z(): return lax.ppermute(value, 'blk', pairs)  140 us
    ppermute x21, waiting for transfers between devices, swap_y(): return lax.ppermute(value, 'uly', [(i, i ^ 2) for i in range(self.ulys)])  84.6 us
    ppermute x20, waiting for transfers between devices, swap_x(): return lax.ppermute(value, 'blk', [(i, i ^ 1) for i in range(self.blocks)])  79.7 us
    ppermute x36, starting transfers between devices, to_z(): return lax.ppermute(value, 'blk', pairs)  77.1 us
    unnamed x247, local copies, waits for them, and re-layouts  40.8 us
    unnamed x1, blocking collectives  40.2 us
    psum x1, blocking collectives, per_device(): bias_part = lax.psum(jnp.sum(mixed_grad.astype(F32), axis=0), 'blk')  27.3 us
    dot_general x5, matrix products, contract_rows(): lax.dot_general(left, right, (((0,), (0,)), ((), ())), preferred_element_...  23.5 us
  transfers between devices with their start and end apart: 104, of which 36 were waited for; matrix products, arithmetic and copies ran while one was open for 41% of the time, Pallas kernels for 0%

profile of v1, /device:TPU:0, one launch (start us, length us, event | category | flops | bytes accessed | tf_op | source)
XLA Modules:
  0.0 921.0 jit_solution(266998674879792503)
XLA Ops:
  0.7 5.1 collective-permute-start.17
  10.8 4.0 all-to-all-start
  24.9 3.3 reshape.617
  28.7 40.2 %all-reduce = bf16[2048]{0:T(1024)(128)(2,1)S(1)} all-reduce(bf16[2048]{0:T(1024)(128)(2,1)S(1)} %dynamic-update-slice), channel_id=1, replica_groups=mesh['blk'=8,'uly'=4] {'blk','uly'}, use_global_device_ids=true, to_apply=%add | all-reduce | flops 2048 | bytes 8192
  71.4 3.8 pad_maximum_fusion.1
  75.2 7.1 constant_dynamic-slice_fusion.1
  119.8 4.3 all-to-all-start.1
  124.1 3.8 collective-permute-start.71
  130.5 10.6 %collective-permute-done.2 = bf16[192,512]{1,0:T(8,128)(2,1)S(1)} collective-permute-done((bf16[192,512]{1,0:T(8,128)(2,1)}, bf16[192,512]{1,0:T(8,128)(2,1)S(1)}, u32[]{:S(2)}, u32[]{:S(2)}) %collective-permute-start.2) | collective-permute-done | bytes 196640 | tf_op jit(solution)/shard_map/ppermute | solution.py:88
  146.2 6.7 collective-permute-done.4
  153.0 7.6 collective-permute-done.6
  165.6 4.4 collective-permute-done.7
  172.7 11.0 %collective-permute-done.34 = bf16[3,192,560]{2,1,0:T(8,128)(2,1)S(1)} collective-permute-done((bf16[3,192,560]{2,1,0:T(8,128)(2,1)S(1)}, bf16[3,192,560]{2,1,0:T(8,128)(2,1)S(1)}, u32[]{:S(2)}, u32[]{:S(2)}) %collective-permute-start.34) | collective-permute-done | bytes 645152 | tf_op jit(solution)/shard_map/ppermute | solution.py:91
  189.4 34.5 %collective-permute-done.30 = bf16[3,192,560]{2,1,0:T(8,128)(2,1)} collective-permute-done((bf16[3,192,560]{2,1,0:T(8,128)(2,1)S(1)}, bf16[3,192,560]{2,1,0:T(8,128)(2,1)}, u32[]{:S(2)}, u32[]{:S(2)}) %collective-permute-start.30) | collective-permute-done | bytes 645152 | tf_op jit(solution)/shard_map/ppermute | solution.py:88
  245.1 14.3 %collective-permute-done.31 = bf16[3,192,560]{2,1,0:T(8,128)(2,1)} collective-permute-done((bf16[3,192,560]{2,1,0:T(8,128)(2,1)}, bf16[3,192,560]{2,1,0:T(8,128)(2,1)}, u32[]{:S(2)}, u32[]{:S(2)}) %collective-permute-start.31) | collective-permute-done | bytes 645152 | tf_op jit(solution)/shard_map/ppermute | solution.py:91
  260.9 12.9 %collective-permute-done.33 = bf16[3,192,560]{2,1,0:T(8,128)(2,1)} collective-permute-done((bf16[3,192,560]{2,1,0:T(8,128)(2,1)}, bf16[3,192,560]{2,1,0:T(8,128)(2,1)}, u32[]{:S(2)}, u32[]{:S(2)}) %collective-permute-start.33) | collective-permute-done | bytes 645152 | tf_op jit(solution)/shard_map/ppermute | solution.py:91
  275.8 4.0 collective-permute-done.11
  282.0 4.1 collective-permute-done.12
  286.1 4.9 collective-permute-done.10
  299.5 51.6 %while.32 = (s32[]{:T(128)}, f32[2,3,256,128]{3,2,1,0:T(8,128)}, f32[2,3,256]{2,1,0:T(4,128)S(1)}, f32[2,3,256]{2,1,0:T(4,128)}, s32[4]{0:T(128)}, /*index=5*/s3...) while((s32[]{:T(128)}, f32[2,3,256,128]{3,2,1,0:T(8,128)}, ...), condition=%wide.region_6.7_spmd.clone, body=%wide.region_2.6_spmd.clone.sunk | while | flops 413788672 | bytes 14168451 | solution.py:302
  321.4 3.4 fusion.311
  334.6 3.4 fusion.311
  347.7 3.4 fusion.311
  356.4 3.7 fusion.207
  365.8 8.8 collective-permute-done.25
  378.9 3.4 collective-permute-start.49
  382.2 8.4 collective-permute-done.37
  391.3 14.6 %collective-permute-done.43 = bf16[128,1536]{1,0:T(8,128)(2,1)S(1)} collective-permute-done((bf16[128,1536]{1,0:T(8,128)(2,1)S(1)}, bf16[128,1536]{1,0:T(8,128)(2,1)S(1)}, u32[]{:S(2)}, u32[]{:S(2)}) %collective-permute-start.43) | collective-permute-done | bytes 393248 | tf_op jit(solution)/shard_map/ppermute | solution.py:88
  408.2 9.8 %collective-permute-done.44 = bf16[128,1536]{1,0:T(8,128)(2,1)S(1)} collective-permute-done((bf16[128,1536]{1,0:T(8,128)(2,1)S(1)}, bf16[128,1536]{1,0:T(8,128)(2,1)S(1)}, u32[]{:S(2)}, u32[]{:S(2)}) %collective-permute-start.44) | collective-permute-done | bytes 393248 | tf_op jit(solution)/shard_map/ppermute | solution.py:94
  418.1 5.5 collective-permute-done.50
  453.2 3.5 multiply_convert_fusion
  458.2 8.1 convolution_convert_fusion.2
  470.7 8.7 convolution_convert_fusion.1
  484.2 4.9 convolution_convert_fusion
  499.5 3.9 copy.240
  503.4 3.9 copy.241
  527.2 14.7 %collective-permute-done.41 = bf16[128,1536]{1,0:T(8,128)(2,1)S(1)} collective-permute-done((bf16[128,1536]{1,0:T(8,128)(2,1)S(1)}, bf16[128,1536]{1,0:T(8,128)(2,1)S(1)}, u32[]{:S(2)}, u32[]{:S(2)}) %collective-permute-start.41) | collective-permute-done | bytes 393248 | tf_op jit(solution)/shard_map/ppermute | solution.py:94
  542.6 7.8 collective-permute-done.47
  551.0 16.2 %collective-permute-done.63 = bf16[128,1536]{1,0:T(8,128)(2,1)S(1)} collective-permute-done((bf16[128,1536]{1,0:T(8,128)(2,1)S(1)}, bf16[128,1536]{1,0:T(8,128)(2,1)S(1)}, u32[]{:S(2)}, u32[]{:S(2)}) %collective-permute-start.63) | collective-permute-done | bytes 393248 | tf_op jit(solution)/shard_map/ppermute | solution.py:94
  567.9 7.8 collective-permute-done.69
  575.7 7.6 collective-permute-start.64
  583.5 6.5 collective-permute-start.70
  592.6 3.7 collective-permute-start.42
  596.2 21.4 %collective-permute-done.70 = bf16[128,1536]{1,0:T(8,128)(2,1)S(1)} collective-permute-done((bf16[128,1536]{1,0:T(8,128)(2,1)S(1)}, bf16[128,1536]{1,0:T(8,128)(2,1)S(1)}, u32[]{:S(2)}, u32[]{:S(2)}) %collective-permute-start.70) | collective-permute-done | bytes 393248 | tf_op jit(solution)/shard_map/ppermute | solution.py:88
  617.7 16.8 %collective-permute-start.54 = (bf16[128,1536]{1,0:T(8,128)(2,1)S(1)}, bf16[128,1536]{1,0:T(8,128)(2,1)S(1)}, u32[]{:S(2)}, u32[]{:S(2)}) collective-permute-start(bf16[128,1536]{1,0:T(8,128)(2,1)S(1)} %fusion.117), channel_id=1, source_target_pairs={{0,8},{4,12},{8,16},{12,20},{16,24},{20,28},{24,0},{28,4},{1,9},{5... | collective-permute-start | bytes 1179656 | tf_op jit(solution)/shard_map/ppermute | solution.py:88
  634.9 14.6 %collective-permute-done.48 = bf16[128,1536]{1,0:T(8,128)(2,1)S(1)} collective-permute-done((bf16[128,1536]{1,0:T(8,128)(2,1)S(1)}, bf16[128,1536]{1,0:T(8,128)(2,1)S(1)}, u32[]{:S(2)}, u32[]{:S(2)}) %collective-permute-start.48) | collective-permute-done | bytes 393248 | tf_op jit(solution)/shard_map/ppermute | solution.py:88
  654.3 6.9 collective-permute-done.77
  662.4 4.8 fusion.40
  669.5 5.5 collective-permute-start.95
  682.9 54.5 %while.33 = (s32[]{:T(128)}, f32[2,3,256,128]{3,2,1,0:T(8,128)S(1)}, f32[4,2,512,2,128]{4,2,0,3,1:T(8,128)}, s32[4]{0:T(128)S(1)}, s32[2,16]{1,0:T(2,128)}, /*in...) while((s32[]{:T(128)}, ...), condition=%wide.region_12.13_spmd.clone, body=%wide.region_10.12_spmd.clone.sunk | while | flops 1015794688 | bytes 34665364 | solution.py:396
  737.4 3.4 select_convert_fusion
  740.8 3.9 slice_select_fusion
  746.6 4.1 all-to-all-start.3
  769.4 4.1 copy.243
  776.7 4.7 broadcast_multiply_fusion
  782.7 4.1 copy.244
  796.9 11.4 %collective-permute-done.90 = bf16[4,48,1536]{2,1,0:T(8,128)(2,1)S(1)} collective-permute-done((bf16[4,48,1536]{2,1,0:T(8,128)(2,1)S(1)}, bf16[4,48,1536]{2,1,0:T(8,128)(2,1)S(1)}, u32[]{:S(2)}, u32[]{:S(2)}) %collective-permute-start.90) | collective-permute-done | bytes 589856 | tf_op jit(solution)/shard_map/ppermute | solution.py:91
  808.5 9.9 %collective-permute-done.80 = bf16[4,256,2,128]{3,1,2,0:T(8,128)(2,1)S(1)} collective-permute-done((bf16[4,256,2,128]{3,1,2,0:T(8,128)(2,1)S(1)}, bf16[4,256,2,128]{3,1,2,0:T(8,128)(2,1)S(1)}, u32[]{:S(2)}, u32[]{:S(2)}) %collective-permute-start.80) | collective-permute-done | bytes 524320 | tf_op jit(solution)/shard_map/ppermute | solution.py:91
  828.4 6.5 collective-permute-done.82
  847.2 27.3 %psum.7 = f32[1,512]{1,0:T(1,128)S(1)} all-reduce(f32[1,512]{1,0:T(1,128)S(1)} %bitcast.810), channel_id=1, replica_groups=mesh['blk'=8,'uly'=4] {'blk'}, use_global_device_ids=true, to_apply=%region_16.17 | all-reduce | flops 512 | bytes 4096 | tf_op jit(solution)/shard_map/psum | solution.py:411
  874.5 5.2 all-gather
  891.9 7.8 collective-permute-done.88
  900.5 3.4 all-to-all-start.2
  910.8 7.0 collective-permute-done.85
  (792 shorter events, 390.7 us)
Async XLA Ops:
  0.7 88.5 %collective-permute-start.17 = (bf16[48,1536]{1,0:T(8,128)(2,1)}, bf16[48,1536]{1,0:T(8,128)(2,1)}, u32[]{:S(2)}, u32[]{:S(2)}) collective-permute-start(bf16[48,1536]{1,0:T(8,128)(2,1)} %param.20), channel_id=1, source_target_pairs={{0,24},{4,28},{8,0},{12,4},{16,8},{20,12},{24,16},{28,20},{1,25},{... | collective-permute-start | bytes 442376 | tf_op jit(solution)/shard_map/ppermute | solution.py:88
  5.8 87.7 %collective-permute-start.19 = (bf16[48,1536]{1,0:T(8,128)(2,1)}, bf16[48,1536]{1,0:T(8,128)(2,1)}, u32[]{:S(2)}, u32[]{:S(2)}) collective-permute-start(bf16[48,1536]{1,0:T(8,128)(2,1)} %param.20), channel_id=1, source_target_pairs={{0,16},{4,20},{8,24},{12,28},{16,0},{20,4},{24,8},{28,12},{1,17},{... | collective-permute-start | bytes 442376 | tf_op jit(solution)/shard_map/ppermute | solution.py:88
  5.8 93.9 %collective-permute-start.21 = (bf16[48,1536]{1,0:T(8,128)(2,1)}, bf16[48,1536]{1,0:T(8,128)(2,1)}, u32[]{:S(2)}, u32[]{:S(2)}) collective-permute-start(bf16[48,1536]{1,0:T(8,128)(2,1)} %param.20), channel_id=1, source_target_pairs={{0,8},{4,12},{8,16},{12,20},{16,24},{20,28},{24,0},{28,4},{1,9},{5... | collective-permute-start | bytes 442376 | tf_op jit(solution)/shard_map/ppermute | solution.py:88
  6.8 82.7 %collective-permute-start.23 = (bf16[48,1536]{1,0:T(8,128)(2,1)}, bf16[48,1536]{1,0:T(8,128)(2,1)}, u32[]{:S(2)}, u32[]{:S(2)}) collective-permute-start(bf16[48,1536]{1,0:T(8,128)(2,1)} %param.20), channel_id=1, source_target_pairs={{0,4},{4,0},{8,12},{12,8},{16,20},{20,16},{24,28},{28,24},{1,5},{5... | collective-permute-start | bytes 442376 | tf_op jit(solution)/shard_map/ppermute | solution.py:91
  10.8 95.4 %all-to-all-start = ((bf16[4,48,512]{2,1,0:T(8,128)(2,1)}), bf16[4,48,512]{2,1,0:T(8,128)(2,1)}, u32[]{:S(2)}, u32[]{:S(2)}) async-start(bf16[4,48,512]{2,1,0:T(8,128)(2,1)} %maximum_bitcast_fusion.17), calls=%async_computation | async-start | bytes 393216 | tf_op jit(solution)/shard_map/all_to_all | solution.py:154
  15.0 127.4 %collective-permute-start.55 = (bf16[128,1536]{1,0:T(8,128)(2,1)S(1)}, bf16[128,1536]{1,0:T(8,128)(2,1)}, u32[]{:S(2)}, u32[]{:S(2)}) collective-permute-start(bf16[128,1536]{1,0:T(8,128)(2,1)S(1)} %reshape.619), channel_id=1, source_target_pairs={{0,2},{1,3},{2,0},{3,1},{4,6},{5,7},{6,4},{7,5},{8,10},{9,11},{10,... | collective-permute-start | bytes 1179656 | tf_op jit(solution)/shard_map/ppermute | solution.py:94
  89.2 73.2 %collective-permute-start.59 = (bf16[128,1536]{1,0:T(8,128)(2,1)S(1)}, bf16[128,1536]{1,0:T(8,128)(2,1)S(1)}, u32[]{:S(2)}, u32[]{:S(2)}) collective-permute-start(bf16[128,1536]{1,0:T(8,128)(2,1)S(1)} %reshape.619), channel_id=1, source_target_pairs={{0,8},{4,12},{8,16},{12,20},{16,24},{20,28},{24,0},{28,4},{1,9},{5... | collective-permute-start | bytes 1179656 | tf_op jit(solution)/shard_map/ppermute | solution.py:88
  93.4 71.0 %collective-permute-start.65 = (bf16[128,1536]{1,0:T(8,128)(2,1)S(1)}, bf16[128,1536]{1,0:T(8,128)(2,1)}, u32[]{:S(2)}, u32[]{:S(2)}) collective-permute-start(bf16[128,1536]{1,0:T(8,128)(2,1)S(1)} %reshape.619), channel_id=1, source_target_pairs={{0,16},{4,20},{8,24},{12,28},{16,0},{20,4},{24,8},{28,12},{1,17},{... | collective-permute-start | bytes 1179656 | tf_op jit(solution)/shard_map/ppermute | solution.py:88
  99.7 29.2 %collective-permute-start = (bf16[128,1536]{1,0:T(8,128)(2,1)}, bf16[128,1536]{1,0:T(8,128)(2,1)}, u32[]{:S(2)}, u32[]{:S(2)}) collective-permute-start(bf16[128,1536]{1,0:T(8,128)(2,1)} %multiply_convert_fusion.13), channel_id=1, source_target_pairs={{0,2},{1,3},{2,0},{3,1},{4,6},{5,7},{6,4},{7,5},{8,10},{9,11},{10,... | collective-permute-start | bytes 1179656 | tf_op jit(solution)/shard_map/ppermute | solution.py:94
  119.8 118.8 %all-to-all-start.1 = ((bf16[4,2,48,1536]{3,2,1,0:T(8,128)(2,1)}), bf16[4,2,48,1536]{3,2,1,0:T(8,128)(2,1)}, u32[]{:S(2)}, u32[]{:S(2)}) async-start(bf16[4,2,48,1536]{3,2,1,0:T(8,128)(2,1)} %constant_dynamic-slice_fusion.5), calls=%async_computation.1 | async-start | bytes 2359296 | tf_op jit(solution)/shard_map/all_to_all | solution.py:154
  124.1 47.5 %collective-permute-start.71 = (bf16[128,1536]{1,0:T(8,128)(2,1)S(1)}, bf16[128,1536]{1,0:T(8,128)(2,1)S(1)}, u32[]{:S(2)}, u32[]{:S(2)}) collective-permute-start(bf16[128,1536]{1,0:T(8,128)(2,1)S(1)} %reshape.619), channel_id=1, source_target_pairs={{0,24},{4,28},{8,0},{12,4},{16,8},{20,12},{24,16},{28,20},{1,25},{... | collective-permute-start | bytes 1179656 | tf_op jit(solution)/shard_map/ppermute | solution.py:88
  160.6 28.5 %collective-permute-start.28 = (bf16[3,192,560]{2,1,0:T(8,128)(2,1)S(1)}, bf16[3,192,560]{2,1,0:T(8,128)(2,1)}, u32[]{:S(2)}, u32[]{:S(2)}) collective-permute-start(bf16[3,192,560]{2,1,0:T(8,128)(2,1)S(1)} %bitcast.797), channel_id=1, source_target_pairs={{0,24},{4,28},{8,0},{12,4},{16,8},{20,12},{24,16},{28,20},{1,25},{... | collective-permute-start | bytes 1935368 | tf_op jit(solution)/shard_map/ppermute | solution.py:88
  162.4 21.3 %collective-permute-start.34 = (bf16[3,192,560]{2,1,0:T(8,128)(2,1)S(1)}, bf16[3,192,560]{2,1,0:T(8,128)(2,1)S(1)}, u32[]{:S(2)}, u32[]{:S(2)}) collective-permute-start(bf16[3,192,560]{2,1,0:T(8,128)(2,1)S(1)} %bitcast.799), channel_id=1, source_target_pairs={{0,4},{4,0},{8,12},{12,8},{16,20},{20,16},{24,28},{28,24},{1,5},{5... | collective-permute-start | bytes 1935368 | tf_op jit(solution)/shard_map/ppermute | solution.py:91
  164.4 19.3 %collective-permute-start.60 = (bf16[128,1536]{1,0:T(8,128)(2,1)S(1)}, bf16[128,1536]{1,0:T(8,128)(2,1)S(1)}, u32[]{:S(2)}, u32[]{:S(2)}) collective-permute-start(bf16[128,1536]{1,0:T(8,128)(2,1)S(1)} %collective-permute-done.59), channel_id=1, source_target_pairs={{0,2},{1,3},{2,0},{3,1},{4,6},{5,7},{6,4},{7,5},{8,10},{9,11},{10,... | collective-permute-start | bytes 1179656 | tf_op jit(solution)/shard_map/ppermute | solution.py:94
  172.6 51.3 %collective-permute-start.30 = (bf16[3,192,560]{2,1,0:T(8,128)(2,1)S(1)}, bf16[3,192,560]{2,1,0:T(8,128)(2,1)}, u32[]{:S(2)}, u32[]{:S(2)}) collective-permute-start(bf16[3,192,560]{2,1,0:T(8,128)(2,1)S(1)} %bitcast.798), channel_id=1, source_target_pairs={{0,16},{4,20},{8,24},{12,28},{16,0},{20,4},{24,8},{28,12},{1,17},{... | collective-permute-start | bytes 1935368 | tf_op jit(solution)/shard_map/ppermute | solution.py:88
  183.7 40.2 %collective-permute-start.32 = (bf16[3,192,560]{2,1,0:T(8,128)(2,1)S(1)}, bf16[3,192,560]{2,1,0:T(8,128)(2,1)}, u32[]{:S(2)}, u32[]{:S(2)}) collective-permute-start(bf16[3,192,560]{2,1,0:T(8,128)(2,1)S(1)} %bitcast.796), channel_id=1, source_target_pairs={{0,8},{4,12},{8,16},{12,20},{16,24},{20,28},{24,0},{28,4},{1,9},{5... | collective-permute-start | bytes 1935368 | tf_op jit(solution)/shard_map/ppermute | solution.py:88
  183.7 43.3 %collective-permute-start.1 = (bf16[2,128,1536]{2,1,0:T(8,128)(2,1)S(1)}, bf16[2,128,1536]{2,1,0:T(8,128)(2,1)S(1)}, u32[]{:S(2)}, u32[]{:S(2)}) collective-permute-start(bf16[2,128,1536]{2,1,0:T(8,128)(2,1)S(1)} %pad_maximum_fusion.6), channel_id=1, source_target_pairs={{0,1},{1,0},{2,3},{3,2},{4,5},{5,4},{6,7},{7,6},{8,9},{9,8},{10,11... | collective-permute-start | bytes 2359304 | tf_op jit(solution)/shard_map/ppermute | solution.py:97
  185.1 40.9 %collective-permute-start.72 = (bf16[128,1536]{1,0:T(8,128)(2,1)S(1)}, bf16[128,1536]{1,0:T(8,128)(2,1)S(1)}, u32[]{:S(2)}, u32[]{:S(2)}) collective-permute-start(bf16[128,1536]{1,0:T(8,128)(2,1)S(1)} %collective-permute-done.71), channel_id=1, source_target_pairs={{0,2},{1,3},{2,0},{3,1},{4,6},{5,7},{6,4},{7,5},{8,10},{9,11},{10,... | collective-permute-start | bytes 1179656 | tf_op jit(solution)/shard_map/ppermute | solution.py:94
  189.2 45.1 %collective-permute-start.56 = (bf16[256,1536]{1,0:T(8,128)(2,1)}, bf16[256,1536]{1,0:T(8,128)(2,1)}, u32[]{:S(2)}, u32[]{:S(2)}) collective-permute-start(bf16[256,1536]{1,0:T(8,128)(2,1)} %pad_maximum_fusion.11), channel_id=1, source_target_pairs={{0,1},{1,0},{2,3},{3,2},{4,5},{5,4},{6,7},{7,6},{8,9},{9,8},{10,11... | collective-permute-start | bytes 2359304 | tf_op jit(solution)/shard_map/ppermute | solution.py:97
  223.9 19.7 %collective-permute-start.29 = (bf16[3,192,560]{2,1,0:T(8,128)(2,1)}, bf16[3,192,560]{2,1,0:T(8,128)(2,1)}, u32[]{:S(2)}, u32[]{:S(2)}) collective-permute-start(bf16[3,192,560]{2,1,0:T(8,128)(2,1)} %collective-permute-done.28), channel_id=1, source_target_pairs={{0,4},{4,0},{8,12},{12,8},{16,20},{20,16},{24,28},{28,24},{1,5},{5... | collective-permute-start | bytes 1935368 | tf_op jit(solution)/shard_map/ppermute | solution.py:91
  223.9 35.5 %collective-permute-start.31 = (bf16[3,192,560]{2,1,0:T(8,128)(2,1)}, bf16[3,192,560]{2,1,0:T(8,128)(2,1)}, u32[]{:S(2)}, u32[]{:S(2)}) collective-permute-start(bf16[3,192,560]{2,1,0:T(8,128)(2,1)} %collective-permute-done.30), channel_id=1, source_target_pairs={{0,4},{4,0},{8,12},{12,8},{16,20},{20,16},{24,28},{28,24},{1,5},{5... | collective-permute-start | bytes 1935368 | tf_op jit(solution)/shard_map/ppermute | solution.py:91
  226.0 47.9 %collective-permute-start.33 = (bf16[3,192,560]{2,1,0:T(8,128)(2,1)}, bf16[3,192,560]{2,1,0:T(8,128)(2,1)}, u32[]{:S(2)}, u32[]{:S(2)}) collective-permute-start(bf16[3,192,560]{2,1,0:T(8,128)(2,1)} %collective-permute-done.32), channel_id=1, source_target_pairs={{0,4},{4,0},{8,12},{12,8},{16,20},{20,16},{24,28},{28,24},{1,5},{5... | collective-permute-start | bytes 1935368 | tf_op jit(solution)/shard_map/ppermute | solution.py:91
  227.0 133.1 %collective-permute-start.61 = (bf16[256,1536]{1,0:T(8,128)(2,1)}, bf16[256,1536]{1,0:T(8,128)(2,1)}, u32[]{:S(2)}, u32[]{:S(2)}) collective-permute-start(bf16[256,1536]{1,0:T(8,128)(2,1)} %pad_maximum_fusion.12), channel_id=1, source_target_pairs={{0,1},{1,0},{2,3},{3,2},{4,5},{5,4},{6,7},{7,6},{8,9},{9,8},{10,11... | collective-permute-start | bytes 2359304 | tf_op jit(solution)/shard_map/ppermute | solution.py:97
  234.2 130.3 %collective-permute-start.67 = (bf16[256,1536]{1,0:T(8,128)(2,1)}, bf16[256,1536]{1,0:T(8,128)(2,1)}, u32[]{:S(2)}, u32[]{:S(2)}) collective-permute-start(bf16[256,1536]{1,0:T(8,128)(2,1)} %pad_maximum_fusion.13), channel_id=1, source_target_pairs={{0,1},{1,0},{2,3},{3,2},{4,5},{5,4},{6,7},{7,6},{8,9},{9,8},{10,11... | collective-permute-start | bytes 2359304 | tf_op jit(solution)/shard_map/ppermute | solution.py:97
  243.7 31.8 %collective-permute-start.15 = (bf16[256,2,128]{2,0,1:T(8,128)(2,1)S(1)}, bf16[256,2,128]{2,0,1:T(8,128)(2,1)S(1)}, u32[]{:S(2)}, u32[]{:S(2)}) collective-permute-start(bf16[256,2,128]{2,0,1:T(8,128)(2,1)S(1)} %get-tuple-element.575), channel_id=1, source_target_pairs={{0,4},{4,0},{8,12},{12,8},{16,20},{20,16},{24,28},{28,24},{1,5},{5... | collective-permute-start | bytes 393224 | tf_op jit(solution)/shard_map/ppermute | solution.py:91
  259.5 20.6 %collective-permute-start.13 = (bf16[256,2,128]{2,0,1:T(8,128)(2,1)S(1)}, bf16[256,2,128]{2,0,1:T(8,128)(2,1)S(1)}, u32[]{:S(2)}, u32[]{:S(2)}) collective-permute-start(bf16[256,2,128]{2,0,1:T(8,128)(2,1)S(1)} %get-tuple-element.575), channel_id=1, source_target_pairs={{0,8},{4,12},{8,16},{12,20},{16,24},{20,28},{24,0},{28,4},{1,9},{5... | collective-permute-start | bytes 393224 | tf_op jit(solution)/shard_map/ppermute | solution.py:88
  280.1 97.6 %collective-permute-start.73 = (bf16[256,1536]{1,0:T(8,128)(2,1)}, bf16[256,1536]{1,0:T(8,128)(2,1)}, u32[]{:S(2)}, u32[]{:S(2)}) collective-permute-start(bf16[256,1536]{1,0:T(8,128)(2,1)} %pad_maximum_fusion.14), channel_id=1, source_target_pairs={{0,1},{1,0},{2,3},{3,2},{4,5},{5,4},{6,7},{7,6},{8,9},{9,8},{10,11... | collective-permute-start | bytes 2359304 | tf_op jit(solution)/shard_map/ppermute | solution.py:97
  376.7 29.3 %collective-permute-start.43 = (bf16[128,1536]{1,0:T(8,128)(2,1)S(1)}, bf16[128,1536]{1,0:T(8,128)(2,1)S(1)}, u32[]{:S(2)}, u32[]{:S(2)}) collective-permute-start(bf16[128,1536]{1,0:T(8,128)(2,1)S(1)} %get-tuple-element.463), channel_id=1, source_target_pairs={{0,16},{4,20},{8,24},{12,28},{16,0},{20,4},{24,8},{28,12},{1,17},{... | collective-permute-start | bytes 1179656 | tf_op jit(solution)/shard_map/ppermute | solution.py:88
  378.9 27.7 %collective-permute-start.49 = (bf16[128,1536]{1,0:T(8,128)(2,1)S(1)}, bf16[128,1536]{1,0:T(8,128)(2,1)S(1)}, u32[]{:S(2)}, u32[]{:S(2)}) collective-permute-start(bf16[128,1536]{1,0:T(8,128)(2,1)S(1)} %get-tuple-element.463), channel_id=1, source_target_pairs={{0,24},{4,28},{8,0},{12,4},{16,8},{20,12},{24,16},{28,20},{1,25},{... | collective-permute-start | bytes 1179656 | tf_op jit(solution)/shard_map/ppermute | solution.py:88
  390.6 17.5 %collective-permute-start.38 = (bf16[128,1536]{1,0:T(8,128)(2,1)S(1)}, bf16[128,1536]{1,0:T(8,128)(2,1)S(1)}, u32[]{:S(2)}, u32[]{:S(2)}) collective-permute-start(bf16[128,1536]{1,0:T(8,128)(2,1)S(1)} %collective-permute-done.37), channel_id=1, source_target_pairs={{0,2},{1,3},{2,0},{3,1},{4,6},{5,7},{6,4},{7,5},{8,10},{9,11},{10,... | collective-permute-start | bytes 1179656 | tf_op jit(solution)/shard_map/ppermute | solution.py:94
  391.2 32.5 %collective-permute-start.27 = (bf16[256,1536]{1,0:T(8,128)(2,1)S(1)}, bf16[256,1536]{1,0:T(8,128)(2,1)S(1)}, u32[]{:S(2)}, u32[]{:S(2)}) collective-permute-start(bf16[256,1536]{1,0:T(8,128)(2,1)S(1)} %pad_maximum_fusion.7), channel_id=1, source_target_pairs={{0,1},{1,0},{2,3},{3,2},{4,5},{5,4},{6,7},{7,6},{8,9},{9,8},{10,11... | collective-permute-start | bytes 2359304 | tf_op jit(solution)/shard_map/ppermute | solution.py:97
  406.6 17.0 %collective-permute-start.50 = (bf16[128,1536]{1,0:T(8,128)(2,1)S(1)}, bf16[128,1536]{1,0:T(8,128)(2,1)S(1)}, u32[]{:S(2)}, u32[]{:S(2)}) collective-permute-start(bf16[128,1536]{1,0:T(8,128)(2,1)S(1)} %collective-permute-done.49), channel_id=1, source_target_pairs={{0,2},{1,3},{2,0},{3,1},{4,6},{5,7},{6,4},{7,5},{8,10},{9,11},{10,... | collective-permute-start | bytes 1179656 | tf_op jit(solution)/shard_map/ppermute | solution.py:94
  408.2 28.6 %collective-permute-start.39 = (bf16[256,1536]{1,0:T(8,128)(2,1)S(1)}, bf16[256,1536]{1,0:T(8,128)(2,1)S(1)}, u32[]{:S(2)}, u32[]{:S(2)}) collective-permute-start(bf16[256,1536]{1,0:T(8,128)(2,1)S(1)} %pad_maximum_fusion.8), channel_id=1, source_target_pairs={{0,1},{1,0},{2,3},{3,2},{4,5},{5,4},{6,7},{7,6},{8,9},{9,8},{10,11... | collective-permute-start | bytes 2359304 | tf_op jit(solution)/shard_map/ppermute | solution.py:97
  418.1 21.2 %collective-permute-start.45 = (bf16[256,1536]{1,0:T(8,128)(2,1)S(1)}, bf16[256,1536]{1,0:T(8,128)(2,1)S(1)}, u32[]{:S(2)}, u32[]{:S(2)}) collective-permute-start(bf16[256,1536]{1,0:T(8,128)(2,1)S(1)} %pad_maximum_fusion.9), channel_id=1, source_target_pairs={{0,1},{1,0},{2,3},{3,2},{4,5},{5,4},{6,7},{7,6},{8,9},{9,8},{10,11... | collective-permute-start | bytes 2359304 | tf_op jit(solution)/shard_map/ppermute | solution.py:97
  423.7 18.2 %collective-permute-start.51 = (bf16[256,1536]{1,0:T(8,128)(2,1)S(1)}, bf16[256,1536]{1,0:T(8,128)(2,1)S(1)}, u32[]{:S(2)}, u32[]{:S(2)}) collective-permute-start(bf16[256,1536]{1,0:T(8,128)(2,1)S(1)} %pad_maximum_fusion.10), channel_id=1, source_target_pairs={{0,1},{1,0},{2,3},{3,2},{4,5},{5,4},{6,7},{7,6},{8,9},{9,8},{10,11... | collective-permute-start | bytes 2359304 | tf_op jit(solution)/shard_map/ppermute | solution.py:97
  436.1 79.4 %collective-permute-start.35 = (bf16[2,128,1536]{2,1,0:T(8,128)(2,1)}, bf16[2,128,1536]{2,1,0:T(8,128)(2,1)}, u32[]{:S(2)}, u32[]{:S(2)}) collective-permute-start(bf16[2,128,1536]{2,1,0:T(8,128)(2,1)} %bitcast.95), channel_id=1, source_target_pairs={{0,1},{1,0},{2,3},{3,2},{4,5},{5,4},{6,7},{7,6},{8,9},{9,8},{10,11... | collective-permute-start | bytes 2359304 | tf_op jit(solution)/shard_map/ppermute | solution.py:97
  436.6 80.8 %collective-permute-start.57 = (bf16[2,128,1536]{2,1,0:T(8,128)(2,1)}, bf16[2,128,1536]{2,1,0:T(8,128)(2,1)}, u32[]{:S(2)}, u32[]{:S(2)}) collective-permute-start(bf16[2,128,1536]{2,1,0:T(8,128)(2,1)} %bitcast.111), channel_id=1, source_target_pairs={{0,1},{1,0},{2,3},{3,2},{4,5},{5,4},{6,7},{7,6},{8,9},{9,8},{10,11... | collective-permute-start | bytes 2359304 | tf_op jit(solution)/shard_map/ppermute | solution.py:97
  514.8 147.6 %collective-permute-start.94 = (bf16[3,4,192,560]{3,2,1,0:T(8,128)(2,1)}, bf16[3,4,192,560]{3,2,1,0:T(8,128)(2,1)}, u32[]{:S(2)}, u32[]{:S(2)}) collective-permute-start(bf16[3,4,192,560]{3,2,1,0:T(8,128)(2,1)} %select_bitcast_fusion), channel_id=1, source_target_pairs={{0,4},{4,0},{8,12},{12,8},{16,20},{20,16},{24,28},{28,24},{1,5},{5... | collective-permute-start | bytes 7741448 | tf_op jit(solution)/shard_map/ppermute | solution.py:91
  521.5 70.3 %collective-permute-start.58 = (bf16[128,1536]{1,0:T(8,128)(2,1)S(1)}, bf16[128,1536]{1,0:T(8,128)(2,1)S(1)}, u32[]{:S(2)}, u32[]{:S(2)}) collective-permute-start(bf16[128,1536]{1,0:T(8,128)(2,1)S(1)} %fusion.150), channel_id=1, source_target_pairs={{0,2},{1,3},{2,0},{3,1},{4,6},{5,7},{6,4},{7,5},{8,10},{9,11},{10,... | collective-permute-start | bytes 1179656 | tf_op jit(solution)/shard_map/ppermute | solution.py:94
  523.0 18.9 %collective-permute-start.41 = (bf16[128,1536]{1,0:T(8,128)(2,1)S(1)}, bf16[128,1536]{1,0:T(8,128)(2,1)S(1)}, u32[]{:S(2)}, u32[]{:S(2)}) collective-permute-start(bf16[128,1536]{1,0:T(8,128)(2,1)S(1)} %fusion.147), channel_id=1, source_target_pairs={{0,2},{1,3},{2,0},{3,1},{4,6},{5,7},{6,4},{7,5},{8,10},{9,11},{10,... | collective-permute-start | bytes 1179656 | tf_op jit(solution)/shard_map/ppermute | solution.py:94
  524.4 26.0 %collective-permute-start.47 = (bf16[128,1536]{1,0:T(8,128)(2,1)S(1)}, bf16[128,1536]{1,0:T(8,128)(2,1)S(1)}, u32[]{:S(2)}, u32[]{:S(2)}) collective-permute-start(bf16[128,1536]{1,0:T(8,128)(2,1)S(1)} %fusion.148), channel_id=1, source_target_pairs={{0,2},{1,3},{2,0},{3,1},{4,6},{5,7},{6,4},{7,5},{8,10},{9,11},{10,... | collective-permute-start | bytes 1179656 | tf_op jit(solution)/shard_map/ppermute | solution.py:94
  525.9 64.2 %collective-permute-start.53 = (bf16[128,1536]{1,0:T(8,128)(2,1)S(1)}, bf16[128,1536]{1,0:T(8,128)(2,1)S(1)}, u32[]{:S(2)}, u32[]{:S(2)}) collective-permute-start(bf16[128,1536]{1,0:T(8,128)(2,1)S(1)} %fusion.149), channel_id=1, source_target_pairs={{0,2},{1,3},{2,0},{3,1},{4,6},{5,7},{6,4},{7,5},{8,10},{9,11},{10,... | collective-permute-start | bytes 1179656 | tf_op jit(solution)/shard_map/ppermute | solution.py:94
  542.0 25.3 %collective-permute-start.63 = (bf16[128,1536]{1,0:T(8,128)(2,1)S(1)}, bf16[128,1536]{1,0:T(8,128)(2,1)S(1)}, u32[]{:S(2)}, u32[]{:S(2)}) collective-permute-start(bf16[128,1536]{1,0:T(8,128)(2,1)S(1)} %fusion.151), channel_id=1, source_target_pairs={{0,2},{1,3},{2,0},{3,1},{4,6},{5,7},{6,4},{7,5},{8,10},{9,11},{10,... | collective-permute-start | bytes 1179656 | tf_op jit(solution)/shard_map/ppermute | solution.py:94
  550.4 25.3 %collective-permute-start.69 = (bf16[128,1536]{1,0:T(8,128)(2,1)S(1)}, bf16[128,1536]{1,0:T(8,128)(2,1)S(1)}, u32[]{:S(2)}, u32[]{:S(2)}) collective-permute-start(bf16[128,1536]{1,0:T(8,128)(2,1)S(1)} %fusion.152), channel_id=1, source_target_pairs={{0,2},{1,3},{2,0},{3,1},{4,6},{5,7},{6,4},{7,5},{8,10},{9,11},{10,... | collective-permute-start | bytes 1179656 | tf_op jit(solution)/shard_map/ppermute | solution.py:94
  567.2 16.2 %collective-permute-start.75 = (bf16[128,1536]{1,0:T(8,128)(2,1)S(1)}, bf16[128,1536]{1,0:T(8,128)(2,1)S(1)}, u32[]{:S(2)}, u32[]{:S(2)}) collective-permute-start(bf16[128,1536]{1,0:T(8,128)(2,1)S(1)} %fusion.153), channel_id=1, source_target_pairs={{0,2},{1,3},{2,0},{3,1},{4,6},{5,7},{6,4},{7,5},{8,10},{9,11},{10,... | collective-permute-start | bytes 1179656 | tf_op jit(solution)/shard_map/ppermute | solution.py:94
  575.7 16.9 %collective-permute-start.64 = (bf16[128,1536]{1,0:T(8,128)(2,1)S(1)}, bf16[128,1536]{1,0:T(8,128)(2,1)S(1)}, u32[]{:S(2)}, u32[]{:S(2)}) collective-permute-start(bf16[128,1536]{1,0:T(8,128)(2,1)S(1)} %fusion.111), channel_id=1, source_target_pairs={{0,24},{4,28},{8,0},{12,4},{16,8},{20,12},{24,16},{28,20},{1,25},{... | collective-permute-start | bytes 1179656 | tf_op jit(solution)/shard_map/ppermute | solution.py:88
  583.5 34.2 %collective-permute-start.70 = (bf16[128,1536]{1,0:T(8,128)(2,1)S(1)}, bf16[128,1536]{1,0:T(8,128)(2,1)S(1)}, u32[]{:S(2)}, u32[]{:S(2)}) collective-permute-start(bf16[128,1536]{1,0:T(8,128)(2,1)S(1)} %fusion.109), channel_id=1, source_target_pairs={{0,16},{4,20},{8,24},{12,28},{16,0},{20,4},{24,8},{28,12},{1,17},{... | collective-permute-start | bytes 1179656 | tf_op jit(solution)/shard_map/ppermute | solution.py:88
  590.1 27.6 %collective-permute-start.76 = (bf16[128,1536]{1,0:T(8,128)(2,1)S(1)}, bf16[128,1536]{1,0:T(8,128)(2,1)S(1)}, u32[]{:S(2)}, u32[]{:S(2)}) collective-permute-start(bf16[128,1536]{1,0:T(8,128)(2,1)S(1)} %fusion.107), channel_id=1, source_target_pairs={{0,8},{4,12},{8,16},{12,20},{16,24},{20,28},{24,0},{28,4},{1,9},{5... | collective-permute-start | bytes 1179656 | tf_op jit(solution)/shard_map/ppermute | solution.py:88
  591.9 43.0 %collective-permute-start.36 = (bf16[128,1536]{1,0:T(8,128)(2,1)S(1)}, bf16[128,1536]{1,0:T(8,128)(2,1)S(1)}, u32[]{:S(2)}, u32[]{:S(2)}) collective-permute-start(bf16[128,1536]{1,0:T(8,128)(2,1)S(1)} %fusion.146), channel_id=1, source_target_pairs={{0,2},{1,3},{2,0},{3,1},{4,6},{5,7},{6,4},{7,5},{8,10},{9,11},{10,... | collective-permute-start | bytes 1179656 | tf_op jit(solution)/shard_map/ppermute | solution.py:94
  592.6 42.3 %collective-permute-start.42 = (bf16[128,1536]{1,0:T(8,128)(2,1)S(1)}, bf16[128,1536]{1,0:T(8,128)(2,1)S(1)}, u32[]{:S(2)}, u32[]{:S(2)}) collective-permute-start(bf16[128,1536]{1,0:T(8,128)(2,1)S(1)} %fusion.121), channel_id=1, source_target_pairs={{0,24},{4,28},{8,0},{12,4},{16,8},{20,12},{24,16},{28,20},{1,25},{... | collective-permute-start | bytes 1179656 | tf_op jit(solution)/shard_map/ppermute | solution.py:88
  617.7 31.8 %collective-permute-start.48 = (bf16[128,1536]{1,0:T(8,128)(2,1)S(1)}, bf16[128,1536]{1,0:T(8,128)(2,1)S(1)}, u32[]{:S(2)}, u32[]{:S(2)}) collective-permute-start(bf16[128,1536]{1,0:T(8,128)(2,1)S(1)} %fusion.119), channel_id=1, source_target_pairs={{0,16},{4,20},{8,24},{12,28},{16,0},{20,4},{24,8},{28,12},{1,17},{... | collective-permute-start | bytes 1179656 | tf_op jit(solution)/shard_map/ppermute | solution.py:88
  617.7 31.8 %collective-permute-start.54 = (bf16[128,1536]{1,0:T(8,128)(2,1)S(1)}, bf16[128,1536]{1,0:T(8,128)(2,1)S(1)}, u32[]{:S(2)}, u32[]{:S(2)}) collective-permute-start(bf16[128,1536]{1,0:T(8,128)(2,1)S(1)} %fusion.117), channel_id=1, source_target_pairs={{0,8},{4,12},{8,16},{12,20},{16,24},{20,28},{24,0},{28,4},{1,9},{5... | collective-permute-start | bytes 1179656 | tf_op jit(solution)/shard_map/ppermute | solution.py:88
  669.5 82.8 %collective-permute-start.95 = (bf16[3,192,560]{2,1,0:T(8,128)(2,1)}, bf16[3,192,560]{2,1,0:T(8,128)(2,1)}, u32[]{:S(2)}, u32[]{:S(2)}) collective-permute-start(bf16[3,192,560]{2,1,0:T(8,128)(2,1)} %get-tuple-element.484), channel_id=1, source_target_pairs={{0,24},{4,28},{8,0},{12,4},{16,8},{20,12},{24,16},{28,20},{1,25},{... | collective-permute-start | bytes 1935368 | tf_op jit(solution)/shard_map/ppermute | solution.py:88
  675.0 78.4 %collective-permute-start.96 = (bf16[3,192,560]{2,1,0:T(8,128)(2,1)}, bf16[3,192,560]{2,1,0:T(8,128)(2,1)}, u32[]{:S(2)}, u32[]{:S(2)}) collective-permute-start(bf16[3,192,560]{2,1,0:T(8,128)(2,1)} %get-tuple-element.483), channel_id=1, source_target_pairs={{0,16},{4,20},{8,24},{12,28},{16,0},{20,4},{24,8},{28,12},{1,17},{... | collective-permute-start | bytes 1935368 | tf_op jit(solution)/shard_map/ppermute | solution.py:88
  675.0 79.7 %collective-permute-start.97 = (bf16[3,192,560]{2,1,0:T(8,128)(2,1)}, bf16[3,192,560]{2,1,0:T(8,128)(2,1)}, u32[]{:S(2)}, u32[]{:S(2)}) collective-permute-start(bf16[3,192,560]{2,1,0:T(8,128)(2,1)} %get-tuple-element.482), channel_id=1, source_target_pairs={{0,8},{4,12},{8,16},{12,20},{16,24},{20,28},{24,0},{28,4},{1,9},{5... | collective-permute-start | bytes 1935368 | tf_op jit(solution)/shard_map/ppermute | solution.py:88
  746.6 45.3 %all-to-all-start.3 = ((bf16[4,2,48,1536]{3,2,1,0:T(8,128)(2,1)}), bf16[4,2,48,1536]{3,2,1,0:T(8,128)(2,1)S(1)}, u32[]{:S(2)}, u32[]{:S(2)}) async-start(bf16[4,2,48,1536]{3,2,1,0:T(8,128)(2,1)} %bitcast.676), calls=%async_computation.3 | async-start | bytes 2359296 | tf_op jit(solution)/shard_map/all_to_all | solution.py:154
  751.8 42.0 %collective-permute-start.79 = (bf16[2048,2,128]{2,0,1:T(8,128)(2,1)}, bf16[2048,2,128]{2,0,1:T(8,128)(2,1)}, u32[]{:S(2)}, u32[]{:S(2)}) collective-permute-start(bf16[2048,2,128]{2,0,1:T(8,128)(2,1)} %bitcast.135), channel_id=1, source_target_pairs={{0,1},{1,0},{2,3},{3,2},{4,5},{5,4},{6,7},{7,6},{8,9},{9,8},{10,11... | collective-permute-start | bytes 3145736 | tf_op jit(solution)/shard_map/ppermute | solution.py:97
  792.0 16.3 %collective-permute-start.90 = (bf16[4,48,1536]{2,1,0:T(8,128)(2,1)S(1)}, bf16[4,48,1536]{2,1,0:T(8,128)(2,1)S(1)}, u32[]{:S(2)}, u32[]{:S(2)}) collective-permute-start(bf16[4,48,1536]{2,1,0:T(8,128)(2,1)S(1)} %fusion.135), channel_id=1, source_target_pairs={{0,4},{4,0},{8,12},{12,8},{16,20},{20,16},{24,28},{28,24},{1,5},{5... | collective-permute-start | bytes 1769480 | tf_op jit(solution)/shard_map/ppermute | solution.py:91
  796.0 22.5 %collective-permute-start.80 = (bf16[4,256,2,128]{3,1,2,0:T(8,128)(2,1)S(1)}, bf16[4,256,2,128]{3,1,2,0:T(8,128)(2,1)S(1)}, u32[]{:S(2)}, u32[]{:S(2)}) collective-permute-start(bf16[4,256,2,128]{3,1,2,0:T(8,128)(2,1)S(1)} %select_bitcast_fusion.15), channel_id=1, source_target_pairs={{0,4},{4,0},{8,12},{12,8},{16,20},{20,16},{24,28},{28,24},{1,5},{5... | collective-permute-start | bytes 1572872 | tf_op jit(solution)/shard_map/ppermute | solution.py:91
  824.3 20.8 %collective-permute-start.91 = (bf16[48,1536]{1,0:T(8,128)(2,1)}, bf16[48,1536]{1,0:T(8,128)(2,1)}, u32[]{:S(2)}, u32[]{:S(2)}) collective-permute-start(bf16[48,1536]{1,0:T(8,128)(2,1)} %get-tuple-element.538), channel_id=1, source_target_pairs={{0,8},{4,12},{8,16},{12,20},{16,24},{20,28},{24,0},{28,4},{1,9},{5... | collective-permute-start | bytes 442376 | tf_op jit(solution)/shard_map/ppermute | solution.py:88
  824.8 20.3 %collective-permute-start.92 = (bf16[48,1536]{1,0:T(8,128)(2,1)}, bf16[48,1536]{1,0:T(8,128)(2,1)}, u32[]{:S(2)}, u32[]{:S(2)}) collective-permute-start(bf16[48,1536]{1,0:T(8,128)(2,1)} %get-tuple-element.540), channel_id=1, source_target_pairs={{0,16},{4,20},{8,24},{12,28},{16,0},{20,4},{24,8},{28,12},{1,17},{... | collective-permute-start | bytes 442376 | tf_op jit(solution)/shard_map/ppermute | solution.py:88
  827.1 18.1 %collective-permute-start.93 = (bf16[48,1536]{1,0:T(8,128)(2,1)}, bf16[48,1536]{1,0:T(8,128)(2,1)}, u32[]{:S(2)}, u32[]{:S(2)}) collective-permute-start(bf16[48,1536]{1,0:T(8,128)(2,1)} %get-tuple-element.539), channel_id=1, source_target_pairs={{0,24},{4,28},{8,0},{12,4},{16,8},{20,12},{24,16},{28,20},{1,25},{... | collective-permute-start | bytes 442376 | tf_op jit(solution)/shard_map/ppermute | solution.py:88
  841.4 38.8 %collective-permute-start.86 = (bf16[4,192,512]{2,1,0:T(8,128)(2,1)}, bf16[4,192,512]{2,1,0:T(8,128)(2,1)}, u32[]{:S(2)}, u32[]{:S(2)}) collective-permute-start(bf16[4,192,512]{2,1,0:T(8,128)(2,1)} %fusion.103), channel_id=1, source_target_pairs={{0,4},{4,0},{8,12},{12,8},{16,20},{20,16},{24,28},{28,24},{1,5},{5... | collective-permute-start | bytes 2359304 | tf_op jit(solution)/shard_map/ppermute | solution.py:91
  845.1 42.6 %collective-permute-start.84 = (bf16[2,128,1536]{2,1,0:T(8,128)(2,1)}, bf16[2,128,1536]{2,1,0:T(8,128)(2,1)}, u32[]{:S(2)}, u32[]{:S(2)}) collective-permute-start(bf16[2,128,1536]{2,1,0:T(8,128)(2,1)} %fusion.105), channel_id=1, source_target_pairs={{0,1},{1,0},{2,3},{3,2},{4,5},{5,4},{6,7},{7,6},{8,9},{9,8},{10,11... | collective-permute-start | bytes 2359304 | tf_op jit(solution)/shard_map/ppermute | solution.py:97
  (160 other events, 1835.7 us)

commit v2 on v1

v2 whole, which is shorter than its diff:
```python
import functools
import math

import jax
import jax.numpy as jnp
from jax import lax
from jax.experimental import pallas as pl
from jax.experimental.pallas import tpu as pltpu
from jax.sharding import PartitionSpec as P

HEADS = 12
KV_HEADS = 2
HEAD_DIM = 128
SPAN = 128
PAIR = 2


EPS = 1e-06
THETA = 1000000.0
FLOOR = -1e30
LOG2E = 1.4426950408889634
BF16 = jnp.bfloat16
F32 = jnp.float32
SMALL = pl.CostEstimate(flops=1, transcendentals=0, bytes_accessed=1)
VMEM_LIMIT = 48 * 1024 * 1024

def norm_rows(rows):
    factor = lax.rsqrt(jnp.mean(rows * rows, axis=-1, keepdims=True) + EPS)
    return (rows * factor, factor)


def norm_back(scaled, unit, factor):
    return factor * (scaled - unit * jnp.mean(scaled * unit, axis=-1, keepdims=True))


def matmul(left, right):
    return jnp.dot(left, right, preferred_element_type=F32)


def contract_rows(left, right):
    return lax.dot_general(left, right, (((0,), (0,)), ((), ())), preferred_element_type=F32)


def contract_cols(left, right):
    return lax.dot_general(left, right, (((1,), (1,)), ((), ())), preferred_element_type=F32)


def positions(order, rows):
    table = jnp.arange(order.shape[1], dtype=jnp.int32)
    slots = rows // SPAN
    picked = jnp.where(slots[None, :, None] == table[None, None, :], order[:, None, :], 0)
    return jnp.sum(picked, axis=-1) * SPAN + (rows % SPAN)[None, :]


def rope_tables(places):
    index = jnp.arange(HEAD_DIM // 2).astype(F32)
    freq = THETA ** (-2.0 * index / HEAD_DIM)
    angle = places.astype(F32)[..., None] * freq
    cosine, sine = jnp.cos(angle), jnp.sin(angle)
    cosine = jnp.concatenate([cosine, cosine], axis=-1)
    return (cosine, jnp.concatenate([-sine, sine], axis=-1))


def dot_nn(left, right):
    return lax.dot_general(left, right, (((1,), (0,)), ((), ())), preferred_element_type=F32)


def dot_nt(left, right):
    return lax.dot_general(left, right, (((1,), (1,)), ((), ())), preferred_element_type=F32)


def dot_tn(left, right):
    return lax.dot_general(left, right, (((0,), (0,)), ((), ())), preferred_element_type=F32)


def call(kernel, scalars, arrays, outs, **options):
    return pl.pallas_call(
        kernel,
        grid_spec=pltpu.PrefetchScalarGridSpec(
            num_scalar_prefetch=len(scalars),
            grid=(1,),
            in_specs=[
                pl.BlockSpec(memory_space=pltpu.HBM) if i in options.get("far", ()) else whole(array.shape)
                for i, array in enumerate(arrays)
            ],
            out_specs=[whole(out.shape) for out in outs],
            scratch_shapes=options.get("scratch", ()),
        ),
        out_shape=outs,
        compiler_params=pltpu.CompilerParams(vmem_limit_bytes=VMEM_LIMIT),
        cost_estimate=SMALL,
    )(*scalars, *arrays)


def whole(shape):
    return pl.BlockSpec(shape, lambda *unused: (0,) * len(shape))


def turn(field):
    return pltpu.roll(field, HEAD_DIM // 2, 1)


AT_Z, AT_X, AT_Y, AT_C, AT_B, AT_U = range(6)


def mix_kernel(depth, group, place, own, near, across, cosine, sine, *rest):
    pieces, far = rest[:depth], rest[depth : 2 * depth]
    units, weights, query, kind, bias_rows, flags = rest[2 * depth :]
    u = place[AT_U]
    rows = weights.shape[1]
    copies = []

    def bring(source, target):
        copies.append(pltpu.make_async_copy(source, target, flags.at[len(copies)]))
        copies[-1].start()

    for d in range(depth):
        from_z = lax.rem(place[AT_Z] - d + depth, depth)
        for k in range(PAIR):
            piece = far[d] if k else pieces[d]
            from_x = place[AT_X] if k == 0 else 1 - place[AT_X]
            bring(piece.at[pl.ds(0, rows)], weights.at[from_z * PAIR + from_x])
            bring(piece.at[pl.ds(rows, 16)], bias_rows.at[PAIR * d + k])
    bring(own, units.at[u])
    bring(near, units.at[u ^ 2])
    bring(across.at[0], units.at[u ^ 1])
    bring(across.at[1], units.at[u ^ 3])
    for copy in copies:
        copy.wait()
    bias = jnp.sum(bias_rows[...].astype(F32), axis=(0, 1))[None]
    model = units.shape[2]
    all_weights = weights[...].reshape(model, weights.shape[2])
    is_key = place[AT_C] == 0
    for i in range(units.shape[0]):
        mixed = dot_nn(units[i], all_weights) + bias
        cos, sin = cosine[i], sine[i]
        for h in range(group):
            field = mixed[:, h * HEAD_DIM : (h + 1) * HEAD_DIM]
            query[i, :, h * HEAD_DIM : (h + 1) * HEAD_DIM] = (field * cos + turn(field) * sin).astype(
                BF16
            )
        field = mixed[:, group * HEAD_DIM :]
        turned = field * cos + turn(field) * sin
        kind[i] = jnp.where(is_key, turned, field).astype(BF16)


def stack_heads(block, group):
    block = block.reshape(SPAN, group * HEAD_DIM)
    return jnp.concatenate(
        [block[:, h * HEAD_DIM : (h + 1) * HEAD_DIM] for h in range(group)], axis=0
    )


def key_mask(first_key, keys, place, group):
    key = first_key + lax.broadcasted_iota(jnp.int32, (keys, group * SPAN), 0)
    row = lax.broadcasted_iota(jnp.int32, (keys, group * SPAN), 1) % SPAN
    return key <= place * SPAN + row


def attend_kernel(
    depth, spans, chunk, group, scale, order, place, query, a_own, a_far, b_own, b_far, out, lse, kv
):
    seq = pl.program_id(0)
    core, x, z = place[AT_C], place[AT_X], place[AT_Z]
    step = query.shape[0] // spans
    slots = depth * PAIR * spans

    def settle(slot, unused):
        blk, span = slot // spans, lax.rem(slot, spans)
        d = lax.rem(z - blk // PAIR + depth, depth)
        there = pl.ds(pl.multiple_of(order[seq, slot] * SPAN, SPAN), SPAN)
        here = pl.ds(span * step, step)
        for mine, other, far in ((a_own, b_own, False), (a_far, b_far, True)):

            @pl.when((lax.rem(blk, PAIR) != x) == far)
            def unused_copy():
                kv[0, core, there] = mine[d, here, 0].reshape(SPAN, HEAD_DIM)
                kv[0, 1 - core, there] = other[d, here, 0].reshape(SPAN, HEAD_DIM)

        return 0

    lax.fori_loop(0, slots, settle, 0)
    for span in range(spans):
        spot = order[seq, place[AT_B] * spans + span]
        queries = stack_heads(query[span * step : (span + 1) * step, 0], group)

        def advance(index, state, masked):
            peak, total, summed = state
            keys = pl.ds(pl.multiple_of(index * chunk, chunk), chunk)
            scores = dot_nt(kv[0, 0, keys], queries)
            if masked:
                allowed = key_mask(index * chunk, chunk, spot, group)
                scores = jnp.where(allowed, scores, FLOOR)
            new_peak = jnp.maximum(peak, jnp.max(scores, axis=0, keepdims=True))
            weights = jnp.exp2((scores - new_peak) * scale)
            fade = jnp.exp2((peak - new_peak) * scale)
            total = total * fade + jnp.sum(weights, axis=0, keepdims=True)
            summed = summed * fade + dot_tn(kv[0, 1, keys], weights.astype(BF16))
            return new_peak, total, summed

        start = (
            jnp.full((1, group * SPAN), FLOOR, F32),
            jnp.zeros((1, group * SPAN), F32),
            jnp.zeros((HEAD_DIM, group * SPAN), F32),
        )
        last = spot * SPAN // chunk
        state = lax.fori_loop(0, last, lambda i, s: advance(i, s, False), start)
        peak, total, summed = advance(last, state, True)
        lse[0, span] = peak * scale + jnp.log2(total)
        result = (summed / total).T.astype(BF16)
        for h in range(group):
            out[span * step : (span + 1) * step, 0, :, h * HEAD_DIM : (h + 1) * HEAD_DIM] = result[
                h * SPAN : (h + 1) * SPAN
            ].reshape(step, SPAN // step, HEAD_DIM)


def attend_back_kernel(
    depth,
    spans,
    chunk,
    group,
    scale,
    factor,
    order,
    place,
    query,
    kv,
    grad,
    out,
    lse,
    cosine,
    sine,
    query_grad,
    keep_own,
    keep_far,
    send_both,
    sums,
):
    seq = pl.program_id(0)
    core, x, z = place[AT_C], place[AT_X], place[AT_Z]
    step = query.shape[0] // spans
    slots = depth * PAIR * spans
    sums[...] = jnp.zeros(sums.shape, F32)
    for span in range(spans):
        spot = order[seq, place[AT_B] * spans + span]
        at = slice(span * step, (span + 1) * step)
        queries = stack_heads(query[at, 0], group)
        grads = stack_heads(grad[at, 0], group)
        results = stack_heads(out[at, 0], group)
        delta = jnp.sum(
            (grads.astype(F32) * results.astype(F32)).T, axis=0, keepdims=True
        )
        level = lse[0, span]

        def advance(index, total, masked):
            keys = pl.ds(pl.multiple_of(index * chunk, chunk), chunk)
            key, value = kv[0, 0, keys], kv[0, 1, keys]
            probs = jnp.exp2(dot_nt(key, queries) * scale - level)
            if masked:
                probs = jnp.where(key_mask(index * chunk, chunk, spot, group), probs, 0.0)
            score_grad = (probs * (dot_nt(value, grads) - delta)).astype(BF16)
            sums[1, keys] += dot_nn(probs.astype(BF16), grads)
            sums[0, keys] += dot_nn(score_grad, queries)
            return total + dot_tn(key, score_grad)

        last = spot * SPAN // chunk
        total = jnp.zeros((HEAD_DIM, group * SPAN), F32)
        total = lax.fori_loop(0, last, lambda i, s: advance(i, s, False), total)
        total = (advance(last, total, True) * factor).T
        cos = cosine[at, 0].reshape(SPAN, HEAD_DIM)
        sin = sine[at, 0].reshape(SPAN, HEAD_DIM)
        for h in range(group):
            field = total[h * SPAN : (h + 1) * SPAN]
            field = (field * cos - turn(field) * sin).astype(BF16)
            query_grad[at, 0, :, h * HEAD_DIM : (h + 1) * HEAD_DIM] = field.reshape(
                step, SPAN // step, HEAD_DIM
            )

    keep_scale = jnp.where(core == 0, factor, 1.0)
    send_scale = jnp.where(core == 0, 1.0, factor)

    def settle(slot, unused):
        blk, span = slot // spans, lax.rem(slot, spans)
        d = lax.rem(z - blk // PAIR + depth, depth)
        there = pl.ds(pl.multiple_of(order[seq, slot] * SPAN, SPAN), SPAN)
        here = pl.ds(span * step, step)
        shape = (step, SPAN // step, HEAD_DIM)
        for keep, send, far in ((keep_own, 0, False), (keep_far, 1, True)):

            @pl.when((lax.rem(blk, PAIR) != x) == far)
            def unused_copy():
                keep[d, here, 0] = (sums[core, there] * keep_scale).astype(BF16).reshape(shape)
                send_both[send, d, here, 0] = (sums[1 - core, there] * send_scale).astype(BF16).reshape(shape)

        return 0

    lax.fori_loop(0, slots, settle, 0)


def project_kernel(transposed, place, *refs):
    count = (len(refs) - 2) // 2
    lefts, rights, (keep, send) = refs[:count], refs[count : 2 * count], refs[2 * count :]
    u = place[AT_U]
    dot = dot_nt if transposed else dot_nn
    for at, target, spot in ((1, send, 0), (3, send, 1), (0, keep, 0), (2, keep, 1)):
        total = None
        for left, right in zip(lefts, rights):
            part = dot(left[u ^ at], right[...])
            total = part if total is None else total + part
        target[spot] = total.astype(target.dtype)


def heads_grad_kernel(place, own, near, across, weights, out):
    u = place[AT_U]
    for at, piece in ((0, own[...]), (2, near[...]), (1, across[0]), (3, across[1])):
        out[u ^ at] = dot_nt(piece, weights[...]).astype(BF16)


def out_share_kernel(place, own, near, across, attended, out):
    u = place[AT_U]
    total = dot_tn(attended[u], own[...])
    total = total + dot_tn(attended[u ^ 2], near[...])
    total = total + dot_tn(attended[u ^ 1], across[0])
    total = total + dot_tn(attended[u ^ 3], across[1])
    out[...] = total.astype(BF16)


def split_tiles_kernel(depth, place, gate, upper, down, gain, *rest):
    pieces, parts = rest[:depth], rest[depth]
    units = parts.shape[3]
    for i, (tile, scaled) in enumerate(((gate, True), (upper, True), (down, False))):
        for k in range(depth):
            part = tile[:, k * units : (k + 1) * units]
            if scaled:
                part = (part.astype(F32) * gain[...]).astype(BF16)
            parts[k, i] = part
    for d in range(depth):
        pieces[d][...] = parts[lax.rem(place[AT_Z] + d, depth)]


def merge_tiles_kernel(depth, place, *refs):
    mine, far, outs = refs[:depth], refs[depth : 2 * depth], refs[2 * depth :]
    for d in range(depth):
        from_z = lax.rem(place[AT_Z] - d + depth, depth)
        for i, out in enumerate(outs):
            out[from_z * PAIR + place[AT_X]] = mine[d][i]
            out[from_z * PAIR + 1 - place[AT_X]] = far[d][i]


def by_source_kernel(place, source, target):
    depth, ulys = source.shape[:2]
    for d in range(depth):
        from_z = lax.rem(place[AT_Z] - d + depth, depth)
        for m, other in enumerate((0, 2, 1, 3)):
            target[place[AT_U] ^ other, from_z] = source[d, m]


def sort_rows_kernel(depth, place, *refs):
    mine, far, outs, rows = refs[:depth], refs[depth : 2 * depth], refs[2 * depth : -1], refs[-1]
    share = outs[0].shape[0]
    for d in range(depth):
        from_z = lax.rem(place[AT_Z] - d + depth, depth)
        rows[from_z * PAIR + place[AT_X]] = mine[d][...]
        rows[from_z * PAIR + 1 - place[AT_X]] = far[d][...]
    for m, out in enumerate(outs):
        out[...] = rows[pl.ds((place[AT_U] ^ m) * share, share)]


def place_rows_kernel(place, *refs):
    out = refs[-1]
    for m, part in enumerate(refs[:-1]):
        out[:, place[AT_U] ^ m] = part[...]


def choose_kernel(place, *refs):
    shares, (keep, send) = refs[:-2], refs[-2:]
    for i, share in enumerate(shares):
        keep[:, i] = share[:, place[AT_X]]
        send[:, i] = share[:, 1 - place[AT_X]]


def fold_kernel(depth, place, keep, got, *outs):
    for d in range(depth):
        at = lax.rem(place[AT_Z] + d, depth)
        outs[d][...] = (keep[at].astype(F32) + got[at].astype(F32)).astype(BF16)


def split_uly_kernel(place, pieces, own, near):
    total = None
    parts = []
    for m in range(4):
        total = None
        for z in range(pieces.shape[0]):
            part = pieces[z, 0, place[AT_U] ^ m].astype(F32)
            total = part if total is None else total + part
        parts.append(total.astype(BF16))
    own[0], own[1], near[0], near[1] = parts


def pick_uly_kernel(place, share, own, near):
    own[0], own[1] = share[:, place[AT_U]], share[:, place[AT_U] ^ 1]
    near[0], near[1] = share[:, place[AT_U] ^ 2], share[:, place[AT_U] ^ 3]


def group_rows_kernel(place, own, near, across, keep, send, rows):
    share = own.shape[1]
    for m, part in ((0, own[0]), (2, near[0]), (1, across[0]), (3, across[1])):
        rows[pl.ds((place[AT_U] ^ m) * share, share)] = part
    for z in range(keep.shape[0]):
        keep[z, 0] = rows[z * PAIR + place[AT_X]]
        send[z, 0] = rows[z * PAIR + 1 - place[AT_X]]


def finish_qkv_kernel(place, *refs):
    heads, kinds = refs[:3], refs[3:6]
    weight, gain, grad, grad_gain, bias, head_parts, kind_parts = refs[6:]
    width, side = heads[0].shape[2], heads[0].shape[2] * 4
    for parts, (own, near, across) in ((head_parts, heads), (kind_parts, kinds)):
        parts[place[AT_U]] = own[0]
        parts[place[AT_U] ^ 2] = near[0]
        parts[place[AT_U] ^ 1] = across[0]
        parts[place[AT_U] ^ 3] = across[1]
    total = jnp.zeros(grad_gain.shape, F32)
    for u in range(4):
        bias[u] = kind_parts[u, :16].astype(F32)
        start = side + (u % 2) * KV_HEADS * HEAD_DIM + (u // 2) * HEAD_DIM
        for at, part in (
            (slice(u * width, (u + 1) * width), head_parts[u]),
            (slice(start, start + HEAD_DIM), kind_parts[u, 16:]),
        ):
            part = part.astype(F32)
            grad[:, at] = part * gain[...]
            total = total + jnp.sum(part * weight[:, at].astype(F32), axis=1, keepdims=True)
    grad_gain[...] = total


def finish_kernel(depth, gates, uppers, downs, gate, upper, gain, grad_gate, grad_upper, grad_down, grad_gain):
    units = downs.shape[3]
    total = jnp.zeros(grad_gain.shape, F32)
    for k in range(depth):
        at = slice(k * units, (k + 1) * units)
        part = gates[k, 0].astype(F32)
        grad_gate[:, at] = part * gain[...]
        total = total + jnp.sum(part * gate[:, at].astype(F32), axis=1, keepdims=True)
        part = uppers[k, 0].astype(F32)
        grad_upper[:, at] = part * gain[...]
        total = total + jnp.sum(part * upper[:, at].astype(F32), axis=1, keepdims=True)
        grad_down[:, at] = downs[k, 0].astype(F32)
    grad_gain[...] = total


def like(shape, kind=BF16):
    return jax.ShapeDtypeStruct(shape, kind)


def together(*values):
    return lax.optimization_barrier(values)


def after(value, *others):
    return lax.optimization_barrier((value, others))[0]


class Grid:
    def __init__(self):
        self.blocks = lax.axis_size("blk")
        self.ulys = lax.axis_size("uly")
        self.depth = self.blocks // PAIR
        self.b = lax.axis_index("blk")
        self.u = lax.axis_index("uly")
        self.z = self.b // PAIR
        self.x = self.b % PAIR
        self.y = self.u // 2
        self.c = self.u % 2

    def to_z(self, value, step):
        pairs = [
            (z * PAIR + x, ((z + step) % self.depth) * PAIR + x)
            for z in range(self.depth)
            for x in range(PAIR)
        ]
        return lax.ppermute(value, "blk", pairs)

    def swap_x(self, value):
        return lax.ppermute(value, "blk", [(i, i ^ 1) for i in range(self.blocks)])

    def swap_y(self, value):
        return lax.ppermute(value, "uly", [(i, i ^ 2) for i in range(self.ulys)])

    def swap_both(self, value):
        return lax.ppermute(value, "uly", [(i, i ^ 3) for i in range(self.ulys)])

    def swap_core(self, value):
        return lax.ppermute(value, "uly", [(i, i ^ 1) for i in range(self.ulys)])


def paired(bit, mine, other, axis):
    low = jnp.where(bit == 0, mine, other)
    high = jnp.where(bit == 0, other, mine)
    return jnp.stack([low, high], axis=axis)


def pick(bit, array, axis):
    low = lax.index_in_dim(array, 0, axis, keepdims=False)
    high = lax.index_in_dim(array, 1, axis, keepdims=False)
    return jnp.where(bit == 0, low, high), jnp.where(bit == 0, high, low)


def order_z(grid, pieces):
    stacked = jnp.stack(pieces[::-1] + pieces[::-1][:-1])
    start = (grid.depth - 1 - grid.z) % grid.depth
    return lax.dynamic_slice_in_dim(stacked, start, grid.depth, 0)


def gather_uly(grid, value):
    both = paired(grid.y, value, grid.swap_y(value), 0)
    every = paired(grid.c, both, grid.swap_core(both), 1)
    return every.reshape((grid.ulys,) + value.shape)


def scatter_uly(grid, parts, kind=BF16):
    parts = parts.reshape((2, 2) + parts.shape[1:])
    keep, send = pick(grid.c, parts, 1)
    both = keep.astype(F32) + grid.swap_core(send.astype(kind)).astype(F32)
    keep, send = pick(grid.y, both, 0)
    return keep + grid.swap_y(send.astype(kind)).astype(F32)


def gather_blk(grid, value):
    pieces = [value] + [grid.to_z(value, d) for d in range(1, grid.depth)]
    pairs = [paired(grid.x, piece, grid.swap_x(piece), 0) for piece in pieces]
    return order_z(grid, pairs)


def exchange_z(grid, parts):
    pieces = [lax.dynamic_index_in_dim(parts, grid.z, 0, keepdims=False)]
    for d in range(1, grid.depth):
        there = (grid.z + d) % grid.depth
        pieces.append(grid.to_z(lax.dynamic_index_in_dim(parts, there, 0, keepdims=False), d))
    return pieces


def exchange_z_all(grid, parts):
    groups = [[z * PAIR + x for z in range(grid.depth)] for x in range(PAIR)]
    return lax.all_to_all(
        parts, "blk", split_axis=0, concat_axis=0, axis_index_groups=groups, tiled=True
    )


def scatter_blk(grid, parts):
    keep, send = pick(grid.x, parts, 1)
    both = keep.astype(F32) + grid.swap_x(send.astype(BF16)).astype(F32)
    return jnp.sum(exchange_z_all(grid, both.astype(BF16)).astype(F32), axis=0)


def exchange_uly(parts):
    return lax.all_to_all(parts, "uly", split_axis=0, concat_axis=0, tiled=True)


def per_device(
    tokens,
    span_order,
    attn_gain,
    qkv_weight,
    qkv_bias,
    out_weight,
    ffn_gain,
    gate_weight,
    up_weight,
    down_weight,
    cotangent,
):
    grid = Grid()
    local_rows, seqs, model = tokens.shape
    count = local_rows * seqs
    ulys = grid.ulys
    depth = grid.depth
    blocks = grid.blocks
    cycle_rows = local_rows * ulys
    spans = cycle_rows // SPAN
    slots = blocks * spans
    group = HEADS // ulys
    factor = 1.0 / math.sqrt(HEAD_DIM)
    width = group * HEAD_DIM
    columns = width + HEAD_DIM
    shard = qkv_weight.shape[0]
    block_model = shard * ulys
    chunk = math.gcd(slots, 4) * SPAN
    side = HEADS * HEAD_DIM
    place = jnp.stack([grid.z, grid.x, grid.y, grid.c, grid.b, grid.u]).astype(jnp.int32)

    def by_seq(array):
        return jnp.transpose(array, (1, 0, 2)).reshape(count, model)

    def by_row(array):
        return jnp.transpose(array.reshape(seqs, local_rows, model), (1, 0, 2))

    def by_uly(array):
        lead = array.shape[0]
        heads = array[:, :side].reshape(lead, ulys, width)
        kinds = array[:, side:].reshape(lead, 2, KV_HEADS, HEAD_DIM)
        kinds = jnp.transpose(kinds, (0, 2, 1, 3)).reshape(lead, ulys, HEAD_DIM)
        return jnp.transpose(jnp.concatenate([heads, kinds], axis=-1), (1, 0, 2))

    rows = by_seq(tokens).astype(F32)
    unit_one, factor_one = norm_rows(rows)
    unit_own = unit_one.astype(BF16)
    unit_near = grid.swap_y(unit_own)
    gain_one = attn_gain.astype(F32)[:, None]
    scaled = (qkv_weight.astype(F32) * gain_one).astype(BF16)
    heads_share = blocks // ulys
    owned_columns = qkv_bias.shape[0]
    column_start = (grid.b * ulys + grid.u) * owned_columns
    bias_row = lax.dynamic_update_slice(
        jnp.zeros((16, owned_columns * blocks * ulys), BF16),
        jnp.pad(qkv_bias[None], ((0, 15), (0, 0))),
        (0, column_start),
    )
    by_head = by_uly(jnp.concatenate([scaled, bias_row], axis=0))
    by_head = exchange_uly(by_head)
    block_rows = jnp.concatenate(
        [by_head[:, :shard].reshape(block_model, columns), jnp.sum(by_head[:, shard:], axis=0)],
        axis=0,
    )
    qkv_mine = [block_rows] + [grid.to_z(block_rows, d) for d in range(1, depth)]
    first_far = grid.swap_x(block_rows)
    cot_flat = by_seq(cotangent)
    *qkv_mine, first_far, unit_near = together(*qkv_mine, first_far, unit_near)

    gain_two = ffn_gain.astype(F32)[:, None]
    hidden_units = gate_weight.shape[1] // depth
    tile_pieces = call(
        functools.partial(split_tiles_kernel, depth),
        [place],
        [gate_weight, up_weight, down_weight.T, gain_two],
        [like((3, block_model, hidden_units))] * depth,
        scratch=[pltpu.VMEM((depth, 3, block_model, hidden_units), BF16)],
    )
    qkv_far = [first_far] + [grid.swap_x(piece) for piece in qkv_mine[1:]]
    unit_across = grid.swap_core(jnp.stack([unit_own, unit_near]))
    out_first, cot_first = after((out_weight, cot_flat), *qkv_mine[1:])
    out_mine = [out_first] + [grid.to_z(out_first, d) for d in range(1, depth)]
    cot_near = grid.swap_y(cot_first)
    *held, unit_across, cot_near = together(*qkv_far, *out_mine, unit_across, cot_near)
    qkv_far, out_mine = held[:depth], held[depth:]
    unit_parts = (unit_own, unit_near, unit_across)

    head_rows = grid.b * cycle_rows + jnp.arange(cycle_rows, dtype=jnp.int32)
    places = positions(span_order, head_rows).reshape(seqs, ulys, local_rows)
    places = jnp.transpose(places, (1, 0, 2)).reshape(ulys, count)
    cosine, sine = rope_tables(places)
    units, qkv_part, query, kind = call(
        functools.partial(mix_kernel, depth, group),
        [place],
        [*unit_parts, cosine, sine, *qkv_mine, *qkv_far],
        [
            like((ulys, count, model)),
            like((blocks, block_model, columns)),
            like((ulys, count, width)),
            like((ulys, count, HEAD_DIM)),
        ],
        scratch=[
            pltpu.VMEM((blocks, 16, columns), BF16),
            pltpu.SemaphoreType.DMA((2 * blocks + ulys,)),
        ],
        far=(0, 1, 2, *range(5, 2 * depth + 5)),
    )
    units = units.reshape(ulys * count, model)
    qkv_part = qkv_part.reshape(model, columns)
    order = sorted(range(1, depth), key=lambda d: (min(d, depth - d), d))
    kinds = [kind] + [grid.to_z(kind, d) for d in range(1, depth)]
    *held, kind = after((*out_mine, *tile_pieces, kind), kind)
    out_mine, tile_pieces = held[:depth], held[depth:]
    out_far = [grid.swap_x(piece) for piece in out_mine]
    tile_mine = {0: tile_pieces[0]}
    tile_mine[order[0]] = grid.to_z(tile_pieces[order[0]], order[0])
    *held, cot_near = together(*kinds, *out_far, cot_near)
    kinds, out_far = held[:depth], held[depth:]

    a_own = jnp.stack(kinds)
    a_far = grid.swap_x(a_own)
    b_own = grid.swap_core(a_own)
    out_sets = call(
        functools.partial(sort_rows_kernel, depth),
        [place],
        [*out_mine, *out_far],
        [like((blocks // ulys, shard, model))] * ulys,
        scratch=[pltpu.VMEM((blocks, shard, model), BF16)],
    )
    out_sets = [
        out_sets[0],
        grid.swap_core(out_sets[1]),
        grid.swap_y(out_sets[2]),
        grid.swap_both(out_sets[3]),
    ]
    middle, late = order[1:-1], order[-1]
    for d in middle:
        tile_mine[d] = grid.to_z(after(tile_pieces[d], *kinds), d)
    a_far, b_own, tile_mine[order[0]], *held = together(
        a_far, b_own, tile_mine[order[0]], *[tile_mine[d] for d in middle]
    )
    tile_mine.update(zip(middle, held))

    b_far = grid.swap_core(a_far)
    tile_far = {0: grid.swap_x(after(tile_mine[0], a_far))}
    tile_far[order[0]] = grid.swap_x(tile_mine[order[0]])
    tile_mine[late] = grid.to_z(after(tile_pieces[late], a_far), late)

    def over_uly(piece):
        both = jnp.concatenate([piece, grid.swap_y(piece)], axis=0)
        return jnp.concatenate([both, grid.swap_core(both)], axis=0)

    grad_rows = cot_flat.astype(F32)

    scale = factor * LOG2E
    kv_shape = (depth, ulys, seqs, local_rows, HEAD_DIM)
    kv_spec = pl.BlockSpec(
        (depth, ulys, 1, local_rows, HEAD_DIM), lambda s, *unused: (0, 0, s, 0, 0)
    )
    heads_shape = (ulys, seqs, local_rows, width)
    heads_spec = pl.BlockSpec((ulys, 1, local_rows, width), lambda s, *unused: (0, s, 0, 0))
    lse_spec = pl.BlockSpec((1, spans, 1, group * SPAN), lambda s, *unused: (s, 0, 0, 0))
    table_shape = (ulys, seqs, local_rows, HEAD_DIM)
    table_spec = pl.BlockSpec((ulys, 1, local_rows, HEAD_DIM), lambda s, *unused: (0, s, 0, 0))
    sorted_spec = pl.BlockSpec((1, 2, slots * SPAN, HEAD_DIM), lambda s, *unused: (s, 0, 0, 0))
    params = pltpu.CompilerParams(vmem_limit_bytes=VMEM_LIMIT)
    query = query.reshape(heads_shape)
    attended, lse, kv = pl.pallas_call(
        functools.partial(attend_kernel, depth, spans, chunk, group, scale),
        grid_spec=pltpu.PrefetchScalarGridSpec(
            num_scalar_prefetch=2,
            grid=(seqs,),
            in_specs=[heads_spec] + [kv_spec] * 4,
            out_specs=[heads_spec, lse_spec, sorted_spec],
        ),
        out_shape=[
            like(heads_shape),
            like((seqs, spans, 1, group * SPAN), F32),
            like((seqs, 2, slots * SPAN, HEAD_DIM)),
        ],
        compiler_params=params,
        cost_estimate=SMALL,
    )(span_order, place, query, *[part.reshape(kv_shape) for part in (a_own, a_far, b_own, b_far)])
    flat = attended.reshape(ulys, count, width)
    out_sets = after(tuple(out_sets), attended)
    (out_part,) = call(
        place_rows_kernel, [place], out_sets, [like((blocks // ulys, ulys, shard, model))]
    )
    out_part = out_part.reshape(width, model)
    keep, send = call(
        functools.partial(project_kernel, False),
        [place],
        [flat, out_part],
        [like((2, count, model), F32), like((2, count, model))],
    )
    got = grid.swap_core(send)
    got, tile_far[0] = together(got, tile_far[0])
    both = keep + got.astype(F32)
    for d in middle:
        tile_far[d] = grid.swap_x(after(tile_mine[d], got))
    got = grid.swap_y(both[1].astype(BF16))
    got, tile_far[order[0]], tile_mine[late], *held = together(
        got, tile_far[order[0]], tile_mine[late], *[tile_far[d] for d in middle]
    )
    tile_far.update(zip(middle, held))
    hidden = rows + both[0] + got.astype(F32)

    unit_two, factor_two = norm_rows(hidden)
    mid_own = unit_two.astype(BF16)
    mid_near = grid.swap_y(mid_own)
    mid_pieces = [mid_own, grid.to_z(mid_own, 1)]
    cot_pieces = [cot_first, grid.to_z(after(cot_first, got), 1)]
    tile_far[late] = grid.swap_x(after(tile_mine[late], got))
    mid_near, mid_pieces[1] = together(mid_near, mid_pieces[1])
    for d in range(2, depth):
        mid_pieces.append(grid.to_z(mid_pieces[-1], 1))
        cot_pieces.append(grid.to_z(cot_pieces[-1], 1))

    def chunk_of(own, near):
        both = jnp.concatenate([own, near], axis=0)
        return jnp.concatenate([both, grid.swap_core(both)], axis=0)

    mid_chunks = [chunk_of(mid_own, mid_near)] + [over_uly(piece) for piece in mid_pieces[1:]]
    cot_chunks = [chunk_of(cot_first, cot_near)] + [over_uly(piece) for piece in cot_pieces[1:]]
    gate_used, upper_used, down_used = [
        tile.reshape(model, hidden_units)
        for tile in call(
            functools.partial(merge_tiles_kernel, depth),
            [place],
            [tile_mine[d] for d in range(depth)] + [tile_far[d] for d in range(depth)],
            [like((blocks, block_model, hidden_units))] * 3,
        )
    ]
    actives, gate_grads, upper_grads, back_chunks = [], [], [], []
    for mid, cot in zip(mid_chunks, cot_chunks):
        gate = matmul(mid, gate_used)
        upper = matmul(mid, upper_used)
        sigmoid = jax.nn.sigmoid(gate)
        active_grad = matmul(cot, down_used)
        actives.append((gate * sigmoid * upper).astype(BF16))
        gate_grad = (active_grad * upper * sigmoid * (1.0 + gate * (1.0 - sigmoid))).astype(BF16)
        upper_grad = (active_grad * gate * sigmoid).astype(BF16)
        gate_grads.append(gate_grad)
        upper_grads.append(upper_grad)
        back_chunks.append(
            contract_cols(gate_grad, gate_used) + contract_cols(upper_grad, upper_used)
        )
    def over_core(chunk):
        chunk = chunk.reshape(2, 2, count, model)
        return chunk[0].astype(F32) + grid.swap_core(chunk[1].astype(BF16)).astype(F32)

    def over_y(both):
        return both[0] + grid.swap_y(both[1].astype(BF16)).astype(F32)

    def halve(shares, rows):
        shape = (depth, PAIR, *rows, shares[0].shape[-1])
        shares = [share.astype(BF16).reshape(shape) for share in shares]
        half = like((depth, len(shares), *rows, shape[-1]))
        return call(choose_kernel, [place], shares, [half] * 2)

    def fold(keep, got):
        return exchange_z_all(grid, (keep.astype(F32) + got.astype(F32)).astype(BF16))

    z_groups = [[z * PAIR + x for z in range(depth)] for x in range(PAIR)]
    tile_rows = (block_model,)
    mid_parts = [over_y(over_core(chunk)) for chunk in back_chunks]
    back_pieces = [grid.to_z(mid_parts[d].astype(BF16), -d) for d in range(1, depth)]
    mid_all = after(jnp.concatenate(mid_chunks), *back_chunks)
    cot_all = jnp.concatenate(cot_chunks)
    active_all = jnp.concatenate(actives)
    gate_keep, gate_send = halve([contract_rows(mid_all, jnp.concatenate(gate_grads))], tile_rows)
    upper_keep, upper_send = halve(
        [contract_rows(after(mid_all, gate_send), jnp.concatenate(upper_grads))], tile_rows
    )
    active_now = after(active_all, upper_send)
    down_keep, down_send = halve([contract_rows(cot_all, active_now)], tile_rows)
    gate_got = grid.swap_x(gate_send)
    upper_got = grid.swap_x(after(upper_send, gate_got))
    down_got = grid.swap_x(after(down_send, upper_got))
    first, gate_got, upper_got, down_send, *back_pieces = together(
        mid_parts[0], gate_got, upper_got, down_send, *back_pieces
    )
    mid_grad = first + sum(piece.astype(F32) for piece in back_pieces)

    hidden_grad = grad_rows + norm_back(mid_grad, unit_two, factor_two)
    branch_own = hidden_grad.astype(BF16)
    branch_near = grid.swap_y(branch_own)
    out_all = contract_cols(after(active_all, branch_own), down_used).astype(BF16)
    gate_owned = fold(*after((gate_keep, gate_got), branch_own))
    branch_near, out_all, down_got = together(branch_near, out_all, down_got)
    branch_across = grid.swap_core(jnp.stack([branch_own, branch_near]))
    branch_parts = (branch_own, branch_near, branch_across)
    (grad_heads,) = call(
        heads_grad_kernel, [place], [*branch_parts, out_part], [like((ulys, count, width))]
    )

    grad_heads = grad_heads.reshape(heads_shape)
    both_spec = pl.BlockSpec(
        (2, depth, ulys, 1, local_rows, HEAD_DIM), lambda s, *unused: (0, 0, 0, s, 0, 0)
    )
    query_grad, keep_own, keep_far, send_both = pl.pallas_call(
        functools.partial(attend_back_kernel, depth, spans, chunk, group, scale, factor),
        grid_spec=pltpu.PrefetchScalarGridSpec(
            num_scalar_prefetch=2,
            grid=(seqs,),
            in_specs=[heads_spec, sorted_spec]
            + [heads_spec] * 2
            + [lse_spec]
            + [table_spec] * 2,
            out_specs=[heads_spec] + [kv_spec] * 2 + [both_spec],
            scratch_shapes=[pltpu.VMEM((2, slots * SPAN, HEAD_DIM), F32)],
        ),
        out_shape=[like(heads_shape)] + [like(kv_shape)] * 2 + [like((2, *kv_shape))],
        compiler_params=params,
        cost_estimate=SMALL,
    )(
        span_order,
        place,
        query,
        kv,
        grad_heads,
        attended,
        lse,
        cosine.reshape(table_shape),
        sine.reshape(table_shape),
    )
    got_far, got_own = [
        jnp.concatenate([grid.swap_core(part) for part in jnp.split(send_both[k], 2, axis=0)])
        for k in (1, 0)
    ]
    query_grad = query_grad.reshape(ulys * count, width)
    got_far, got_own, query_grad, gate_owned = together(got_far, got_own, query_grad, gate_owned)
    upper_owned = fold(*after((upper_keep, upper_got), gate_owned))
    (out_all,) = call(
        by_source_kernel,
        [place],
        [after(out_all, got_far).reshape(depth, ulys, count, model)],
        [like((ulys, depth, count, model))],
    )
    from_x = grid.swap_x((keep_far.astype(F32) + got_far.astype(F32)).astype(BF16))
    share_parts = after(branch_parts, got_far)
    (out_share,) = call(out_share_kernel, [place], [*share_parts, flat], [like((width, model))])
    out_own, out_near = call(
        pick_uly_kernel,
        [place],
        [out_share.reshape(heads_share, ulys, shard, model)],
        [like((2, heads_share, shard, model))] * 2,
    )
    head_keep, head_send = halve([contract_rows(units, query_grad)], (ulys, shard))
    from_x, head_send, out_near, out_all = together(from_x, head_send, out_near, out_all)
    out_all = lax.psum_scatter(out_all, "uly", scatter_dimension=0, tiled=False)
    out_all = lax.psum_scatter(
        out_all, "blk", scatter_dimension=0, axis_index_groups=z_groups, tiled=False
    )
    kind_parts = keep_own.astype(F32) + got_own.astype(F32) + from_x.astype(F32)
    kind_parts = kind_parts.astype(BF16)
    kind_back = [grid.to_z(kind_parts[d], -d) for d in range(1, depth)]
    head_got = grid.swap_x(head_send)
    out_near = grid.swap_y(out_near)
    *kind_back, out_near, kind_parts, head_got, upper_owned = together(
        *kind_back, out_near, kind_parts, head_got, upper_owned
    )
    out_across = grid.swap_core(jnp.stack([out_own[1], out_near[1]]))
    head_pieces = fold(head_keep, head_got)
    kind_grad = kind_parts[0].astype(F32)
    for piece in kind_back:
        kind_grad = kind_grad + piece.astype(F32)
    kind_grad = kind_grad.reshape(ulys * count, HEAD_DIM)
    turned = jnp.roll(kind_grad, HEAD_DIM // 2, axis=1)
    is_key = grid.c == 0
    flat_cosine = cosine.reshape(ulys * count, HEAD_DIM)
    flat_sine = sine.reshape(ulys * count, HEAD_DIM)
    kind_grad = jnp.where(is_key, kind_grad * flat_cosine - turned * flat_sine, kind_grad)
    kind_grad = kind_grad.astype(BF16)

    bias = jnp.sum(query_grad.astype(F32), axis=0).reshape(group, HEAD_DIM)
    bias = jnp.concatenate([bias, jnp.sum(kind_grad.astype(F32), axis=0)[None]], axis=0)
    bias = jnp.pad(bias.astype(BF16), ((0, 16 - group - 1), (0, 0)))
    bias = jnp.broadcast_to(bias, (blocks, ulys, 16, HEAD_DIM))
    share = contract_rows(units, kind_grad).astype(BF16)
    share = share.reshape(blocks, ulys, shard, HEAD_DIM)
    share = jnp.concatenate([bias, share], axis=2)
    kind_keep, kind_send = halve([share], (ulys, shard + 16))
    kind_got = grid.swap_x(kind_send)
    keep, send = call(
        functools.partial(project_kernel, True),
        [place],
        [
            query_grad.reshape(ulys, count, width),
            kind_grad.reshape(ulys, count, HEAD_DIM),
            qkv_part[:, :width],
            qkv_part[:, width:],
        ],
        [like((2, count, model), F32), like((2, count, model))],
    )
    send, kind_got, out_across = after((send, kind_got, out_across), send)
    both = keep + grid.swap_core(send).astype(F32)
    out_keep, out_send = call(
        group_rows_kernel,
        [place],
        [out_own, out_near, out_across],
        [like((depth, 1, shard, model))] * 2,
        scratch=[pltpu.VMEM((blocks, shard, model), BF16)],
    )
    out_got = grid.swap_x(out_send)
    down_owned = fold(*after((down_keep, down_got), head_pieces))
    out_pieces = fold(*after((out_keep, out_got), down_owned))
    kind_pieces = call(
        functools.partial(fold_kernel, depth),
        [place],
        [kind_keep, kind_got],
        [like(kind_keep.shape[1:])] * depth,
    )
    kind_pieces = [kind_pieces[0]] + [grid.to_z(kind_pieces[d], d) for d in range(1, depth)]
    kind_pieces = jnp.stack(kind_pieces)

    def to_owners(pieces):
        own, near = call(
            split_uly_kernel, [place], [pieces], [like((2, *pieces.shape[3:]))] * 2
        )
        near = grid.swap_y(near)
        return own, near, grid.swap_core(jnp.stack([own[1], near[1]]))

    head_owned = to_owners(head_pieces)
    kind_owned = to_owners(kind_pieces)
    grad_qkv, grad_gain_one, bias = call(
        finish_qkv_kernel,
        [place],
        [*head_owned, *kind_owned, qkv_weight, gain_one],
        [
            like(qkv_weight.shape, F32),
            like((shard, 1), F32),
            like((ulys, 16, HEAD_DIM), F32),
        ],
        scratch=[
            pltpu.VMEM((ulys, shard, width), BF16),
            pltpu.VMEM((ulys, shard + 16, HEAD_DIM), BF16),
        ],
    )
    grad_gain_one = grad_gain_one[:, 0]
    kind_bias = bias[:, group].reshape(KV_HEADS, 2, HEAD_DIM)
    bias = jnp.concatenate(
        [bias[:, :group].reshape(-1), jnp.transpose(kind_bias, (1, 0, 2)).reshape(-1)]
    )
    grad_bias = lax.dynamic_slice_in_dim(bias, column_start, owned_columns, 0)
    grad_out = jnp.sum(out_pieces[:, 0].astype(F32), axis=0)
    result = hidden + after(out_all, grad_qkv).astype(F32)
    output = by_row(result.astype(BF16))
    normed_grad = both[0] + grid.swap_y(both[1].astype(BF16)).astype(F32)
    grad_tokens = by_row(hidden_grad + norm_back(normed_grad, unit_one, factor_one))
    tile_shape = gate_weight.shape
    grad_gate, grad_upper, grad_down, gain_part = call(
        functools.partial(finish_kernel, depth),
        [],
        [*after((gate_owned, upper_owned, down_owned), head_pieces), gate_weight, up_weight, gain_two],
        [like(tile_shape, F32)] * 3 + [like((block_model, 1), F32)],
    )
    grad_down = grad_down.T
    grad_gain_two = scatter_uly(grid, gain_part.reshape(ulys, -1), F32)
    return (
        output,
        grad_tokens,
        grad_gain_one,
        grad_qkv,
        grad_bias,
        grad_out,
        grad_gain_two.reshape(-1),
        grad_gate,
        grad_upper,
        grad_down,
    )


def solution(mesh):
    in_specs = (
        P(("blk", "uly"), None, None),
        P(),
        P(("blk", "uly")),
        P(("blk", "uly"), None),
        P(("blk", "uly")),
        P(("blk", "uly"), None),
        P("blk"),
        P("blk", "uly"),
        P("blk", "uly"),
        P("uly", "blk"),
        P(("blk", "uly"), None, None),
    )
    out_specs = (
        P(("blk", "uly"), None, None),
        P(("blk", "uly"), None, None),
        P(("blk", "uly")),
        P(("blk", "uly"), None),
        P(("blk", "uly")),
        P(("blk", "uly"), None),
        P(("blk", "uly")),
        P("blk", "uly"),
        P("blk", "uly"),
        P("uly", "blk"),
    )
    return jax.shard_map(
        per_device, mesh=mesh, in_specs=in_specs, out_specs=out_specs, check_vma=False
    )
```

time: 935 us -> 639 us (0.68)
  other arithmetic: 136 us -> 55.6 us
  blocking collectives: 72.6 us -> 0 us
  Pallas kernels: 0 us -> 70.8 us
  matrix products: 127 us -> 61.8 us
  local copies, waits for them, and re-layouts: 131 us -> 70.4 us
  waiting for transfers between devices: 305 us -> 248 us
  starting transfers between devices: 139 us -> 107 us
  between operations: 3.6 us -> 16.5 us
    pallas_call x0 -> x24, Pallas kernels: none -> 70.8 us  [the longest x22 48.2 us: call(): pl.pallas_call(kernel, grid_spec=pltpu.PrefetchScalarGridSpec(num_scalar_...]
    dot_general x28 -> x0, matrix products: 60.9 us -> none  [the longest x4 13.3 us: forward_step(): jnp.einsum('shrk,ksd->shrd', weights.astype(BF16), block[:, :, 1], prefer...]
    ppermute x21, waiting for transfers between devices: 84.6 us -> 36.3 us  [swap_y(): return lax.ppermute(value, 'uly', [(i, i ^ 2) for i in range(self.ulys)])]
    ppermute x36 -> x27, starting transfers between devices: 77.1 us -> 32.8 us  [to_z(): return lax.ppermute(value, 'blk', pairs)]
    unnamed x1 -> x0, blocking collectives: 40.2 us -> none
    all_to_all x0 -> x5, waiting for transfers between devices: none -> 31.1 us  [exchange_z_all(): lax.all_to_all(parts, 'blk', split_axis=0, concat_axis=0, axis_index_grou...]
    ppermute x36 -> x27, waiting for transfers between devices: 140 us -> 110 us  [to_z(): return lax.ppermute(value, 'blk', pairs)]
    psum x1 -> x0, blocking collectives: 27.3 us -> none  [per_device(): bias_part = lax.psum(jnp.sum(mixed_grad.astype(F32), axis=0), 'blk')]
  transfers between devices with their start and end apart: 104 -> 104, of which waited for: 36 -> 45; matrix products, arithmetic and copies ran while one was open for 41% -> 22% of each run, Pallas kernels for 0% -> 10%
where the time goes in v2:
time: 639 us; the launch traced here: 630 us
  waiting for transfers between devices  248 us (39%)
  starting transfers between devices  107 us (17%)
  Pallas kernels  70.8 us (11%)
  local copies, waits for them, and re-layouts  70.4 us (11%)
  matrix products  61.8 us (10%)
  other arithmetic  55.6 us (9%)
  between operations  16.5 us (3%)
    ppermute x27, waiting for transfers between devices, to_z(): return lax.ppermute(value, 'blk', pairs)  110 us
    ppermute x20, waiting for transfers between devices, swap_x(): return lax.ppermute(value, 'blk', [(i, i ^ 1) for i in range(self.blocks)])  64.3 us
    pallas_call x22, Pallas kernels, call(): pl.pallas_call(kernel, grid_spec=pltpu.PrefetchScalarGridSpec(num_scalar_...  48.2 us
    unnamed x252, local copies, waits for them, and re-layouts  47.1 us
    ppermute x21, waiting for transfers between devices, swap_y(): return lax.ppermute(value, 'uly', [(i, i ^ 2) for i in range(self.ulys)])  36.3 us
    ppermute x27, starting transfers between devices, to_z(): return lax.ppermute(value, 'blk', pairs)  32.8 us
    all_to_all x5, waiting for transfers between devices, exchange_z_all(): lax.all_to_all(parts, 'blk', split_axis=0, concat_axis=0, axis_index_grou...  31.1 us
    ppermute x20, starting transfers between devices, swap_x(): return lax.ppermute(value, 'blk', [(i, i ^ 1) for i in range(self.blocks)])  23.5 us
  transfers between devices with their start and end apart: 104, of which 45 were waited for; matrix products, arithmetic and copies ran while one was open for 22% of the time, Pallas kernels for 10%

profile of v2, /device:TPU:0, one launch (start us, length us, event | category | flops | bytes accessed | tf_op | source)
XLA Modules:
  0.0 630.3 jit_solution(10789924964435181409)
XLA Ops:
  11.2 4.2 all-to-all-start
  24.2 2.6 collective-permute-start.1
  29.9 2.6 collective-permute-done.rest_1_
  32.5 7.5 %collective-permute-done.1.rest_2_ = bf16[208,512]{1,0:T(8,128)(2,1)S(1)} collective-permute-done((bf16[208,512]{1,0:T(8,128)(2,1)S(1)}, bf16[208,512]{1,0:T(8,128)(2,1)S(1)}, u32[]{:S(2)}, u32[]{:S(2)}) %collective-permute-start.1) | collective-permute-done | bytes 213024 | tf_op jit(solution)/shard_map/ppermute | solution.py:482
  41.1 5.2 collective-permute-start.8
  49.5 2.6 collective-permute-done.8.refs_1_
  53.5 4.6 collective-permute-done.9.refs_2_
  62.1 4.2 collective-permute-done.6.rest_6_
  66.4 3.6 collective-permute-done.7.rest_7_
  71.8 5.6 shard_map.186
  80.9 3.4 collective-permute-start.14
  92.1 5.4 collective-permute-done.15
  103.6 15.2 %collective-permute-done.22.refs_1_ = bf16[3,192,560]{2,1,0:T(8,128)(2,1)S(1)} collective-permute-done((bf16[3,192,560]{2,1,0:T(8,128)(2,1)S(1)}, bf16[3,192,560]{2,1,0:T(8,128)(2,1)S(1)}, u32[]{:S(2)}, u32[]{:S(2)}) %collective-permute-start.22) | collective-permute-done | bytes 645152 | tf_op jit(solution)/shard_map/ppermute | solution.py:482
  118.8 13.9 %collective-permute-done.23.refs_3_ = bf16[3,192,560]{2,1,0:T(8,128)(2,1)S(1)} collective-permute-done((bf16[3,192,560]{2,1,0:T(8,128)(2,1)S(1)}, bf16[3,192,560]{2,1,0:T(8,128)(2,1)S(1)}, u32[]{:S(2)}, u32[]{:S(2)}) %collective-permute-start.23) | collective-permute-done | bytes 645152 | tf_op jit(solution)/shard_map/ppermute | solution.py:482
  139.1 9.9 %shard_map.188 = (bf16[4,2,64,384]{3,2,1,0:T(8,128)(2,1)S(1)}, f32[2,2,1,384]{3,2,1,0:T(1,128)S(1)}, bf16[2,2,2048,128]{3,2,1,0:T(8,128)(2,1)S(1)}) custom-call(s32[2,16]{1,0:T(2,128)S(1)} %copy-done.56, s32[6]{0:T(128)S(1)} %stack.92.place, bf16[4,2,64,384]{3,2,1,0:T(8,128)(2,1)S(1)} %bitcast.244, bf16[4,4,2,64,128]{4,3,2,1,0:T(8,128)(2,1)S(1)} %pad_maximum_fusion.15.a_own, ...), custom_call_target="tpu_custom_call" | custom-call | flops 1 | bytes 1 | tf_op jit(solution)/shard_map/pallas_call | solution.py:728
  157.6 16.7 %collective-permute-done.29.refs_4_ = bf16[3,192,560]{2,1,0:T(8,128)(2,1)S(1)} collective-permute-done((bf16[3,192,560]{2,1,0:T(8,128)(2,1)S(1)}, bf16[3,192,560]{2,1,0:T(8,128)(2,1)S(1)}, u32[]{:S(2)}, u32[]{:S(2)}) %collective-permute-start.29) | collective-permute-done | bytes 645152 | tf_op jit(solution)/shard_map/ppermute | solution.py:485
  179.9 10.2 %collective-permute-done.31.refs_5_ = bf16[3,192,560]{2,1,0:T(8,128)(2,1)S(1)} collective-permute-done((bf16[3,192,560]{2,1,0:T(8,128)(2,1)S(1)}, bf16[3,192,560]{2,1,0:T(8,128)(2,1)S(1)}, u32[]{:S(2)}, u32[]{:S(2)}) %collective-permute-start.31) | collective-permute-done | bytes 645152 | tf_op jit(solution)/shard_map/ppermute | solution.py:485
  191.6 13.4 %collective-permute-done.33.refs_7_ = bf16[3,192,560]{2,1,0:T(8,128)(2,1)S(1)} collective-permute-done((bf16[3,192,560]{2,1,0:T(8,128)(2,1)S(1)}, bf16[3,192,560]{2,1,0:T(8,128)(2,1)S(1)}, u32[]{:S(2)}, u32[]{:S(2)}) %collective-permute-start.33) | collective-permute-done | bytes 645152 | tf_op jit(solution)/shard_map/ppermute | solution.py:485
  212.3 4.2 collective-permute-done.36
  216.5 4.3 collective-permute-done.37
  222.2 6.9 %collective-permute-done.49 = bf16[128,1536]{1,0:T(8,128)(2,1)S(1)} collective-permute-done((bf16[128,1536]{1,0:T(8,128)(2,1)}, bf16[128,1536]{1,0:T(8,128)(2,1)S(1)}, u32[]{:S(2)}, u32[]{:S(2)}) %collective-permute-start.49) | collective-permute-done | bytes 393248 | tf_op jit(solution)/shard_map/ppermute | solution.py:482
  232.1 3.5 shard_map.192
  235.6 2.9 fusion.14
  240.1 3.8 collective-permute-done.52
  256.3 5.2 collective-permute-done.53
  277.9 6.6 %collective-permute-done.56 = bf16[128,1536]{1,0:T(8,128)(2,1)S(1)} collective-permute-done((bf16[128,1536]{1,0:T(8,128)(2,1)S(1)}, bf16[128,1536]{1,0:T(8,128)(2,1)S(1)}, u32[]{:S(2)}, u32[]{:S(2)}) %collective-permute-start.56) | collective-permute-done | bytes 393248 | tf_op jit(solution)/shard_map/ppermute | solution.py:488
  308.3 3.2 convolution_add_fusion
  311.5 5.0 convolution_convert_fusion.3
  316.5 2.7 copy.107
  322.5 7.9 %convolution_convert_fusion.2 = bf16[1536,560]{0,1:T(8,128)(2,1)} fusion(bf16[2048,1536]{1,0:T(8,128)(2,1)} %copy-done.95, bf16[512,560]{0,1:T(8,128)(2,1)} %copy-done.113, bf16[512,560]{0,1:T(8,128)(2,1)S(1)} %copy-done.112, bf16[512,560]{0,1:T(8,128)(2,1)S(1)} %copy-done.110, bf16[512,560]{0,1:T(8,128)(2,1)S(1)} %copy-done.108), kind=kOutput, calls=%fused_computation.6 | convolution fusion | flops 3533250560 | bytes 10305536 | tf_op jit(solution)/shard_map/dot_general | solution.py:41
  332.1 2.7 copy.108
  348.3 9.7 %collective-permute-done.64 = bf16[128,1536]{1,0:T(8,128)(2,1)S(1)} collective-permute-done((bf16[128,1536]{1,0:T(8,128)(2,1)S(1)}, bf16[128,1536]{1,0:T(8,128)(2,1)S(1)}, u32[]{:S(2)}, u32[]{:S(2)}) %collective-permute-start.64) | collective-permute-done | bytes 393248 | tf_op jit(solution)/shard_map/ppermute | solution.py:488
  359.9 5.1 collective-permute-done.67
  365.9 4.9 convolution_convert_fusion.1
  370.7 2.7 copy.109
  374.2 10.4 %collective-permute-done.65 = bf16[128,1536]{1,0:T(8,128)(2,1)} collective-permute-done((bf16[128,1536]{1,0:T(8,128)(2,1)}, bf16[128,1536]{1,0:T(8,128)(2,1)}, u32[]{:S(2)}, u32[]{:S(2)}) %collective-permute-start.65) | collective-permute-done | bytes 393248 | tf_op jit(solution)/shard_map/ppermute | solution.py:482
  387.2 2.9 fusion.88
  391.3 7.2 %convolution_convert_fusion = bf16[2048,1536]{1,0:T(8,128)(2,1)} fusion(bf16[2048,560]{0,1:T(8,128)(2,1)S(1)} %copy-done.79, bf16[1536,560]{1,0:T(8,128)(2,1)S(1)} %bitcast.323), kind=kOutput, calls=%fused_computation | convolution fusion | flops 3526361088 | bytes 10305536 | tf_op jit(solution)/shard_map/dot_general | solution.py:45
  398.5 2.4 collective-permute-done.69.near
  400.9 9.1 %collective-permute-done.70 = bf16[4,1,192,560]{3,2,1,0:T(8,128)(2,1)S(1)} collective-permute-done((bf16[4,1,192,560]{3,2,1,0:T(8,128)(2,1)S(1)}, bf16[4,1,192,560]{3,2,1,0:T(8,128)(2,1)S(1)}, u32[]{:S(2)}, u32[]{:S(2)}) %collective-permute-start.70) | collective-permute-done | bytes 860192 | tf_op jit(solution)/shard_map/ppermute | solution.py:485
  414.3 3.5 all-to-all-start.1
  419.8 3.2 shard_map.196
  423.0 12.8 %shard_map.197 = (bf16[4,2,64,384]{3,2,1,0:T(8,128)(2,1)S(1)}, bf16[4,4,2,64,128]{4,3,2,1,0:T(8,128)(2,1)S(1)}, bf16[4,4,2,64,128]{4,3,2,1,0:T(8,128)(2,1)S(1)}, bf16[2,4,4,2,64,128]{5,4,3,2,1,0:T(8,128)(2,1)S(1)}) custom-call(s32[2,16]{1,0:T(2,128)S(1)} %copy-done.56, s32[6]{0:T(128)S(1)} %stack.92.place, bf16[4,2,64,384]{3,2,1,0:T(8,128)(2,1)S(1)} %bitcast.245, ...), custom_call_target="tpu_custom_call" | custom-call | flops 1 | bytes 1 | tf_op jit(solution)/shard_map/pallas_call | solution.py:861
  439.8 3.3 all-to-all-done.1.gates
  446.2 2.4 convolution_convert_fusion.4
  450.9 3.1 shard_map.199
  455.5 6.4 %shard_map.201 = bf16[4,4,128,1536]{3,2,1,0:T(8,128)(2,1)} custom-call(s32[6]{0:T(128)S(1)} %stack.92.place, bf16[4,4,128,1536]{3,2,1,0:T(8,128)(2,1)} %bitcast.275), custom_call_target="tpu_custom_call" | custom-call | flops 1 | bytes 1 | tf_op jit(solution)/shard_map/pallas_call | solution.py:77
  465.4 3.7 all-to-all-start.2
  474.7 3.7 collective-permute-start.77
  480.4 8.8 %collective-permute-done.77 = bf16[4,2,64,128]{3,2,1,0:T(8,128)(2,1)S(1)} collective-permute-done((bf16[4,2,64,128]{3,2,1,0:T(8,128)(2,1)}, bf16[4,2,64,128]{3,2,1,0:T(8,128)(2,1)S(1)}, u32[]{:S(2)}, u32[]{:S(2)}) %collective-permute-start.77) | collective-permute-done | bytes 131104 | tf_op jit(solution)/shard_map/ppermute | solution.py:482
  489.2 15.3 %collective-permute-done.78 = bf16[4,2,64,128]{3,2,1,0:T(8,128)(2,1)S(1)} collective-permute-done((bf16[4,2,64,128]{3,2,1,0:T(8,128)(2,1)}, bf16[4,2,64,128]{3,2,1,0:T(8,128)(2,1)S(1)}, u32[]{:S(2)}, u32[]{:S(2)}) %collective-permute-start.78) | collective-permute-done | bytes 131104 | tf_op jit(solution)/shard_map/ppermute | solution.py:482
  506.8 3.7 all-to-all-start.3
  517.2 3.2 shard_map.204
  521.6 2.8 collective-permute-done.84.got
  525.0 3.8 collective-permute-start.88
  531.3 4.8 collective-permute-done.87
  540.6 2.7 add_convert_fusion
  543.3 3.5 all-to-all-start.4
  546.8 3.1 convert_add_fusion
  554.2 2.6 shard_map.208
  573.9 15.7 %all-to-all-done.4.downs = bf16[4,1,192,560]{3,2,1,0:T(8,128)(2,1)S(1)} async-done(((bf16[4,1,192,560]{3,2,1,0:T(8,128)(2,1)}), bf16[4,1,192,560]{3,2,1,0:T(8,128)(2,1)S(1)}, u32[]{:S(2)}, u32[]{:S(2)}) %all-to-all-start.4) | async-done | bytes 860192 | tf_op jit(solution)/shard_map/all_to_all | solution.py:545
  592.8 4.4 shard_map.209
  599.8 3.5 all-to-all-start.5
  607.9 12.1 %all-to-all-done.5 = bf16[4,1,48,1536]{3,2,1,0:T(8,128)(2,1)S(1)} async-done(((bf16[4,1,48,1536]{3,2,1,0:T(8,128)(2,1)}), bf16[4,1,48,1536]{3,2,1,0:T(8,128)(2,1)S(1)}, u32[]{:S(2)}, u32[]{:S(2)}) %all-to-all-start.5) | async-done | bytes 589856 | tf_op jit(solution)/shard_map/all_to_all | solution.py:545
  (593 shorter events, 237.8 us)
Async XLA Ops:
  16.6 13.2 %collective-permute-start.4 = (bf16[128,1536]{1,0:T(8,128)(2,1)S(1)}, bf16[128,1536]{1,0:T(8,128)(2,1)S(1)}, u32[]{:S(2)}, u32[]{:S(2)}) collective-permute-start(bf16[128,1536]{1,0:T(8,128)(2,1)S(1)} %fusion.50.own), channel_id=1, source_target_pairs={{0,2},{1,3},{2,0},{3,1},{4,6},{5,7},{6,4},{7,5},{8,10},{9,11},{10,... | collective-permute-start | bytes 1179656 | tf_op jit(solution)/shard_map/ppermute | solution.py:488
  24.2 15.8 %collective-permute-start.1 = (bf16[208,512]{1,0:T(8,128)(2,1)S(1)}, bf16[208,512]{1,0:T(8,128)(2,1)S(1)}, u32[]{:S(2)}, u32[]{:S(2)}) collective-permute-start(bf16[208,512]{1,0:T(8,128)(2,1)S(1)} %pad_maximum_fusion.25.rest_0_), channel_id=1, source_target_pairs={{0,16},{4,20},{8,24},{12,28},{16,0},{20,4},{24,8},{28,12},{1,17},{... | collective-permute-start | bytes 638984 | tf_op jit(solution)/shard_map/ppermute | solution.py:482
  26.8 13.2 %collective-permute-start.2 = (bf16[208,512]{1,0:T(8,128)(2,1)S(1)}, bf16[208,512]{1,0:T(8,128)(2,1)}, u32[]{:S(2)}, u32[]{:S(2)}) collective-permute-start(bf16[208,512]{1,0:T(8,128)(2,1)S(1)} %pad_maximum_fusion.25.rest_0_), channel_id=1, source_target_pairs={{0,24},{4,28},{8,0},{12,4},{16,8},{20,12},{24,16},{28,20},{1,25},{... | collective-permute-start | bytes 638984 | tf_op jit(solution)/shard_map/ppermute | solution.py:482
  41.1 28.9 %collective-permute-start.11 = (bf16[2,128,1536]{2,1,0:T(8,128)(2,1)}, bf16[2,128,1536]{2,1,0:T(8,128)(2,1)}, u32[]{:S(2)}, u32[]{:S(2)}) collective-permute-start(bf16[2,128,1536]{2,1,0:T(8,128)(2,1)} %pad_maximum_fusion.2), channel_id=1, source_target_pairs={{0,1},{1,0},{2,3},{3,2},{4,5},{5,4},{6,7},{7,6},{8,9},{9,8},{10,11... | collective-permute-start | bytes 2359304 | tf_op jit(solution)/shard_map/ppermute | solution.py:494
  48.7 21.3 %collective-permute-start.12 = (bf16[128,1536]{1,0:T(8,128)(2,1)}, bf16[128,1536]{1,0:T(8,128)(2,1)}, u32[]{:S(2)}, u32[]{:S(2)}) collective-permute-start(bf16[128,1536]{1,0:T(8,128)(2,1)} %bitcast.15), channel_id=1, source_target_pairs={{0,2},{1,3},{2,0},{3,1},{4,6},{5,7},{6,4},{7,5},{8,10},{9,11},{10,... | collective-permute-start | bytes 1179656 | tf_op jit(solution)/shard_map/ppermute | solution.py:488
  97.5 21.3 %collective-permute-start.22 = (bf16[3,192,560]{2,1,0:T(8,128)(2,1)S(1)}, bf16[3,192,560]{2,1,0:T(8,128)(2,1)S(1)}, u32[]{:S(2)}, u32[]{:S(2)}) collective-permute-start(bf16[3,192,560]{2,1,0:T(8,128)(2,1)S(1)} %get-tuple-element.203), channel_id=1, source_target_pairs={{0,8},{4,12},{8,16},{12,20},{16,24},{20,28},{24,0},{28,4},{1,9},{5... | collective-permute-start | bytes 1935368 | tf_op jit(solution)/shard_map/ppermute | solution.py:482
  101.8 30.9 %collective-permute-start.23 = (bf16[3,192,560]{2,1,0:T(8,128)(2,1)S(1)}, bf16[3,192,560]{2,1,0:T(8,128)(2,1)S(1)}, u32[]{:S(2)}, u32[]{:S(2)}) collective-permute-start(bf16[3,192,560]{2,1,0:T(8,128)(2,1)S(1)} %get-tuple-element.205), channel_id=1, source_target_pairs={{0,24},{4,28},{8,0},{12,4},{16,8},{20,12},{24,16},{28,20},{1,25},{... | collective-permute-start | bytes 1935368 | tf_op jit(solution)/shard_map/ppermute | solution.py:482
  102.0 16.7 %collective-permute-start.20 = (bf16[4,4,128,128]{3,2,1,0:T(8,128)(2,1)S(1)}, bf16[4,4,128,128]{3,2,1,0:T(8,128)(2,1)S(1)}, u32[]{:S(2)}, u32[]{:S(2)}) collective-permute-start(bf16[4,4,128,128]{3,2,1,0:T(8,128)(2,1)S(1)} %pad_maximum_fusion.16), channel_id=1, source_target_pairs={{0,4},{4,0},{8,12},{12,8},{16,20},{20,16},{24,28},{28,24},{1,5},{5... | collective-permute-start | bytes 1572872 | tf_op jit(solution)/shard_map/ppermute | solution.py:485
  103.6 15.2 %collective-permute-start.21 = (bf16[4,4,128,128]{3,2,1,0:T(8,128)(2,1)S(1)}, bf16[4,4,128,128]{3,2,1,0:T(8,128)(2,1)S(1)}, u32[]{:S(2)}, u32[]{:S(2)}) collective-permute-start(bf16[4,4,128,128]{3,2,1,0:T(8,128)(2,1)S(1)} %pad_maximum_fusion.16), channel_id=1, source_target_pairs={{0,1},{1,0},{2,3},{3,2},{4,5},{5,4},{6,7},{7,6},{8,9},{9,8},{10,11... | collective-permute-start | bytes 1572872 | tf_op jit(solution)/shard_map/ppermute | solution.py:494
  137.0 13.3 %collective-permute-start.25 = (bf16[2,48,1536]{2,1,0:T(8,128)(2,1)S(1)}, bf16[2,48,1536]{2,1,0:T(8,128)(2,1)S(1)}, u32[]{:S(2)}, u32[]{:S(2)}) collective-permute-start(bf16[2,48,1536]{2,1,0:T(8,128)(2,1)S(1)} %get-tuple-element.214), channel_id=1, source_target_pairs={{0,1},{1,0},{2,3},{3,2},{4,5},{5,4},{6,7},{7,6},{8,9},{9,8},{10,11... | collective-permute-start | bytes 884744 | tf_op jit(solution)/shard_map/ppermute | solution.py:494
  137.6 12.7 %collective-permute-start.26 = (bf16[2,48,1536]{2,1,0:T(8,128)(2,1)S(1)}, bf16[2,48,1536]{2,1,0:T(8,128)(2,1)S(1)}, u32[]{:S(2)}, u32[]{:S(2)}) collective-permute-start(bf16[2,48,1536]{2,1,0:T(8,128)(2,1)S(1)} %get-tuple-element.215), channel_id=1, source_target_pairs={{0,2},{1,3},{2,0},{3,1},{4,6},{5,7},{6,4},{7,5},{8,10},{9,11},{10,... | collective-permute-start | bytes 884744 | tf_op jit(solution)/shard_map/ppermute | solution.py:488
  138.3 13.8 %collective-permute-start.27 = (bf16[2,48,1536]{2,1,0:T(8,128)(2,1)S(1)}, bf16[2,48,1536]{2,1,0:T(8,128)(2,1)S(1)}, u32[]{:S(2)}, u32[]{:S(2)}) collective-permute-start(bf16[2,48,1536]{2,1,0:T(8,128)(2,1)S(1)} %get-tuple-element.216), channel_id=1, source_target_pairs={{0,3},{1,2},{2,1},{3,0},{4,7},{5,6},{6,5},{7,4},{8,11},{9,10},{10,... | collective-permute-start | bytes 884744 | tf_op jit(solution)/shard_map/ppermute | solution.py:491
  154.2 20.1 %collective-permute-start.28 = (bf16[2,128,1536]{2,1,0:T(8,128)(2,1)S(1)}, bf16[2,128,1536]{2,1,0:T(8,128)(2,1)S(1)}, u32[]{:S(2)}, u32[]{:S(2)}) collective-permute-start(bf16[2,128,1536]{2,1,0:T(8,128)(2,1)S(1)} %get-tuple-element.222), channel_id=1, source_target_pairs={{0,1},{1,0},{2,3},{3,2},{4,5},{5,4},{6,7},{7,6},{8,9},{9,8},{10,11... | collective-permute-start | bytes 2359304 | tf_op jit(solution)/shard_map/ppermute | solution.py:494
  154.9 19.3 %collective-permute-start.29 = (bf16[3,192,560]{2,1,0:T(8,128)(2,1)S(1)}, bf16[3,192,560]{2,1,0:T(8,128)(2,1)S(1)}, u32[]{:S(2)}, u32[]{:S(2)}) collective-permute-start(bf16[3,192,560]{2,1,0:T(8,128)(2,1)S(1)} %get-tuple-element.224.refs_0_), channel_id=1, source_target_pairs={{0,4},{4,0},{8,12},{12,8},{16,20},{20,16},{24,28},{28,24},{1,5},{5... | collective-permute-start | bytes 1935368 | tf_op jit(solution)/shard_map/ppermute | solution.py:485
  156.4 33.6 %collective-permute-start.31 = (bf16[3,192,560]{2,1,0:T(8,128)(2,1)S(1)}, bf16[3,192,560]{2,1,0:T(8,128)(2,1)S(1)}, u32[]{:S(2)}, u32[]{:S(2)}) collective-permute-start(bf16[3,192,560]{2,1,0:T(8,128)(2,1)S(1)} %collective-permute-done.22.refs_1_), channel_id=1, source_target_pairs={{0,4},{4,0},{8,12},{12,8},{16,20},{20,16},{24,28},{28,24},{1,5},{5... | collective-permute-start | bytes 1935368 | tf_op jit(solution)/shard_map/ppermute | solution.py:485
  157.0 34.6 %collective-permute-start.32 = (bf16[3,192,560]{2,1,0:T(8,128)(2,1)S(1)}, bf16[3,192,560]{2,1,0:T(8,128)(2,1)S(1)}, u32[]{:S(2)}, u32[]{:S(2)}) collective-permute-start(bf16[3,192,560]{2,1,0:T(8,128)(2,1)S(1)} %get-tuple-element.228), channel_id=1, source_target_pairs={{0,16},{4,20},{8,24},{12,28},{16,0},{20,4},{24,8},{28,12},{1,17},{... | collective-permute-start | bytes 1935368 | tf_op jit(solution)/shard_map/ppermute | solution.py:482
  174.5 30.5 %collective-permute-start.33 = (bf16[3,192,560]{2,1,0:T(8,128)(2,1)S(1)}, bf16[3,192,560]{2,1,0:T(8,128)(2,1)S(1)}, u32[]{:S(2)}, u32[]{:S(2)}) collective-permute-start(bf16[3,192,560]{2,1,0:T(8,128)(2,1)S(1)} %collective-permute-done.23.refs_3_), channel_id=1, source_target_pairs={{0,4},{4,0},{8,12},{12,8},{16,20},{20,16},{24,28},{28,24},{1,5},{5... | collective-permute-start | bytes 1935368 | tf_op jit(solution)/shard_map/ppermute | solution.py:485
  176.1 15.4 %collective-permute-start.30 = (bf16[128,1536]{1,0:T(8,128)(2,1)S(1)}, bf16[128,1536]{1,0:T(8,128)(2,1)S(1)}, u32[]{:S(2)}, u32[]{:S(2)}) collective-permute-start(bf16[128,1536]{1,0:T(8,128)(2,1)S(1)} %fusion.53), channel_id=1, source_target_pairs={{0,2},{1,3},{2,0},{3,1},{4,6},{5,7},{6,4},{7,5},{8,10},{9,11},{10,... | collective-permute-start | bytes 1179656 | tf_op jit(solution)/shard_map/ppermute | solution.py:488
  179.8 30.1 %collective-permute-start.34 = (bf16[256,1536]{1,0:T(8,128)(2,1)S(1)}, bf16[256,1536]{1,0:T(8,128)(2,1)S(1)}, u32[]{:S(2)}, u32[]{:S(2)}) collective-permute-start(bf16[256,1536]{1,0:T(8,128)(2,1)S(1)} %pad_maximum_fusion.3), channel_id=1, source_target_pairs={{0,1},{1,0},{2,3},{3,2},{4,5},{5,4},{6,7},{7,6},{8,9},{9,8},{10,11... | collective-permute-start | bytes 2359304 | tf_op jit(solution)/shard_map/ppermute | solution.py:494
  206.9 13.8 %collective-permute-start.37 = (bf16[128,1536]{1,0:T(8,128)(2,1)S(1)}, bf16[128,1536]{1,0:T(8,128)(2,1)S(1)}, u32[]{:S(2)}, u32[]{:S(2)}) collective-permute-start(bf16[128,1536]{1,0:T(8,128)(2,1)S(1)} %get-tuple-element.337), channel_id=1, source_target_pairs={{0,8},{4,12},{8,16},{12,20},{16,24},{20,28},{24,0},{28,4},{1,9},{5... | collective-permute-start | bytes 1179656 | tf_op jit(solution)/shard_map/ppermute | solution.py:482
  209.3 19.9 %collective-permute-start.49 = (bf16[128,1536]{1,0:T(8,128)(2,1)}, bf16[128,1536]{1,0:T(8,128)(2,1)S(1)}, u32[]{:S(2)}, u32[]{:S(2)}) collective-permute-start(bf16[128,1536]{1,0:T(8,128)(2,1)} %bitcast.15), channel_id=1, source_target_pairs={{0,8},{4,12},{8,16},{12,20},{16,24},{20,28},{24,0},{28,4},{1,9},{5... | collective-permute-start | bytes 1179656 | tf_op jit(solution)/shard_map/ppermute | solution.py:482
  210.8 21.3 %collective-permute-start.35 = (bf16[3,192,560]{2,1,0:T(8,128)(2,1)S(1)}, bf16[3,192,560]{2,1,0:T(8,128)(2,1)S(1)}, u32[]{:S(2)}, u32[]{:S(2)}) collective-permute-start(bf16[3,192,560]{2,1,0:T(8,128)(2,1)S(1)} %collective-permute-done.32.refs_2_), channel_id=1, source_target_pairs={{0,4},{4,0},{8,12},{12,8},{16,20},{20,16},{24,28},{28,24},{1,5},{5... | collective-permute-start | bytes 1935368 | tf_op jit(solution)/shard_map/ppermute | solution.py:485
  220.8 18.6 %collective-permute-start.43 = (bf16[128,1536]{1,0:T(8,128)(2,1)S(1)}, bf16[128,1536]{1,0:T(8,128)(2,1)S(1)}, u32[]{:S(2)}, u32[]{:S(2)}) collective-permute-start(bf16[128,1536]{1,0:T(8,128)(2,1)S(1)} %collective-permute-done.37), channel_id=1, source_target_pairs={{0,8},{4,12},{8,16},{12,20},{16,24},{20,28},{24,0},{28,4},{1,9},{5... | collective-permute-start | bytes 1179656 | tf_op jit(solution)/shard_map/ppermute | solution.py:482
  220.8 17.8 %collective-permute-start.41 = (bf16[128,1536]{1,0:T(8,128)(2,1)S(1)}, bf16[128,1536]{1,0:T(8,128)(2,1)S(1)}, u32[]{:S(2)}, u32[]{:S(2)}) collective-permute-start(bf16[128,1536]{1,0:T(8,128)(2,1)S(1)} %collective-permute-done.37), channel_id=1, source_target_pairs={{0,2},{1,3},{2,0},{3,1},{4,6},{5,7},{6,4},{7,5},{8,10},{9,11},{10,... | collective-permute-start | bytes 1179656 | tf_op jit(solution)/shard_map/ppermute | solution.py:488
  222.2 23.6 %collective-permute-start.38 = (bf16[256,1536]{1,0:T(8,128)(2,1)S(1)}, bf16[256,1536]{1,0:T(8,128)(2,1)S(1)}, u32[]{:S(2)}, u32[]{:S(2)}) collective-permute-start(bf16[256,1536]{1,0:T(8,128)(2,1)S(1)} %pad_maximum_fusion.4), channel_id=1, source_target_pairs={{0,1},{1,0},{2,3},{3,2},{4,5},{5,4},{6,7},{7,6},{8,9},{9,8},{10,11... | collective-permute-start | bytes 2359304 | tf_op jit(solution)/shard_map/ppermute | solution.py:494
  238.6 22.9 %collective-permute-start.42 = (bf16[256,1536]{1,0:T(8,128)(2,1)S(1)}, bf16[256,1536]{1,0:T(8,128)(2,1)S(1)}, u32[]{:S(2)}, u32[]{:S(2)}) collective-permute-start(bf16[256,1536]{1,0:T(8,128)(2,1)S(1)} %pad_maximum_fusion.6), channel_id=1, source_target_pairs={{0,1},{1,0},{2,3},{3,2},{4,5},{5,4},{6,7},{7,6},{8,9},{9,8},{10,11... | collective-permute-start | bytes 2359304 | tf_op jit(solution)/shard_map/ppermute | solution.py:494
  238.8 28.8 %collective-permute-start.51 = (bf16[256,1536]{1,0:T(8,128)(2,1)S(1)}, bf16[256,1536]{1,0:T(8,128)(2,1)S(1)}, u32[]{:S(2)}, u32[]{:S(2)}) collective-permute-start(bf16[256,1536]{1,0:T(8,128)(2,1)S(1)} %pad_maximum_fusion.5), channel_id=1, source_target_pairs={{0,1},{1,0},{2,3},{3,2},{4,5},{5,4},{6,7},{7,6},{8,9},{9,8},{10,11... | collective-permute-start | bytes 2359304 | tf_op jit(solution)/shard_map/ppermute | solution.py:494
  239.3 25.1 %collective-permute-start.46 = (bf16[128,1536]{1,0:T(8,128)(2,1)S(1)}, bf16[128,1536]{1,0:T(8,128)(2,1)S(1)}, u32[]{:S(2)}, u32[]{:S(2)}) collective-permute-start(bf16[128,1536]{1,0:T(8,128)(2,1)S(1)} %collective-permute-done.43), channel_id=1, source_target_pairs={{0,8},{4,12},{8,16},{12,20},{16,24},{20,28},{24,0},{28,4},{1,9},{5... | collective-permute-start | bytes 1179656 | tf_op jit(solution)/shard_map/ppermute | solution.py:482
  245.8 15.6 %collective-permute-start.53 = (bf16[128,1536]{1,0:T(8,128)(2,1)S(1)}, bf16[128,1536]{1,0:T(8,128)(2,1)S(1)}, u32[]{:S(2)}, u32[]{:S(2)}) collective-permute-start(bf16[128,1536]{1,0:T(8,128)(2,1)S(1)} %collective-permute-done.52), channel_id=1, source_target_pairs={{0,2},{1,3},{2,0},{3,1},{4,6},{5,7},{6,4},{7,5},{8,10},{9,11},{10,... | collective-permute-start | bytes 1179656 | tf_op jit(solution)/shard_map/ppermute | solution.py:488
  261.4 23.1 %collective-permute-start.39 = (bf16[2,128,1536]{2,1,0:T(8,128)(2,1)S(1)}, bf16[2,128,1536]{2,1,0:T(8,128)(2,1)S(1)}, u32[]{:S(2)}, u32[]{:S(2)}) collective-permute-start(bf16[2,128,1536]{2,1,0:T(8,128)(2,1)S(1)} %bitcast.287), channel_id=1, source_target_pairs={{0,1},{1,0},{2,3},{3,2},{4,5},{5,4},{6,7},{7,6},{8,9},{9,8},{10,11... | collective-permute-start | bytes 2359304 | tf_op jit(solution)/shard_map/ppermute | solution.py:494
  261.5 23.9 %collective-permute-start.45 = (bf16[256,1536]{1,0:T(8,128)(2,1)S(1)}, bf16[256,1536]{1,0:T(8,128)(2,1)S(1)}, u32[]{:S(2)}, u32[]{:S(2)}) collective-permute-start(bf16[256,1536]{1,0:T(8,128)(2,1)S(1)} %pad_maximum_fusion.8), channel_id=1, source_target_pairs={{0,1},{1,0},{2,3},{3,2},{4,5},{5,4},{6,7},{7,6},{8,9},{9,8},{10,11... | collective-permute-start | bytes 2359304 | tf_op jit(solution)/shard_map/ppermute | solution.py:494
  264.4 24.7 %collective-permute-start.54 = (bf16[256,1536]{1,0:T(8,128)(2,1)S(1)}, bf16[256,1536]{1,0:T(8,128)(2,1)S(1)}, u32[]{:S(2)}, u32[]{:S(2)}) collective-permute-start(bf16[256,1536]{1,0:T(8,128)(2,1)S(1)} %pad_maximum_fusion.7), channel_id=1, source_target_pairs={{0,1},{1,0},{2,3},{3,2},{4,5},{5,4},{6,7},{7,6},{8,9},{9,8},{10,11... | collective-permute-start | bytes 2359304 | tf_op jit(solution)/shard_map/ppermute | solution.py:494
  267.6 16.8 %collective-permute-start.56 = (bf16[128,1536]{1,0:T(8,128)(2,1)S(1)}, bf16[128,1536]{1,0:T(8,128)(2,1)S(1)}, u32[]{:S(2)}, u32[]{:S(2)}) collective-permute-start(bf16[128,1536]{1,0:T(8,128)(2,1)S(1)} %collective-permute-done.55), channel_id=1, source_target_pairs={{0,2},{1,3},{2,0},{3,1},{4,6},{5,7},{6,4},{7,5},{8,10},{9,11},{10,... | collective-permute-start | bytes 1179656 | tf_op jit(solution)/shard_map/ppermute | solution.py:488
  277.8 21.6 %collective-permute-start.60 = (bf16[2,128,1536]{2,1,0:T(8,128)(2,1)S(1)}, bf16[2,128,1536]{2,1,0:T(8,128)(2,1)S(1)}, u32[]{:S(2)}, u32[]{:S(2)}) collective-permute-start(bf16[2,128,1536]{2,1,0:T(8,128)(2,1)S(1)} %bitcast.288), channel_id=1, source_target_pairs={{0,1},{1,0},{2,3},{3,2},{4,5},{5,4},{6,7},{7,6},{8,9},{9,8},{10,11... | collective-permute-start | bytes 2359304 | tf_op jit(solution)/shard_map/ppermute | solution.py:494
  284.5 17.7 %collective-permute-start.48 = (bf16[256,1536]{1,0:T(8,128)(2,1)S(1)}, bf16[256,1536]{1,0:T(8,128)(2,1)S(1)}, u32[]{:S(2)}, u32[]{:S(2)}) collective-permute-start(bf16[256,1536]{1,0:T(8,128)(2,1)S(1)} %pad_maximum_fusion.10), channel_id=1, source_target_pairs={{0,1},{1,0},{2,3},{3,2},{4,5},{5,4},{6,7},{7,6},{8,9},{9,8},{10,11... | collective-permute-start | bytes 2359304 | tf_op jit(solution)/shard_map/ppermute | solution.py:494
  284.5 19.9 %collective-permute-start.57 = (bf16[256,1536]{1,0:T(8,128)(2,1)S(1)}, bf16[256,1536]{1,0:T(8,128)(2,1)S(1)}, u32[]{:S(2)}, u32[]{:S(2)}) collective-permute-start(bf16[256,1536]{1,0:T(8,128)(2,1)S(1)} %pad_maximum_fusion.9), channel_id=1, source_target_pairs={{0,1},{1,0},{2,3},{3,2},{4,5},{5,4},{6,7},{7,6},{8,9},{9,8},{10,11... | collective-permute-start | bytes 2359304 | tf_op jit(solution)/shard_map/ppermute | solution.py:494
  285.4 15.8 %collective-permute-start.40 = (bf16[128,1536]{1,0:T(8,128)(2,1)S(1)}, bf16[128,1536]{1,0:T(8,128)(2,1)S(1)}, u32[]{:S(2)}, u32[]{:S(2)}) collective-permute-start(bf16[128,1536]{1,0:T(8,128)(2,1)S(1)} %fusion.54), channel_id=1, source_target_pairs={{0,2},{1,3},{2,0},{3,1},{4,6},{5,7},{6,4},{7,5},{8,10},{9,11},{10,... | collective-permute-start | bytes 1179656 | tf_op jit(solution)/shard_map/ppermute | solution.py:488
  296.7 47.6 %collective-permute-start.63 = (bf16[2,128,1536]{2,1,0:T(8,128)(2,1)}, bf16[2,128,1536]{2,1,0:T(8,128)(2,1)}, u32[]{:S(2)}, u32[]{:S(2)}) collective-permute-start(bf16[2,128,1536]{2,1,0:T(8,128)(2,1)} %bitcast.52), channel_id=1, source_target_pairs={{0,1},{1,0},{2,3},{3,2},{4,5},{5,4},{6,7},{7,6},{8,9},{9,8},{10,11... | collective-permute-start | bytes 2359304 | tf_op jit(solution)/shard_map/ppermute | solution.py:494
  300.5 39.4 %collective-permute-start.61 = (bf16[128,1536]{1,0:T(8,128)(2,1)}, bf16[128,1536]{1,0:T(8,128)(2,1)}, u32[]{:S(2)}, u32[]{:S(2)}) collective-permute-start(bf16[128,1536]{1,0:T(8,128)(2,1)} %fusion.55), channel_id=1, source_target_pairs={{0,2},{1,3},{2,0},{3,1},{4,6},{5,7},{6,4},{7,5},{8,10},{9,11},{10,... | collective-permute-start | bytes 1179656 | tf_op jit(solution)/shard_map/ppermute | solution.py:488
  320.9 38.1 %collective-permute-start.58 = (bf16[4,1,192,560]{3,2,1,0:T(8,128)(2,1)}, bf16[4,1,192,560]{3,2,1,0:T(8,128)(2,1)}, u32[]{:S(2)}, u32[]{:S(2)}) collective-permute-start(bf16[4,1,192,560]{3,2,1,0:T(8,128)(2,1)} %get-tuple-element.246), channel_id=1, source_target_pairs={{0,4},{4,0},{8,12},{12,8},{16,20},{20,16},{24,28},{28,24},{1,5},{5... | collective-permute-start | bytes 2580488 | tf_op jit(solution)/shard_map/ppermute | solution.py:485
  342.3 31.9 %collective-permute-start.62 = (bf16[128,1536]{1,0:T(8,128)(2,1)}, bf16[128,1536]{1,0:T(8,128)(2,1)}, u32[]{:S(2)}, u32[]{:S(2)}) collective-permute-start(bf16[128,1536]{1,0:T(8,128)(2,1)} %fusion.45), channel_id=1, source_target_pairs={{0,24},{4,28},{8,0},{12,4},{16,8},{20,12},{24,16},{28,20},{1,25},{... | collective-permute-start | bytes 1179656 | tf_op jit(solution)/shard_map/ppermute | solution.py:482
  346.9 18.2 %collective-permute-start.67 = (bf16[128,1536]{1,0:T(8,128)(2,1)S(1)}, bf16[128,1536]{1,0:T(8,128)(2,1)S(1)}, u32[]{:S(2)}, u32[]{:S(2)}) collective-permute-start(bf16[128,1536]{1,0:T(8,128)(2,1)S(1)} %fusion.57), channel_id=1, source_target_pairs={{0,2},{1,3},{2,0},{3,1},{4,6},{5,7},{6,4},{7,5},{8,10},{9,11},{10,... | collective-permute-start | bytes 1179656 | tf_op jit(solution)/shard_map/ppermute | solution.py:488
  358.8 25.8 %collective-permute-start.65 = (bf16[128,1536]{1,0:T(8,128)(2,1)}, bf16[128,1536]{1,0:T(8,128)(2,1)}, u32[]{:S(2)}, u32[]{:S(2)}) collective-permute-start(bf16[128,1536]{1,0:T(8,128)(2,1)} %fusion.43), channel_id=1, source_target_pairs={{0,16},{4,20},{8,24},{12,28},{16,0},{20,4},{24,8},{28,12},{1,17},{... | collective-permute-start | bytes 1179656 | tf_op jit(solution)/shard_map/ppermute | solution.py:482
  359.0 25.6 %collective-permute-start.59 = (bf16[4,1,192,560]{3,2,1,0:T(8,128)(2,1)}, bf16[4,1,192,560]{3,2,1,0:T(8,128)(2,1)}, u32[]{:S(2)}, u32[]{:S(2)}) collective-permute-start(bf16[4,1,192,560]{3,2,1,0:T(8,128)(2,1)} %get-tuple-element.249), channel_id=1, source_target_pairs={{0,4},{4,0},{8,12},{12,8},{16,20},{20,16},{24,28},{28,24},{1,5},{5... | collective-permute-start | bytes 2580488 | tf_op jit(solution)/shard_map/ppermute | solution.py:485
  365.9 18.8 %collective-permute-start.68 = (bf16[128,1536]{1,0:T(8,128)(2,1)}, bf16[128,1536]{1,0:T(8,128)(2,1)}, u32[]{:S(2)}, u32[]{:S(2)}) collective-permute-start(bf16[128,1536]{1,0:T(8,128)(2,1)} %fusion.41), channel_id=1, source_target_pairs={{0,8},{4,12},{8,16},{12,20},{16,24},{20,28},{24,0},{28,4},{1,9},{5... | collective-permute-start | bytes 1179656 | tf_op jit(solution)/shard_map/ppermute | solution.py:482
  386.2 23.7 %collective-permute-start.70 = (bf16[4,1,192,560]{3,2,1,0:T(8,128)(2,1)S(1)}, bf16[4,1,192,560]{3,2,1,0:T(8,128)(2,1)S(1)}, u32[]{:S(2)}, u32[]{:S(2)}) collective-permute-start(bf16[4,1,192,560]{3,2,1,0:T(8,128)(2,1)S(1)} %get-tuple-element.257), channel_id=1, source_target_pairs={{0,4},{4,0},{8,12},{12,8},{16,20},{20,16},{24,28},{28,24},{1,5},{5... | collective-permute-start | bytes 2580488 | tf_op jit(solution)/shard_map/ppermute | solution.py:485
  414.3 28.8 %all-to-all-start.1 = ((bf16[4,1,192,560]{3,2,1,0:T(8,128)(2,1)}), bf16[4,1,192,560]{3,2,1,0:T(8,128)(2,1)S(1)}, u32[]{:S(2)}, u32[]{:S(2)}) async-start(bf16[4,1,192,560]{3,2,1,0:T(8,128)(2,1)} %add_convert_fusion.2), calls=%async_computation.1 | async-start | bytes 1966080 | tf_op jit(solution)/shard_map/all_to_all | solution.py:545
  417.8 132.1 %reduce-scatter.3.cloned.1.call-start = ((), (), s32[]{:S(2)}) async-start(), calls=%async_computation.8 | async-start | bytes 7864320 | tf_op jit(solution)/shard_map/reduce_scatter | solution.py:911
  445.3 16.6 %collective-permute-start.76 = (bf16[4,4,2,64,128]{4,3,2,1,0:T(8,128)(2,1)}, bf16[4,4,2,64,128]{4,3,2,1,0:T(8,128)(2,1)}, u32[]{:S(2)}, u32[]{:S(2)}) collective-permute-start(bf16[4,4,2,64,128]{4,3,2,1,0:T(8,128)(2,1)} %add_convert_fusion.6), channel_id=1, source_target_pairs={{0,4},{4,0},{8,12},{12,8},{16,20},{20,16},{24,28},{28,24},{1,5},{5... | collective-permute-start | bytes 1572872 | tf_op jit(solution)/shard_map/ppermute | solution.py:485
  465.4 39.1 %all-to-all-start.2 = ((bf16[4,1,192,560]{3,2,1,0:T(8,128)(2,1)}), bf16[4,1,192,560]{3,2,1,0:T(8,128)(2,1)S(1)}, u32[]{:S(2)}, u32[]{:S(2)}) async-start(bf16[4,1,192,560]{3,2,1,0:T(8,128)(2,1)} %add_convert_fusion.1), calls=%async_computation.4 | async-start | bytes 1966080 | tf_op jit(solution)/shard_map/all_to_all | solution.py:545
  469.1 35.4 %collective-permute-start.80 = (bf16[2,2,48,1536]{3,2,1,0:T(8,128)(2,1)}, bf16[2,2,48,1536]{3,2,1,0:T(8,128)(2,1)}, u32[]{:S(2)}, u32[]{:S(2)}) collective-permute-start(bf16[2,2,48,1536]{3,2,1,0:T(8,128)(2,1)} %copy-done.58), channel_id=1, source_target_pairs={{0,2},{1,3},{2,0},{3,1},{4,6},{5,7},{6,4},{7,5},{8,10},{9,11},{10,... | collective-permute-start | bytes 1769480 | tf_op jit(solution)/shard_map/ppermute | solution.py:488
  470.3 34.2 %collective-permute-start.81 = (bf16[4,1,4,48,384]{4,3,2,1,0:T(8,128)(2,1)}, bf16[4,1,4,48,384]{4,3,2,1,0:T(8,128)(2,1)}, u32[]{:S(2)}, u32[]{:S(2)}) collective-permute-start(bf16[4,1,4,48,384]{4,3,2,1,0:T(8,128)(2,1)} %copy-done.57), channel_id=1, source_target_pairs={{0,4},{4,0},{8,12},{12,8},{16,20},{20,16},{24,28},{28,24},{1,5},{5... | collective-permute-start | bytes 1769480 | tf_op jit(solution)/shard_map/ppermute | solution.py:485
  474.7 14.5 %collective-permute-start.77 = (bf16[4,2,64,128]{3,2,1,0:T(8,128)(2,1)}, bf16[4,2,64,128]{3,2,1,0:T(8,128)(2,1)S(1)}, u32[]{:S(2)}, u32[]{:S(2)}) collective-permute-start(bf16[4,2,64,128]{3,2,1,0:T(8,128)(2,1)} %get-tuple-element.364), channel_id=1, source_target_pairs={{0,24},{4,28},{8,0},{12,4},{16,8},{20,12},{24,16},{28,20},{1,25},{... | collective-permute-start | bytes 393224 | tf_op jit(solution)/shard_map/ppermute | solution.py:482
  478.4 26.1 %collective-permute-start.78 = (bf16[4,2,64,128]{3,2,1,0:T(8,128)(2,1)}, bf16[4,2,64,128]{3,2,1,0:T(8,128)(2,1)S(1)}, u32[]{:S(2)}, u32[]{:S(2)}) collective-permute-start(bf16[4,2,64,128]{3,2,1,0:T(8,128)(2,1)} %get-tuple-element.363), channel_id=1, source_target_pairs={{0,16},{4,20},{8,24},{12,28},{16,0},{20,4},{24,8},{28,12},{1,17},{... | collective-permute-start | bytes 393224 | tf_op jit(solution)/shard_map/ppermute | solution.py:482
  478.4 26.1 %collective-permute-start.79 = (bf16[4,2,64,128]{3,2,1,0:T(8,128)(2,1)S(1)}, bf16[4,2,64,128]{3,2,1,0:T(8,128)(2,1)S(1)}, u32[]{:S(2)}, u32[]{:S(2)}) collective-permute-start(bf16[4,2,64,128]{3,2,1,0:T(8,128)(2,1)S(1)} %get-tuple-element.362), channel_id=1, source_target_pairs={{0,8},{4,12},{8,16},{12,20},{16,24},{20,28},{24,0},{28,4},{1,9},{5... | collective-permute-start | bytes 393224 | tf_op jit(solution)/shard_map/ppermute | solution.py:482
  506.8 31.7 %all-to-all-start.3 = ((bf16[4,1,4,48,384]{4,3,2,1,0:T(8,128)(2,1)}), bf16[4,1,4,48,384]{4,3,2,1,0:T(8,128)(2,1)S(1)}, u32[]{:S(2)}, u32[]{:S(2)}) async-start(bf16[4,1,4,48,384]{4,3,2,1,0:T(8,128)(2,1)} %add_convert_fusion.4), calls=%async_computation.5 | async-start | bytes 1179648 | tf_op jit(solution)/shard_map/all_to_all | solution.py:545
  524.4 22.4 %collective-permute-start.91 = (bf16[2,128,1536]{2,1,0:T(8,128)(2,1)}, bf16[2,128,1536]{2,1,0:T(8,128)(2,1)}, u32[]{:S(2)}, u32[]{:S(2)}) collective-permute-start(bf16[2,128,1536]{2,1,0:T(8,128)(2,1)} %get-tuple-element.312), channel_id=1, source_target_pairs={{0,1},{1,0},{2,3},{3,2},{4,5},{5,4},{6,7},{7,6},{8,9},{9,8},{10,11... | collective-permute-start | bytes 2359304 | tf_op jit(solution)/shard_map/ppermute | solution.py:494
  537.3 21.4 %collective-permute-start.89 = (bf16[2,64,128]{2,1,0:T(8,128)(2,1)}, bf16[2,64,128]{2,1,0:T(8,128)(2,1)}, u32[]{:S(2)}, u32[]{:S(2)}) collective-permute-start(bf16[2,64,128]{2,1,0:T(8,128)(2,1)} %get-tuple-element.308), channel_id=1, source_target_pairs={{0,2},{1,3},{2,0},{3,1},{4,6},{5,7},{6,4},{7,5},{8,10},{9,11},{10,... | collective-permute-start | bytes 98312 | tf_op jit(solution)/shard_map/ppermute | solution.py:488
  539.7 19.7 %collective-permute-start.82 = (bf16[2,48,384]{2,1,0:T(8,128)(2,1)}, bf16[2,48,384]{2,1,0:T(8,128)(2,1)}, u32[]{:S(2)}, u32[]{:S(2)}) collective-permute-start(bf16[2,48,384]{2,1,0:T(8,128)(2,1)} %get-tuple-element.291), channel_id=1, source_target_pairs={{0,2},{1,3},{2,0},{3,1},{4,6},{5,7},{6,4},{7,5},{8,10},{9,11},{10,... | collective-permute-start | bytes 221192 | tf_op jit(solution)/shard_map/ppermute | solution.py:488
  543.3 46.3 %all-to-all-start.4 = ((bf16[4,1,192,560]{3,2,1,0:T(8,128)(2,1)}), bf16[4,1,192,560]{3,2,1,0:T(8,128)(2,1)S(1)}, u32[]{:S(2)}, u32[]{:S(2)}) async-start(bf16[4,1,192,560]{3,2,1,0:T(8,128)(2,1)} %add_convert_fusion), calls=%async_computation.6 | async-start | bytes 1966080 | tf_op jit(solution)/shard_map/all_to_all | solution.py:545
  546.8 74.0 %reduce-scatter.5.cloned.1.call-start = ((), (), s32[]{:S(2)}) async-start(), calls=%async_computation.9 | async-start | bytes 1966080 | tf_op jit(solution)/shard_map/reduce_scatter | solution.py:912
  551.9 20.2 %collective-permute-start.92 = (bf16[128,1536]{1,0:T(8,128)(2,1)}, bf16[128,1536]{1,0:T(8,128)(2,1)}, u32[]{:S(2)}, u32[]{:S(2)}) collective-permute-start(bf16[128,1536]{1,0:T(8,128)(2,1)} %fusion.58), channel_id=1, source_target_pairs={{0,2},{1,3},{2,0},{3,1},{4,6},{5,7},{6,4},{7,5},{8,10},{9,11},{10,... | collective-permute-start | bytes 1179656 | tf_op jit(solution)/shard_map/ppermute | solution.py:488
  557.6 39.6 %collective-permute-start.93 = (bf16[4,1,48,1536]{3,2,1,0:T(8,128)(2,1)}, bf16[4,1,48,1536]{3,2,1,0:T(8,128)(2,1)}, u32[]{:S(2)}, u32[]{:S(2)}) collective-permute-start(bf16[4,1,48,1536]{3,2,1,0:T(8,128)(2,1)} %get-tuple-element.317), channel_id=1, source_target_pairs={{0,4},{4,0},{8,12},{12,8},{16,20},{20,16},{24,28},{28,24},{1,5},{5... | collective-permute-start | bytes 1769480 | tf_op jit(solution)/shard_map/ppermute | solution.py:485
  599.8 20.1 %all-to-all-start.5 = ((bf16[4,1,48,1536]{3,2,1,0:T(8,128)(2,1)}), bf16[4,1,48,1536]{3,2,1,0:T(8,128)(2,1)S(1)}, u32[]{:S(2)}, u32[]{:S(2)}) async-start(bf16[4,1,48,1536]{3,2,1,0:T(8,128)(2,1)} %add_convert_fusion.3), calls=%async_computation.7 | async-start | bytes 1179648 | tf_op jit(solution)/shard_map/all_to_all | solution.py:545
  (160 other events, 1210.2 us)
Sparse Core Ops, SparseCore 0:
  462.0 57.3 reduce-scatter.2
  550.1 45.7 reduce-scatter.4

commit v3 on v2

--- a/solution.py
+++ b/solution.py
@@ -347,29 +347,34 @@
             out[from_z * PAIR + 1 - place[AT_X]] = far[d][i]
 
 
-def by_source_kernel(place, source, target):
-    depth, ulys = source.shape[:2]
-    for d in range(depth):
+def down_kernel(depth, place, *refs):
+    actives, (weight, out) = refs[:depth], refs[depth:]
+    count = out.shape[2]
+    for d, active in enumerate(actives):
         from_z = lax.rem(place[AT_Z] - d + depth, depth)
-        for m, other in enumerate((0, 2, 1, 3)):
-            target[place[AT_U] ^ other, from_z] = source[d, m]
-
-
-def sort_rows_kernel(depth, place, *refs):
-    mine, far, outs, rows = refs[:depth], refs[depth : 2 * depth], refs[2 * depth : -1], refs[-1]
-    share = outs[0].shape[0]
-    for d in range(depth):
-        from_z = lax.rem(place[AT_Z] - d + depth, depth)
-        rows[from_z * PAIR + place[AT_X]] = mine[d][...]
-        rows[from_z * PAIR + 1 - place[AT_X]] = far[d][...]
-    for m, out in enumerate(outs):
-        out[...] = rows[pl.ds((place[AT_U] ^ m) * share, share)]
-
-
-def place_rows_kernel(place, *refs):
-    out = refs[-1]
-    for m, part in enumerate(refs[:-1]):
-        out[:, place[AT_U] ^ m] = part[...]
+        rows = dot_nt(active[...], weight[...])
+        for i, other in enumerate((0, 2, 1, 3)):
+            out[place[AT_U] ^ other, from_z] = rows[i * count : (i + 1) * count].astype(BF16)
+
+
+def sort_rows_kernel(place, mine, far, own, near, rows):
+    share = own.shape[1]
+    for z in range(mine.shape[0]):
+        rows[z * PAIR + place[AT_X]] = mine[z]
+        rows[z * PAIR + 1 - place[AT_X]] = far[z]
+
+    def part(m):
+        return rows[pl.ds((place[AT_U] ^ m) * share, share)]
+
+    own[0], own[1] = part(0), part(1)
+    near[0], near[1] = part(2), part(3)
+
+
+def place_rows_kernel(place, own, near, across, out):
+    out[:, place[AT_U]] = own[0]
+    out[:, place[AT_U] ^ 2] = near[0]
+    out[:, place[AT_U] ^ 1] = across[0]
+    out[:, place[AT_U] ^ 3] = across[1]
 
 
 def choose_kernel(place, *refs):
@@ -547,10 +552,8 @@
     )
 
 
-def scatter_blk(grid, parts):
-    keep, send = pick(grid.x, parts, 1)
-    both = keep.astype(F32) + grid.swap_x(send.astype(BF16)).astype(F32)
-    return jnp.sum(exchange_z_all(grid, both.astype(BF16)).astype(F32), axis=0)
+def spread_z(grid, value):
+    return exchange_z_all(grid, jnp.broadcast_to(value, (grid.depth, *value.shape)))
 
 
 def exchange_uly(parts):
@@ -624,25 +627,29 @@
     )
     qkv_mine = [block_rows] + [grid.to_z(block_rows, d) for d in range(1, depth)]
     first_far = grid.swap_x(block_rows)
-    cot_flat = by_seq(cotangent)
+    first_arrived = qkv_mine[1]
     *qkv_mine, first_far, unit_near = together(*qkv_mine, first_far, unit_near)
 
     gain_two = ffn_gain.astype(F32)[:, None]
     hidden_units = gate_weight.shape[1] // depth
+    order = sorted(range(1, depth), key=lambda d: (min(d, depth - d), d))
+    early, middle, late = order[0], order[1:-1], order[-1]
+    split_in = after((gate_weight, up_weight, down_weight), first_arrived)
+    split_in = (*split_in[:2], split_in[2].T)
     tile_pieces = call(
         functools.partial(split_tiles_kernel, depth),
         [place],
-        [gate_weight, up_weight, down_weight.T, gain_two],
+        [*split_in, gain_two],
         [like((3, block_model, hidden_units))] * depth,
         scratch=[pltpu.VMEM((depth, 3, block_model, hidden_units), BF16)],
     )
     qkv_far = [first_far] + [grid.swap_x(piece) for piece in qkv_mine[1:]]
     unit_across = grid.swap_core(jnp.stack([unit_own, unit_near]))
-    out_first, cot_first = after((out_weight, cot_flat), *qkv_mine[1:])
-    out_mine = [out_first] + [grid.to_z(out_first, d) for d in range(1, depth)]
-    cot_near = grid.swap_y(cot_first)
-    *held, unit_across, cot_near = together(*qkv_far, *out_mine, unit_across, cot_near)
-    qkv_far, out_mine = held[:depth], held[depth:]
+    out_first, early_piece = after((out_weight, tile_pieces[early]), *qkv_mine[1:])
+    tile_mine = {0: tile_pieces[0], early: grid.to_z(early_piece, early)}
+    out_mine = spread_z(grid, out_first)
+    tile_far = {0: grid.swap_x(after(tile_pieces[0], qkv_far[1]))}
+    *qkv_far, unit_across = together(*qkv_far, unit_across)
     unit_parts = (unit_own, unit_near, unit_across)
 
     head_rows = grid.b * cycle_rows + jnp.arange(cycle_rows, dtype=jnp.int32)
@@ -667,44 +674,41 @@
     )
     units = units.reshape(ulys * count, model)
     qkv_part = qkv_part.reshape(model, columns)
-    order = sorted(range(1, depth), key=lambda d: (min(d, depth - d), d))
     kinds = [kind] + [grid.to_z(kind, d) for d in range(1, depth)]
-    *held, kind = after((*out_mine, *tile_pieces, kind), kind)
-    out_mine, tile_pieces = held[:depth], held[depth:]
-    out_far = [grid.swap_x(piece) for piece in out_mine]
-    tile_mine = {0: tile_pieces[0]}
-    tile_mine[order[0]] = grid.to_z(tile_pieces[order[0]], order[0])
-    *held, cot_near = together(*kinds, *out_far, cot_near)
-    kinds, out_far = held[:depth], held[depth:]
+    out_mine, cot_flat = after((out_mine, by_seq(cotangent)), kind)
+    out_far = grid.swap_x(out_mine)
+    cot_first = cot_flat
+    cot_near = grid.swap_y(cot_first)
+    *held, late_pair, late_down = after(
+        (*[tile_pieces[d] for d in middle], tile_pieces[late][:2], tile_pieces[late][2:]), kinds[1]
+    )
+    for d, piece in zip(middle, held):
+        tile_mine[d] = grid.to_z(piece, d)
+    out_far, cot_near, tile_mine[early], tile_far[0], *kinds = together(
+        out_far, cot_near, tile_mine[early], tile_far[0], *kinds
+    )
+    late_pair = grid.to_z(after(late_pair, kinds[-1]), late)
 
     a_own = jnp.stack(kinds)
     a_far = grid.swap_x(a_own)
     b_own = grid.swap_core(a_own)
-    out_sets = call(
-        functools.partial(sort_rows_kernel, depth),
+    out_own, out_near = call(
+        sort_rows_kernel,
         [place],
-        [*out_mine, *out_far],
-        [like((blocks // ulys, shard, model))] * ulys,
+        [out_mine, out_far],
+        [like((2, heads_share, shard, model))] * 2,
         scratch=[pltpu.VMEM((blocks, shard, model), BF16)],
     )
-    out_sets = [
-        out_sets[0],
-        grid.swap_core(out_sets[1]),
-        grid.swap_y(out_sets[2]),
-        grid.swap_both(out_sets[3]),
-    ]
-    middle, late = order[1:-1], order[-1]
-    for d in middle:
-        tile_mine[d] = grid.to_z(after(tile_pieces[d], *kinds), d)
-    a_far, b_own, tile_mine[order[0]], *held = together(
-        a_far, b_own, tile_mine[order[0]], *[tile_mine[d] for d in middle]
+    out_near = grid.swap_y(out_near)
+    a_far, b_own, out_near, *held = together(
+        a_far, b_own, out_near, *[tile_mine[d] for d in middle]
     )
     tile_mine.update(zip(middle, held))
 
     b_far = grid.swap_core(a_far)
-    tile_far = {0: grid.swap_x(after(tile_mine[0], a_far))}
-    tile_far[order[0]] = grid.swap_x(tile_mine[order[0]])
-    tile_mine[late] = grid.to_z(after(tile_pieces[late], a_far), late)
+    out_across = grid.swap_core(jnp.stack([out_own[1], out_near[1]]))
+    tile_far[early] = grid.swap_x(after(tile_mine[early], a_far))
+    b_far, out_across = together(b_far, out_across)
 
     def over_uly(piece):
         both = jnp.concatenate([piece, grid.swap_y(piece)], axis=0)
@@ -742,9 +746,15 @@
         cost_estimate=SMALL,
     )(span_order, place, query, *[part.reshape(kv_shape) for part in (a_own, a_far, b_own, b_far)])
     flat = attended.reshape(ulys, count, width)
-    out_sets = after(tuple(out_sets), attended)
+    out_own, tile_far[early], late_pair, attended = together(
+        out_own, tile_far[early], late_pair, attended
+    )
+    late_down = grid.to_z(after(late_down, attended), late)
+    flat = attended.reshape(ulys, count, width)
+    for d in middle:
+        tile_far[d] = grid.swap_x(after(tile_mine[d], attended))
     (out_part,) = call(
-        place_rows_kernel, [place], out_sets, [like((blocks // ulys, ulys, shard, model))]
+        place_rows_kernel, [place], [out_own, out_near, out_across], [like((heads_share, ulys, shard, model))]
     )
     out_part = out_part.reshape(width, model)
     keep, send = call(
@@ -754,15 +764,12 @@
         [like((2, count, model), F32), like((2, count, model))],
     )
     got = grid.swap_core(send)
-    got, tile_far[0] = together(got, tile_far[0])
     both = keep + got.astype(F32)
-    for d in middle:
-        tile_far[d] = grid.swap_x(after(tile_mine[d], got))
     got = grid.swap_y(both[1].astype(BF16))
-    got, tile_far[order[0]], tile_mine[late], *held = together(
-        got, tile_far[order[0]], tile_mine[late], *[tile_far[d] for d in middle]
-    )
+    got, late_down, *held = together(got, late_down, *[tile_far[d] for d in middle])
+    tile_mine[late] = jnp.concatenate([late_pair, late_down])
     tile_far.update(zip(middle, held))
+    tile_far[late] = grid.swap_x(after(tile_mine[late], got))
     hidden = rows + both[0] + got.astype(F32)
 
     unit_two, factor_two = norm_rows(hidden)
@@ -770,8 +777,7 @@
     mid_near = grid.swap_y(mid_own)
     mid_pieces = [mid_own, grid.to_z(mid_own, 1)]
     cot_pieces = [cot_first, grid.to_z(after(cot_first, got), 1)]
-    tile_far[late] = grid.swap_x(after(tile_mine[late], got))
-    mid_near, mid_pieces[1] = together(mid_near, mid_pieces[1])
+    mid_near, tile_far[late] = together(mid_near, tile_far[late])
     for d in range(2, depth):
         mid_pieces.append(grid.to_z(mid_pieces[-1], 1))
         cot_pieces.append(grid.to_z(cot_pieces[-1], 1))
@@ -823,38 +829,38 @@
 
     z_groups = [[z * PAIR + x for z in range(depth)] for x in range(PAIR)]
     tile_rows = (block_model,)
-    mid_parts = [over_y(over_core(chunk)) for chunk in back_chunks]
+    boths = [over_core(chunk) for chunk in back_chunks]
+    mid_parts = [over_y(both) for both in boths]
     back_pieces = [grid.to_z(mid_parts[d].astype(BF16), -d) for d in range(1, depth)]
-    mid_all = after(jnp.concatenate(mid_chunks), *back_chunks)
-    cot_all = jnp.concatenate(cot_chunks)
-    active_all = jnp.concatenate(actives)
-    gate_keep, gate_send = halve([contract_rows(mid_all, jnp.concatenate(gate_grads))], tile_rows)
-    upper_keep, upper_send = halve(
-        [contract_rows(after(mid_all, gate_send), jnp.concatenate(upper_grads))], tile_rows
-    )
-    active_now = after(active_all, upper_send)
-    down_keep, down_send = halve([contract_rows(cot_all, active_now)], tile_rows)
+    mid_all = jnp.concatenate(mid_chunks)
+    mid_now = after(mid_all, back_chunks[-1], *boths[:-1], *mid_parts[:-1])
+    gate_keep, gate_send = halve([contract_rows(mid_now, jnp.concatenate(gate_grads))], tile_rows)
+    mid_now = after(mid_all, gate_send, *mid_parts, back_pieces[0])
+    upper_keep, upper_send = halve([contract_rows(mid_now, jnp.concatenate(upper_grads))], tile_rows)
     gate_got = grid.swap_x(gate_send)
-    upper_got = grid.swap_x(after(upper_send, gate_got))
-    down_got = grid.swap_x(after(down_send, upper_got))
-    first, gate_got, upper_got, down_send, *back_pieces = together(
-        mid_parts[0], gate_got, upper_got, down_send, *back_pieces
+    first, gate_got, upper_send, *back_pieces = together(
+        mid_parts[0], gate_got, upper_send, *back_pieces
     )
     mid_grad = first + sum(piece.astype(F32) for piece in back_pieces)
 
     hidden_grad = grad_rows + norm_back(mid_grad, unit_two, factor_two)
     branch_own = hidden_grad.astype(BF16)
     branch_near = grid.swap_y(branch_own)
-    out_all = contract_cols(after(active_all, branch_own), down_used).astype(BF16)
+    upper_got = grid.swap_x(after(upper_send, gate_got))
     gate_owned = fold(*after((gate_keep, gate_got), branch_own))
-    branch_near, out_all, down_got = together(branch_near, out_all, down_got)
+    held = after((*cot_chunks, *actives), branch_own)
+    cot_all, active_all = [jnp.concatenate(part) for part in (held[:depth], held[depth:])]
+    down_keep, down_send = halve([contract_rows(cot_all, active_all)], tile_rows)
+    down_send, branch_near, upper_got = together(down_send, branch_near, upper_got)
+    down_got = grid.swap_x(down_send)
     branch_across = grid.swap_core(jnp.stack([branch_own, branch_near]))
     branch_parts = (branch_own, branch_near, branch_across)
     (grad_heads,) = call(
         heads_grad_kernel, [place], [*branch_parts, out_part], [like((ulys, count, width))]
     )
 
-    grad_heads = grad_heads.reshape(heads_shape)
+    grad_heads, gate_owned = together(grad_heads.reshape(heads_shape), gate_owned)
+    upper_owned = fold(*after((upper_keep, upper_got), gate_owned))
     both_spec = pl.BlockSpec(
         (2, depth, ulys, 1, local_rows, HEAD_DIM), lambda s, *unused: (0, 0, 0, s, 0, 0)
     )
@@ -889,12 +895,13 @@
         for k in (1, 0)
     ]
     query_grad = query_grad.reshape(ulys * count, width)
-    got_far, got_own, query_grad, gate_owned = together(got_far, got_own, query_grad, gate_owned)
-    upper_owned = fold(*after((upper_keep, upper_got), gate_owned))
+    got_far, got_own, query_grad, upper_owned = together(
+        got_far, got_own, query_grad, upper_owned
+    )
     (out_all,) = call(
-        by_source_kernel,
+        functools.partial(down_kernel, depth),
         [place],
-        [after(out_all, got_far).reshape(depth, ulys, count, model)],
+        [*after(tuple(actives), got_far), down_used],
         [like((ulys, depth, count, model))],
     )
     from_x = grid.swap_x((keep_far.astype(F32) + got_far.astype(F32)).astype(BF16))
@@ -907,21 +914,19 @@
         [like((2, heads_share, shard, model))] * 2,
     )
     head_keep, head_send = halve([contract_rows(units, query_grad)], (ulys, shard))
-    from_x, head_send, out_near, out_all = together(from_x, head_send, out_near, out_all)
+    from_x, head_send, out_near, out_all, down_got = together(
+        from_x, head_send, out_near, out_all, down_got
+    )
     out_all = lax.psum_scatter(out_all, "uly", scatter_dimension=0, tiled=False)
-    out_all = lax.psum_scatter(
-        out_all, "blk", scatter_dimension=0, axis_index_groups=z_groups, tiled=False
-    )
     kind_parts = keep_own.astype(F32) + got_own.astype(F32) + from_x.astype(F32)
     kind_parts = kind_parts.astype(BF16)
     kind_back = [grid.to_z(kind_parts[d], -d) for d in range(1, depth)]
     head_got = grid.swap_x(head_send)
     out_near = grid.swap_y(out_near)
-    *kind_back, out_near, kind_parts, head_got, upper_owned = together(
-        *kind_back, out_near, kind_parts, head_got, upper_owned
+    *kind_back, out_near, kind_parts, head_got = together(
+        *kind_back, out_near, kind_parts, head_got
     )
     out_across = grid.swap_core(jnp.stack([out_own[1], out_near[1]]))
-    head_pieces = fold(head_keep, head_got)
     kind_grad = kind_parts[0].astype(F32)
     for piece in kind_back:
         kind_grad = kind_grad + piece.astype(F32)
@@ -942,19 +947,11 @@
     share = jnp.concatenate([bias, share], axis=2)
     kind_keep, kind_send = halve([share], (ulys, shard + 16))
     kind_got = grid.swap_x(kind_send)
-    keep, send = call(
-        functools.partial(project_kernel, True),
-        [place],
-        [
-            query_grad.reshape(ulys, count, width),
-            kind_grad.reshape(ulys, count, HEAD_DIM),
-            qkv_part[:, :width],
-            qkv_part[:, width:],
-        ],
-        [like((2, count, model), F32), like((2, count, model))],
-    )
-    send, kind_got, out_across = after((send, kind_got, out_across), send)
-    both = keep + grid.swap_core(send).astype(F32)
+    out_all = lax.psum_scatter(
+        after(out_all, kind_send), "blk", scatter_dimension=0, axis_index_groups=z_groups, tiled=False
+    )
+    head_pieces = fold(*after((head_keep, head_got), kind_send))
+    out_across = after(out_across, kind_send)
     out_keep, out_send = call(
         group_rows_kernel,
         [place],
@@ -962,9 +959,7 @@
         [like((depth, 1, shard, model))] * 2,
         scratch=[pltpu.VMEM((blocks, shard, model), BF16)],
     )
-    out_got = grid.swap_x(out_send)
-    down_owned = fold(*after((down_keep, down_got), head_pieces))
-    out_pieces = fold(*after((out_keep, out_got), down_owned))
+    out_got = grid.swap_x(after(out_send, kind_got))
     kind_pieces = call(
         functools.partial(fold_kernel, depth),
         [place],
@@ -973,6 +968,28 @@
     )
     kind_pieces = [kind_pieces[0]] + [grid.to_z(kind_pieces[d], d) for d in range(1, depth)]
     kind_pieces = jnp.stack(kind_pieces)
+    kind_pieces, out_got = together(kind_pieces, out_got)
+    kind_now = after(kind_grad, kind_pieces)
+    keep, send = call(
+        functools.partial(project_kernel, True),
+        [place],
+        [
+            query_grad.reshape(ulys, count, width),
+            kind_now.reshape(ulys, count, HEAD_DIM),
+            qkv_part[:, :width],
+            qkv_part[:, width:],
+        ],
+        [like((2, count, model), F32), like((2, count, model))],
+    )
+    both = keep + grid.swap_core(send).astype(F32)
+    down_owned = fold(*after((down_keep, down_got), head_pieces))
+    out_pieces = call(
+        functools.partial(fold_kernel, depth),
+        [place],
+        [out_keep, out_got],
+        [like(out_keep.shape[1:])] * depth,
+    )
+    out_pieces = [out_pieces[0]] + [grid.to_z(out_pieces[d], d) for d in range(1, depth)]
 
     def to_owners(pieces):
         own, near = call(
@@ -1003,7 +1020,7 @@
         [bias[:, :group].reshape(-1), jnp.transpose(kind_bias, (1, 0, 2)).reshape(-1)]
     )
     grad_bias = lax.dynamic_slice_in_dim(bias, column_start, owned_columns, 0)
-    grad_out = jnp.sum(out_pieces[:, 0].astype(F32), axis=0)
+    grad_out = sum(piece[0].astype(F32) for piece in out_pieces)
     result = hidden + after(out_all, grad_qkv).astype(F32)
     output = by_row(result.astype(BF16))
     normed_grad = both[0] + grid.swap_y(both[1].astype(BF16)).astype(F32)
@@ -1012,7 +1029,7 @@
     grad_gate, grad_upper, grad_down, gain_part = call(
         functools.partial(finish_kernel, depth),
         [],
-        [*after((gate_owned, upper_owned, down_owned), head_pieces), gate_weight, up_weight, gain_two],
+        [gate_owned, upper_owned, after(down_owned, grad_qkv), gate_weight, up_weight, gain_two],
         [like(tile_shape, F32)] * 3 + [like((block_model, 1), F32)],
     )
     grad_down = grad_down.T

time: 639 us -> 589 us (0.922)
  waiting for transfers between devices: 248 us -> 199 us
  starting transfers between devices: 107 us -> 126 us
  local copies, waits for them, and re-layouts: 70.4 us -> 54.9 us
    ppermute x20 -> x17, waiting for transfers between devices: 64.3 us -> 32.1 us  [swap_x(): return lax.ppermute(value, 'blk', [(i, i ^ 1) for i in range(self.blocks)])]
    ppermute x27 -> x28, starting transfers between devices: 32.8 us -> 55 us  [to_z(): return lax.ppermute(value, 'blk', pairs)]
    unnamed x252 -> x256, local copies, waits for them, and re-layouts: 47.1 us -> 29.1 us
    ppermute x27 -> x28, waiting for transfers between devices: 110 us -> 97.8 us  [to_z(): return lax.ppermute(value, 'blk', pairs)]
    dot_general x9 -> x8, matrix products: 21.1 us -> 12 us  [contract_cols(): lax.dot_general(left, right, (((1,), (1,)), ((), ())), preferred_element_...]
    all_to_all x5, starting transfers between devices: 17.9 us -> 24.9 us  [exchange_z_all(): lax.all_to_all(parts, 'blk', split_axis=0, concat_axis=0, axis_index_grou...]
    ppermute x20 -> x17, starting transfers between devices: 23.5 us -> 18.1 us  [swap_x(): return lax.ppermute(value, 'blk', [(i, i ^ 1) for i in range(self.blocks)])]
    pallas_call x22 -> x23, Pallas kernels: 48.2 us -> 53.6 us  [call(): pl.pallas_call(kernel, grid_spec=pltpu.PrefetchScalarGridSpec(num_scalar_...]
  transfers between devices with their start and end apart: 104 -> 101, of which waited for: 45 -> 41; matrix products, arithmetic and copies ran while one was open for 22% -> 21% of each run, Pallas kernels for 10% -> 12%
where the time goes in v3:
time: 589 us; the launch traced here: 580 us
  waiting for transfers between devices  199 us (34%)
  starting transfers between devices  126 us (21%)
  Pallas kernels  72.3 us (12%)
  matrix products  57.1 us (10%)
  local copies, waits for them, and re-layouts  54.9 us (9%)
  other arithmetic  54.5 us (9%)
  between operations  16.5 us (3%)
    ppermute x28, waiting for transfers between devices, to_z(): return lax.ppermute(value, 'blk', pairs)  97.8 us
    ppermute x28, starting transfers between devices, to_z(): return lax.ppermute(value, 'blk', pairs)  55 us
    pallas_call x23, Pallas kernels, call(): pl.pallas_call(kernel, grid_spec=pltpu.PrefetchScalarGridSpec(num_scalar_...  53.6 us
    ppermute x21, waiting for transfers between devices, swap_y(): return lax.ppermute(value, 'uly', [(i, i ^ 2) for i in range(self.ulys)])  37.6 us
    ppermute x17, waiting for transfers between devices, swap_x(): return lax.ppermute(value, 'blk', [(i, i ^ 1) for i in range(self.blocks)])  32.1 us
    unnamed x256, local copies, waits for them, and re-layouts  29.1 us
    all_to_all x5, waiting for transfers between devices, exchange_z_all(): lax.all_to_all(parts, 'blk', split_axis=0, concat_axis=0, axis_index_grou...  27.6 us
    all_to_all x5, starting transfers between devices, exchange_z_all(): lax.all_to_all(parts, 'blk', split_axis=0, concat_axis=0, axis_index_grou...  24.9 us
  transfers between devices with their start and end apart: 101, of which 41 were waited for; matrix products, arithmetic and copies ran while one was open for 21% of the time, Pallas kernels for 12%

profile of v3, /device:TPU:0, one launch (start us, length us, event | category | flops | bytes accessed | tf_op | source)
XLA Modules:
  0.0 580.2 jit_solution(16404319006676054929)
XLA Ops:
  11.2 4.2 all-to-all-start
  18.8 2.9 collective-permute-start.4
  28.5 2.6 collective-permute-start.1
  34.1 3.0 collective-permute-done.rest_1_
  37.1 8.3 %collective-permute-done.1.rest_2_ = bf16[208,512]{1,0:T(8,128)(2,1)} collective-permute-done((bf16[208,512]{1,0:T(8,128)(2,1)}, bf16[208,512]{1,0:T(8,128)(2,1)}, u32[]{:S(2)}, u32[]{:S(2)}) %collective-permute-start.1) | collective-permute-done | bytes 213024 | tf_op jit(solution)/shard_map/ppermute | solution.py:487
  51.9 7.5 %all-to-all-start.1 = ((bf16[4,48,1536]{2,1,0:T(8,128)(2,1)}), bf16[4,48,1536]{2,1,0:T(8,128)(2,1)S(1)}, u32[]{:S(2)}, u32[]{:S(2)}) async-start(bf16[4,48,1536]{2,1,0:T(8,128)(2,1)} %broadcast_in_dim.58), calls=%async_computation.1 | async-start | bytes 1179648 | tf_op jit(solution)/shard_map/all_to_all | solution.py:550
  73.4 4.6 collective-permute-done.7.rest_7_
  78.0 4.7 shard_map.187
  83.9 6.4 %all-to-all-done.1.mine = bf16[4,48,1536]{2,1,0:T(8,128)(2,1)S(1)} async-done(((bf16[4,48,1536]{2,1,0:T(8,128)(2,1)}), bf16[4,48,1536]{2,1,0:T(8,128)(2,1)S(1)}, u32[]{:S(2)}, u32[]{:S(2)}) %all-to-all-start.1) | async-done | bytes 589856 | tf_op jit(solution)/shard_map/all_to_all | solution.py:550
  92.5 8.2 %collective-permute-done.13 = bf16[4,128,128]{2,1,0:T(8,128)(2,1)S(1)} collective-permute-done((bf16[4,128,128]{2,1,0:T(8,128)(2,1)S(1)}, bf16[4,128,128]{2,1,0:T(8,128)(2,1)S(1)}, u32[]{:S(2)}, u32[]{:S(2)}) %collective-permute-start.13) | collective-permute-done | bytes 131104 | tf_op jit(solution)/shard_map/ppermute | solution.py:487
  102.8 3.4 collective-permute-start.19
  109.9 10.1 %collective-permute-done.19.refs_3_ = bf16[3,192,560]{2,1,0:T(8,128)(2,1)S(1)} collective-permute-done((bf16[3,192,560]{2,1,0:T(8,128)(2,1)}, bf16[3,192,560]{2,1,0:T(8,128)(2,1)S(1)}, u32[]{:S(2)}, u32[]{:S(2)}) %collective-permute-start.19) | collective-permute-done | bytes 645152 | tf_op jit(solution)/shard_map/ppermute | solution.py:487
  123.7 3.1 collective-permute-start.21
  126.9 7.9 %shard_map.189 = (bf16[4,2,64,384]{3,2,1,0:T(8,128)(2,1)S(1)}, f32[2,2,1,384]{3,2,1,0:T(1,128)S(1)}, bf16[2,2,2048,128]{3,2,1,0:T(8,128)(2,1)S(1)}) custom-call(s32[2,16]{1,0:T(2,128)S(1)} %copy-done.53, s32[6]{0:T(128)S(1)} %stack.95.place, bf16[4,2,64,384]{3,2,1,0:T(8,128)(2,1)S(1)} %bitcast.236, bf16[4,4,2,64,128]{4,3,2,1,0:T(8,128)(2,1)S(1)} %pad_maximum_fusion.16.a_own, ...), custom_call_target="tpu_custom_call" | custom-call | flops 1 | bytes 1 | tf_op jit(solution)/shard_map/pallas_call | solution.py:732
  144.0 3.8 collective-permute-start.26
  147.9 6.9 %collective-permute-done.26 = bf16[1,192,560]{2,1,0:T(8,128)(2,1)S(1)} collective-permute-done((bf16[1,192,560]{2,1,0:T(8,128)(2,1)S(1)}, bf16[1,192,560]{2,1,0:T(8,128)(2,1)S(1)}, u32[]{:S(2)}, u32[]{:S(2)}) %collective-permute-start.26) | collective-permute-done | bytes 215072 | tf_op jit(solution)/shard_map/ppermute | solution.py:487
  154.8 4.8 collective-permute-done.27.refs_7_
  162.5 16.5 %collective-permute-start.34 = (bf16[128,1536]{1,0:T(8,128)(2,1)S(1)}, bf16[128,1536]{1,0:T(8,128)(2,1)S(1)}, u32[]{:S(2)}, u32[]{:S(2)}) collective-permute-start(bf16[128,1536]{1,0:T(8,128)(2,1)S(1)} %get-tuple-element.351), channel_id=1, source_target_pairs={{0,8},{4,12},{8,16},{12,20},{16,24},{20,28},{24,0},{28,4},{1,9},{5... | collective-permute-start | bytes 1179656 | tf_op jit(solution)/shard_map/ppermute | solution.py:487
  179.3 12.5 %collective-permute-done.34 = bf16[128,1536]{1,0:T(8,128)(2,1)S(1)} collective-permute-done((bf16[128,1536]{1,0:T(8,128)(2,1)S(1)}, bf16[128,1536]{1,0:T(8,128)(2,1)S(1)}, u32[]{:S(2)}, u32[]{:S(2)}) %collective-permute-start.34) | collective-permute-done | bytes 393248 | tf_op jit(solution)/shard_map/ppermute | solution.py:487
  191.8 8.4 %collective-permute-done.43 = bf16[128,1536]{1,0:T(8,128)(2,1)S(1)} collective-permute-done((bf16[128,1536]{1,0:T(8,128)(2,1)S(1)}, bf16[128,1536]{1,0:T(8,128)(2,1)S(1)}, u32[]{:S(2)}, u32[]{:S(2)}) %collective-permute-start.43) | collective-permute-done | bytes 393248 | tf_op jit(solution)/shard_map/ppermute | solution.py:487
  201.2 4.9 shard_map.192
  206.1 2.9 fusion.80
  212.6 3.1 collective-permute-done.44
  215.8 11.5 %collective-permute-done.45 = bf16[128,1536]{1,0:T(8,128)(2,1)S(1)} collective-permute-done((bf16[128,1536]{1,0:T(8,128)(2,1)S(1)}, bf16[128,1536]{1,0:T(8,128)(2,1)S(1)}, u32[]{:S(2)}, u32[]{:S(2)}) %collective-permute-start.45) | collective-permute-done | bytes 393248 | tf_op jit(solution)/shard_map/ppermute | solution.py:487
  227.7 8.5 %collective-permute-done.51 = bf16[128,1536]{1,0:T(8,128)(2,1)S(1)} collective-permute-done((bf16[128,1536]{1,0:T(8,128)(2,1)S(1)}, bf16[128,1536]{1,0:T(8,128)(2,1)S(1)}, u32[]{:S(2)}, u32[]{:S(2)}) %collective-permute-start.51) | collective-permute-done | bytes 393248 | tf_op jit(solution)/shard_map/ppermute | solution.py:493
  238.4 2.7 multiply_convert_fusion.3
  251.2 2.6 multiply_convert_fusion.2
  258.6 6.9 %collective-permute-done.41 = bf16[128,1536]{1,0:T(8,128)(2,1)S(1)} collective-permute-done((bf16[128,1536]{1,0:T(8,128)(2,1)S(1)}, bf16[128,1536]{1,0:T(8,128)(2,1)S(1)}, u32[]{:S(2)}, u32[]{:S(2)}) %collective-permute-start.41) | collective-permute-done | bytes 393248 | tf_op jit(solution)/shard_map/ppermute | solution.py:493
  269.5 2.7 multiply_convert_fusion.1
  282.7 2.6 multiply_convert_fusion
  295.5 8.6 %collective-permute-done.54 = bf16[128,1536]{1,0:T(8,128)(2,1)S(1)} collective-permute-done((bf16[128,1536]{1,0:T(8,128)(2,1)S(1)}, bf16[128,1536]{1,0:T(8,128)(2,1)S(1)}, u32[]{:S(2)}, u32[]{:S(2)}) %collective-permute-start.54) | collective-permute-done | bytes 393248 | tf_op jit(solution)/shard_map/ppermute | solution.py:493
  306.5 5.2 collective-permute-done.55
  316.1 5.2 convolution_convert_fusion.1
  321.3 2.7 copy.294
  329.2 8.1 %convolution_convert_fusion = bf16[1536,560]{0,1:T(8,128)(2,1)} fusion(bf16[2048,1536]{1,0:T(8,128)(2,1)} %copy-done.106, bf16[512,560]{1,0:T(8,128)(2,1)} %copy-done.94, bf16[512,560]{1,0:T(8,128)(2,1)S(1)} %copy-done.93, bf16[512,560]{1,0:T(8,128)(2,1)S(1)} %copy-done.91, bf16[512,560]{1,0:T(8,128)(2,1)S(1)} %copy-done.89), kind=kOutput, calls=%fused_computation.13 | convolution fusion | flops 3533250560 | bytes 10305536 | tf_op jit(solution)/shard_map/dot_general | solution.py:41
  337.3 2.7 copy.295
  341.7 6.9 %collective-permute-done.56 = bf16[4,1,192,560]{3,2,1,0:T(8,128)(2,1)} collective-permute-done((bf16[4,1,192,560]{3,2,1,0:T(8,128)(2,1)}, bf16[4,1,192,560]{3,2,1,0:T(8,128)(2,1)}, u32[]{:S(2)}, u32[]{:S(2)}) %collective-permute-start.56) | collective-permute-done | bytes 860192 | tf_op jit(solution)/shard_map/ppermute | solution.py:490
  350.2 2.6 fusion.77
  356.4 4.5 all-to-all-start.2
  360.9 7.0 %fusion.8 = bf16[1536,560]{0,1:T(8,128)(2,1)} fusion(bf16[512,1536]{1,0:T(8,128)(2,1)} %copy-done.98, bf16[512,1536]{1,0:T(8,128)(2,1)} %copy-done.102, bf16[512,1536]{1,0:T(8,128)(2,1)} %copy-done.100, bf16[512,1536]{1,0:T(8,128)(2,1)} %copy-done.101, bf16[512,560]{1,0:T(8,128)(2,1)} %get-tuple-element.289.refs_3_, bf16[512,560]{1,0:T(8,128)(2,1)S(1)} %copy-done.39, ...), kind=kOutput, calls=%fused_computation.12 | convolution fusion | flops 3558416384 | bytes 10305536 | tf_op jit(solution)/shard_map/dot_general | solution.py:41
  367.9 2.7 copy.304
  378.7 3.0 shard_map.196
  385.8 4.0 all-to-all-start.3
  391.5 10.8 %shard_map.197 = (bf16[4,2,64,384]{3,2,1,0:T(8,128)(2,1)S(1)}, bf16[4,4,2,64,128]{4,3,2,1,0:T(8,128)(2,1)S(1)}, bf16[4,4,2,64,128]{4,3,2,1,0:T(8,128)(2,1)S(1)}, bf16[2,4,4,2,64,128]{5,4,3,2,1,0:T(8,128)(2,1)S(1)}) custom-call(s32[2,16]{1,0:T(2,128)S(1)} %copy-done.53, s32[6]{0:T(128)S(1)} %stack.95.place, bf16[4,2,64,384]{3,2,1,0:T(8,128)(2,1)S(1)} %bitcast.237, ...), custom_call_target="tpu_custom_call" | custom-call | flops 1 | bytes 1 | tf_op jit(solution)/shard_map/pallas_call | solution.py:867
  406.2 8.2 %all-to-all-done.3.uppers = bf16[4,1,192,560]{3,2,1,0:T(8,128)(2,1)S(1)} async-done(((bf16[4,1,192,560]{3,2,1,0:T(8,128)(2,1)}), bf16[4,1,192,560]{3,2,1,0:T(8,128)(2,1)S(1)}, u32[]{:S(2)}, u32[]{:S(2)}) %all-to-all-start.3) | async-done | bytes 860192 | tf_op jit(solution)/shard_map/all_to_all | solution.py:550
  419.9 3.6 shard_map.199
  425.0 8.4 %shard_map.201 = bf16[4,4,128,1536]{3,2,1,0:T(8,128)(2,1)} custom-call(s32[6]{0:T(128)S(1)} %stack.95.place, bf16[512,560]{1,0:T(8,128)(2,1)S(1)} %copy-done.36, bf16[512,560]{1,0:T(8,128)(2,1)S(1)} %copy-done.38, bf16[512,560]{1,0:T(8,128)(2,1)S(1)} %copy-done.40, bf16[512,560]{1,0:T(8,128)(2,1)S(1)} %copy-done.41, bf16[1536,560]{1,0:T(8,128)(2,1)S(1)} %bitcast.235), custom_call_target="tpu_custom_call" | custom-call | flops 1 | bytes 1 | tf_op jit(solution)/shard_map/pallas_call | solution.py:77
  433.5 5.4 collective-permute-done.69
  442.9 6.6 %collective-permute-start.71 = (bf16[4,2,64,128]{3,2,1,0:T(8,128)(2,1)S(1)}, bf16[4,2,64,128]{3,2,1,0:T(8,128)(2,1)S(1)}, u32[]{:S(2)}, u32[]{:S(2)}) collective-permute-start(bf16[4,2,64,128]{3,2,1,0:T(8,128)(2,1)S(1)} %get-tuple-element.378), channel_id=1, source_target_pairs={{0,24},{4,28},{8,0},{12,4},{16,8},{20,12},{24,16},{28,20},{1,25},{... | collective-permute-start | bytes 393224 | tf_op jit(solution)/shard_map/ppermute | solution.py:487
  450.4 3.0 collective-permute-done.71
  453.4 5.8 collective-permute-done.72
  467.2 4.3 all-to-all-start.4
  475.3 4.6 collective-permute-done.78.got
  484.7 3.5 collective-permute-start.81
  490.2 3.1 collective-permute-done.80
  496.6 3.3 shard_map.208
  503.4 4.6 all-to-all-start.5
  509.3 3.8 collective-permute-done.76.refs_1_
  514.5 3.2 collective-permute-done.84.refs_4_
  521.3 3.8 collective-permute-start.90
  529.0 3.1 convert_add_fusion
  532.1 12.9 %all-to-all-done.5.downs = bf16[4,1,192,560]{3,2,1,0:T(8,128)(2,1)S(1)} async-done(((bf16[4,1,192,560]{3,2,1,0:T(8,128)(2,1)}), bf16[4,1,192,560]{3,2,1,0:T(8,128)(2,1)S(1)}, u32[]{:S(2)}, u32[]{:S(2)}) %all-to-all-start.5) | async-done | bytes 860192 | tf_op jit(solution)/shard_map/all_to_all | solution.py:550
  546.2 5.6 shard_map.210
  555.4 9.8 %collective-permute-done.89 = bf16[1,48,1536]{2,1,0:T(8,128)(2,1)} collective-permute-done((bf16[1,48,1536]{2,1,0:T(8,128)(2,1)}, bf16[1,48,1536]{2,1,0:T(8,128)(2,1)}, u32[]{:S(2)}, u32[]{:S(2)}) %collective-permute-start.89) | collective-permute-done | bytes 147488 | tf_op jit(solution)/shard_map/ppermute | solution.py:487
  (601 shorter events, 205.0 us)
Async XLA Ops:
  18.8 18.2 %collective-permute-start.4 = (bf16[128,1536]{1,0:T(8,128)(2,1)S(1)}, bf16[128,1536]{1,0:T(8,128)(2,1)S(1)}, u32[]{:S(2)}, u32[]{:S(2)}) collective-permute-start(bf16[128,1536]{1,0:T(8,128)(2,1)S(1)} %fusion.41.own), channel_id=1, source_target_pairs={{0,2},{1,3},{2,0},{3,1},{4,6},{5,7},{6,4},{7,5},{8,10},{9,11},{10,... | collective-permute-start | bytes 1179656 | tf_op jit(solution)/shard_map/ppermute | solution.py:493
  28.5 16.9 %collective-permute-start.1 = (bf16[208,512]{1,0:T(8,128)(2,1)}, bf16[208,512]{1,0:T(8,128)(2,1)}, u32[]{:S(2)}, u32[]{:S(2)}) collective-permute-start(bf16[208,512]{1,0:T(8,128)(2,1)} %pad_maximum_fusion.25.rest_0_), channel_id=1, source_target_pairs={{0,16},{4,20},{8,24},{12,28},{16,0},{20,4},{24,8},{28,12},{1,17},{... | collective-permute-start | bytes 638984 | tf_op jit(solution)/shard_map/ppermute | solution.py:487
  31.1 14.3 %collective-permute-start.2 = (bf16[208,512]{1,0:T(8,128)(2,1)}, bf16[208,512]{1,0:T(8,128)(2,1)}, u32[]{:S(2)}, u32[]{:S(2)}) collective-permute-start(bf16[208,512]{1,0:T(8,128)(2,1)} %pad_maximum_fusion.25.rest_0_), channel_id=1, source_target_pairs={{0,24},{4,28},{8,0},{12,4},{16,8},{20,12},{24,16},{28,20},{1,25},{... | collective-permute-start | bytes 638984 | tf_op jit(solution)/shard_map/ppermute | solution.py:487
  51.9 38.3 %all-to-all-start.1 = ((bf16[4,48,1536]{2,1,0:T(8,128)(2,1)}), bf16[4,48,1536]{2,1,0:T(8,128)(2,1)S(1)}, u32[]{:S(2)}, u32[]{:S(2)}) async-start(bf16[4,48,1536]{2,1,0:T(8,128)(2,1)} %broadcast_in_dim.58), calls=%async_computation.1 | async-start | bytes 1179648 | tf_op jit(solution)/shard_map/all_to_all | solution.py:550
  60.4 17.6 %collective-permute-start.8 = (bf16[2,128,1536]{2,1,0:T(8,128)(2,1)}, bf16[2,128,1536]{2,1,0:T(8,128)(2,1)S(1)}, u32[]{:S(2)}, u32[]{:S(2)}) collective-permute-start(bf16[2,128,1536]{2,1,0:T(8,128)(2,1)} %pad_maximum_fusion.1), channel_id=1, source_target_pairs={{0,1},{1,0},{2,3},{3,2},{4,5},{5,4},{6,7},{7,6},{8,9},{9,8},{10,11... | collective-permute-start | bytes 2359304 | tf_op jit(solution)/shard_map/ppermute | solution.py:499
  62.6 15.4 %collective-permute-start.7 = (bf16[208,512]{1,0:T(8,128)(2,1)}, bf16[208,512]{1,0:T(8,128)(2,1)S(1)}, u32[]{:S(2)}, u32[]{:S(2)}) collective-permute-start(bf16[208,512]{1,0:T(8,128)(2,1)} %collective-permute-done.2.rest_3_), channel_id=1, source_target_pairs={{0,4},{4,0},{8,12},{12,8},{16,20},{20,16},{24,28},{28,24},{1,5},{5... | collective-permute-start | bytes 638984 | tf_op jit(solution)/shard_map/ppermute | solution.py:490
  64.1 28.4 %collective-permute-start.11 = (bf16[3,192,560]{2,1,0:T(8,128)(2,1)}, bf16[3,192,560]{2,1,0:T(8,128)(2,1)}, u32[]{:S(2)}, u32[]{:S(2)}) collective-permute-start(bf16[3,192,560]{2,1,0:T(8,128)(2,1)} %copy-done.55), channel_id=1, source_target_pairs={{0,8},{4,12},{8,16},{12,20},{16,24},{20,28},{24,0},{28,4},{1,9},{5... | collective-permute-start | bytes 1935368 | tf_op jit(solution)/shard_map/ppermute | solution.py:487
  68.8 33.9 %collective-permute-start.12 = (bf16[3,192,560]{2,1,0:T(8,128)(2,1)S(1)}, bf16[3,192,560]{2,1,0:T(8,128)(2,1)}, u32[]{:S(2)}, u32[]{:S(2)}) collective-permute-start(bf16[3,192,560]{2,1,0:T(8,128)(2,1)S(1)} %copy-done.33), channel_id=1, source_target_pairs={{0,4},{4,0},{8,12},{12,8},{16,20},{20,16},{24,28},{28,24},{1,5},{5... | collective-permute-start | bytes 1935368 | tf_op jit(solution)/shard_map/ppermute | solution.py:490
  90.3 16.9 %collective-permute-start.9 = (bf16[4,48,1536]{2,1,0:T(8,128)(2,1)S(1)}, bf16[4,48,1536]{2,1,0:T(8,128)(2,1)S(1)}, u32[]{:S(2)}, u32[]{:S(2)}) collective-permute-start(bf16[4,48,1536]{2,1,0:T(8,128)(2,1)S(1)} %all-to-all-done.1.mine), channel_id=1, source_target_pairs={{0,4},{4,0},{8,12},{12,8},{16,20},{20,16},{24,28},{28,24},{1,5},{5... | collective-permute-start | bytes 1769480 | tf_op jit(solution)/shard_map/ppermute | solution.py:490
  91.8 15.4 %collective-permute-start.10 = (bf16[128,1536]{1,0:T(8,128)(2,1)}, bf16[128,1536]{1,0:T(8,128)(2,1)S(1)}, u32[]{:S(2)}, u32[]{:S(2)}) collective-permute-start(bf16[128,1536]{1,0:T(8,128)(2,1)} %bitcast.268), channel_id=1, source_target_pairs={{0,2},{1,3},{2,0},{3,1},{4,6},{5,7},{6,4},{7,5},{8,10},{9,11},{10,... | collective-permute-start | bytes 1179656 | tf_op jit(solution)/shard_map/ppermute | solution.py:493
  102.8 17.3 %collective-permute-start.19 = (bf16[3,192,560]{2,1,0:T(8,128)(2,1)}, bf16[3,192,560]{2,1,0:T(8,128)(2,1)S(1)}, u32[]{:S(2)}, u32[]{:S(2)}) collective-permute-start(bf16[3,192,560]{2,1,0:T(8,128)(2,1)} %copy-done.54), channel_id=1, source_target_pairs={{0,24},{4,28},{8,0},{12,4},{16,8},{20,12},{24,16},{28,20},{1,25},{... | collective-permute-start | bytes 1935368 | tf_op jit(solution)/shard_map/ppermute | solution.py:487
  107.9 13.7 %collective-permute-start.18 = (bf16[2,2,48,1536]{3,2,1,0:T(8,128)(2,1)S(1)}, bf16[2,2,48,1536]{3,2,1,0:T(8,128)(2,1)S(1)}, u32[]{:S(2)}, u32[]{:S(2)}) collective-permute-start(bf16[2,2,48,1536]{3,2,1,0:T(8,128)(2,1)S(1)} %get-tuple-element.207), channel_id=1, source_target_pairs={{0,2},{1,3},{2,0},{3,1},{4,6},{5,7},{6,4},{7,5},{8,10},{9,11},{10,... | collective-permute-start | bytes 1769480 | tf_op jit(solution)/shard_map/ppermute | solution.py:493
  121.6 16.8 %collective-permute-start.20 = (bf16[3,192,560]{2,1,0:T(8,128)(2,1)}, bf16[3,192,560]{2,1,0:T(8,128)(2,1)S(1)}, u32[]{:S(2)}, u32[]{:S(2)}) collective-permute-start(bf16[3,192,560]{2,1,0:T(8,128)(2,1)} %collective-permute-done.11.refs_1_), channel_id=1, source_target_pairs={{0,4},{4,0},{8,12},{12,8},{16,20},{20,16},{24,28},{28,24},{1,5},{5... | collective-permute-start | bytes 1935368 | tf_op jit(solution)/shard_map/ppermute | solution.py:490
  123.7 14.5 %collective-permute-start.21 = (bf16[2,192,560]{2,1,0:T(8,128)(2,1)S(1)}, bf16[2,192,560]{2,1,0:T(8,128)(2,1)S(1)}, u32[]{:S(2)}, u32[]{:S(2)}) collective-permute-start(bf16[2,192,560]{2,1,0:T(8,128)(2,1)S(1)} %slice.178), channel_id=1, source_target_pairs={{0,16},{4,20},{8,24},{12,28},{16,0},{20,4},{24,8},{28,12},{1,17},{... | collective-permute-start | bytes 1290248 | tf_op jit(solution)/shard_map/ppermute | solution.py:487
  140.7 18.9 %collective-permute-start.27 = (bf16[3,192,560]{2,1,0:T(8,128)(2,1)S(1)}, bf16[3,192,560]{2,1,0:T(8,128)(2,1)S(1)}, u32[]{:S(2)}, u32[]{:S(2)}) collective-permute-start(bf16[3,192,560]{2,1,0:T(8,128)(2,1)S(1)} %collective-permute-done.19.refs_3_), channel_id=1, source_target_pairs={{0,4},{4,0},{8,12},{12,8},{16,20},{20,16},{24,28},{28,24},{1,5},{5... | collective-permute-start | bytes 1935368 | tf_op jit(solution)/shard_map/ppermute | solution.py:490
  143.2 16.4 %collective-permute-start.25 = (bf16[128,1536]{1,0:T(8,128)(2,1)S(1)}, bf16[128,1536]{1,0:T(8,128)(2,1)S(1)}, u32[]{:S(2)}, u32[]{:S(2)}) collective-permute-start(bf16[128,1536]{1,0:T(8,128)(2,1)S(1)} %fusion.44), channel_id=1, source_target_pairs={{0,2},{1,3},{2,0},{3,1},{4,6},{5,7},{6,4},{7,5},{8,10},{9,11},{10,... | collective-permute-start | bytes 1179656 | tf_op jit(solution)/shard_map/ppermute | solution.py:493
  147.8 31.4 %collective-permute-start.28 = (bf16[256,1536]{1,0:T(8,128)(2,1)S(1)}, bf16[256,1536]{1,0:T(8,128)(2,1)S(1)}, u32[]{:S(2)}, u32[]{:S(2)}) collective-permute-start(bf16[256,1536]{1,0:T(8,128)(2,1)S(1)} %pad_maximum_fusion.2), channel_id=1, source_target_pairs={{0,1},{1,0},{2,3},{3,2},{4,5},{5,4},{6,7},{7,6},{8,9},{9,8},{10,11... | collective-permute-start | bytes 2359304 | tf_op jit(solution)/shard_map/ppermute | solution.py:499
  159.9 41.2 %collective-permute-start.30 = (bf16[3,192,560]{2,1,0:T(8,128)(2,1)S(1)}, bf16[3,192,560]{2,1,0:T(8,128)(2,1)S(1)}, u32[]{:S(2)}, u32[]{:S(2)}) collective-permute-start(bf16[3,192,560]{2,1,0:T(8,128)(2,1)S(1)} %constant_dynamic-update-slice_fusion.3.refs_2_), channel_id=1, source_target_pairs={{0,4},{4,0},{8,12},{12,8},{16,20},{20,16},{24,28},{28,24},{1,5},{5... | collective-permute-start | bytes 1935368 | tf_op jit(solution)/shard_map/ppermute | solution.py:490
  162.5 29.3 %collective-permute-start.34 = (bf16[128,1536]{1,0:T(8,128)(2,1)S(1)}, bf16[128,1536]{1,0:T(8,128)(2,1)S(1)}, u32[]{:S(2)}, u32[]{:S(2)}) collective-permute-start(bf16[128,1536]{1,0:T(8,128)(2,1)S(1)} %get-tuple-element.351), channel_id=1, source_target_pairs={{0,8},{4,12},{8,16},{12,20},{16,24},{20,28},{24,0},{28,4},{1,9},{5... | collective-permute-start | bytes 1179656 | tf_op jit(solution)/shard_map/ppermute | solution.py:487
  179.0 21.2 %collective-permute-start.43 = (bf16[128,1536]{1,0:T(8,128)(2,1)S(1)}, bf16[128,1536]{1,0:T(8,128)(2,1)S(1)}, u32[]{:S(2)}, u32[]{:S(2)}) collective-permute-start(bf16[128,1536]{1,0:T(8,128)(2,1)S(1)} %bitcast.271), channel_id=1, source_target_pairs={{0,8},{4,12},{8,16},{12,20},{16,24},{20,28},{24,0},{28,4},{1,9},{5... | collective-permute-start | bytes 1179656 | tf_op jit(solution)/shard_map/ppermute | solution.py:487
  179.1 21.9 %collective-permute-start.29 = (bf16[128,1536]{1,0:T(8,128)(2,1)S(1)}, bf16[128,1536]{1,0:T(8,128)(2,1)S(1)}, u32[]{:S(2)}, u32[]{:S(2)}) collective-permute-start(bf16[128,1536]{1,0:T(8,128)(2,1)S(1)} %get-tuple-element.351), channel_id=1, source_target_pairs={{0,2},{1,3},{2,0},{3,1},{4,6},{5,7},{6,4},{7,5},{8,10},{9,11},{10,... | collective-permute-start | bytes 1179656 | tf_op jit(solution)/shard_map/ppermute | solution.py:493
  191.8 18.8 %collective-permute-start.37 = (bf16[128,1536]{1,0:T(8,128)(2,1)S(1)}, bf16[128,1536]{1,0:T(8,128)(2,1)S(1)}, u32[]{:S(2)}, u32[]{:S(2)}) collective-permute-start(bf16[128,1536]{1,0:T(8,128)(2,1)S(1)} %collective-permute-done.34), channel_id=1, source_target_pairs={{0,8},{4,12},{8,16},{12,20},{16,24},{20,28},{24,0},{28,4},{1,9},{5... | collective-permute-start | bytes 1179656 | tf_op jit(solution)/shard_map/ppermute | solution.py:487
  191.8 18.0 %collective-permute-start.35 = (bf16[128,1536]{1,0:T(8,128)(2,1)S(1)}, bf16[128,1536]{1,0:T(8,128)(2,1)S(1)}, u32[]{:S(2)}, u32[]{:S(2)}) collective-permute-start(bf16[128,1536]{1,0:T(8,128)(2,1)S(1)} %collective-permute-done.34), channel_id=1, source_target_pairs={{0,2},{1,3},{2,0},{3,1},{4,6},{5,7},{6,4},{7,5},{8,10},{9,11},{10,... | collective-permute-start | bytes 1179656 | tf_op jit(solution)/shard_map/ppermute | solution.py:493
  200.2 15.5 %collective-permute-start.44 = (bf16[128,1536]{1,0:T(8,128)(2,1)S(1)}, bf16[128,1536]{1,0:T(8,128)(2,1)S(1)}, u32[]{:S(2)}, u32[]{:S(2)}) collective-permute-start(bf16[128,1536]{1,0:T(8,128)(2,1)S(1)} %collective-permute-done.43), channel_id=1, source_target_pairs={{0,8},{4,12},{8,16},{12,20},{16,24},{20,28},{24,0},{28,4},{1,9},{5... | collective-permute-start | bytes 1179656 | tf_op jit(solution)/shard_map/ppermute | solution.py:487
  201.1 35.2 %collective-permute-start.31 = (bf16[256,1536]{1,0:T(8,128)(2,1)S(1)}, bf16[256,1536]{1,0:T(8,128)(2,1)S(1)}, u32[]{:S(2)}, u32[]{:S(2)}) collective-permute-start(bf16[256,1536]{1,0:T(8,128)(2,1)S(1)} %pad_maximum_fusion.3), channel_id=1, source_target_pairs={{0,1},{1,0},{2,3},{3,2},{4,5},{5,4},{6,7},{7,6},{8,9},{9,8},{10,11... | collective-permute-start | bytes 2359304 | tf_op jit(solution)/shard_map/ppermute | solution.py:499
  209.9 37.1 %collective-permute-start.36 = (bf16[256,1536]{1,0:T(8,128)(2,1)S(1)}, bf16[256,1536]{1,0:T(8,128)(2,1)S(1)}, u32[]{:S(2)}, u32[]{:S(2)}) collective-permute-start(bf16[256,1536]{1,0:T(8,128)(2,1)S(1)} %pad_maximum_fusion.4), channel_id=1, source_target_pairs={{0,1},{1,0},{2,3},{3,2},{4,5},{5,4},{6,7},{7,6},{8,9},{9,8},{10,11... | collective-permute-start | bytes 2359304 | tf_op jit(solution)/shard_map/ppermute | solution.py:499
  210.5 39.1 %collective-permute-start.49 = (bf16[256,1536]{1,0:T(8,128)(2,1)S(1)}, bf16[256,1536]{1,0:T(8,128)(2,1)S(1)}, u32[]{:S(2)}, u32[]{:S(2)}) collective-permute-start(bf16[256,1536]{1,0:T(8,128)(2,1)S(1)} %pad_maximum_fusion.8), channel_id=1, source_target_pairs={{0,1},{1,0},{2,3},{3,2},{4,5},{5,4},{6,7},{7,6},{8,9},{9,8},{10,11... | collective-permute-start | bytes 2359304 | tf_op jit(solution)/shard_map/ppermute | solution.py:499
  210.6 16.8 %collective-permute-start.38 = (bf16[128,1536]{1,0:T(8,128)(2,1)S(1)}, bf16[128,1536]{1,0:T(8,128)(2,1)S(1)}, u32[]{:S(2)}, u32[]{:S(2)}) collective-permute-start(bf16[128,1536]{1,0:T(8,128)(2,1)S(1)} %collective-permute-done.37), channel_id=1, source_target_pairs={{0,2},{1,3},{2,0},{3,1},{4,6},{5,7},{6,4},{7,5},{8,10},{9,11},{10,... | collective-permute-start | bytes 1179656 | tf_op jit(solution)/shard_map/ppermute | solution.py:493
  227.4 18.6 %collective-permute-start.40 = (bf16[128,1536]{1,0:T(8,128)(2,1)S(1)}, bf16[128,1536]{1,0:T(8,128)(2,1)S(1)}, u32[]{:S(2)}, u32[]{:S(2)}) collective-permute-start(bf16[128,1536]{1,0:T(8,128)(2,1)S(1)} %collective-permute-done.37), channel_id=1, source_target_pairs={{0,8},{4,12},{8,16},{12,20},{16,24},{20,28},{24,0},{28,4},{1,9},{5... | collective-permute-start | bytes 1179656 | tf_op jit(solution)/shard_map/ppermute | solution.py:487
  236.2 30.2 %collective-permute-start.39 = (bf16[256,1536]{1,0:T(8,128)(2,1)S(1)}, bf16[256,1536]{1,0:T(8,128)(2,1)S(1)}, u32[]{:S(2)}, u32[]{:S(2)}) collective-permute-start(bf16[256,1536]{1,0:T(8,128)(2,1)S(1)} %pad_maximum_fusion.5), channel_id=1, source_target_pairs={{0,1},{1,0},{2,3},{3,2},{4,5},{5,4},{6,7},{7,6},{8,9},{9,8},{10,11... | collective-permute-start | bytes 2359304 | tf_op jit(solution)/shard_map/ppermute | solution.py:499
  236.3 31.8 %collective-permute-start.52 = (bf16[256,1536]{1,0:T(8,128)(2,1)S(1)}, bf16[256,1536]{1,0:T(8,128)(2,1)S(1)}, u32[]{:S(2)}, u32[]{:S(2)}) collective-permute-start(bf16[256,1536]{1,0:T(8,128)(2,1)S(1)} %pad_maximum_fusion.9), channel_id=1, source_target_pairs={{0,1},{1,0},{2,3},{3,2},{4,5},{5,4},{6,7},{7,6},{8,9},{9,8},{10,11... | collective-permute-start | bytes 2359304 | tf_op jit(solution)/shard_map/ppermute | solution.py:499
  246.0 19.6 %collective-permute-start.46 = (bf16[128,1536]{1,0:T(8,128)(2,1)S(1)}, bf16[128,1536]{1,0:T(8,128)(2,1)S(1)}, u32[]{:S(2)}, u32[]{:S(2)}) collective-permute-start(bf16[128,1536]{1,0:T(8,128)(2,1)S(1)} %collective-permute-done.45), channel_id=1, source_target_pairs={{0,2},{1,3},{2,0},{3,1},{4,6},{5,7},{6,4},{7,5},{8,10},{9,11},{10,... | collective-permute-start | bytes 1179656 | tf_op jit(solution)/shard_map/ppermute | solution.py:493
  246.9 18.6 %collective-permute-start.41 = (bf16[128,1536]{1,0:T(8,128)(2,1)S(1)}, bf16[128,1536]{1,0:T(8,128)(2,1)S(1)}, u32[]{:S(2)}, u32[]{:S(2)}) collective-permute-start(bf16[128,1536]{1,0:T(8,128)(2,1)S(1)} %collective-permute-done.40), channel_id=1, source_target_pairs={{0,2},{1,3},{2,0},{3,1},{4,6},{5,7},{6,4},{7,5},{8,10},{9,11},{10,... | collective-permute-start | bytes 1179656 | tf_op jit(solution)/shard_map/ppermute | solution.py:493
  249.6 27.9 %collective-permute-start.32 = (bf16[2,128,1536]{2,1,0:T(8,128)(2,1)S(1)}, bf16[2,128,1536]{2,1,0:T(8,128)(2,1)S(1)}, u32[]{:S(2)}, u32[]{:S(2)}) collective-permute-start(bf16[2,128,1536]{2,1,0:T(8,128)(2,1)S(1)} %bitcast.282), channel_id=1, source_target_pairs={{0,1},{1,0},{2,3},{3,2},{4,5},{5,4},{6,7},{7,6},{8,9},{9,8},{10,11... | collective-permute-start | bytes 2359304 | tf_op jit(solution)/shard_map/ppermute | solution.py:499
  265.5 25.0 %collective-permute-start.50 = (bf16[2,128,1536]{2,1,0:T(8,128)(2,1)S(1)}, bf16[2,128,1536]{2,1,0:T(8,128)(2,1)S(1)}, u32[]{:S(2)}, u32[]{:S(2)}) collective-permute-start(bf16[2,128,1536]{2,1,0:T(8,128)(2,1)S(1)} %bitcast.283), channel_id=1, source_target_pairs={{0,1},{1,0},{2,3},{3,2},{4,5},{5,4},{6,7},{7,6},{8,9},{9,8},{10,11... | collective-permute-start | bytes 2359304 | tf_op jit(solution)/shard_map/ppermute | solution.py:499
  265.6 13.9 %collective-permute-start.42 = (bf16[256,1536]{1,0:T(8,128)(2,1)S(1)}, bf16[256,1536]{1,0:T(8,128)(2,1)S(1)}, u32[]{:S(2)}, u32[]{:S(2)}) collective-permute-start(bf16[256,1536]{1,0:T(8,128)(2,1)S(1)} %pad_maximum_fusion.6), channel_id=1, source_target_pairs={{0,1},{1,0},{2,3},{3,2},{4,5},{5,4},{6,7},{7,6},{8,9},{9,8},{10,11... | collective-permute-start | bytes 2359304 | tf_op jit(solution)/shard_map/ppermute | solution.py:499
  266.4 14.6 %collective-permute-start.47 = (bf16[256,1536]{1,0:T(8,128)(2,1)S(1)}, bf16[256,1536]{1,0:T(8,128)(2,1)S(1)}, u32[]{:S(2)}, u32[]{:S(2)}) collective-permute-start(bf16[256,1536]{1,0:T(8,128)(2,1)S(1)} %pad_maximum_fusion.7), channel_id=1, source_target_pairs={{0,1},{1,0},{2,3},{3,2},{4,5},{5,4},{6,7},{7,6},{8,9},{9,8},{10,11... | collective-permute-start | bytes 2359304 | tf_op jit(solution)/shard_map/ppermute | solution.py:499
  276.9 17.4 %collective-permute-start.53 = (bf16[2,128,1536]{2,1,0:T(8,128)(2,1)S(1)}, bf16[2,128,1536]{2,1,0:T(8,128)(2,1)S(1)}, u32[]{:S(2)}, u32[]{:S(2)}) collective-permute-start(bf16[2,128,1536]{2,1,0:T(8,128)(2,1)S(1)} %bitcast.284), channel_id=1, source_target_pairs={{0,1},{1,0},{2,3},{3,2},{4,5},{5,4},{6,7},{7,6},{8,9},{9,8},{10,11... | collective-permute-start | bytes 2359304 | tf_op jit(solution)/shard_map/ppermute | solution.py:499
  278.5 14.7 %collective-permute-start.33 = (bf16[128,1536]{1,0:T(8,128)(2,1)S(1)}, bf16[128,1536]{1,0:T(8,128)(2,1)S(1)}, u32[]{:S(2)}, u32[]{:S(2)}) collective-permute-start(bf16[128,1536]{1,0:T(8,128)(2,1)S(1)} %fusion.45), channel_id=1, source_target_pairs={{0,2},{1,3},{2,0},{3,1},{4,6},{5,7},{6,4},{7,5},{8,10},{9,11},{10,... | collective-permute-start | bytes 1179656 | tf_op jit(solution)/shard_map/ppermute | solution.py:493
  293.3 19.7 %collective-permute-start.57 = (bf16[2,128,1536]{2,1,0:T(8,128)(2,1)S(1)}, bf16[2,128,1536]{2,1,0:T(8,128)(2,1)S(1)}, u32[]{:S(2)}, u32[]{:S(2)}) collective-permute-start(bf16[2,128,1536]{2,1,0:T(8,128)(2,1)S(1)} %bitcast.285), channel_id=1, source_target_pairs={{0,1},{1,0},{2,3},{3,2},{4,5},{5,4},{6,7},{7,6},{8,9},{9,8},{10,11... | collective-permute-start | bytes 2359304 | tf_op jit(solution)/shard_map/ppermute | solution.py:499
  294.6 17.2 %collective-permute-start.55 = (bf16[128,1536]{1,0:T(8,128)(2,1)S(1)}, bf16[128,1536]{1,0:T(8,128)(2,1)S(1)}, u32[]{:S(2)}, u32[]{:S(2)}) collective-permute-start(bf16[128,1536]{1,0:T(8,128)(2,1)S(1)} %fusion.47), channel_id=1, source_target_pairs={{0,2},{1,3},{2,0},{3,1},{4,6},{5,7},{6,4},{7,5},{8,10},{9,11},{10,... | collective-permute-start | bytes 1179656 | tf_op jit(solution)/shard_map/ppermute | solution.py:493
  304.9 24.2 %collective-permute-start.59 = (bf16[128,1536]{1,0:T(8,128)(2,1)}, bf16[128,1536]{1,0:T(8,128)(2,1)S(1)}, u32[]{:S(2)}, u32[]{:S(2)}) collective-permute-start(bf16[128,1536]{1,0:T(8,128)(2,1)} %fusion.36), channel_id=1, source_target_pairs={{0,24},{4,28},{8,0},{12,4},{16,8},{20,12},{24,16},{28,20},{1,25},{... | collective-permute-start | bytes 1179656 | tf_op jit(solution)/shard_map/ppermute | solution.py:487
  312.6 29.1 %collective-permute-start.60 = (bf16[128,1536]{1,0:T(8,128)(2,1)}, bf16[128,1536]{1,0:T(8,128)(2,1)}, u32[]{:S(2)}, u32[]{:S(2)}) collective-permute-start(bf16[128,1536]{1,0:T(8,128)(2,1)} %fusion.35), channel_id=1, source_target_pairs={{0,16},{4,20},{8,24},{12,28},{16,0},{20,4},{24,8},{28,12},{1,17},{... | collective-permute-start | bytes 1179656 | tf_op jit(solution)/shard_map/ppermute | solution.py:487
  325.8 22.8 %collective-permute-start.56 = (bf16[4,1,192,560]{3,2,1,0:T(8,128)(2,1)}, bf16[4,1,192,560]{3,2,1,0:T(8,128)(2,1)}, u32[]{:S(2)}, u32[]{:S(2)}) collective-permute-start(bf16[4,1,192,560]{3,2,1,0:T(8,128)(2,1)} %get-tuple-element.245), channel_id=1, source_target_pairs={{0,4},{4,0},{8,12},{12,8},{16,20},{20,16},{24,28},{28,24},{1,5},{5... | collective-permute-start | bytes 2580488 | tf_op jit(solution)/shard_map/ppermute | solution.py:490
  328.0 13.7 %collective-permute-start.61 = (bf16[128,1536]{1,0:T(8,128)(2,1)}, bf16[128,1536]{1,0:T(8,128)(2,1)}, u32[]{:S(2)}, u32[]{:S(2)}) collective-permute-start(bf16[128,1536]{1,0:T(8,128)(2,1)} %fusion.34), channel_id=1, source_target_pairs={{0,8},{4,12},{8,16},{12,20},{16,24},{20,28},{24,0},{28,4},{1,9},{5... | collective-permute-start | bytes 1179656 | tf_op jit(solution)/shard_map/ppermute | solution.py:487
  352.7 20.6 %collective-permute-start.62 = (bf16[128,1536]{1,0:T(8,128)(2,1)S(1)}, bf16[128,1536]{1,0:T(8,128)(2,1)}, u32[]{:S(2)}, u32[]{:S(2)}) collective-permute-start(bf16[128,1536]{1,0:T(8,128)(2,1)S(1)} %get-tuple-element.282.own), channel_id=1, source_target_pairs={{0,2},{1,3},{2,0},{3,1},{4,6},{5,7},{6,4},{7,5},{8,10},{9,11},{10,... | collective-permute-start | bytes 1179656 | tf_op jit(solution)/shard_map/ppermute | solution.py:493
  353.7 21.6 %collective-permute-start.63 = (bf16[4,1,192,560]{3,2,1,0:T(8,128)(2,1)}, bf16[4,1,192,560]{3,2,1,0:T(8,128)(2,1)}, u32[]{:S(2)}, u32[]{:S(2)}) collective-permute-start(bf16[4,1,192,560]{3,2,1,0:T(8,128)(2,1)} %get-tuple-element.263), channel_id=1, source_target_pairs={{0,4},{4,0},{8,12},{12,8},{16,20},{20,16},{24,28},{28,24},{1,5},{5... | collective-permute-start | bytes 2580488 | tf_op jit(solution)/shard_map/ppermute | solution.py:490
  356.4 27.0 %all-to-all-start.2 = ((bf16[4,1,192,560]{3,2,1,0:T(8,128)(2,1)}), bf16[4,1,192,560]{3,2,1,0:T(8,128)(2,1)}, u32[]{:S(2)}, u32[]{:S(2)}) async-start(bf16[4,1,192,560]{3,2,1,0:T(8,128)(2,1)} %add_convert_fusion.2), calls=%async_computation.2 | async-start | bytes 1966080 | tf_op jit(solution)/shard_map/all_to_all | solution.py:550
  385.8 28.6 %all-to-all-start.3 = ((bf16[4,1,192,560]{3,2,1,0:T(8,128)(2,1)}), bf16[4,1,192,560]{3,2,1,0:T(8,128)(2,1)S(1)}, u32[]{:S(2)}, u32[]{:S(2)}) async-start(bf16[4,1,192,560]{3,2,1,0:T(8,128)(2,1)} %add_convert_fusion.1), calls=%async_computation.3 | async-start | bytes 1966080 | tf_op jit(solution)/shard_map/all_to_all | solution.py:550
  389.8 139.2 %reduce-scatter.3.cloned.1.call-start = ((), (), s32[]{:S(2)}) async-start(), calls=%async_computation.8 | async-start | bytes 7864320 | tf_op jit(solution)/shard_map/reduce_scatter | solution.py:920
  403.6 29.9 %collective-permute-start.70 = (bf16[4,1,192,560]{3,2,1,0:T(8,128)(2,1)}, bf16[4,1,192,560]{3,2,1,0:T(8,128)(2,1)}, u32[]{:S(2)}, u32[]{:S(2)}) collective-permute-start(bf16[4,1,192,560]{3,2,1,0:T(8,128)(2,1)} %get-tuple-element.290), channel_id=1, source_target_pairs={{0,4},{4,0},{8,12},{12,8},{16,20},{20,16},{24,28},{28,24},{1,5},{5... | collective-permute-start | bytes 2580488 | tf_op jit(solution)/shard_map/ppermute | solution.py:490
  416.7 22.1 %collective-permute-start.69 = (bf16[4,4,2,64,128]{4,3,2,1,0:T(8,128)(2,1)}, bf16[4,4,2,64,128]{4,3,2,1,0:T(8,128)(2,1)}, u32[]{:S(2)}, u32[]{:S(2)}) collective-permute-start(bf16[4,4,2,64,128]{4,3,2,1,0:T(8,128)(2,1)} %add_convert_fusion.5), channel_id=1, source_target_pairs={{0,4},{4,0},{8,12},{12,8},{16,20},{20,16},{24,28},{28,24},{1,5},{5... | collective-permute-start | bytes 1572872 | tf_op jit(solution)/shard_map/ppermute | solution.py:490
  438.9 20.3 %collective-permute-start.74 = (bf16[2,2,48,1536]{3,2,1,0:T(8,128)(2,1)}, bf16[2,2,48,1536]{3,2,1,0:T(8,128)(2,1)}, u32[]{:S(2)}, u32[]{:S(2)}) collective-permute-start(bf16[2,2,48,1536]{3,2,1,0:T(8,128)(2,1)} %copy-done.57), channel_id=1, source_target_pairs={{0,2},{1,3},{2,0},{3,1},{4,6},{5,7},{6,4},{7,5},{8,10},{9,11},{10,... | collective-permute-start | bytes 1769480 | tf_op jit(solution)/shard_map/ppermute | solution.py:493
  440.1 19.1 %collective-permute-start.75 = (bf16[4,1,4,48,384]{4,3,2,1,0:T(8,128)(2,1)}, bf16[4,1,4,48,384]{4,3,2,1,0:T(8,128)(2,1)}, u32[]{:S(2)}, u32[]{:S(2)}) collective-permute-start(bf16[4,1,4,48,384]{4,3,2,1,0:T(8,128)(2,1)} %copy-done.56), channel_id=1, source_target_pairs={{0,4},{4,0},{8,12},{12,8},{16,20},{20,16},{24,28},{28,24},{1,5},{5... | collective-permute-start | bytes 1769480 | tf_op jit(solution)/shard_map/ppermute | solution.py:490
  467.2 27.8 %all-to-all-start.4 = ((bf16[4,1,4,48,384]{4,3,2,1,0:T(8,128)(2,1)}), bf16[4,1,4,48,384]{4,3,2,1,0:T(8,128)(2,1)S(1)}, u32[]{:S(2)}, u32[]{:S(2)}) async-start(bf16[4,1,4,48,384]{4,3,2,1,0:T(8,128)(2,1)} %add_convert_fusion.3), calls=%async_computation.6 | async-start | bytes 1179648 | tf_op jit(solution)/shard_map/all_to_all | solution.py:550
  480.6 15.0 %collective-permute-start.83 = (bf16[4,1,48,1536]{3,2,1,0:T(8,128)(2,1)}, bf16[4,1,48,1536]{3,2,1,0:T(8,128)(2,1)}, u32[]{:S(2)}, u32[]{:S(2)}) collective-permute-start(bf16[4,1,48,1536]{3,2,1,0:T(8,128)(2,1)} %get-tuple-element.318), channel_id=1, source_target_pairs={{0,4},{4,0},{8,12},{12,8},{16,20},{20,16},{24,28},{28,24},{1,5},{5... | collective-permute-start | bytes 1769480 | tf_op jit(solution)/shard_map/ppermute | solution.py:490
  501.0 28.0 %collective-permute-start.86 = (bf16[2,128,1536]{2,1,0:T(8,128)(2,1)}, bf16[2,128,1536]{2,1,0:T(8,128)(2,1)}, u32[]{:S(2)}, u32[]{:S(2)}) collective-permute-start(bf16[2,128,1536]{2,1,0:T(8,128)(2,1)} %get-tuple-element.327), channel_id=1, source_target_pairs={{0,1},{1,0},{2,3},{3,2},{4,5},{5,4},{6,7},{7,6},{8,9},{9,8},{10,11... | collective-permute-start | bytes 2359304 | tf_op jit(solution)/shard_map/ppermute | solution.py:499
  503.4 41.6 %all-to-all-start.5 = ((bf16[4,1,192,560]{3,2,1,0:T(8,128)(2,1)}), bf16[4,1,192,560]{3,2,1,0:T(8,128)(2,1)S(1)}, u32[]{:S(2)}, u32[]{:S(2)}) async-start(bf16[4,1,192,560]{3,2,1,0:T(8,128)(2,1)} %add_convert_fusion), calls=%async_computation.7 | async-start | bytes 1966080 | tf_op jit(solution)/shard_map/all_to_all | solution.py:550
  508.0 62.9 %reduce-scatter.5.cloned.1.call-start = ((), (), s32[]{:S(2)}) async-start(), calls=%async_computation.9 | async-start | bytes 1966080 | tf_op jit(solution)/shard_map/reduce_scatter | solution.py:950
  521.3 34.1 %collective-permute-start.90 = (bf16[1,48,1536]{2,1,0:T(8,128)(2,1)}, bf16[1,48,1536]{2,1,0:T(8,128)(2,1)}, u32[]{:S(2)}, u32[]{:S(2)}) collective-permute-start(bf16[1,48,1536]{2,1,0:T(8,128)(2,1)} %get-tuple-element.335), channel_id=1, source_target_pairs={{0,24},{4,28},{8,0},{12,4},{16,8},{20,12},{24,16},{28,20},{1,25},{... | collective-permute-start | bytes 442376 | tf_op jit(solution)/shard_map/ppermute | solution.py:487
  525.1 40.2 %collective-permute-start.89 = (bf16[1,48,1536]{2,1,0:T(8,128)(2,1)}, bf16[1,48,1536]{2,1,0:T(8,128)(2,1)}, u32[]{:S(2)}, u32[]{:S(2)}) collective-permute-start(bf16[1,48,1536]{2,1,0:T(8,128)(2,1)} %get-tuple-element.334), channel_id=1, source_target_pairs={{0,16},{4,20},{8,24},{12,28},{16,0},{20,4},{24,8},{28,12},{1,17},{... | collective-permute-start | bytes 442376 | tf_op jit(solution)/shard_map/ppermute | solution.py:487
  525.1 40.2 %collective-permute-start.88 = (bf16[1,48,1536]{2,1,0:T(8,128)(2,1)}, bf16[1,48,1536]{2,1,0:T(8,128)(2,1)}, u32[]{:S(2)}, u32[]{:S(2)}) collective-permute-start(bf16[1,48,1536]{2,1,0:T(8,128)(2,1)} %get-tuple-element.333), channel_id=1, source_target_pairs={{0,8},{4,12},{8,16},{12,20},{16,24},{20,28},{24,0},{28,4},{1,9},{5... | collective-permute-start | bytes 442376 | tf_op jit(solution)/shard_map/ppermute | solution.py:487
  553.3 14.4 %collective-permute-start.87 = (bf16[128,1536]{1,0:T(8,128)(2,1)S(1)}, bf16[128,1536]{1,0:T(8,128)(2,1)S(1)}, u32[]{:S(2)}, u32[]{:S(2)}) collective-permute-start(bf16[128,1536]{1,0:T(8,128)(2,1)S(1)} %fusion.49), channel_id=1, source_target_pairs={{0,2},{1,3},{2,0},{3,1},{4,6},{5,7},{6,4},{7,5},{8,10},{9,11},{10,... | collective-permute-start | bytes 1179656 | tf_op jit(solution)/shard_map/ppermute | solution.py:493
  553.4 13.7 %collective-permute-start.92 = (f32[48]{0:T(128)S(1)}, f32[48]{0:T(128)S(1)}, u32[]{:S(2)}, u32[]{:S(2)}) collective-permute-start(f32[48]{0:T(128)S(1)} %fusion.68), channel_id=1, source_target_pairs={{0,2},{1,3},{2,0},{3,1},{4,6},{5,7},{6,4},{7,5},{8,10},{9,11},{10,... | collective-permute-start | bytes 584 | tf_op jit(solution)/shard_map/ppermute | solution.py:493
  (160 other events, 1208.3 us)
Sparse Core Ops, SparseCore 0:
  439.0 60.9 reduce-scatter.2
  529.1 41.4 reduce-scatter.4

commit v4 on v3

--- a/solution.py
+++ b/solution.py
@@ -325,15 +325,42 @@
     out[...] = total.astype(BF16)
 
 
+def pack_of(rows):
+    return 2 if rows % 32 == 0 else 1
+
+
+def packed(rows, units):
+    pack = pack_of(rows)
+    return (rows // pack, units * pack)
+
+
+def put_packed(target, index, part):
+    rows, units = part.shape
+    size = rows // pack_of(rows)
+    for j in range(pack_of(rows)):
+        target[(*index, slice(None), slice(j * units, (j + 1) * units))] = part[
+            j * size : (j + 1) * size
+        ]
+
+
+def get_packed(source, index, rows):
+    pack = pack_of(rows)
+    units = source.shape[-1] // pack
+    return jnp.concatenate(
+        [source[(*index, slice(None), slice(j * units, (j + 1) * units))] for j in range(pack)],
+        axis=0,
+    )
+
+
 def split_tiles_kernel(depth, place, gate, upper, down, gain, *rest):
     pieces, parts = rest[:depth], rest[depth]
-    units = parts.shape[3]
+    units = gate.shape[1] // depth
     for i, (tile, scaled) in enumerate(((gate, True), (upper, True), (down, False))):
         for k in range(depth):
             part = tile[:, k * units : (k + 1) * units]
             if scaled:
                 part = (part.astype(F32) * gain[...]).astype(BF16)
-            parts[k, i] = part
+            put_packed(parts, (k, i), part)
     for d in range(depth):
         pieces[d][...] = parts[lax.rem(place[AT_Z] + d, depth)]
 
@@ -343,8 +370,9 @@
     for d in range(depth):
         from_z = lax.rem(place[AT_Z] - d + depth, depth)
         for i, out in enumerate(outs):
-            out[from_z * PAIR + place[AT_X]] = mine[d][i]
-            out[from_z * PAIR + 1 - place[AT_X]] = far[d][i]
+            rows = out.shape[1]
+            out[from_z * PAIR + place[AT_X]] = get_packed(mine[d], (i,), rows)
+            out[from_z * PAIR + 1 - place[AT_X]] = get_packed(far[d], (i,), rows)
 
 
 def down_kernel(depth, place, *refs):
@@ -375,6 +403,12 @@
     out[:, place[AT_U] ^ 2] = near[0]
     out[:, place[AT_U] ^ 1] = across[0]
     out[:, place[AT_U] ^ 3] = across[1]
+
+
+def choose_tile_kernel(place, share, keep, send):
+    for z in range(share.shape[0]):
+        put_packed(keep, (z, 0), share[z, place[AT_X]])
+        put_packed(send, (z, 0), share[z, 1 - place[AT_X]])
 
 
 def choose_kernel(place, *refs):
@@ -440,17 +474,17 @@
 
 
 def finish_kernel(depth, gates, uppers, downs, gate, upper, gain, grad_gate, grad_upper, grad_down, grad_gain):
-    units = downs.shape[3]
+    rows, units = gate.shape[0], gate.shape[1] // depth
     total = jnp.zeros(grad_gain.shape, F32)
     for k in range(depth):
         at = slice(k * units, (k + 1) * units)
-        part = gates[k, 0].astype(F32)
+        part = get_packed(gates, (k, 0), rows).astype(F32)
         grad_gate[:, at] = part * gain[...]
         total = total + jnp.sum(part * gate[:, at].astype(F32), axis=1, keepdims=True)
-        part = uppers[k, 0].astype(F32)
+        part = get_packed(uppers, (k, 0), rows).astype(F32)
         grad_upper[:, at] = part * gain[...]
         total = total + jnp.sum(part * upper[:, at].astype(F32), axis=1, keepdims=True)
-        grad_down[:, at] = downs[k, 0].astype(F32)
+        grad_down[:, at] = get_packed(downs, (k, 0), rows).astype(F32)
     grad_gain[...] = total
 
 
@@ -640,8 +674,8 @@
         functools.partial(split_tiles_kernel, depth),
         [place],
         [*split_in, gain_two],
-        [like((3, block_model, hidden_units))] * depth,
-        scratch=[pltpu.VMEM((depth, 3, block_model, hidden_units), BF16)],
+        [like((3, *packed(block_model, hidden_units)))] * depth,
+        scratch=[pltpu.VMEM((depth, 3, *packed(block_model, hidden_units)), BF16)],
     )
     qkv_far = [first_far] + [grid.swap_x(piece) for piece in qkv_mine[1:]]
     unit_across = grid.swap_core(jnp.stack([unit_own, unit_near]))
@@ -824,19 +858,23 @@
         half = like((depth, len(shares), *rows, shape[-1]))
         return call(choose_kernel, [place], shares, [half] * 2)
 
+    def halve_tile(share):
+        share = share.astype(BF16).reshape(depth, PAIR, block_model, hidden_units)
+        half = like((depth, 1, *packed(block_model, hidden_units)))
+        return call(choose_tile_kernel, [place], [share], [half] * 2)
+
     def fold(keep, got):
         return exchange_z_all(grid, (keep.astype(F32) + got.astype(F32)).astype(BF16))
 
     z_groups = [[z * PAIR + x for z in range(depth)] for x in range(PAIR)]
-    tile_rows = (block_model,)
     boths = [over_core(chunk) for chunk in back_chunks]
     mid_parts = [over_y(both) for both in boths]
     back_pieces = [grid.to_z(mid_parts[d].astype(BF16), -d) for d in range(1, depth)]
     mid_all = jnp.concatenate(mid_chunks)
     mid_now = after(mid_all, back_chunks[-1], *boths[:-1], *mid_parts[:-1])
-    gate_keep, gate_send = halve([contract_rows(mid_now, jnp.concatenate(gate_grads))], tile_rows)
+    gate_keep, gate_send = halve_tile(contract_rows(mid_now, jnp.concatenate(gate_grads)))
     mid_now = after(mid_all, gate_send, *mid_parts, back_pieces[0])
-    upper_keep, upper_send = halve([contract_rows(mid_now, jnp.concatenate(upper_grads))], tile_rows)
+    upper_keep, upper_send = halve_tile(contract_rows(mid_now, jnp.concatenate(upper_grads)))
     gate_got = grid.swap_x(gate_send)
     first, gate_got, upper_send, *back_pieces = together(
         mid_parts[0], gate_got, upper_send, *back_pieces
@@ -850,7 +888,7 @@
     gate_owned = fold(*after((gate_keep, gate_got), branch_own))
     held = after((*cot_chunks, *actives), branch_own)
     cot_all, active_all = [jnp.concatenate(part) for part in (held[:depth], held[depth:])]
-    down_keep, down_send = halve([contract_rows(cot_all, active_all)], tile_rows)
+    down_keep, down_send = halve_tile(contract_rows(cot_all, active_all))
     down_send, branch_near, upper_got = together(down_send, branch_near, upper_got)
     down_got = grid.swap_x(down_send)
     branch_across = grid.swap_core(jnp.stack([branch_own, branch_near]))

time: 589 us -> 575 us (0.976)
  starting transfers between devices: 126 us -> 118 us
    ppermute x28, starting transfers between devices: 55 us -> 42.7 us  [to_z(): return lax.ppermute(value, 'blk', pairs)]
    ppermute x28, waiting for transfers between devices: 97.8 us -> 106 us  [to_z(): return lax.ppermute(value, 'blk', pairs)]
    all_to_all x5, waiting for transfers between devices: 27.6 us -> 20 us  [exchange_z_all(): lax.all_to_all(parts, 'blk', split_axis=0, concat_axis=0, axis_index_grou...]
    unnamed x256 -> x258, local copies, waits for them, and re-layouts: 29.1 us -> 27.9 us
  transfers between devices with their start and end apart: 101 -> 101, of which waited for: 41 -> 36; matrix products, arithmetic and copies ran while one was open for 21% -> 22% of each run, Pallas kernels for 12% -> 13%
where the time goes in v4:
time: 575 us; the launch traced here: 568 us
  waiting for transfers between devices  194 us (34%)
  starting transfers between devices  118 us (21%)
  Pallas kernels  77.1 us (13%)
  matrix products  59.1 us (10%)
  other arithmetic  53.4 us (9%)
  local copies, waits for them, and re-layouts  50.6 us (9%)
  between operations  16.5 us (3%)
    ppermute x28, waiting for transfers between devices, to_z(): return lax.ppermute(value, 'blk', pairs)  106 us
    pallas_call x23, Pallas kernels, call(): pl.pallas_call(kernel, grid_spec=pltpu.PrefetchScalarGridSpec(num_scalar_...  55.8 us
    ppermute x28, starting transfers between devices, to_z(): return lax.ppermute(value, 'blk', pairs)  42.7 us
    ppermute x21, waiting for transfers between devices, swap_y(): return lax.ppermute(value, 'uly', [(i, i ^ 2) for i in range(self.ulys)])  34.2 us
    ppermute x17, waiting for transfers between devices, swap_x(): return lax.ppermute(value, 'blk', [(i, i ^ 1) for i in range(self.blocks)])  30.8 us
    unnamed x258, local copies, waits for them, and re-layouts  27.9 us
    dot_general x12, matrix products, matmul(): return jnp.dot(left, right, preferred_element_type=F32)  25.5 us
    all_to_all x5, starting transfers between devices, exchange_z_all(): lax.all_to_all(parts, 'blk', split_axis=0, concat_axis=0, axis_index_grou...  24.8 us
  transfers between devices with their start and end apart: 101, of which 36 were waited for; matrix products, arithmetic and copies ran while one was open for 22% of the time, Pallas kernels for 13%

profile of v4, /device:TPU:0, one launch (start us, length us, event | category | flops | bytes accessed | tf_op | source)
XLA Modules:
  0.0 568.0 jit_solution(7009085643954303988)
XLA Ops:
  11.2 4.2 all-to-all-start
  18.8 2.8 collective-permute-start.4
  28.5 2.6 collective-permute-start.1
  34.1 3.0 collective-permute-done.rest_1_
  37.0 8.3 %collective-permute-done.1.rest_2_ = bf16[208,512]{1,0:T(8,128)(2,1)} collective-permute-done((bf16[208,512]{1,0:T(8,128)(2,1)}, bf16[208,512]{1,0:T(8,128)(2,1)}, u32[]{:S(2)}, u32[]{:S(2)}) %collective-permute-start.1) | collective-permute-done | bytes 213024 | tf_op jit(solution)/shard_map/ppermute | solution.py:521
  45.4 3.2 shard_map.186
  51.3 7.3 %all-to-all-start.1 = ((bf16[4,48,1536]{2,1,0:T(8,128)(2,1)}), bf16[4,48,1536]{2,1,0:T(8,128)(2,1)S(1)}, u32[]{:S(2)}, u32[]{:S(2)}) async-start(bf16[4,48,1536]{2,1,0:T(8,128)(2,1)} %broadcast_in_dim.58), calls=%async_computation.1 | async-start | bytes 1179648 | tf_op jit(solution)/shard_map/all_to_all | solution.py:584
  71.8 4.6 collective-permute-done.7.rest_7_
  76.4 4.6 shard_map.187
  82.2 5.7 all-to-all-done.1.mine
  90.1 8.2 %collective-permute-done.13 = bf16[4,128,128]{2,1,0:T(8,128)(2,1)S(1)} collective-permute-done((bf16[4,128,128]{2,1,0:T(8,128)(2,1)S(1)}, bf16[4,128,128]{2,1,0:T(8,128)(2,1)S(1)}, u32[]{:S(2)}, u32[]{:S(2)}) %collective-permute-start.13) | collective-permute-done | bytes 131104 | tf_op jit(solution)/shard_map/ppermute | solution.py:521
  98.4 11.7 %collective-permute-start.19 = (bf16[3,96,1120]{2,1,0:T(8,128)(2,1)}, bf16[3,96,1120]{2,1,0:T(8,128)(2,1)S(1)}, u32[]{:S(2)}, u32[]{:S(2)}) collective-permute-start(bf16[3,96,1120]{2,1,0:T(8,128)(2,1)} %copy-done.53), channel_id=1, source_target_pairs={{0,24},{4,28},{8,0},{12,4},{16,8},{20,12},{24,16},{28,20},{1,25},{... | collective-permute-start | bytes 1935368 | tf_op jit(solution)/shard_map/ppermute | solution.py:521
  112.9 5.7 %collective-permute-done.19.refs_3_ = bf16[3,96,1120]{2,1,0:T(8,128)(2,1)S(1)} collective-permute-done((bf16[3,96,1120]{2,1,0:T(8,128)(2,1)}, bf16[3,96,1120]{2,1,0:T(8,128)(2,1)S(1)}, u32[]{:S(2)}, u32[]{:S(2)}) %collective-permute-start.19) | collective-permute-done | bytes 645152 | tf_op jit(solution)/shard_map/ppermute | solution.py:521
  118.6 6.7 %collective-permute-done.16 = bf16[4,4,128,128]{3,2,1,0:T(8,128)(2,1)S(1)} collective-permute-done((bf16[4,4,128,128]{3,2,1,0:T(8,128)(2,1)S(1)}, bf16[4,4,128,128]{3,2,1,0:T(8,128)(2,1)S(1)}, u32[]{:S(2)}, u32[]{:S(2)}) %collective-permute-start.16) | collective-permute-done | bytes 524320 | tf_op jit(solution)/shard_map/ppermute | solution.py:524
  126.0 3.1 collective-permute-start.21
  129.1 9.2 %shard_map.189 = (bf16[4,2,64,384]{3,2,1,0:T(8,128)(2,1)S(1)}, f32[2,2,1,384]{3,2,1,0:T(1,128)S(1)}, bf16[2,2,2048,128]{3,2,1,0:T(8,128)(2,1)S(1)}) custom-call(s32[2,16]{1,0:T(2,128)S(1)} %copy-done.52, s32[6]{0:T(128)S(1)} %stack.95.place, bf16[4,2,64,384]{3,2,1,0:T(8,128)(2,1)S(1)} %bitcast.236, bf16[4,4,2,64,128]{4,3,2,1,0:T(8,128)(2,1)S(1)} %pad_maximum_fusion.16.a_own, ...), custom_call_target="tpu_custom_call" | custom-call | flops 1 | bytes 1 | tf_op jit(solution)/shard_map/pallas_call | solution.py:766
  139.7 8.8 %collective-permute-done.21 = bf16[2,96,1120]{2,1,0:T(8,128)(2,1)S(1)} collective-permute-done((bf16[2,96,1120]{2,1,0:T(8,128)(2,1)S(1)}, bf16[2,96,1120]{2,1,0:T(8,128)(2,1)S(1)}, u32[]{:S(2)}, u32[]{:S(2)}) %collective-permute-start.21) | collective-permute-done | bytes 430112 | tf_op jit(solution)/shard_map/ppermute | solution.py:521
  154.0 13.3 %collective-permute-done.26 = bf16[1,96,1120]{2,1,0:T(8,128)(2,1)S(1)} collective-permute-done((bf16[1,96,1120]{2,1,0:T(8,128)(2,1)S(1)}, bf16[1,96,1120]{2,1,0:T(8,128)(2,1)S(1)}, u32[]{:S(2)}, u32[]{:S(2)}) %collective-permute-start.26) | collective-permute-done | bytes 215072 | tf_op jit(solution)/shard_map/ppermute | solution.py:521
  171.6 13.2 %collective-permute-done.34 = bf16[128,1536]{1,0:T(8,128)(2,1)S(1)} collective-permute-done((bf16[128,1536]{1,0:T(8,128)(2,1)S(1)}, bf16[128,1536]{1,0:T(8,128)(2,1)S(1)}, u32[]{:S(2)}, u32[]{:S(2)}) %collective-permute-start.34) | collective-permute-done | bytes 393248 | tf_op jit(solution)/shard_map/ppermute | solution.py:521
  185.1 8.1 %collective-permute-done.43 = bf16[128,1536]{1,0:T(8,128)(2,1)S(1)} collective-permute-done((bf16[128,1536]{1,0:T(8,128)(2,1)S(1)}, bf16[128,1536]{1,0:T(8,128)(2,1)S(1)}, u32[]{:S(2)}, u32[]{:S(2)}) %collective-permute-start.43) | collective-permute-done | bytes 393248 | tf_op jit(solution)/shard_map/ppermute | solution.py:521
  193.8 5.4 shard_map.192
  199.2 2.9 fusion.80
  205.4 3.0 collective-permute-done.44
  209.6 10.1 %collective-permute-done.45 = bf16[128,1536]{1,0:T(8,128)(2,1)S(1)} collective-permute-done((bf16[128,1536]{1,0:T(8,128)(2,1)S(1)}, bf16[128,1536]{1,0:T(8,128)(2,1)S(1)}, u32[]{:S(2)}, u32[]{:S(2)}) %collective-permute-start.45) | collective-permute-done | bytes 393248 | tf_op jit(solution)/shard_map/ppermute | solution.py:521
  220.7 7.5 %collective-permute-done.51 = bf16[128,1536]{1,0:T(8,128)(2,1)S(1)} collective-permute-done((bf16[128,1536]{1,0:T(8,128)(2,1)S(1)}, bf16[128,1536]{1,0:T(8,128)(2,1)S(1)}, u32[]{:S(2)}, u32[]{:S(2)}) %collective-permute-start.51) | collective-permute-done | bytes 393248 | tf_op jit(solution)/shard_map/ppermute | solution.py:527
  228.9 2.7 fusion.42
  231.6 3.8 multiply_convert_fusion.3
  247.1 2.6 multiply_convert_fusion.2
  254.4 6.6 %collective-permute-done.41 = bf16[128,1536]{1,0:T(8,128)(2,1)S(1)} collective-permute-done((bf16[128,1536]{1,0:T(8,128)(2,1)S(1)}, bf16[128,1536]{1,0:T(8,128)(2,1)S(1)}, u32[]{:S(2)}, u32[]{:S(2)}) %collective-permute-start.41) | collective-permute-done | bytes 393248 | tf_op jit(solution)/shard_map/ppermute | solution.py:527
  265.0 2.6 multiply_convert_fusion.1
  290.3 8.6 %collective-permute-done.54 = bf16[128,1536]{1,0:T(8,128)(2,1)S(1)} collective-permute-done((bf16[128,1536]{1,0:T(8,128)(2,1)S(1)}, bf16[128,1536]{1,0:T(8,128)(2,1)S(1)}, u32[]{:S(2)}, u32[]{:S(2)}) %collective-permute-start.54) | collective-permute-done | bytes 393248 | tf_op jit(solution)/shard_map/ppermute | solution.py:527
  302.2 4.5 collective-permute-done.55
  311.8 5.2 convolution_convert_fusion.1
  317.0 2.7 copy.294
  326.5 7.9 %convolution_convert_fusion = bf16[1536,560]{0,1:T(8,128)(2,1)} fusion(bf16[2048,1536]{1,0:T(8,128)(2,1)} %copy-done.107, bf16[512,560]{1,0:T(8,128)(2,1)} %copy-done.90, bf16[512,560]{1,0:T(8,128)(2,1)S(1)} %copy-done.89, bf16[512,560]{1,0:T(8,128)(2,1)S(1)} %copy-done.87, bf16[512,560]{1,0:T(8,128)(2,1)S(1)} %copy-done.85), kind=kOutput, calls=%fused_computation.13 | convolution fusion | flops 3533250560 | bytes 10305536 | tf_op jit(solution)/shard_map/dot_general | solution.py:41
  334.4 2.7 copy.295
  339.0 3.4 collective-permute-done.56
  349.8 4.4 all-to-all-start.2
  354.3 7.0 %fusion.8 = bf16[1536,560]{0,1:T(8,128)(2,1)} fusion(bf16[512,1536]{1,0:T(8,128)(2,1)} %copy-done.98, bf16[512,1536]{1,0:T(8,128)(2,1)} %copy-done.103, bf16[512,1536]{1,0:T(8,128)(2,1)} %copy-done.102, bf16[512,1536]{1,0:T(8,128)(2,1)} %copy-done.99, bf16[512,560]{1,0:T(8,128)(2,1)} %get-tuple-element.289.refs_3_, bf16[512,560]{1,0:T(8,128)(2,1)S(1)} %copy-done.36, ...), kind=kOutput, calls=%fused_computation.12 | convolution fusion | flops 3558416384 | bytes 10305536 | tf_op jit(solution)/shard_map/dot_general | solution.py:41
  361.3 2.7 copy.304
  370.2 3.0 shard_map.196
  376.7 5.0 all-to-all-start.3
  383.4 12.1 %shard_map.197 = (bf16[4,2,64,384]{3,2,1,0:T(8,128)(2,1)S(1)}, bf16[4,4,2,64,128]{4,3,2,1,0:T(8,128)(2,1)S(1)}, bf16[4,4,2,64,128]{4,3,2,1,0:T(8,128)(2,1)S(1)}, bf16[2,4,4,2,64,128]{5,4,3,2,1,0:T(8,128)(2,1)S(1)}) custom-call(s32[2,16]{1,0:T(2,128)S(1)} %copy-done.52, s32[6]{0:T(128)S(1)} %stack.95.place, bf16[4,2,64,384]{3,2,1,0:T(8,128)(2,1)S(1)} %bitcast.237, ...), custom_call_target="tpu_custom_call" | custom-call | flops 1 | bytes 1 | tf_op jit(solution)/shard_map/pallas_call | solution.py:905
  399.8 4.3 all-to-all-done.3.uppers
  410.4 3.4 shard_map.199
  414.5 8.4 %shard_map.201 = bf16[4,4,128,1536]{3,2,1,0:T(8,128)(2,1)} custom-call(s32[6]{0:T(128)S(1)} %stack.95.place, bf16[512,560]{1,0:T(8,128)(2,1)S(1)} %copy-done.33, bf16[512,560]{1,0:T(8,128)(2,1)S(1)} %copy-done.35, bf16[512,560]{1,0:T(8,128)(2,1)S(1)} %copy-done.37, bf16[512,560]{1,0:T(8,128)(2,1)S(1)} %copy-done.38, bf16[1536,560]{1,0:T(8,128)(2,1)S(1)} %bitcast.235), custom_call_target="tpu_custom_call" | custom-call | flops 1 | bytes 1 | tf_op jit(solution)/shard_map/pallas_call | solution.py:77
  422.9 7.4 %collective-permute-done.69 = bf16[4,4,2,64,128]{4,3,2,1,0:T(8,128)(2,1)} collective-permute-done((bf16[4,4,2,64,128]{4,3,2,1,0:T(8,128)(2,1)}, bf16[4,4,2,64,128]{4,3,2,1,0:T(8,128)(2,1)}, u32[]{:S(2)}, u32[]{:S(2)}) %collective-permute-start.69) | collective-permute-done | bytes 524320 | tf_op jit(solution)/shard_map/ppermute | solution.py:524
  436.4 3.2 collective-permute-start.71
  440.6 3.0 collective-permute-done.71
  443.6 6.5 %collective-permute-done.72 = bf16[4,2,64,128]{3,2,1,0:T(8,128)(2,1)S(1)} collective-permute-done((bf16[4,2,64,128]{3,2,1,0:T(8,128)(2,1)S(1)}, bf16[4,2,64,128]{3,2,1,0:T(8,128)(2,1)S(1)}, u32[]{:S(2)}, u32[]{:S(2)}) %collective-permute-start.72) | collective-permute-done | bytes 131104 | tf_op jit(solution)/shard_map/ppermute | solution.py:521
  458.3 3.6 all-to-all-start.4
  462.8 2.6 shard_map.205
  465.4 4.6 collective-permute-done.78.got
  474.4 3.5 collective-permute-start.81
  480.0 3.1 collective-permute-done.80
  486.2 3.2 shard_map.208
  492.8 4.5 all-to-all-start.5
  498.7 3.7 collective-permute-done.76.refs_1_
  503.9 3.2 collective-permute-done.84.refs_4_
  509.6 3.8 collective-permute-start.90
  517.6 3.1 convert_add_fusion
  520.7 9.8 %all-to-all-done.5.downs = bf16[4,1,96,1120]{3,2,1,0:T(8,128)(2,1)S(1)} async-done(((bf16[4,1,96,1120]{3,2,1,0:T(8,128)(2,1)}), bf16[4,1,96,1120]{3,2,1,0:T(8,128)(2,1)S(1)}, u32[]{:S(2)}, u32[]{:S(2)}) %all-to-all-start.5) | async-done | bytes 860192 | tf_op jit(solution)/shard_map/all_to_all | solution.py:584
  531.3 5.9 %shard_map.210 = (f32[192,2240]{1,0:T(8,128)}, f32[192,2240]{1,0:T(8,128)}, f32[192,2240]{1,0:T(8,128)}, f32[192,1]{1,0:T(8,128)S(1)}) custom-call(bf16[4,1,96,1120]{3,2,1,0:T(8,128)(2,1)} %all-to-all-done.2.gates, bf16[4,1,96,1120]{3,2,1,0:T(8,128)(2,1)S(1)} %all-to-all-done.3.uppers, bf16[4,1,96,1120]{3,2,1,0:T(8,128)(2,1)S(1)} %all-to-all-done.5.downs, ...), custom_call_target="tpu_custom_call" | custom-call | flops 1 | bytes 1 | tf_op jit(solution)/shard_map/pallas_call | solution.py:77
  542.5 10.5 %collective-permute-done.89 = bf16[1,48,1536]{2,1,0:T(8,128)(2,1)} collective-permute-done((bf16[1,48,1536]{2,1,0:T(8,128)(2,1)}, bf16[1,48,1536]{2,1,0:T(8,128)(2,1)}, u32[]{:S(2)}, u32[]{:S(2)}) %collective-permute-start.89) | collective-permute-done | bytes 147488 | tf_op jit(solution)/shard_map/ppermute | solution.py:521
  (603 shorter events, 199.3 us)
Async XLA Ops:
  18.8 18.2 %collective-permute-start.4 = (bf16[128,1536]{1,0:T(8,128)(2,1)S(1)}, bf16[128,1536]{1,0:T(8,128)(2,1)S(1)}, u32[]{:S(2)}, u32[]{:S(2)}) collective-permute-start(bf16[128,1536]{1,0:T(8,128)(2,1)S(1)} %fusion.41.own), channel_id=1, source_target_pairs={{0,2},{1,3},{2,0},{3,1},{4,6},{5,7},{6,4},{7,5},{8,10},{9,11},{10,... | collective-permute-start | bytes 1179656 | tf_op jit(solution)/shard_map/ppermute | solution.py:527
  28.5 16.9 %collective-permute-start.1 = (bf16[208,512]{1,0:T(8,128)(2,1)}, bf16[208,512]{1,0:T(8,128)(2,1)}, u32[]{:S(2)}, u32[]{:S(2)}) collective-permute-start(bf16[208,512]{1,0:T(8,128)(2,1)} %pad_maximum_fusion.25.rest_0_), channel_id=1, source_target_pairs={{0,16},{4,20},{8,24},{12,28},{16,0},{20,4},{24,8},{28,12},{1,17},{... | collective-permute-start | bytes 638984 | tf_op jit(solution)/shard_map/ppermute | solution.py:521
  31.1 14.3 %collective-permute-start.2 = (bf16[208,512]{1,0:T(8,128)(2,1)}, bf16[208,512]{1,0:T(8,128)(2,1)}, u32[]{:S(2)}, u32[]{:S(2)}) collective-permute-start(bf16[208,512]{1,0:T(8,128)(2,1)} %pad_maximum_fusion.25.rest_0_), channel_id=1, source_target_pairs={{0,24},{4,28},{8,0},{12,4},{16,8},{20,12},{24,16},{28,20},{1,25},{... | collective-permute-start | bytes 638984 | tf_op jit(solution)/shard_map/ppermute | solution.py:521
  51.3 36.6 %all-to-all-start.1 = ((bf16[4,48,1536]{2,1,0:T(8,128)(2,1)}), bf16[4,48,1536]{2,1,0:T(8,128)(2,1)S(1)}, u32[]{:S(2)}, u32[]{:S(2)}) async-start(bf16[4,48,1536]{2,1,0:T(8,128)(2,1)} %broadcast_in_dim.58), calls=%async_computation.1 | async-start | bytes 1179648 | tf_op jit(solution)/shard_map/all_to_all | solution.py:584
  58.7 17.7 %collective-permute-start.8 = (bf16[2,128,1536]{2,1,0:T(8,128)(2,1)S(1)}, bf16[2,128,1536]{2,1,0:T(8,128)(2,1)S(1)}, u32[]{:S(2)}, u32[]{:S(2)}) collective-permute-start(bf16[2,128,1536]{2,1,0:T(8,128)(2,1)S(1)} %pad_maximum_fusion.1), channel_id=1, source_target_pairs={{0,1},{1,0},{2,3},{3,2},{4,5},{5,4},{6,7},{7,6},{8,9},{9,8},{10,11... | collective-permute-start | bytes 2359304 | tf_op jit(solution)/shard_map/ppermute | solution.py:533
  61.0 15.4 %collective-permute-start.7 = (bf16[208,512]{1,0:T(8,128)(2,1)}, bf16[208,512]{1,0:T(8,128)(2,1)S(1)}, u32[]{:S(2)}, u32[]{:S(2)}) collective-permute-start(bf16[208,512]{1,0:T(8,128)(2,1)} %collective-permute-done.2.rest_3_), channel_id=1, source_target_pairs={{0,4},{4,0},{8,12},{12,8},{16,20},{20,16},{24,28},{28,24},{1,5},{5... | collective-permute-start | bytes 638984 | tf_op jit(solution)/shard_map/ppermute | solution.py:524
  62.5 27.6 %collective-permute-start.11 = (bf16[3,96,1120]{2,1,0:T(8,128)(2,1)}, bf16[3,96,1120]{2,1,0:T(8,128)(2,1)}, u32[]{:S(2)}, u32[]{:S(2)}) collective-permute-start(bf16[3,96,1120]{2,1,0:T(8,128)(2,1)} %get-tuple-element.197), channel_id=1, source_target_pairs={{0,8},{4,12},{8,16},{12,20},{16,24},{20,28},{24,0},{28,4},{1,9},{5... | collective-permute-start | bytes 1935368 | tf_op jit(solution)/shard_map/ppermute | solution.py:521
  67.2 31.2 %collective-permute-start.12 = (bf16[3,96,1120]{2,1,0:T(8,128)(2,1)}, bf16[3,96,1120]{2,1,0:T(8,128)(2,1)}, u32[]{:S(2)}, u32[]{:S(2)}) collective-permute-start(bf16[3,96,1120]{2,1,0:T(8,128)(2,1)} %get-tuple-element.199.refs_0_), channel_id=1, source_target_pairs={{0,4},{4,0},{8,12},{12,8},{16,20},{20,16},{24,28},{28,24},{1,5},{5... | collective-permute-start | bytes 1935368 | tf_op jit(solution)/shard_map/ppermute | solution.py:524
  87.9 22.2 %collective-permute-start.9 = (bf16[4,48,1536]{2,1,0:T(8,128)(2,1)S(1)}, bf16[4,48,1536]{2,1,0:T(8,128)(2,1)S(1)}, u32[]{:S(2)}, u32[]{:S(2)}) collective-permute-start(bf16[4,48,1536]{2,1,0:T(8,128)(2,1)S(1)} %all-to-all-done.1.mine), channel_id=1, source_target_pairs={{0,4},{4,0},{8,12},{12,8},{16,20},{20,16},{24,28},{28,24},{1,5},{5... | collective-permute-start | bytes 1769480 | tf_op jit(solution)/shard_map/ppermute | solution.py:524
  89.4 20.7 %collective-permute-start.10 = (bf16[128,1536]{1,0:T(8,128)(2,1)}, bf16[128,1536]{1,0:T(8,128)(2,1)S(1)}, u32[]{:S(2)}, u32[]{:S(2)}) collective-permute-start(bf16[128,1536]{1,0:T(8,128)(2,1)} %bitcast.268), channel_id=1, source_target_pairs={{0,2},{1,3},{2,0},{3,1},{4,6},{5,7},{6,4},{7,5},{8,10},{9,11},{10,... | collective-permute-start | bytes 1179656 | tf_op jit(solution)/shard_map/ppermute | solution.py:527
  90.1 20.0 %collective-permute-start.14 = (bf16[4,128,128]{2,1,0:T(8,128)(2,1)S(1)}, bf16[4,128,128]{2,1,0:T(8,128)(2,1)S(1)}, u32[]{:S(2)}, u32[]{:S(2)}) collective-permute-start(bf16[4,128,128]{2,1,0:T(8,128)(2,1)S(1)} %get-tuple-element.203), channel_id=1, source_target_pairs={{0,16},{4,20},{8,24},{12,28},{16,0},{20,4},{24,8},{28,12},{1,17},{... | collective-permute-start | bytes 393224 | tf_op jit(solution)/shard_map/ppermute | solution.py:521
  98.4 20.2 %collective-permute-start.19 = (bf16[3,96,1120]{2,1,0:T(8,128)(2,1)}, bf16[3,96,1120]{2,1,0:T(8,128)(2,1)S(1)}, u32[]{:S(2)}, u32[]{:S(2)}) collective-permute-start(bf16[3,96,1120]{2,1,0:T(8,128)(2,1)} %copy-done.53), channel_id=1, source_target_pairs={{0,24},{4,28},{8,0},{12,4},{16,8},{20,12},{24,16},{28,20},{1,25},{... | collective-permute-start | bytes 1935368 | tf_op jit(solution)/shard_map/ppermute | solution.py:521
  110.8 14.4 %collective-permute-start.18 = (bf16[2,2,48,1536]{3,2,1,0:T(8,128)(2,1)S(1)}, bf16[2,2,48,1536]{3,2,1,0:T(8,128)(2,1)S(1)}, u32[]{:S(2)}, u32[]{:S(2)}) collective-permute-start(bf16[2,2,48,1536]{3,2,1,0:T(8,128)(2,1)S(1)} %get-tuple-element.207), channel_id=1, source_target_pairs={{0,2},{1,3},{2,0},{3,1},{4,6},{5,7},{6,4},{7,5},{8,10},{9,11},{10,... | collective-permute-start | bytes 1769480 | tf_op jit(solution)/shard_map/ppermute | solution.py:527
  125.3 23.3 %collective-permute-start.20 = (bf16[3,96,1120]{2,1,0:T(8,128)(2,1)}, bf16[3,96,1120]{2,1,0:T(8,128)(2,1)S(1)}, u32[]{:S(2)}, u32[]{:S(2)}) collective-permute-start(bf16[3,96,1120]{2,1,0:T(8,128)(2,1)} %collective-permute-done.11.refs_1_), channel_id=1, source_target_pairs={{0,4},{4,0},{8,12},{12,8},{16,20},{20,16},{24,28},{28,24},{1,5},{5... | collective-permute-start | bytes 1935368 | tf_op jit(solution)/shard_map/ppermute | solution.py:524
  126.0 22.6 %collective-permute-start.21 = (bf16[2,96,1120]{2,1,0:T(8,128)(2,1)S(1)}, bf16[2,96,1120]{2,1,0:T(8,128)(2,1)S(1)}, u32[]{:S(2)}, u32[]{:S(2)}) collective-permute-start(bf16[2,96,1120]{2,1,0:T(8,128)(2,1)S(1)} %slice.178), channel_id=1, source_target_pairs={{0,16},{4,20},{8,24},{12,28},{16,0},{20,4},{24,8},{28,12},{1,17},{... | collective-permute-start | bytes 1290248 | tf_op jit(solution)/shard_map/ppermute | solution.py:521
  150.9 17.3 %collective-permute-start.27 = (bf16[3,96,1120]{2,1,0:T(8,128)(2,1)S(1)}, bf16[3,96,1120]{2,1,0:T(8,128)(2,1)S(1)}, u32[]{:S(2)}, u32[]{:S(2)}) collective-permute-start(bf16[3,96,1120]{2,1,0:T(8,128)(2,1)S(1)} %collective-permute-done.19.refs_3_), channel_id=1, source_target_pairs={{0,4},{4,0},{8,12},{12,8},{16,20},{20,16},{24,28},{28,24},{1,5},{5... | collective-permute-start | bytes 1935368 | tf_op jit(solution)/shard_map/ppermute | solution.py:524
  153.3 14.9 %collective-permute-start.25 = (bf16[128,1536]{1,0:T(8,128)(2,1)S(1)}, bf16[128,1536]{1,0:T(8,128)(2,1)S(1)}, u32[]{:S(2)}, u32[]{:S(2)}) collective-permute-start(bf16[128,1536]{1,0:T(8,128)(2,1)S(1)} %fusion.44), channel_id=1, source_target_pairs={{0,2},{1,3},{2,0},{3,1},{4,6},{5,7},{6,4},{7,5},{8,10},{9,11},{10,... | collective-permute-start | bytes 1179656 | tf_op jit(solution)/shard_map/ppermute | solution.py:527
  153.8 17.7 %collective-permute-start.28 = (bf16[256,1536]{1,0:T(8,128)(2,1)S(1)}, bf16[256,1536]{1,0:T(8,128)(2,1)S(1)}, u32[]{:S(2)}, u32[]{:S(2)}) collective-permute-start(bf16[256,1536]{1,0:T(8,128)(2,1)S(1)} %pad_maximum_fusion.2), channel_id=1, source_target_pairs={{0,1},{1,0},{2,3},{3,2},{4,5},{5,4},{6,7},{7,6},{8,9},{9,8},{10,11... | collective-permute-start | bytes 2359304 | tf_op jit(solution)/shard_map/ppermute | solution.py:533
  168.5 25.2 %collective-permute-start.30 = (bf16[3,96,1120]{2,1,0:T(8,128)(2,1)S(1)}, bf16[3,96,1120]{2,1,0:T(8,128)(2,1)S(1)}, u32[]{:S(2)}, u32[]{:S(2)}) collective-permute-start(bf16[3,96,1120]{2,1,0:T(8,128)(2,1)S(1)} %constant_dynamic-update-slice_fusion.3.refs_2_), channel_id=1, source_target_pairs={{0,4},{4,0},{8,12},{12,8},{16,20},{20,16},{24,28},{28,24},{1,5},{5... | collective-permute-start | bytes 1935368 | tf_op jit(solution)/shard_map/ppermute | solution.py:524
  170.9 13.8 %collective-permute-start.34 = (bf16[128,1536]{1,0:T(8,128)(2,1)S(1)}, bf16[128,1536]{1,0:T(8,128)(2,1)S(1)}, u32[]{:S(2)}, u32[]{:S(2)}) collective-permute-start(bf16[128,1536]{1,0:T(8,128)(2,1)S(1)} %get-tuple-element.351), channel_id=1, source_target_pairs={{0,8},{4,12},{8,16},{12,20},{16,24},{20,28},{24,0},{28,4},{1,9},{5... | collective-permute-start | bytes 1179656 | tf_op jit(solution)/shard_map/ppermute | solution.py:521
  170.9 22.3 %collective-permute-start.43 = (bf16[128,1536]{1,0:T(8,128)(2,1)S(1)}, bf16[128,1536]{1,0:T(8,128)(2,1)S(1)}, u32[]{:S(2)}, u32[]{:S(2)}) collective-permute-start(bf16[128,1536]{1,0:T(8,128)(2,1)S(1)} %bitcast.271), channel_id=1, source_target_pairs={{0,8},{4,12},{8,16},{12,20},{16,24},{20,28},{24,0},{28,4},{1,9},{5... | collective-permute-start | bytes 1179656 | tf_op jit(solution)/shard_map/ppermute | solution.py:521
  171.1 22.2 %collective-permute-start.29 = (bf16[128,1536]{1,0:T(8,128)(2,1)S(1)}, bf16[128,1536]{1,0:T(8,128)(2,1)S(1)}, u32[]{:S(2)}, u32[]{:S(2)}) collective-permute-start(bf16[128,1536]{1,0:T(8,128)(2,1)S(1)} %get-tuple-element.351), channel_id=1, source_target_pairs={{0,2},{1,3},{2,0},{3,1},{4,6},{5,7},{6,4},{7,5},{8,10},{9,11},{10,... | collective-permute-start | bytes 1179656 | tf_op jit(solution)/shard_map/ppermute | solution.py:527
  184.8 18.9 %collective-permute-start.37 = (bf16[128,1536]{1,0:T(8,128)(2,1)S(1)}, bf16[128,1536]{1,0:T(8,128)(2,1)S(1)}, u32[]{:S(2)}, u32[]{:S(2)}) collective-permute-start(bf16[128,1536]{1,0:T(8,128)(2,1)S(1)} %collective-permute-done.34), channel_id=1, source_target_pairs={{0,8},{4,12},{8,16},{12,20},{16,24},{20,28},{24,0},{28,4},{1,9},{5... | collective-permute-start | bytes 1179656 | tf_op jit(solution)/shard_map/ppermute | solution.py:521
  184.8 18.1 %collective-permute-start.35 = (bf16[128,1536]{1,0:T(8,128)(2,1)S(1)}, bf16[128,1536]{1,0:T(8,128)(2,1)S(1)}, u32[]{:S(2)}, u32[]{:S(2)}) collective-permute-start(bf16[128,1536]{1,0:T(8,128)(2,1)S(1)} %collective-permute-done.34), channel_id=1, source_target_pairs={{0,2},{1,3},{2,0},{3,1},{4,6},{5,7},{6,4},{7,5},{8,10},{9,11},{10,... | collective-permute-start | bytes 1179656 | tf_op jit(solution)/shard_map/ppermute | solution.py:527
  193.2 15.2 %collective-permute-start.44 = (bf16[128,1536]{1,0:T(8,128)(2,1)S(1)}, bf16[128,1536]{1,0:T(8,128)(2,1)S(1)}, u32[]{:S(2)}, u32[]{:S(2)}) collective-permute-start(bf16[128,1536]{1,0:T(8,128)(2,1)S(1)} %collective-permute-done.43), channel_id=1, source_target_pairs={{0,8},{4,12},{8,16},{12,20},{16,24},{20,28},{24,0},{28,4},{1,9},{5... | collective-permute-start | bytes 1179656 | tf_op jit(solution)/shard_map/ppermute | solution.py:521
  193.7 34.6 %collective-permute-start.31 = (bf16[256,1536]{1,0:T(8,128)(2,1)S(1)}, bf16[256,1536]{1,0:T(8,128)(2,1)}, u32[]{:S(2)}, u32[]{:S(2)}) collective-permute-start(bf16[256,1536]{1,0:T(8,128)(2,1)S(1)} %pad_maximum_fusion.3), channel_id=1, source_target_pairs={{0,1},{1,0},{2,3},{3,2},{4,5},{5,4},{6,7},{7,6},{8,9},{9,8},{10,11... | collective-permute-start | bytes 2359304 | tf_op jit(solution)/shard_map/ppermute | solution.py:533
  202.9 39.0 %collective-permute-start.36 = (bf16[256,1536]{1,0:T(8,128)(2,1)S(1)}, bf16[256,1536]{1,0:T(8,128)(2,1)S(1)}, u32[]{:S(2)}, u32[]{:S(2)}) collective-permute-start(bf16[256,1536]{1,0:T(8,128)(2,1)S(1)} %pad_maximum_fusion.4), channel_id=1, source_target_pairs={{0,1},{1,0},{2,3},{3,2},{4,5},{5,4},{6,7},{7,6},{8,9},{9,8},{10,11... | collective-permute-start | bytes 2359304 | tf_op jit(solution)/shard_map/ppermute | solution.py:533
  203.5 41.6 %collective-permute-start.49 = (bf16[256,1536]{1,0:T(8,128)(2,1)S(1)}, bf16[256,1536]{1,0:T(8,128)(2,1)S(1)}, u32[]{:S(2)}, u32[]{:S(2)}) collective-permute-start(bf16[256,1536]{1,0:T(8,128)(2,1)S(1)} %pad_maximum_fusion.8), channel_id=1, source_target_pairs={{0,1},{1,0},{2,3},{3,2},{4,5},{5,4},{6,7},{7,6},{8,9},{9,8},{10,11... | collective-permute-start | bytes 2359304 | tf_op jit(solution)/shard_map/ppermute | solution.py:533
  203.6 16.4 %collective-permute-start.38 = (bf16[128,1536]{1,0:T(8,128)(2,1)S(1)}, bf16[128,1536]{1,0:T(8,128)(2,1)S(1)}, u32[]{:S(2)}, u32[]{:S(2)}) collective-permute-start(bf16[128,1536]{1,0:T(8,128)(2,1)S(1)} %collective-permute-done.37), channel_id=1, source_target_pairs={{0,2},{1,3},{2,0},{3,1},{4,6},{5,7},{6,4},{7,5},{8,10},{9,11},{10,... | collective-permute-start | bytes 1179656 | tf_op jit(solution)/shard_map/ppermute | solution.py:527
  220.1 21.4 %collective-permute-start.40 = (bf16[128,1536]{1,0:T(8,128)(2,1)S(1)}, bf16[128,1536]{1,0:T(8,128)(2,1)S(1)}, u32[]{:S(2)}, u32[]{:S(2)}) collective-permute-start(bf16[128,1536]{1,0:T(8,128)(2,1)S(1)} %collective-permute-done.37), channel_id=1, source_target_pairs={{0,8},{4,12},{8,16},{12,20},{16,24},{20,28},{24,0},{28,4},{1,9},{5... | collective-permute-start | bytes 1179656 | tf_op jit(solution)/shard_map/ppermute | solution.py:521
  228.3 33.7 %collective-permute-start.39 = (bf16[256,1536]{1,0:T(8,128)(2,1)S(1)}, bf16[256,1536]{1,0:T(8,128)(2,1)S(1)}, u32[]{:S(2)}, u32[]{:S(2)}) collective-permute-start(bf16[256,1536]{1,0:T(8,128)(2,1)S(1)} %pad_maximum_fusion.5), channel_id=1, source_target_pairs={{0,1},{1,0},{2,3},{3,2},{4,5},{5,4},{6,7},{7,6},{8,9},{9,8},{10,11... | collective-permute-start | bytes 2359304 | tf_op jit(solution)/shard_map/ppermute | solution.py:533
  228.4 35.2 %collective-permute-start.52 = (bf16[256,1536]{1,0:T(8,128)(2,1)S(1)}, bf16[256,1536]{1,0:T(8,128)(2,1)S(1)}, u32[]{:S(2)}, u32[]{:S(2)}) collective-permute-start(bf16[256,1536]{1,0:T(8,128)(2,1)S(1)} %pad_maximum_fusion.9), channel_id=1, source_target_pairs={{0,1},{1,0},{2,3},{3,2},{4,5},{5,4},{6,7},{7,6},{8,9},{9,8},{10,11... | collective-permute-start | bytes 2359304 | tf_op jit(solution)/shard_map/ppermute | solution.py:533
  241.5 19.6 %collective-permute-start.46 = (bf16[128,1536]{1,0:T(8,128)(2,1)S(1)}, bf16[128,1536]{1,0:T(8,128)(2,1)S(1)}, u32[]{:S(2)}, u32[]{:S(2)}) collective-permute-start(bf16[128,1536]{1,0:T(8,128)(2,1)S(1)} %collective-permute-done.45), channel_id=1, source_target_pairs={{0,2},{1,3},{2,0},{3,1},{4,6},{5,7},{6,4},{7,5},{8,10},{9,11},{10,... | collective-permute-start | bytes 1179656 | tf_op jit(solution)/shard_map/ppermute | solution.py:527
  241.9 19.1 %collective-permute-start.41 = (bf16[128,1536]{1,0:T(8,128)(2,1)S(1)}, bf16[128,1536]{1,0:T(8,128)(2,1)S(1)}, u32[]{:S(2)}, u32[]{:S(2)}) collective-permute-start(bf16[128,1536]{1,0:T(8,128)(2,1)S(1)} %collective-permute-done.40), channel_id=1, source_target_pairs={{0,2},{1,3},{2,0},{3,1},{4,6},{5,7},{6,4},{7,5},{8,10},{9,11},{10,... | collective-permute-start | bytes 1179656 | tf_op jit(solution)/shard_map/ppermute | solution.py:527
  245.1 27.9 %collective-permute-start.32 = (bf16[2,128,1536]{2,1,0:T(8,128)(2,1)S(1)}, bf16[2,128,1536]{2,1,0:T(8,128)(2,1)S(1)}, u32[]{:S(2)}, u32[]{:S(2)}) collective-permute-start(bf16[2,128,1536]{2,1,0:T(8,128)(2,1)S(1)} %bitcast.282), channel_id=1, source_target_pairs={{0,1},{1,0},{2,3},{3,2},{4,5},{5,4},{6,7},{7,6},{8,9},{9,8},{10,11... | collective-permute-start | bytes 2359304 | tf_op jit(solution)/shard_map/ppermute | solution.py:533
  261.0 24.3 %collective-permute-start.50 = (bf16[2,128,1536]{2,1,0:T(8,128)(2,1)S(1)}, bf16[2,128,1536]{2,1,0:T(8,128)(2,1)S(1)}, u32[]{:S(2)}, u32[]{:S(2)}) collective-permute-start(bf16[2,128,1536]{2,1,0:T(8,128)(2,1)S(1)} %bitcast.283), channel_id=1, source_target_pairs={{0,1},{1,0},{2,3},{3,2},{4,5},{5,4},{6,7},{7,6},{8,9},{9,8},{10,11... | collective-permute-start | bytes 2359304 | tf_op jit(solution)/shard_map/ppermute | solution.py:533
  262.0 14.0 %collective-permute-start.47 = (bf16[256,1536]{1,0:T(8,128)(2,1)S(1)}, bf16[256,1536]{1,0:T(8,128)(2,1)S(1)}, u32[]{:S(2)}, u32[]{:S(2)}) collective-permute-start(bf16[256,1536]{1,0:T(8,128)(2,1)S(1)} %pad_maximum_fusion.7), channel_id=1, source_target_pairs={{0,1},{1,0},{2,3},{3,2},{4,5},{5,4},{6,7},{7,6},{8,9},{9,8},{10,11... | collective-permute-start | bytes 2359304 | tf_op jit(solution)/shard_map/ppermute | solution.py:533
  272.3 17.3 %collective-permute-start.53 = (bf16[2,128,1536]{2,1,0:T(8,128)(2,1)S(1)}, bf16[2,128,1536]{2,1,0:T(8,128)(2,1)S(1)}, u32[]{:S(2)}, u32[]{:S(2)}) collective-permute-start(bf16[2,128,1536]{2,1,0:T(8,128)(2,1)S(1)} %bitcast.284), channel_id=1, source_target_pairs={{0,1},{1,0},{2,3},{3,2},{4,5},{5,4},{6,7},{7,6},{8,9},{9,8},{10,11... | collective-permute-start | bytes 2359304 | tf_op jit(solution)/shard_map/ppermute | solution.py:533
  274.0 14.7 %collective-permute-start.33 = (bf16[128,1536]{1,0:T(8,128)(2,1)S(1)}, bf16[128,1536]{1,0:T(8,128)(2,1)S(1)}, u32[]{:S(2)}, u32[]{:S(2)}) collective-permute-start(bf16[128,1536]{1,0:T(8,128)(2,1)S(1)} %fusion.45), channel_id=1, source_target_pairs={{0,2},{1,3},{2,0},{3,1},{4,6},{5,7},{6,4},{7,5},{8,10},{9,11},{10,... | collective-permute-start | bytes 1179656 | tf_op jit(solution)/shard_map/ppermute | solution.py:527
  288.6 19.3 %collective-permute-start.57 = (bf16[2,128,1536]{2,1,0:T(8,128)(2,1)S(1)}, bf16[2,128,1536]{2,1,0:T(8,128)(2,1)S(1)}, u32[]{:S(2)}, u32[]{:S(2)}) collective-permute-start(bf16[2,128,1536]{2,1,0:T(8,128)(2,1)S(1)} %bitcast.285), channel_id=1, source_target_pairs={{0,1},{1,0},{2,3},{3,2},{4,5},{5,4},{6,7},{7,6},{8,9},{9,8},{10,11... | collective-permute-start | bytes 2359304 | tf_op jit(solution)/shard_map/ppermute | solution.py:533
  289.9 16.7 %collective-permute-start.55 = (bf16[128,1536]{1,0:T(8,128)(2,1)S(1)}, bf16[128,1536]{1,0:T(8,128)(2,1)S(1)}, u32[]{:S(2)}, u32[]{:S(2)}) collective-permute-start(bf16[128,1536]{1,0:T(8,128)(2,1)S(1)} %fusion.47), channel_id=1, source_target_pairs={{0,2},{1,3},{2,0},{3,1},{4,6},{5,7},{6,4},{7,5},{8,10},{9,11},{10,... | collective-permute-start | bytes 1179656 | tf_op jit(solution)/shard_map/ppermute | solution.py:527
  299.8 26.7 %collective-permute-start.59 = (bf16[128,1536]{1,0:T(8,128)(2,1)}, bf16[128,1536]{1,0:T(8,128)(2,1)}, u32[]{:S(2)}, u32[]{:S(2)}) collective-permute-start(bf16[128,1536]{1,0:T(8,128)(2,1)} %fusion.36), channel_id=1, source_target_pairs={{0,24},{4,28},{8,0},{12,4},{16,8},{20,12},{24,16},{28,20},{1,25},{... | collective-permute-start | bytes 1179656 | tf_op jit(solution)/shard_map/ppermute | solution.py:521
  307.5 31.5 %collective-permute-start.60 = (bf16[128,1536]{1,0:T(8,128)(2,1)}, bf16[128,1536]{1,0:T(8,128)(2,1)}, u32[]{:S(2)}, u32[]{:S(2)}) collective-permute-start(bf16[128,1536]{1,0:T(8,128)(2,1)} %fusion.35), channel_id=1, source_target_pairs={{0,16},{4,20},{8,24},{12,28},{16,0},{20,4},{24,8},{28,12},{1,17},{... | collective-permute-start | bytes 1179656 | tf_op jit(solution)/shard_map/ppermute | solution.py:521
  321.6 20.8 %collective-permute-start.56 = (bf16[4,1,96,1120]{3,2,1,0:T(8,128)(2,1)}, bf16[4,1,96,1120]{3,2,1,0:T(8,128)(2,1)}, u32[]{:S(2)}, u32[]{:S(2)}) collective-permute-start(bf16[4,1,96,1120]{3,2,1,0:T(8,128)(2,1)} %get-tuple-element.245), channel_id=1, source_target_pairs={{0,4},{4,0},{8,12},{12,8},{16,20},{20,16},{24,28},{28,24},{1,5},{5... | collective-permute-start | bytes 2580488 | tf_op jit(solution)/shard_map/ppermute | solution.py:524
  324.0 15.0 %collective-permute-start.61 = (bf16[128,1536]{1,0:T(8,128)(2,1)}, bf16[128,1536]{1,0:T(8,128)(2,1)}, u32[]{:S(2)}, u32[]{:S(2)}) collective-permute-start(bf16[128,1536]{1,0:T(8,128)(2,1)} %fusion.34), channel_id=1, source_target_pairs={{0,8},{4,12},{8,16},{12,20},{16,24},{20,28},{24,0},{28,4},{1,9},{5... | collective-permute-start | bytes 1179656 | tf_op jit(solution)/shard_map/ppermute | solution.py:521
  346.6 20.3 %collective-permute-start.62 = (bf16[128,1536]{1,0:T(8,128)(2,1)S(1)}, bf16[128,1536]{1,0:T(8,128)(2,1)}, u32[]{:S(2)}, u32[]{:S(2)}) collective-permute-start(bf16[128,1536]{1,0:T(8,128)(2,1)S(1)} %get-tuple-element.282.own), channel_id=1, source_target_pairs={{0,2},{1,3},{2,0},{3,1},{4,6},{5,7},{6,4},{7,5},{8,10},{9,11},{10,... | collective-permute-start | bytes 1179656 | tf_op jit(solution)/shard_map/ppermute | solution.py:527
  346.9 19.9 %collective-permute-start.63 = (bf16[4,1,96,1120]{3,2,1,0:T(8,128)(2,1)}, bf16[4,1,96,1120]{3,2,1,0:T(8,128)(2,1)}, u32[]{:S(2)}, u32[]{:S(2)}) collective-permute-start(bf16[4,1,96,1120]{3,2,1,0:T(8,128)(2,1)} %get-tuple-element.263), channel_id=1, source_target_pairs={{0,4},{4,0},{8,12},{12,8},{16,20},{20,16},{24,28},{28,24},{1,5},{5... | collective-permute-start | bytes 2580488 | tf_op jit(solution)/shard_map/ppermute | solution.py:524
  349.8 24.6 %all-to-all-start.2 = ((bf16[4,1,96,1120]{3,2,1,0:T(8,128)(2,1)}), bf16[4,1,96,1120]{3,2,1,0:T(8,128)(2,1)}, u32[]{:S(2)}, u32[]{:S(2)}) async-start(bf16[4,1,96,1120]{3,2,1,0:T(8,128)(2,1)} %add_convert_fusion.2), calls=%async_computation.2 | async-start | bytes 1769472 | tf_op jit(solution)/shard_map/all_to_all | solution.py:584
  376.7 27.5 %all-to-all-start.3 = ((bf16[4,1,96,1120]{3,2,1,0:T(8,128)(2,1)}), bf16[4,1,96,1120]{3,2,1,0:T(8,128)(2,1)S(1)}, u32[]{:S(2)}, u32[]{:S(2)}) async-start(bf16[4,1,96,1120]{3,2,1,0:T(8,128)(2,1)} %add_convert_fusion.1), calls=%async_computation.3 | async-start | bytes 1769472 | tf_op jit(solution)/shard_map/all_to_all | solution.py:584
  381.7 135.8 %reduce-scatter.3.cloned.1.call-start = ((), (), s32[]{:S(2)}) async-start(), calls=%async_computation.8 | async-start | bytes 7864320 | tf_op jit(solution)/shard_map/reduce_scatter | solution.py:958
  396.7 26.2 %collective-permute-start.70 = (bf16[4,1,96,1120]{3,2,1,0:T(8,128)(2,1)}, bf16[4,1,96,1120]{3,2,1,0:T(8,128)(2,1)}, u32[]{:S(2)}, u32[]{:S(2)}) collective-permute-start(bf16[4,1,96,1120]{3,2,1,0:T(8,128)(2,1)} %get-tuple-element.290), channel_id=1, source_target_pairs={{0,4},{4,0},{8,12},{12,8},{16,20},{20,16},{24,28},{28,24},{1,5},{5... | collective-permute-start | bytes 2580488 | tf_op jit(solution)/shard_map/ppermute | solution.py:524
  406.3 24.0 %collective-permute-start.69 = (bf16[4,4,2,64,128]{4,3,2,1,0:T(8,128)(2,1)}, bf16[4,4,2,64,128]{4,3,2,1,0:T(8,128)(2,1)}, u32[]{:S(2)}, u32[]{:S(2)}) collective-permute-start(bf16[4,4,2,64,128]{4,3,2,1,0:T(8,128)(2,1)} %add_convert_fusion.5), channel_id=1, source_target_pairs={{0,4},{4,0},{8,12},{12,8},{16,20},{20,16},{24,28},{28,24},{1,5},{5... | collective-permute-start | bytes 1572872 | tf_op jit(solution)/shard_map/ppermute | solution.py:524
  430.4 19.8 %collective-permute-start.74 = (bf16[2,2,48,1536]{3,2,1,0:T(8,128)(2,1)}, bf16[2,2,48,1536]{3,2,1,0:T(8,128)(2,1)S(1)}, u32[]{:S(2)}, u32[]{:S(2)}) collective-permute-start(bf16[2,2,48,1536]{3,2,1,0:T(8,128)(2,1)} %copy-done.55), channel_id=1, source_target_pairs={{0,2},{1,3},{2,0},{3,1},{4,6},{5,7},{6,4},{7,5},{8,10},{9,11},{10,... | collective-permute-start | bytes 1769480 | tf_op jit(solution)/shard_map/ppermute | solution.py:527
  432.1 18.7 %collective-permute-start.75 = (bf16[4,1,4,48,384]{4,3,2,1,0:T(8,128)(2,1)}, bf16[4,1,4,48,384]{4,3,2,1,0:T(8,128)(2,1)}, u32[]{:S(2)}, u32[]{:S(2)}) collective-permute-start(bf16[4,1,4,48,384]{4,3,2,1,0:T(8,128)(2,1)} %copy-done.54), channel_id=1, source_target_pairs={{0,4},{4,0},{8,12},{12,8},{16,20},{20,16},{24,28},{28,24},{1,5},{5... | collective-permute-start | bytes 1769480 | tf_op jit(solution)/shard_map/ppermute | solution.py:524
  458.3 26.4 %all-to-all-start.4 = ((bf16[4,1,4,48,384]{4,3,2,1,0:T(8,128)(2,1)}), bf16[4,1,4,48,384]{4,3,2,1,0:T(8,128)(2,1)S(1)}, u32[]{:S(2)}, u32[]{:S(2)}) async-start(bf16[4,1,4,48,384]{4,3,2,1,0:T(8,128)(2,1)} %add_convert_fusion.3), calls=%async_computation.6 | async-start | bytes 1179648 | tf_op jit(solution)/shard_map/all_to_all | solution.py:584
  470.7 14.6 %collective-permute-start.83 = (bf16[4,1,48,1536]{3,2,1,0:T(8,128)(2,1)}, bf16[4,1,48,1536]{3,2,1,0:T(8,128)(2,1)}, u32[]{:S(2)}, u32[]{:S(2)}) collective-permute-start(bf16[4,1,48,1536]{3,2,1,0:T(8,128)(2,1)} %get-tuple-element.318), channel_id=1, source_target_pairs={{0,4},{4,0},{8,12},{12,8},{16,20},{20,16},{24,28},{28,24},{1,5},{5... | collective-permute-start | bytes 1769480 | tf_op jit(solution)/shard_map/ppermute | solution.py:524
  490.5 27.0 %collective-permute-start.86 = (bf16[2,128,1536]{2,1,0:T(8,128)(2,1)}, bf16[2,128,1536]{2,1,0:T(8,128)(2,1)}, u32[]{:S(2)}, u32[]{:S(2)}) collective-permute-start(bf16[2,128,1536]{2,1,0:T(8,128)(2,1)} %get-tuple-element.327), channel_id=1, source_target_pairs={{0,1},{1,0},{2,3},{3,2},{4,5},{5,4},{6,7},{7,6},{8,9},{9,8},{10,11... | collective-permute-start | bytes 2359304 | tf_op jit(solution)/shard_map/ppermute | solution.py:533
  492.8 37.6 %all-to-all-start.5 = ((bf16[4,1,96,1120]{3,2,1,0:T(8,128)(2,1)}), bf16[4,1,96,1120]{3,2,1,0:T(8,128)(2,1)S(1)}, u32[]{:S(2)}, u32[]{:S(2)}) async-start(bf16[4,1,96,1120]{3,2,1,0:T(8,128)(2,1)} %add_convert_fusion), calls=%async_computation.7 | async-start | bytes 1769472 | tf_op jit(solution)/shard_map/all_to_all | solution.py:584
  497.4 61.3 %reduce-scatter.5.cloned.1.call-start = ((), (), s32[]{:S(2)}) async-start(), calls=%async_computation.9 | async-start | bytes 1966080 | tf_op jit(solution)/shard_map/reduce_scatter | solution.py:988
  509.6 32.9 %collective-permute-start.90 = (bf16[1,48,1536]{2,1,0:T(8,128)(2,1)}, bf16[1,48,1536]{2,1,0:T(8,128)(2,1)}, u32[]{:S(2)}, u32[]{:S(2)}) collective-permute-start(bf16[1,48,1536]{2,1,0:T(8,128)(2,1)} %get-tuple-element.335), channel_id=1, source_target_pairs={{0,24},{4,28},{8,0},{12,4},{16,8},{20,12},{24,16},{28,20},{1,25},{... | collective-permute-start | bytes 442376 | tf_op jit(solution)/shard_map/ppermute | solution.py:521
  513.4 39.6 %collective-permute-start.89 = (bf16[1,48,1536]{2,1,0:T(8,128)(2,1)}, bf16[1,48,1536]{2,1,0:T(8,128)(2,1)}, u32[]{:S(2)}, u32[]{:S(2)}) collective-permute-start(bf16[1,48,1536]{2,1,0:T(8,128)(2,1)} %get-tuple-element.334), channel_id=1, source_target_pairs={{0,16},{4,20},{8,24},{12,28},{16,0},{20,4},{24,8},{28,12},{1,17},{... | collective-permute-start | bytes 442376 | tf_op jit(solution)/shard_map/ppermute | solution.py:521
  513.4 39.6 %collective-permute-start.88 = (bf16[1,48,1536]{2,1,0:T(8,128)(2,1)}, bf16[1,48,1536]{2,1,0:T(8,128)(2,1)}, u32[]{:S(2)}, u32[]{:S(2)}) collective-permute-start(bf16[1,48,1536]{2,1,0:T(8,128)(2,1)} %get-tuple-element.333), channel_id=1, source_target_pairs={{0,8},{4,12},{8,16},{12,20},{16,24},{20,28},{24,0},{28,4},{1,9},{5... | collective-permute-start | bytes 442376 | tf_op jit(solution)/shard_map/ppermute | solution.py:521
  540.4 15.1 %collective-permute-start.87 = (bf16[128,1536]{1,0:T(8,128)(2,1)S(1)}, bf16[128,1536]{1,0:T(8,128)(2,1)S(1)}, u32[]{:S(2)}, u32[]{:S(2)}) collective-permute-start(bf16[128,1536]{1,0:T(8,128)(2,1)S(1)} %fusion.49), channel_id=1, source_target_pairs={{0,2},{1,3},{2,0},{3,1},{4,6},{5,7},{6,4},{7,5},{8,10},{9,11},{10,... | collective-permute-start | bytes 1179656 | tf_op jit(solution)/shard_map/ppermute | solution.py:527
  540.5 14.4 %collective-permute-start.92 = (f32[48]{0:T(128)S(1)}, f32[48]{0:T(128)S(1)}, u32[]{:S(2)}, u32[]{:S(2)}) collective-permute-start(f32[48]{0:T(128)S(1)} %fusion.68), channel_id=1, source_target_pairs={{0,2},{1,3},{2,0},{3,1},{4,6},{5,7},{6,4},{7,5},{8,10},{9,11},{10,... | collective-permute-start | bytes 584 | tf_op jit(solution)/shard_map/ppermute | solution.py:527
  (161 other events, 1199.0 us)
Sparse Core Ops, SparseCore 0:
  430.5 59.6 reduce-scatter.2
  517.7 40.1 reduce-scatter.4

commit v5 on v4

--- a/solution.py
+++ b/solution.py
@@ -80,10 +80,10 @@
             num_scalar_prefetch=len(scalars),
             grid=(1,),
             in_specs=[
-                pl.BlockSpec(memory_space=pltpu.HBM) if i in options.get("far", ()) else whole(array.shape)
+                pl.BlockSpec(memory_space=pltpu.HBM) if i in options.get("far", ()) else whole(array.shape, options.get("single", False))
                 for i, array in enumerate(arrays)
             ],
-            out_specs=[whole(out.shape) for out in outs],
+            out_specs=[whole(out.shape, options.get("single", False)) for out in outs],
             scratch_shapes=options.get("scratch", ()),
         ),
         out_shape=outs,
@@ -92,8 +92,9 @@
     )(*scalars, *arrays)
 
 
-def whole(shape):
-    return pl.BlockSpec(shape, lambda *unused: (0,) * len(shape))
+def whole(shape, single=False):
+    mode = pl.Buffered(buffer_count=1) if single else None
+    return pl.BlockSpec(shape, lambda *unused: (0,) * len(shape), pipeline_mode=mode)
 
 
 def turn(field):
@@ -405,10 +406,21 @@
     out[:, place[AT_U] ^ 3] = across[1]
 
 
-def choose_tile_kernel(place, share, keep, send):
-    for z in range(share.shape[0]):
-        put_packed(keep, (z, 0), share[z, place[AT_X]])
-        put_packed(send, (z, 0), share[z, 1 - place[AT_X]])
+def weight_grad_kernel(depth, place, *refs):
+    rows, grads, (keep, send, total) = refs[:depth], refs[depth : 2 * depth], refs[2 * depth :]
+    step = total.shape[0] // 4
+    for k in range(4):
+        at = slice(k * step, (k + 1) * step)
+        part = None
+        for row, grad in zip(rows, grads):
+            new = dot_tn(row[:, at], grad[...])
+            part = new if part is None else part + new
+        total[at] = part
+    size = total.shape[0] // (depth * PAIR)
+    for z in range(depth):
+        for out, x in ((keep, place[AT_X]), (send, 1 - place[AT_X])):
+            start = pl.multiple_of((z * PAIR + x) * size, 16)
+            put_packed(out, (z, 0), total[pl.ds(start, size)].astype(BF16))
 
 
 def choose_kernel(place, *refs):
@@ -717,7 +729,7 @@
         (*[tile_pieces[d] for d in middle], tile_pieces[late][:2], tile_pieces[late][2:]), kinds[1]
     )
     for d, piece in zip(middle, held):
-        tile_mine[d] = grid.to_z(piece, d)
+        tile_mine[d] = grid.to_z(after(piece, *kinds[1:]), d)
     out_far, cot_near, tile_mine[early], tile_far[0], *kinds = together(
         out_far, cot_near, tile_mine[early], tile_far[0], *kinds
     )
@@ -810,7 +822,7 @@
     mid_own = unit_two.astype(BF16)
     mid_near = grid.swap_y(mid_own)
     mid_pieces = [mid_own, grid.to_z(mid_own, 1)]
-    cot_pieces = [cot_first, grid.to_z(after(cot_first, got), 1)]
+    cot_pieces = [cot_first, grid.to_z(after(cot_first, mid_near), 1)]
     mid_near, tile_far[late] = together(mid_near, tile_far[late])
     for d in range(2, depth):
         mid_pieces.append(grid.to_z(mid_pieces[-1], 1))
@@ -858,10 +870,16 @@
         half = like((depth, len(shares), *rows, shape[-1]))
         return call(choose_kernel, [place], shares, [half] * 2)
 
-    def halve_tile(share):
-        share = share.astype(BF16).reshape(depth, PAIR, block_model, hidden_units)
+    def weight_grad(rows, grads):
         half = like((depth, 1, *packed(block_model, hidden_units)))
-        return call(choose_tile_kernel, [place], [share], [half] * 2)
+        return call(
+            functools.partial(weight_grad_kernel, depth),
+            [place],
+            [*rows, *grads],
+            [half] * 2,
+            scratch=[pltpu.VMEM((model, hidden_units), F32)],
+            single=depth > 4,
+        )
 
     def fold(keep, got):
         return exchange_z_all(grid, (keep.astype(F32) + got.astype(F32)).astype(BF16))
@@ -870,11 +888,11 @@
     boths = [over_core(chunk) for chunk in back_chunks]
     mid_parts = [over_y(both) for both in boths]
     back_pieces = [grid.to_z(mid_parts[d].astype(BF16), -d) for d in range(1, depth)]
-    mid_all = jnp.concatenate(mid_chunks)
+    mid_all = tuple(mid_chunks)
     mid_now = after(mid_all, back_chunks[-1], *boths[:-1], *mid_parts[:-1])
-    gate_keep, gate_send = halve_tile(contract_rows(mid_now, jnp.concatenate(gate_grads)))
+    gate_keep, gate_send = weight_grad(mid_now, gate_grads)
     mid_now = after(mid_all, gate_send, *mid_parts, back_pieces[0])
-    upper_keep, upper_send = halve_tile(contract_rows(mid_now, jnp.concatenate(upper_grads)))
+    upper_keep, upper_send = weight_grad(mid_now, upper_grads)
     gate_got = grid.swap_x(gate_send)
     first, gate_got, upper_send, *back_pieces = together(
         mid_parts[0], gate_got, upper_send, *back_pieces
@@ -886,9 +904,7 @@
     branch_near = grid.swap_y(branch_own)
     upper_got = grid.swap_x(after(upper_send, gate_got))
     gate_owned = fold(*after((gate_keep, gate_got), branch_own))
-    held = after((*cot_chunks, *actives), branch_own)
-    cot_all, active_all = [jnp.concatenate(part) for part in (held[:depth], held[depth:])]
-    down_keep, down_send = halve_tile(contract_rows(cot_all, active_all))
+    down_keep, down_send = weight_grad(after(tuple(cot_chunks), branch_own), actives)
     down_send, branch_near, upper_got = together(down_send, branch_near, upper_got)
     down_got = grid.swap_x(down_send)
     branch_across = grid.swap_core(jnp.stack([branch_own, branch_near]))

time: 575 us -> 564 us (0.981)
  matrix products: 59.1 us -> 40.6 us
  Pallas kernels: 77.1 us -> 93.4 us
  other arithmetic: 53.4 us -> 45.5 us
    pallas_call x23, Pallas kernels: 55.8 us -> 77.2 us  [call(): pl.pallas_call(kernel, grid_spec=pltpu.PrefetchScalarGridSpec(num_scalar_...]
    dot_general x5 -> x2, matrix products: 21.7 us -> 3.04 us  [contract_rows(): lax.dot_general(left, right, (((0,), (0,)), ((), ())), preferred_element_...]
    ppermute x21, waiting for transfers between devices: 34.2 us -> 45.6 us  [swap_y(): return lax.ppermute(value, 'uly', [(i, i ^ 2) for i in range(self.ulys)])]
    convert_element_type x3 -> x0, local copies, waits for them, and re-layouts: 8.16 us -> none  [halve_tile(): share = share.astype(BF16).reshape(depth, PAIR, block_model, hidden_units)]
    unnamed x258 -> x206, local copies, waits for them, and re-layouts: 27.9 us -> 30.4 us
  transfers between devices with their start and end apart: 101 -> 101, of which waited for: 36 -> 46; matrix products, arithmetic and copies ran while one was open for 22% -> 17% of each run, Pallas kernels for 13% -> 16%
where the time goes in v5:
time: 564 us; the launch traced here: 556 us
  waiting for transfers between devices  198 us (35%)
  starting transfers between devices  115 us (20%)
  Pallas kernels  93.4 us (17%)
  local copies, waits for them, and re-layouts  47.4 us (8%)
  other arithmetic  45.5 us (8%)
  matrix products  40.6 us (7%)
  between operations  16.5 us (3%)
    ppermute x28, waiting for transfers between devices, to_z(): return lax.ppermute(value, 'blk', pairs)  102 us
    pallas_call x23, Pallas kernels, call(): pl.pallas_call(kernel, grid_spec=pltpu.PrefetchScalarGridSpec(num_scalar_...  77.2 us
    ppermute x21, waiting for transfers between devices, swap_y(): return lax.ppermute(value, 'uly', [(i, i ^ 2) for i in range(self.ulys)])  45.6 us
    ppermute x28, starting transfers between devices, to_z(): return lax.ppermute(value, 'blk', pairs)  37.1 us
    unnamed x206, local copies, waits for them, and re-layouts  30.4 us
    ppermute x17, waiting for transfers between devices, swap_x(): return lax.ppermute(value, 'blk', [(i, i ^ 1) for i in range(self.blocks)])  25.9 us
    dot_general x12, matrix products, matmul(): return jnp.dot(left, right, preferred_element_type=F32)  25.6 us
    all_to_all x5, starting transfers between devices, exchange_z_all(): lax.all_to_all(parts, 'blk', split_axis=0, concat_axis=0, axis_index_grou...  25.2 us
  transfers between devices with their start and end apart: 101, of which 46 were waited for; matrix products, arithmetic and copies ran while one was open for 17% of the time, Pallas kernels for 16%

profile of v5, /device:TPU:0, one launch (start us, length us, event | category | flops | bytes accessed | tf_op | source)
XLA Modules:
  0.0 556.5 jit_solution(145446193949160185)
XLA Ops:
  10.6 4.2 all-to-all-start
  16.1 2.9 collective-permute-start.4
  26.2 2.6 collective-permute-start.1
  31.8 2.7 collective-permute-done.rest_1_
  34.5 7.6 %collective-permute-done.1.rest_2_ = bf16[208,512]{1,0:T(8,128)(2,1)} collective-permute-done((bf16[208,512]{1,0:T(8,128)(2,1)S(1)}, bf16[208,512]{1,0:T(8,128)(2,1)}, u32[]{:S(2)}, u32[]{:S(2)}) %collective-permute-start.1) | collective-permute-done | bytes 213024 | tf_op jit(solution)/shard_map/ppermute | solution.py:533
  43.4 3.0 shard_map.186
  49.9 7.4 %all-to-all-start.1 = ((bf16[4,48,1536]{2,1,0:T(8,128)(2,1)}), bf16[4,48,1536]{2,1,0:T(8,128)(2,1)S(1)}, u32[]{:S(2)}, u32[]{:S(2)}) async-start(bf16[4,48,1536]{2,1,0:T(8,128)(2,1)} %broadcast_in_dim.58), calls=%async_computation.1 | async-start | bytes 1179648 | tf_op jit(solution)/shard_map/all_to_all | solution.py:596
  71.0 4.6 collective-permute-done.7.rest_7_
  76.5 6.1 %shard_map.187 = (bf16[4,128,1536]{2,1,0:T(8,128)(2,1)S(1)}, bf16[8,192,512]{2,1,0:T(8,128)(2,1)}, bf16[4,128,384]{2,1,0:T(8,128)(2,1)S(1)}, bf16[4,128,128]{2,1,0:T(8,128)(2,1)S(1)}) custom-call(s32[6]{0:T(128)S(1)} %stack.95.place, bf16[128,1536]{1,0:T(8,128)(2,1)S(1)} %fusion.9.own, bf16[128,1536]{1,0:T(8,128)(2,1)S(1)} %collective-permute-done.4.near, ...), custom_call_target="tpu_custom_call" | custom-call | flops 1 | bytes 1 | tf_op jit(solution)/shard_map/pallas_call | solution.py:77
  88.6 6.5 %collective-permute-done.13 = bf16[4,128,128]{2,1,0:T(8,128)(2,1)S(1)} collective-permute-done((bf16[4,128,128]{2,1,0:T(8,128)(2,1)}, bf16[4,128,128]{2,1,0:T(8,128)(2,1)S(1)}, u32[]{:S(2)}, u32[]{:S(2)}) %collective-permute-start.13) | collective-permute-done | bytes 131104 | tf_op jit(solution)/shard_map/ppermute | solution.py:533
  95.1 7.3 %collective-permute-done.14 = bf16[4,128,128]{2,1,0:T(8,128)(2,1)S(1)} collective-permute-done((bf16[4,128,128]{2,1,0:T(8,128)(2,1)}, bf16[4,128,128]{2,1,0:T(8,128)(2,1)S(1)}, u32[]{:S(2)}, u32[]{:S(2)}) %collective-permute-start.14) | collective-permute-done | bytes 131104 | tf_op jit(solution)/shard_map/ppermute | solution.py:533
  104.7 4.2 collective-permute-done.15
  112.0 9.8 %collective-permute-done.19.refs_3_ = bf16[3,96,1120]{2,1,0:T(8,128)(2,1)S(1)} collective-permute-done((bf16[3,96,1120]{2,1,0:T(8,128)(2,1)}, bf16[3,96,1120]{2,1,0:T(8,128)(2,1)S(1)}, u32[]{:S(2)}, u32[]{:S(2)}) %collective-permute-start.19) | collective-permute-done | bytes 645152 | tf_op jit(solution)/shard_map/ppermute | solution.py:533
  125.6 6.6 %shard_map.189 = (bf16[4,2,64,384]{3,2,1,0:T(8,128)(2,1)S(1)}, f32[2,2,1,384]{3,2,1,0:T(1,128)S(1)}, bf16[2,2,2048,128]{3,2,1,0:T(8,128)(2,1)S(1)}) custom-call(s32[2,16]{1,0:T(2,128)S(1)} %copy-done.53, s32[6]{0:T(128)S(1)} %stack.95.place, bf16[4,2,64,384]{3,2,1,0:T(8,128)(2,1)S(1)} %bitcast.229, bf16[4,4,2,64,128]{4,3,2,1,0:T(8,128)(2,1)S(1)} %pad_maximum_fusion.14.a_own, ...), custom_call_target="tpu_custom_call" | custom-call | flops 1 | bytes 1 | tf_op jit(solution)/shard_map/pallas_call | solution.py:778
  133.5 12.3 %collective-permute-done.21 = bf16[2,96,1120]{2,1,0:T(8,128)(2,1)S(1)} collective-permute-done((bf16[2,96,1120]{2,1,0:T(8,128)(2,1)S(1)}, bf16[2,96,1120]{2,1,0:T(8,128)(2,1)S(1)}, u32[]{:S(2)}, u32[]{:S(2)}) %collective-permute-start.21) | collective-permute-done | bytes 430112 | tf_op jit(solution)/shard_map/ppermute | solution.py:533
  153.1 11.9 %collective-permute-done.26 = bf16[1,96,1120]{2,1,0:T(8,128)(2,1)S(1)} collective-permute-done((bf16[1,96,1120]{2,1,0:T(8,128)(2,1)S(1)}, bf16[1,96,1120]{2,1,0:T(8,128)(2,1)S(1)}, u32[]{:S(2)}, u32[]{:S(2)}) %collective-permute-start.26) | collective-permute-done | bytes 215072 | tf_op jit(solution)/shard_map/ppermute | solution.py:533
  169.8 7.2 %collective-permute-done.29 = bf16[128,1536]{1,0:T(8,128)(2,1)S(1)} collective-permute-done((bf16[128,1536]{1,0:T(8,128)(2,1)S(1)}, bf16[128,1536]{1,0:T(8,128)(2,1)S(1)}, u32[]{:S(2)}, u32[]{:S(2)}) %collective-permute-start.29) | collective-permute-done | bytes 393248 | tf_op jit(solution)/shard_map/ppermute | solution.py:539
  177.1 3.3 collective-permute-done.34
  180.7 3.7 collective-permute-done.30.refs_6_
  185.3 5.3 shard_map.192
  190.7 2.9 fusion.43
  194.3 3.2 collective-permute-done.37
  199.6 9.9 %collective-permute-done.38 = bf16[128,1536]{1,0:T(8,128)(2,1)S(1)} collective-permute-done((bf16[128,1536]{1,0:T(8,128)(2,1)S(1)}, bf16[128,1536]{1,0:T(8,128)(2,1)S(1)}, u32[]{:S(2)}, u32[]{:S(2)}) %collective-permute-start.38) | collective-permute-done | bytes 393248 | tf_op jit(solution)/shard_map/ppermute | solution.py:539
  209.5 5.5 collective-permute-done.48
  215.8 3.2 collective-permute-done.44
  221.0 2.7 fusion.36
  223.7 3.6 multiply_convert_fusion.3
  235.6 5.5 collective-permute-done.51
  245.1 2.6 multiply_convert_fusion.2
  258.8 2.6 multiply_convert_fusion.1
  269.5 2.6 multiply_convert_fusion
  281.2 9.5 %collective-permute-done.54 = bf16[128,1536]{1,0:T(8,128)(2,1)S(1)} collective-permute-done((bf16[128,1536]{1,0:T(8,128)(2,1)S(1)}, bf16[128,1536]{1,0:T(8,128)(2,1)S(1)}, u32[]{:S(2)}, u32[]{:S(2)}) %collective-permute-start.54) | collective-permute-done | bytes 393248 | tf_op jit(solution)/shard_map/ppermute | solution.py:539
  291.6 3.8 collective-permute-start.59
  301.9 8.4 %shard_map.193 = (bf16[4,1,96,1120]{3,2,1,0:T(8,128)(2,1)S(1)}, bf16[4,1,96,1120]{3,2,1,0:T(8,128)(2,1)S(1)}) custom-call(s32[6]{0:T(128)S(1)} %stack.95.place, bf16[512,1536]{1,0:T(8,128)(2,1)S(1)} %pad_maximum_fusion.refs_0_, bf16[512,1536]{1,0:T(8,128)(2,1)} %copy-done.70, bf16[512,1536]{1,0:T(8,128)(2,1)} %copy-done.71, bf16[512,1536]{1,0:T(8,128)(2,1)} %copy-done.69, ...), custom_call_target="tpu_custom_call" | custom-call | flops 1 | bytes 1 | tf_op jit(solution)/shard_map/pallas_call | solution.py:77
  313.0 2.5 collective-permute-start.61
  315.5 9.3 %shard_map.194 = (bf16[4,1,96,1120]{3,2,1,0:T(8,128)(2,1)S(1)}, bf16[4,1,96,1120]{3,2,1,0:T(8,128)(2,1)}) custom-call(s32[6]{0:T(128)S(1)} %stack.95.place, bf16[512,1536]{1,0:T(8,128)(2,1)S(1)} %pad_maximum_fusion.refs_0_, bf16[512,1536]{1,0:T(8,128)(2,1)} %copy-done.70, bf16[512,1536]{1,0:T(8,128)(2,1)} %copy-done.71, bf16[512,1536]{1,0:T(8,128)(2,1)} %copy-done.69, ...), custom_call_target="tpu_custom_call" | custom-call | flops 1 | bytes 1 | tf_op jit(solution)/shard_map/pallas_call | solution.py:77
  324.8 3.1 collective-permute-done.60
  337.1 4.4 all-to-all-start.2
  347.3 9.3 %shard_map.195 = (bf16[4,1,96,1120]{3,2,1,0:T(8,128)(2,1)S(1)}, bf16[4,1,96,1120]{3,2,1,0:T(8,128)(2,1)}) custom-call(s32[6]{0:T(128)S(1)} %stack.95.place, bf16[512,1536]{1,0:T(8,128)(2,1)S(1)} %copy-done.16, bf16[512,1536]{1,0:T(8,128)(2,1)} %copy-done.79, bf16[512,1536]{1,0:T(8,128)(2,1)} %copy-done.77, bf16[512,1536]{1,0:T(8,128)(2,1)} %copy-done.78, ...), custom_call_target="tpu_custom_call" | custom-call | flops 1 | bytes 1 | tf_op jit(solution)/shard_map/pallas_call | solution.py:77
  362.6 2.6 add_convert_fusion.1
  365.2 5.1 all-to-all-start.3
  374.0 9.5 %shard_map.197 = (bf16[4,2,64,384]{3,2,1,0:T(8,128)(2,1)S(1)}, bf16[4,4,2,64,128]{4,3,2,1,0:T(8,128)(2,1)S(1)}, bf16[4,4,2,64,128]{4,3,2,1,0:T(8,128)(2,1)S(1)}, bf16[2,4,4,2,64,128]{5,4,3,2,1,0:T(8,128)(2,1)S(1)}) custom-call(s32[2,16]{1,0:T(2,128)S(1)} %copy-done.53, s32[6]{0:T(128)S(1)} %stack.95.place, bf16[4,2,64,384]{3,2,1,0:T(8,128)(2,1)S(1)} %bitcast.230, ...), custom_call_target="tpu_custom_call" | custom-call | flops 1 | bytes 1 | tf_op jit(solution)/shard_map/pallas_call | solution.py:921
  387.3 5.5 all-to-all-done.3.uppers
  392.8 2.5 add_convert_fusion.5
  395.8 2.4 convolution_convert_fusion
  402.5 8.4 %shard_map.201 = bf16[4,4,128,1536]{3,2,1,0:T(8,128)(2,1)} custom-call(s32[6]{0:T(128)S(1)} %stack.95.place, bf16[512,560]{1,0:T(8,128)(2,1)S(1)} %copy-done.8, bf16[512,560]{1,0:T(8,128)(2,1)S(1)} %copy-done.10, bf16[512,560]{1,0:T(8,128)(2,1)S(1)} %copy-done.12, bf16[512,560]{1,0:T(8,128)(2,1)S(1)} %copy-done.14, bf16[1536,560]{1,0:T(8,128)(2,1)S(1)} %bitcast.228), custom_call_target="tpu_custom_call" | custom-call | flops 1 | bytes 1 | tf_op jit(solution)/shard_map/pallas_call | solution.py:77
  410.9 7.0 %collective-permute-done.69 = bf16[4,4,2,64,128]{4,3,2,1,0:T(8,128)(2,1)} collective-permute-done((bf16[4,4,2,64,128]{4,3,2,1,0:T(8,128)(2,1)}, bf16[4,4,2,64,128]{4,3,2,1,0:T(8,128)(2,1)}, u32[]{:S(2)}, u32[]{:S(2)}) %collective-permute-start.69) | collective-permute-done | bytes 524320 | tf_op jit(solution)/shard_map/ppermute | solution.py:536
  421.9 8.4 %collective-permute-start.71 = (bf16[4,2,64,128]{3,2,1,0:T(8,128)(2,1)}, bf16[4,2,64,128]{3,2,1,0:T(8,128)(2,1)S(1)}, u32[]{:S(2)}, u32[]{:S(2)}) collective-permute-start(bf16[4,2,64,128]{3,2,1,0:T(8,128)(2,1)} %get-tuple-element.376), channel_id=1, source_target_pairs={{0,24},{4,28},{8,0},{12,4},{16,8},{20,12},{24,16},{28,20},{1,25},{... | collective-permute-start | bytes 393224 | tf_op jit(solution)/shard_map/ppermute | solution.py:533
  431.1 3.4 collective-permute-done.71
  434.5 6.2 %collective-permute-done.72 = bf16[4,2,64,128]{3,2,1,0:T(8,128)(2,1)S(1)} collective-permute-done((bf16[4,2,64,128]{3,2,1,0:T(8,128)(2,1)S(1)}, bf16[4,2,64,128]{3,2,1,0:T(8,128)(2,1)S(1)}, u32[]{:S(2)}, u32[]{:S(2)}) %collective-permute-start.72) | collective-permute-done | bytes 131104 | tf_op jit(solution)/shard_map/ppermute | solution.py:533
  447.0 3.8 all-to-all-start.4
  451.9 2.6 shard_map.205
  454.6 4.8 collective-permute-done.78.got
  464.0 3.6 collective-permute-start.81
  469.5 3.3 collective-permute-done.80
  475.2 3.2 shard_map.208
  481.9 4.6 all-to-all-start.5
  488.4 3.3 collective-permute-done.76.refs_1_
  493.5 2.7 collective-permute-done.84.refs_4_
  498.8 3.7 collective-permute-start.90
  506.7 3.1 convert_add_fusion
  509.8 8.5 %all-to-all-done.5.downs = bf16[4,1,96,1120]{3,2,1,0:T(8,128)(2,1)} async-done(((bf16[4,1,96,1120]{3,2,1,0:T(8,128)(2,1)}), bf16[4,1,96,1120]{3,2,1,0:T(8,128)(2,1)}, u32[]{:S(2)}, u32[]{:S(2)}) %all-to-all-start.5) | async-done | bytes 860192 | tf_op jit(solution)/shard_map/all_to_all | solution.py:596
  518.3 6.2 %shard_map.210 = (f32[192,2240]{1,0:T(8,128)}, f32[192,2240]{1,0:T(8,128)}, f32[192,2240]{1,0:T(8,128)}, f32[192,1]{1,0:T(8,128)S(1)}) custom-call(bf16[4,1,96,1120]{3,2,1,0:T(8,128)(2,1)} %all-to-all-done.2.gates, bf16[4,1,96,1120]{3,2,1,0:T(8,128)(2,1)S(1)} %copy-done.4, bf16[4,1,96,1120]{3,2,1,0:T(8,128)(2,1)} %all-to-all-done.5.downs, ...), custom_call_target="tpu_custom_call" | custom-call | flops 1 | bytes 1 | tf_op jit(solution)/shard_map/pallas_call | solution.py:77
  528.2 12.6 %collective-permute-done.89 = bf16[1,48,1536]{2,1,0:T(8,128)(2,1)} collective-permute-done((bf16[1,48,1536]{2,1,0:T(8,128)(2,1)}, bf16[1,48,1536]{2,1,0:T(8,128)(2,1)}, u32[]{:S(2)}, u32[]{:S(2)}) %collective-permute-start.89) | collective-permute-done | bytes 147488 | tf_op jit(solution)/shard_map/ppermute | solution.py:533
  (545 shorter events, 199.1 us)
Async XLA Ops:
  16.1 18.4 %collective-permute-start.4 = (bf16[128,1536]{1,0:T(8,128)(2,1)S(1)}, bf16[128,1536]{1,0:T(8,128)(2,1)S(1)}, u32[]{:S(2)}, u32[]{:S(2)}) collective-permute-start(bf16[128,1536]{1,0:T(8,128)(2,1)S(1)} %fusion.9.own), channel_id=1, source_target_pairs={{0,2},{1,3},{2,0},{3,1},{4,6},{5,7},{6,4},{7,5},{8,10},{9,11},{10,... | collective-permute-start | bytes 1179656 | tf_op jit(solution)/shard_map/ppermute | solution.py:539
  26.2 15.9 %collective-permute-start.1 = (bf16[208,512]{1,0:T(8,128)(2,1)S(1)}, bf16[208,512]{1,0:T(8,128)(2,1)}, u32[]{:S(2)}, u32[]{:S(2)}) collective-permute-start(bf16[208,512]{1,0:T(8,128)(2,1)S(1)} %pad_maximum_fusion.23.rest_0_), channel_id=1, source_target_pairs={{0,16},{4,20},{8,24},{12,28},{16,0},{20,4},{24,8},{28,12},{1,17},{... | collective-permute-start | bytes 638984 | tf_op jit(solution)/shard_map/ppermute | solution.py:533
  28.8 13.3 %collective-permute-start.2 = (bf16[208,512]{1,0:T(8,128)(2,1)S(1)}, bf16[208,512]{1,0:T(8,128)(2,1)}, u32[]{:S(2)}, u32[]{:S(2)}) collective-permute-start(bf16[208,512]{1,0:T(8,128)(2,1)S(1)} %pad_maximum_fusion.23.rest_0_), channel_id=1, source_target_pairs={{0,24},{4,28},{8,0},{12,4},{16,8},{20,12},{24,16},{28,20},{1,25},{... | collective-permute-start | bytes 638984 | tf_op jit(solution)/shard_map/ppermute | solution.py:533
  49.9 36.6 %all-to-all-start.1 = ((bf16[4,48,1536]{2,1,0:T(8,128)(2,1)}), bf16[4,48,1536]{2,1,0:T(8,128)(2,1)S(1)}, u32[]{:S(2)}, u32[]{:S(2)}) async-start(bf16[4,48,1536]{2,1,0:T(8,128)(2,1)} %broadcast_in_dim.58), calls=%async_computation.1 | async-start | bytes 1179648 | tf_op jit(solution)/shard_map/all_to_all | solution.py:596
  58.2 17.4 %collective-permute-start.8 = (bf16[2,128,1536]{2,1,0:T(8,128)(2,1)}, bf16[2,128,1536]{2,1,0:T(8,128)(2,1)}, u32[]{:S(2)}, u32[]{:S(2)}) collective-permute-start(bf16[2,128,1536]{2,1,0:T(8,128)(2,1)} %pad_maximum_fusion.1), channel_id=1, source_target_pairs={{0,1},{1,0},{2,3},{3,2},{4,5},{5,4},{6,7},{7,6},{8,9},{9,8},{10,11... | collective-permute-start | bytes 2359304 | tf_op jit(solution)/shard_map/ppermute | solution.py:545
  60.4 15.2 %collective-permute-start.7 = (bf16[208,512]{1,0:T(8,128)(2,1)}, bf16[208,512]{1,0:T(8,128)(2,1)S(1)}, u32[]{:S(2)}, u32[]{:S(2)}) collective-permute-start(bf16[208,512]{1,0:T(8,128)(2,1)} %collective-permute-done.2.rest_3_), channel_id=1, source_target_pairs={{0,4},{4,0},{8,12},{12,8},{16,20},{20,16},{24,28},{28,24},{1,5},{5... | collective-permute-start | bytes 638984 | tf_op jit(solution)/shard_map/ppermute | solution.py:536
  62.9 47.0 %collective-permute-start.11 = (bf16[3,96,1120]{2,1,0:T(8,128)(2,1)}, bf16[3,96,1120]{2,1,0:T(8,128)(2,1)}, u32[]{:S(2)}, u32[]{:S(2)}) collective-permute-start(bf16[3,96,1120]{2,1,0:T(8,128)(2,1)} %copy-done.55), channel_id=1, source_target_pairs={{0,8},{4,12},{8,16},{12,20},{16,24},{20,28},{24,0},{28,4},{1,9},{5... | collective-permute-start | bytes 1935368 | tf_op jit(solution)/shard_map/ppermute | solution.py:533
  66.4 43.4 %collective-permute-start.12 = (bf16[3,96,1120]{2,1,0:T(8,128)(2,1)}, bf16[3,96,1120]{2,1,0:T(8,128)(2,1)}, u32[]{:S(2)}, u32[]{:S(2)}) collective-permute-start(bf16[3,96,1120]{2,1,0:T(8,128)(2,1)} %get-tuple-element.202.refs_0_), channel_id=1, source_target_pairs={{0,4},{4,0},{8,12},{12,8},{16,20},{20,16},{24,28},{28,24},{1,5},{5... | collective-permute-start | bytes 1935368 | tf_op jit(solution)/shard_map/ppermute | solution.py:536
  86.5 23.4 %collective-permute-start.9 = (bf16[4,48,1536]{2,1,0:T(8,128)(2,1)S(1)}, bf16[4,48,1536]{2,1,0:T(8,128)(2,1)S(1)}, u32[]{:S(2)}, u32[]{:S(2)}) collective-permute-start(bf16[4,48,1536]{2,1,0:T(8,128)(2,1)S(1)} %all-to-all-done.1.mine), channel_id=1, source_target_pairs={{0,4},{4,0},{8,12},{12,8},{16,20},{20,16},{24,28},{28,24},{1,5},{5... | collective-permute-start | bytes 1769480 | tf_op jit(solution)/shard_map/ppermute | solution.py:536
  88.0 21.9 %collective-permute-start.10 = (bf16[128,1536]{1,0:T(8,128)(2,1)}, bf16[128,1536]{1,0:T(8,128)(2,1)S(1)}, u32[]{:S(2)}, u32[]{:S(2)}) collective-permute-start(bf16[128,1536]{1,0:T(8,128)(2,1)} %bitcast.261), channel_id=1, source_target_pairs={{0,2},{1,3},{2,0},{3,1},{4,6},{5,7},{6,4},{7,5},{8,10},{9,11},{10,... | collective-permute-start | bytes 1179656 | tf_op jit(solution)/shard_map/ppermute | solution.py:539
  108.9 12.9 %collective-permute-start.19 = (bf16[3,96,1120]{2,1,0:T(8,128)(2,1)}, bf16[3,96,1120]{2,1,0:T(8,128)(2,1)S(1)}, u32[]{:S(2)}, u32[]{:S(2)}) collective-permute-start(bf16[3,96,1120]{2,1,0:T(8,128)(2,1)} %copy-done.54), channel_id=1, source_target_pairs={{0,24},{4,28},{8,0},{12,4},{16,8},{20,12},{24,16},{28,20},{1,25},{... | collective-permute-start | bytes 1935368 | tf_op jit(solution)/shard_map/ppermute | solution.py:533
  122.1 23.8 %collective-permute-start.20 = (bf16[3,96,1120]{2,1,0:T(8,128)(2,1)}, bf16[3,96,1120]{2,1,0:T(8,128)(2,1)S(1)}, u32[]{:S(2)}, u32[]{:S(2)}) collective-permute-start(bf16[3,96,1120]{2,1,0:T(8,128)(2,1)} %collective-permute-done.11.refs_1_), channel_id=1, source_target_pairs={{0,4},{4,0},{8,12},{12,8},{16,20},{20,16},{24,28},{28,24},{1,5},{5... | collective-permute-start | bytes 1935368 | tf_op jit(solution)/shard_map/ppermute | solution.py:536
  123.3 22.5 %collective-permute-start.21 = (bf16[2,96,1120]{2,1,0:T(8,128)(2,1)S(1)}, bf16[2,96,1120]{2,1,0:T(8,128)(2,1)S(1)}, u32[]{:S(2)}, u32[]{:S(2)}) collective-permute-start(bf16[2,96,1120]{2,1,0:T(8,128)(2,1)S(1)} %slice.178), channel_id=1, source_target_pairs={{0,16},{4,20},{8,24},{12,28},{16,0},{20,4},{24,8},{28,12},{1,17},{... | collective-permute-start | bytes 1290248 | tf_op jit(solution)/shard_map/ppermute | solution.py:533
  148.1 17.4 %collective-permute-start.27 = (bf16[3,96,1120]{2,1,0:T(8,128)(2,1)S(1)}, bf16[3,96,1120]{2,1,0:T(8,128)(2,1)S(1)}, u32[]{:S(2)}, u32[]{:S(2)}) collective-permute-start(bf16[3,96,1120]{2,1,0:T(8,128)(2,1)S(1)} %collective-permute-done.19.refs_3_), channel_id=1, source_target_pairs={{0,4},{4,0},{8,12},{12,8},{16,20},{20,16},{24,28},{28,24},{1,5},{5... | collective-permute-start | bytes 1935368 | tf_op jit(solution)/shard_map/ppermute | solution.py:536
  150.6 14.9 %collective-permute-start.25 = (bf16[128,1536]{1,0:T(8,128)(2,1)S(1)}, bf16[128,1536]{1,0:T(8,128)(2,1)S(1)}, u32[]{:S(2)}, u32[]{:S(2)}) collective-permute-start(bf16[128,1536]{1,0:T(8,128)(2,1)S(1)} %fusion.10), channel_id=1, source_target_pairs={{0,2},{1,3},{2,0},{3,1},{4,6},{5,7},{6,4},{7,5},{8,10},{9,11},{10,... | collective-permute-start | bytes 1179656 | tf_op jit(solution)/shard_map/ppermute | solution.py:539
  152.9 16.8 %collective-permute-start.28 = (bf16[256,1536]{1,0:T(8,128)(2,1)S(1)}, bf16[256,1536]{1,0:T(8,128)(2,1)S(1)}, u32[]{:S(2)}, u32[]{:S(2)}) collective-permute-start(bf16[256,1536]{1,0:T(8,128)(2,1)S(1)} %pad_maximum_fusion.2), channel_id=1, source_target_pairs={{0,1},{1,0},{2,3},{3,2},{4,5},{5,4},{6,7},{7,6},{8,9},{9,8},{10,11... | collective-permute-start | bytes 2359304 | tf_op jit(solution)/shard_map/ppermute | solution.py:545
  168.1 12.2 %collective-permute-start.34 = (bf16[128,1536]{1,0:T(8,128)(2,1)S(1)}, bf16[128,1536]{1,0:T(8,128)(2,1)S(1)}, u32[]{:S(2)}, u32[]{:S(2)}) collective-permute-start(bf16[128,1536]{1,0:T(8,128)(2,1)S(1)} %multiply_convert_fusion.12), channel_id=1, source_target_pairs={{0,8},{4,12},{8,16},{12,20},{16,24},{20,28},{24,0},{28,4},{1,9},{5... | collective-permute-start | bytes 1179656 | tf_op jit(solution)/shard_map/ppermute | solution.py:533
  168.1 16.3 %collective-permute-start.30 = (bf16[3,96,1120]{2,1,0:T(8,128)(2,1)S(1)}, bf16[3,96,1120]{2,1,0:T(8,128)(2,1)S(1)}, u32[]{:S(2)}, u32[]{:S(2)}) collective-permute-start(bf16[3,96,1120]{2,1,0:T(8,128)(2,1)S(1)} %constant_dynamic-update-slice_fusion.3.refs_2_), channel_id=1, source_target_pairs={{0,4},{4,0},{8,12},{12,8},{16,20},{20,16},{24,28},{28,24},{1,5},{5... | collective-permute-start | bytes 1935368 | tf_op jit(solution)/shard_map/ppermute | solution.py:536
  177.1 21.8 %collective-permute-start.43 = (bf16[128,1536]{1,0:T(8,128)(2,1)S(1)}, bf16[128,1536]{1,0:T(8,128)(2,1)S(1)}, u32[]{:S(2)}, u32[]{:S(2)}) collective-permute-start(bf16[128,1536]{1,0:T(8,128)(2,1)S(1)} %bitcast.264), channel_id=1, source_target_pairs={{0,8},{4,12},{8,16},{12,20},{16,24},{20,28},{24,0},{28,4},{1,9},{5... | collective-permute-start | bytes 1179656 | tf_op jit(solution)/shard_map/ppermute | solution.py:533
  180.3 13.3 %collective-permute-start.35 = (bf16[128,1536]{1,0:T(8,128)(2,1)S(1)}, bf16[128,1536]{1,0:T(8,128)(2,1)S(1)}, u32[]{:S(2)}, u32[]{:S(2)}) collective-permute-start(bf16[128,1536]{1,0:T(8,128)(2,1)S(1)} %collective-permute-done.34), channel_id=1, source_target_pairs={{0,2},{1,3},{2,0},{3,1},{4,6},{5,7},{6,4},{7,5},{8,10},{9,11},{10,... | collective-permute-start | bytes 1179656 | tf_op jit(solution)/shard_map/ppermute | solution.py:539
  180.7 16.8 %collective-permute-start.37 = (bf16[128,1536]{1,0:T(8,128)(2,1)S(1)}, bf16[128,1536]{1,0:T(8,128)(2,1)S(1)}, u32[]{:S(2)}, u32[]{:S(2)}) collective-permute-start(bf16[128,1536]{1,0:T(8,128)(2,1)S(1)} %collective-permute-done.34), channel_id=1, source_target_pairs={{0,8},{4,12},{8,16},{12,20},{16,24},{20,28},{24,0},{28,4},{1,9},{5... | collective-permute-start | bytes 1179656 | tf_op jit(solution)/shard_map/ppermute | solution.py:533
  185.3 35.2 %collective-permute-start.31 = (bf16[256,1536]{1,0:T(8,128)(2,1)}, bf16[256,1536]{1,0:T(8,128)(2,1)}, u32[]{:S(2)}, u32[]{:S(2)}) collective-permute-start(bf16[256,1536]{1,0:T(8,128)(2,1)} %pad_maximum_fusion.3), channel_id=1, source_target_pairs={{0,1},{1,0},{2,3},{3,2},{4,5},{5,4},{6,7},{7,6},{8,9},{9,8},{10,11... | collective-permute-start | bytes 2359304 | tf_op jit(solution)/shard_map/ppermute | solution.py:545
  193.7 39.6 %collective-permute-start.36 = (bf16[256,1536]{1,0:T(8,128)(2,1)S(1)}, bf16[256,1536]{1,0:T(8,128)(2,1)S(1)}, u32[]{:S(2)}, u32[]{:S(2)}) collective-permute-start(bf16[256,1536]{1,0:T(8,128)(2,1)S(1)} %pad_maximum_fusion.4), channel_id=1, source_target_pairs={{0,1},{1,0},{2,3},{3,2},{4,5},{5,4},{6,7},{7,6},{8,9},{9,8},{10,11... | collective-permute-start | bytes 2359304 | tf_op jit(solution)/shard_map/ppermute | solution.py:545
  197.4 12.1 %collective-permute-start.38 = (bf16[128,1536]{1,0:T(8,128)(2,1)S(1)}, bf16[128,1536]{1,0:T(8,128)(2,1)S(1)}, u32[]{:S(2)}, u32[]{:S(2)}) collective-permute-start(bf16[128,1536]{1,0:T(8,128)(2,1)S(1)} %collective-permute-done.37), channel_id=1, source_target_pairs={{0,2},{1,3},{2,0},{3,1},{4,6},{5,7},{6,4},{7,5},{8,10},{9,11},{10,... | collective-permute-start | bytes 1179656 | tf_op jit(solution)/shard_map/ppermute | solution.py:539
  198.9 16.3 %collective-permute-start.40 = (bf16[128,1536]{1,0:T(8,128)(2,1)S(1)}, bf16[128,1536]{1,0:T(8,128)(2,1)S(1)}, u32[]{:S(2)}, u32[]{:S(2)}) collective-permute-start(bf16[128,1536]{1,0:T(8,128)(2,1)S(1)} %collective-permute-done.37), channel_id=1, source_target_pairs={{0,8},{4,12},{8,16},{12,20},{16,24},{20,28},{24,0},{28,4},{1,9},{5... | collective-permute-start | bytes 1179656 | tf_op jit(solution)/shard_map/ppermute | solution.py:533
  198.9 16.2 %collective-permute-start.48 = (bf16[128,1536]{1,0:T(8,128)(2,1)S(1)}, bf16[128,1536]{1,0:T(8,128)(2,1)S(1)}, u32[]{:S(2)}, u32[]{:S(2)}) collective-permute-start(bf16[128,1536]{1,0:T(8,128)(2,1)S(1)} %collective-permute-done.43), channel_id=1, source_target_pairs={{0,2},{1,3},{2,0},{3,1},{4,6},{5,7},{6,4},{7,5},{8,10},{9,11},{10,... | collective-permute-start | bytes 1179656 | tf_op jit(solution)/shard_map/ppermute | solution.py:539
  215.1 37.3 %collective-permute-start.39 = (bf16[256,1536]{1,0:T(8,128)(2,1)S(1)}, bf16[256,1536]{1,0:T(8,128)(2,1)S(1)}, u32[]{:S(2)}, u32[]{:S(2)}) collective-permute-start(bf16[256,1536]{1,0:T(8,128)(2,1)S(1)} %pad_maximum_fusion.5), channel_id=1, source_target_pairs={{0,1},{1,0},{2,3},{3,2},{4,5},{5,4},{6,7},{7,6},{8,9},{9,8},{10,11... | collective-permute-start | bytes 2359304 | tf_op jit(solution)/shard_map/ppermute | solution.py:545
  215.2 26.6 %collective-permute-start.49 = (bf16[256,1536]{1,0:T(8,128)(2,1)S(1)}, bf16[256,1536]{1,0:T(8,128)(2,1)S(1)}, u32[]{:S(2)}, u32[]{:S(2)}) collective-permute-start(bf16[256,1536]{1,0:T(8,128)(2,1)S(1)} %pad_maximum_fusion.8), channel_id=1, source_target_pairs={{0,1},{1,0},{2,3},{3,2},{4,5},{5,4},{6,7},{7,6},{8,9},{9,8},{10,11... | collective-permute-start | bytes 2359304 | tf_op jit(solution)/shard_map/ppermute | solution.py:545
  219.1 16.4 %collective-permute-start.41 = (bf16[128,1536]{1,0:T(8,128)(2,1)S(1)}, bf16[128,1536]{1,0:T(8,128)(2,1)S(1)}, u32[]{:S(2)}, u32[]{:S(2)}) collective-permute-start(bf16[128,1536]{1,0:T(8,128)(2,1)S(1)} %collective-permute-done.40), channel_id=1, source_target_pairs={{0,2},{1,3},{2,0},{3,1},{4,6},{5,7},{6,4},{7,5},{8,10},{9,11},{10,... | collective-permute-start | bytes 1179656 | tf_op jit(solution)/shard_map/ppermute | solution.py:539
  220.5 20.7 %collective-permute-start.45 = (bf16[128,1536]{1,0:T(8,128)(2,1)S(1)}, bf16[128,1536]{1,0:T(8,128)(2,1)S(1)}, u32[]{:S(2)}, u32[]{:S(2)}) collective-permute-start(bf16[128,1536]{1,0:T(8,128)(2,1)S(1)} %collective-permute-done.44), channel_id=1, source_target_pairs={{0,8},{4,12},{8,16},{12,20},{16,24},{20,28},{24,0},{28,4},{1,9},{5... | collective-permute-start | bytes 1179656 | tf_op jit(solution)/shard_map/ppermute | solution.py:533
  235.4 19.4 %collective-permute-start.32 = (bf16[2,128,1536]{2,1,0:T(8,128)(2,1)S(1)}, bf16[2,128,1536]{2,1,0:T(8,128)(2,1)S(1)}, u32[]{:S(2)}, u32[]{:S(2)}) collective-permute-start(bf16[2,128,1536]{2,1,0:T(8,128)(2,1)S(1)} %bitcast.276), channel_id=1, source_target_pairs={{0,1},{1,0},{2,3},{3,2},{4,5},{5,4},{6,7},{7,6},{8,9},{9,8},{10,11... | collective-permute-start | bytes 2359304 | tf_op jit(solution)/shard_map/ppermute | solution.py:545
  241.1 25.3 %collective-permute-start.42 = (bf16[256,1536]{1,0:T(8,128)(2,1)S(1)}, bf16[256,1536]{1,0:T(8,128)(2,1)S(1)}, u32[]{:S(2)}, u32[]{:S(2)}) collective-permute-start(bf16[256,1536]{1,0:T(8,128)(2,1)S(1)} %pad_maximum_fusion.6), channel_id=1, source_target_pairs={{0,1},{1,0},{2,3},{3,2},{4,5},{5,4},{6,7},{7,6},{8,9},{9,8},{10,11... | collective-permute-start | bytes 2359304 | tf_op jit(solution)/shard_map/ppermute | solution.py:545
  241.2 16.1 %collective-permute-start.52 = (bf16[256,1536]{1,0:T(8,128)(2,1)S(1)}, bf16[256,1536]{1,0:T(8,128)(2,1)S(1)}, u32[]{:S(2)}, u32[]{:S(2)}) collective-permute-start(bf16[256,1536]{1,0:T(8,128)(2,1)S(1)} %pad_maximum_fusion.9), channel_id=1, source_target_pairs={{0,1},{1,0},{2,3},{3,2},{4,5},{5,4},{6,7},{7,6},{8,9},{9,8},{10,11... | collective-permute-start | bytes 2359304 | tf_op jit(solution)/shard_map/ppermute | solution.py:545
  241.9 12.3 %collective-permute-start.46 = (bf16[128,1536]{1,0:T(8,128)(2,1)S(1)}, bf16[128,1536]{1,0:T(8,128)(2,1)S(1)}, u32[]{:S(2)}, u32[]{:S(2)}) collective-permute-start(bf16[128,1536]{1,0:T(8,128)(2,1)S(1)} %collective-permute-done.45), channel_id=1, source_target_pairs={{0,2},{1,3},{2,0},{3,1},{4,6},{5,7},{6,4},{7,5},{8,10},{9,11},{10,... | collective-permute-start | bytes 1179656 | tf_op jit(solution)/shard_map/ppermute | solution.py:539
  252.4 24.8 %collective-permute-start.50 = (bf16[2,128,1536]{2,1,0:T(8,128)(2,1)S(1)}, bf16[2,128,1536]{2,1,0:T(8,128)(2,1)S(1)}, u32[]{:S(2)}, u32[]{:S(2)}) collective-permute-start(bf16[2,128,1536]{2,1,0:T(8,128)(2,1)S(1)} %bitcast.275), channel_id=1, source_target_pairs={{0,1},{1,0},{2,3},{3,2},{4,5},{5,4},{6,7},{7,6},{8,9},{9,8},{10,11... | collective-permute-start | bytes 2359304 | tf_op jit(solution)/shard_map/ppermute | solution.py:545
  254.2 13.8 %collective-permute-start.47 = (bf16[256,1536]{1,0:T(8,128)(2,1)S(1)}, bf16[256,1536]{1,0:T(8,128)(2,1)S(1)}, u32[]{:S(2)}, u32[]{:S(2)}) collective-permute-start(bf16[256,1536]{1,0:T(8,128)(2,1)S(1)} %pad_maximum_fusion.7), channel_id=1, source_target_pairs={{0,1},{1,0},{2,3},{3,2},{4,5},{5,4},{6,7},{7,6},{8,9},{9,8},{10,11... | collective-permute-start | bytes 2359304 | tf_op jit(solution)/shard_map/ppermute | solution.py:545
  266.1 13.6 %collective-permute-start.53 = (bf16[2,128,1536]{2,1,0:T(8,128)(2,1)S(1)}, bf16[2,128,1536]{2,1,0:T(8,128)(2,1)S(1)}, u32[]{:S(2)}, u32[]{:S(2)}) collective-permute-start(bf16[2,128,1536]{2,1,0:T(8,128)(2,1)S(1)} %bitcast.277), channel_id=1, source_target_pairs={{0,1},{1,0},{2,3},{3,2},{4,5},{5,4},{6,7},{7,6},{8,9},{9,8},{10,11... | collective-permute-start | bytes 2359304 | tf_op jit(solution)/shard_map/ppermute | solution.py:545
  279.8 15.6 %collective-permute-start.57 = (bf16[2,128,1536]{2,1,0:T(8,128)(2,1)S(1)}, bf16[2,128,1536]{2,1,0:T(8,128)(2,1)S(1)}, u32[]{:S(2)}, u32[]{:S(2)}) collective-permute-start(bf16[2,128,1536]{2,1,0:T(8,128)(2,1)S(1)} %bitcast.278), channel_id=1, source_target_pairs={{0,1},{1,0},{2,3},{3,2},{4,5},{5,4},{6,7},{7,6},{8,9},{9,8},{10,11... | collective-permute-start | bytes 2359304 | tf_op jit(solution)/shard_map/ppermute | solution.py:545
  280.2 19.0 %collective-permute-start.55 = (bf16[128,1536]{1,0:T(8,128)(2,1)S(1)}, bf16[128,1536]{1,0:T(8,128)(2,1)S(1)}, u32[]{:S(2)}, u32[]{:S(2)}) collective-permute-start(bf16[128,1536]{1,0:T(8,128)(2,1)S(1)} %fusion.13), channel_id=1, source_target_pairs={{0,2},{1,3},{2,0},{3,1},{4,6},{5,7},{6,4},{7,5},{8,10},{9,11},{10,... | collective-permute-start | bytes 1179656 | tf_op jit(solution)/shard_map/ppermute | solution.py:539
  291.6 23.9 %collective-permute-start.59 = (bf16[128,1536]{1,0:T(8,128)(2,1)}, bf16[128,1536]{1,0:T(8,128)(2,1)S(1)}, u32[]{:S(2)}, u32[]{:S(2)}) collective-permute-start(bf16[128,1536]{1,0:T(8,128)(2,1)} %fusion.4), channel_id=1, source_target_pairs={{0,24},{4,28},{8,0},{12,4},{16,8},{20,12},{24,16},{28,20},{1,25},{... | collective-permute-start | bytes 1179656 | tf_op jit(solution)/shard_map/ppermute | solution.py:533
  296.4 15.5 %collective-permute-start.58 = (bf16[128,1536]{1,0:T(8,128)(2,1)}, bf16[128,1536]{1,0:T(8,128)(2,1)}, u32[]{:S(2)}, u32[]{:S(2)}) collective-permute-start(bf16[128,1536]{1,0:T(8,128)(2,1)} %fusion.14), channel_id=1, source_target_pairs={{0,2},{1,3},{2,0},{3,1},{4,6},{5,7},{6,4},{7,5},{8,10},{9,11},{10,... | collective-permute-start | bytes 1179656 | tf_op jit(solution)/shard_map/ppermute | solution.py:539
  300.0 27.8 %collective-permute-start.60 = (bf16[128,1536]{1,0:T(8,128)(2,1)}, bf16[128,1536]{1,0:T(8,128)(2,1)S(1)}, u32[]{:S(2)}, u32[]{:S(2)}) collective-permute-start(bf16[128,1536]{1,0:T(8,128)(2,1)} %fusion.3), channel_id=1, source_target_pairs={{0,16},{4,20},{8,24},{12,28},{16,0},{20,4},{24,8},{28,12},{1,17},{... | collective-permute-start | bytes 1179656 | tf_op jit(solution)/shard_map/ppermute | solution.py:533
  310.3 19.6 %collective-permute-start.56 = (bf16[4,1,96,1120]{3,2,1,0:T(8,128)(2,1)S(1)}, bf16[4,1,96,1120]{3,2,1,0:T(8,128)(2,1)}, u32[]{:S(2)}, u32[]{:S(2)}) collective-permute-start(bf16[4,1,96,1120]{3,2,1,0:T(8,128)(2,1)S(1)} %get-tuple-element.252), channel_id=1, source_target_pairs={{0,4},{4,0},{8,12},{12,8},{16,20},{20,16},{24,28},{28,24},{1,5},{5... | collective-permute-start | bytes 2580488 | tf_op jit(solution)/shard_map/ppermute | solution.py:536
  313.0 14.9 %collective-permute-start.61 = (bf16[128,1536]{1,0:T(8,128)(2,1)S(1)}, bf16[128,1536]{1,0:T(8,128)(2,1)S(1)}, u32[]{:S(2)}, u32[]{:S(2)}) collective-permute-start(bf16[128,1536]{1,0:T(8,128)(2,1)S(1)} %fusion.2), channel_id=1, source_target_pairs={{0,8},{4,12},{8,16},{12,20},{16,24},{20,28},{24,0},{28,4},{1,9},{5... | collective-permute-start | bytes 1179656 | tf_op jit(solution)/shard_map/ppermute | solution.py:533
  330.2 26.4 %collective-permute-start.63 = (bf16[4,1,96,1120]{3,2,1,0:T(8,128)(2,1)}, bf16[4,1,96,1120]{3,2,1,0:T(8,128)(2,1)}, u32[]{:S(2)}, u32[]{:S(2)}) collective-permute-start(bf16[4,1,96,1120]{3,2,1,0:T(8,128)(2,1)} %get-tuple-element.269), channel_id=1, source_target_pairs={{0,4},{4,0},{8,12},{12,8},{16,20},{20,16},{24,28},{28,24},{1,5},{5... | collective-permute-start | bytes 2580488 | tf_op jit(solution)/shard_map/ppermute | solution.py:536
  333.0 23.5 %collective-permute-start.62 = (bf16[128,1536]{1,0:T(8,128)(2,1)S(1)}, bf16[128,1536]{1,0:T(8,128)(2,1)S(1)}, u32[]{:S(2)}, u32[]{:S(2)}) collective-permute-start(bf16[128,1536]{1,0:T(8,128)(2,1)S(1)} %get-tuple-element.288.own), channel_id=1, source_target_pairs={{0,2},{1,3},{2,0},{3,1},{4,6},{5,7},{6,4},{7,5},{8,10},{9,11},{10,... | collective-permute-start | bytes 1179656 | tf_op jit(solution)/shard_map/ppermute | solution.py:539
  337.1 25.5 %all-to-all-start.2 = ((bf16[4,1,96,1120]{3,2,1,0:T(8,128)(2,1)}), bf16[4,1,96,1120]{3,2,1,0:T(8,128)(2,1)}, u32[]{:S(2)}, u32[]{:S(2)}) async-start(bf16[4,1,96,1120]{3,2,1,0:T(8,128)(2,1)} %add_convert_fusion.2), calls=%async_computation.2 | async-start | bytes 1769472 | tf_op jit(solution)/shard_map/all_to_all | solution.py:596
  365.2 27.6 %all-to-all-start.3 = ((bf16[4,1,96,1120]{3,2,1,0:T(8,128)(2,1)}), bf16[4,1,96,1120]{3,2,1,0:T(8,128)(2,1)S(1)}, u32[]{:S(2)}, u32[]{:S(2)}) async-start(bf16[4,1,96,1120]{3,2,1,0:T(8,128)(2,1)} %add_convert_fusion.1), calls=%async_computation.3 | async-start | bytes 1769472 | tf_op jit(solution)/shard_map/all_to_all | solution.py:596
  370.3 136.4 %reduce-scatter.3.cloned.1.call-start = ((), (), s32[]{:S(2)}) async-start(), calls=%async_computation.8 | async-start | bytes 7864320 | tf_op jit(solution)/shard_map/reduce_scatter | solution.py:974
  384.7 26.2 %collective-permute-start.70 = (bf16[4,1,96,1120]{3,2,1,0:T(8,128)(2,1)}, bf16[4,1,96,1120]{3,2,1,0:T(8,128)(2,1)}, u32[]{:S(2)}, u32[]{:S(2)}) collective-permute-start(bf16[4,1,96,1120]{3,2,1,0:T(8,128)(2,1)} %get-tuple-element.296), channel_id=1, source_target_pairs={{0,4},{4,0},{8,12},{12,8},{16,20},{20,16},{24,28},{28,24},{1,5},{5... | collective-permute-start | bytes 2580488 | tf_op jit(solution)/shard_map/ppermute | solution.py:536
  395.3 22.6 %collective-permute-start.69 = (bf16[4,4,2,64,128]{4,3,2,1,0:T(8,128)(2,1)}, bf16[4,4,2,64,128]{4,3,2,1,0:T(8,128)(2,1)}, u32[]{:S(2)}, u32[]{:S(2)}) collective-permute-start(bf16[4,4,2,64,128]{4,3,2,1,0:T(8,128)(2,1)} %add_convert_fusion.5), channel_id=1, source_target_pairs={{0,4},{4,0},{8,12},{12,8},{16,20},{20,16},{24,28},{28,24},{1,5},{5... | collective-permute-start | bytes 1572872 | tf_op jit(solution)/shard_map/ppermute | solution.py:536
  417.9 22.8 %collective-permute-start.74 = (bf16[2,2,48,1536]{3,2,1,0:T(8,128)(2,1)}, bf16[2,2,48,1536]{3,2,1,0:T(8,128)(2,1)S(1)}, u32[]{:S(2)}, u32[]{:S(2)}) collective-permute-start(bf16[2,2,48,1536]{3,2,1,0:T(8,128)(2,1)} %copy-done.57), channel_id=1, source_target_pairs={{0,2},{1,3},{2,0},{3,1},{4,6},{5,7},{6,4},{7,5},{8,10},{9,11},{10,... | collective-permute-start | bytes 1769480 | tf_op jit(solution)/shard_map/ppermute | solution.py:539
  418.5 22.2 %collective-permute-start.75 = (bf16[4,1,4,48,384]{4,3,2,1,0:T(8,128)(2,1)}, bf16[4,1,4,48,384]{4,3,2,1,0:T(8,128)(2,1)}, u32[]{:S(2)}, u32[]{:S(2)}) collective-permute-start(bf16[4,1,4,48,384]{4,3,2,1,0:T(8,128)(2,1)} %copy-done.56), channel_id=1, source_target_pairs={{0,4},{4,0},{8,12},{12,8},{16,20},{20,16},{24,28},{28,24},{1,5},{5... | collective-permute-start | bytes 1769480 | tf_op jit(solution)/shard_map/ppermute | solution.py:536
  421.9 12.6 %collective-permute-start.71 = (bf16[4,2,64,128]{3,2,1,0:T(8,128)(2,1)}, bf16[4,2,64,128]{3,2,1,0:T(8,128)(2,1)S(1)}, u32[]{:S(2)}, u32[]{:S(2)}) collective-permute-start(bf16[4,2,64,128]{3,2,1,0:T(8,128)(2,1)} %get-tuple-element.376), channel_id=1, source_target_pairs={{0,24},{4,28},{8,0},{12,4},{16,8},{20,12},{24,16},{28,20},{1,25},{... | collective-permute-start | bytes 393224 | tf_op jit(solution)/shard_map/ppermute | solution.py:533
  447.0 26.7 %all-to-all-start.4 = ((bf16[4,1,4,48,384]{4,3,2,1,0:T(8,128)(2,1)}), bf16[4,1,4,48,384]{4,3,2,1,0:T(8,128)(2,1)S(1)}, u32[]{:S(2)}, u32[]{:S(2)}) async-start(bf16[4,1,4,48,384]{4,3,2,1,0:T(8,128)(2,1)} %add_convert_fusion.3), calls=%async_computation.6 | async-start | bytes 1179648 | tf_op jit(solution)/shard_map/all_to_all | solution.py:596
  459.4 14.8 %collective-permute-start.83 = (bf16[4,1,48,1536]{3,2,1,0:T(8,128)(2,1)}, bf16[4,1,48,1536]{3,2,1,0:T(8,128)(2,1)}, u32[]{:S(2)}, u32[]{:S(2)}) collective-permute-start(bf16[4,1,48,1536]{3,2,1,0:T(8,128)(2,1)} %get-tuple-element.324), channel_id=1, source_target_pairs={{0,4},{4,0},{8,12},{12,8},{16,20},{20,16},{24,28},{28,24},{1,5},{5... | collective-permute-start | bytes 1769480 | tf_op jit(solution)/shard_map/ppermute | solution.py:536
  479.6 27.1 %collective-permute-start.86 = (bf16[2,128,1536]{2,1,0:T(8,128)(2,1)}, bf16[2,128,1536]{2,1,0:T(8,128)(2,1)}, u32[]{:S(2)}, u32[]{:S(2)}) collective-permute-start(bf16[2,128,1536]{2,1,0:T(8,128)(2,1)} %get-tuple-element.333), channel_id=1, source_target_pairs={{0,1},{1,0},{2,3},{3,2},{4,5},{5,4},{6,7},{7,6},{8,9},{9,8},{10,11... | collective-permute-start | bytes 2359304 | tf_op jit(solution)/shard_map/ppermute | solution.py:545
  481.9 36.4 %all-to-all-start.5 = ((bf16[4,1,96,1120]{3,2,1,0:T(8,128)(2,1)}), bf16[4,1,96,1120]{3,2,1,0:T(8,128)(2,1)}, u32[]{:S(2)}, u32[]{:S(2)}) async-start(bf16[4,1,96,1120]{3,2,1,0:T(8,128)(2,1)} %add_convert_fusion), calls=%async_computation.7 | async-start | bytes 1769472 | tf_op jit(solution)/shard_map/all_to_all | solution.py:596
  486.5 60.5 %reduce-scatter.5.cloned.1.call-start = ((), (), s32[]{:S(2)}) async-start(), calls=%async_computation.9 | async-start | bytes 1966080 | tf_op jit(solution)/shard_map/reduce_scatter | solution.py:1004
  498.8 29.4 %collective-permute-start.90 = (bf16[1,48,1536]{2,1,0:T(8,128)(2,1)}, bf16[1,48,1536]{2,1,0:T(8,128)(2,1)}, u32[]{:S(2)}, u32[]{:S(2)}) collective-permute-start(bf16[1,48,1536]{2,1,0:T(8,128)(2,1)} %get-tuple-element.341), channel_id=1, source_target_pairs={{0,24},{4,28},{8,0},{12,4},{16,8},{20,12},{24,16},{28,20},{1,25},{... | collective-permute-start | bytes 442376 | tf_op jit(solution)/shard_map/ppermute | solution.py:533
  502.6 38.2 %collective-permute-start.89 = (bf16[1,48,1536]{2,1,0:T(8,128)(2,1)}, bf16[1,48,1536]{2,1,0:T(8,128)(2,1)}, u32[]{:S(2)}, u32[]{:S(2)}) collective-permute-start(bf16[1,48,1536]{2,1,0:T(8,128)(2,1)} %get-tuple-element.340), channel_id=1, source_target_pairs={{0,16},{4,20},{8,24},{12,28},{16,0},{20,4},{24,8},{28,12},{1,17},{... | collective-permute-start | bytes 442376 | tf_op jit(solution)/shard_map/ppermute | solution.py:533
  502.6 38.2 %collective-permute-start.88 = (bf16[1,48,1536]{2,1,0:T(8,128)(2,1)S(1)}, bf16[1,48,1536]{2,1,0:T(8,128)(2,1)}, u32[]{:S(2)}, u32[]{:S(2)}) collective-permute-start(bf16[1,48,1536]{2,1,0:T(8,128)(2,1)S(1)} %get-tuple-element.339), channel_id=1, source_target_pairs={{0,8},{4,12},{8,16},{12,20},{16,24},{20,28},{24,0},{28,4},{1,9},{5... | collective-permute-start | bytes 442376 | tf_op jit(solution)/shard_map/ppermute | solution.py:533
  526.0 17.1 %collective-permute-start.87 = (bf16[128,1536]{1,0:T(8,128)(2,1)S(1)}, bf16[128,1536]{1,0:T(8,128)(2,1)S(1)}, u32[]{:S(2)}, u32[]{:S(2)}) collective-permute-start(bf16[128,1536]{1,0:T(8,128)(2,1)S(1)} %fusion.15), channel_id=1, source_target_pairs={{0,2},{1,3},{2,0},{3,1},{4,6},{5,7},{6,4},{7,5},{8,10},{9,11},{10,... | collective-permute-start | bytes 1179656 | tf_op jit(solution)/shard_map/ppermute | solution.py:539
  526.1 16.5 %collective-permute-start.92 = (f32[48]{0:T(128)S(1)}, f32[48]{0:T(128)S(1)}, u32[]{:S(2)}, u32[]{:S(2)}) collective-permute-start(f32[48]{0:T(128)S(1)} %fusion.34), channel_id=1, source_target_pairs={{0,2},{1,3},{2,0},{3,1},{4,6},{5,7},{6,4},{7,5},{8,10},{9,11},{10,... | collective-permute-start | bytes 584 | tf_op jit(solution)/shard_map/ppermute | solution.py:539
  (136 other events, 1025.6 us)
Sparse Core Ops, SparseCore 0:
  418.0 62.4 reduce-scatter.2
  506.8 40.1 reduce-scatter.4

commit v6 on v5

--- a/solution.py
+++ b/solution.py
@@ -299,14 +299,19 @@
 
 
 def project_kernel(transposed, place, *refs):
-    count = (len(refs) - 2) // 2
-    lefts, rights, (keep, send) = refs[:count], refs[count : 2 * count], refs[2 * count :]
+    lefts, (weights, keep, send) = refs[:-3], refs[-3:]
     u = place[AT_U]
     dot = dot_nt if transposed else dot_nn
+    rights, start = [], 0
+    for left in lefts:
+        size = left.shape[-1]
+        at = slice(start, start + size)
+        rights.append(weights[:, at] if transposed else weights[at])
+        start += size
     for at, target, spot in ((1, send, 0), (3, send, 1), (0, keep, 0), (2, keep, 1)):
         total = None
         for left, right in zip(lefts, rights):
-            part = dot(left[u ^ at], right[...])
+            part = dot(left[u ^ at], right)
             total = part if total is None else total + part
         target[spot] = total.astype(target.dtype)
 
@@ -894,9 +899,7 @@
     mid_now = after(mid_all, gate_send, *mid_parts, back_pieces[0])
     upper_keep, upper_send = weight_grad(mid_now, upper_grads)
     gate_got = grid.swap_x(gate_send)
-    first, gate_got, upper_send, *back_pieces = together(
-        mid_parts[0], gate_got, upper_send, *back_pieces
-    )
+    first, upper_send, *back_pieces = together(mid_parts[0], upper_send, *back_pieces)
     mid_grad = first + sum(piece.astype(F32) for piece in back_pieces)
 
     hidden_grad = grad_rows + norm_back(mid_grad, unit_two, factor_two)
@@ -1030,8 +1033,7 @@
         [
             query_grad.reshape(ulys, count, width),
             kind_now.reshape(ulys, count, HEAD_DIM),
-            qkv_part[:, :width],
-            qkv_part[:, width:],
+            qkv_part,
         ],
         [like((2, count, model), F32), like((2, count, model))],
     )

time: 564 us -> 564 us (level)
    unnamed x206 -> x210, local copies, waits for them, and re-layouts: 30.4 us -> 31.9 us
  transfers between devices with their start and end apart: 101 -> 101, of which waited for: 46 -> 47; matrix products, arithmetic and copies ran while one was open for 17% -> 16% of each run, Pallas kernels for 16% -> 16%
where the time goes in v6:
time: 564 us; the launch traced here: 557 us
  waiting for transfers between devices  199 us (35%)
  starting transfers between devices  112 us (20%)
  Pallas kernels  96.2 us (17%)
  local copies, waits for them, and re-layouts  47.7 us (8%)
  other arithmetic  44.7 us (8%)
  matrix products  40.7 us (7%)
  between operations  16.4 us (3%)
    ppermute x28, waiting for transfers between devices, to_z(): return lax.ppermute(value, 'blk', pairs)  98.3 us
    pallas_call x23, Pallas kernels, call(): pl.pallas_call(kernel, grid_spec=pltpu.PrefetchScalarGridSpec(num_scalar_...  76.2 us
    ppermute x21, waiting for transfers between devices, swap_y(): return lax.ppermute(value, 'uly', [(i, i ^ 2) for i in range(self.ulys)])  47.5 us
    ppermute x28, starting transfers between devices, to_z(): return lax.ppermute(value, 'blk', pairs)  35.3 us
    unnamed x210, local copies, waits for them, and re-layouts  31.9 us
    ppermute x17, waiting for transfers between devices, swap_x(): return lax.ppermute(value, 'blk', [(i, i ^ 1) for i in range(self.blocks)])  27.7 us
    dot_general x12, matrix products, matmul(): return jnp.dot(left, right, preferred_element_type=F32)  25.7 us
    all_to_all x5, starting transfers between devices, exchange_z_all(): lax.all_to_all(parts, 'blk', split_axis=0, concat_axis=0, axis_index_grou...  24.5 us
  transfers between devices with their start and end apart: 101, of which 47 were waited for; matrix products, arithmetic and copies ran while one was open for 16% of the time, Pallas kernels for 16%

profile of v6, /device:TPU:0, one launch (start us, length us, event | category | flops | bytes accessed | tf_op | source)
XLA Modules:
  0.0 556.5 jit_solution(2481375234662265193)
XLA Ops:
  10.6 4.2 all-to-all-start
  16.1 2.8 collective-permute-start.4
  26.2 2.6 collective-permute-start.1
  31.8 2.7 collective-permute-done.rest_1_
  34.5 7.6 %collective-permute-done.1.rest_2_ = bf16[208,512]{1,0:T(8,128)(2,1)} collective-permute-done((bf16[208,512]{1,0:T(8,128)(2,1)S(1)}, bf16[208,512]{1,0:T(8,128)(2,1)}, u32[]{:S(2)}, u32[]{:S(2)}) %collective-permute-start.1) | collective-permute-done | bytes 213024 | tf_op jit(solution)/shard_map/ppermute | solution.py:538
  43.4 3.0 shard_map.186
  49.9 7.4 %all-to-all-start.1 = ((bf16[4,48,1536]{2,1,0:T(8,128)(2,1)}), bf16[4,48,1536]{2,1,0:T(8,128)(2,1)S(1)}, u32[]{:S(2)}, u32[]{:S(2)}) async-start(bf16[4,48,1536]{2,1,0:T(8,128)(2,1)} %broadcast_in_dim.58), calls=%async_computation.1 | async-start | bytes 1179648 | tf_op jit(solution)/shard_map/all_to_all | solution.py:601
  71.0 4.6 collective-permute-done.7.rest_7_
  76.5 6.1 %shard_map.187 = (bf16[4,128,1536]{2,1,0:T(8,128)(2,1)S(1)}, bf16[8,192,512]{2,1,0:T(8,128)(2,1)}, bf16[4,128,384]{2,1,0:T(8,128)(2,1)S(1)}, bf16[4,128,128]{2,1,0:T(8,128)(2,1)S(1)}) custom-call(s32[6]{0:T(128)S(1)} %stack.95.place, bf16[128,1536]{1,0:T(8,128)(2,1)S(1)} %fusion.9.own, bf16[128,1536]{1,0:T(8,128)(2,1)S(1)} %collective-permute-done.4.near, ...), custom_call_target="tpu_custom_call" | custom-call | flops 1 | bytes 1 | tf_op jit(solution)/shard_map/pallas_call | solution.py:77
  88.6 6.5 %collective-permute-done.13 = bf16[4,128,128]{2,1,0:T(8,128)(2,1)S(1)} collective-permute-done((bf16[4,128,128]{2,1,0:T(8,128)(2,1)}, bf16[4,128,128]{2,1,0:T(8,128)(2,1)S(1)}, u32[]{:S(2)}, u32[]{:S(2)}) %collective-permute-start.13) | collective-permute-done | bytes 131104 | tf_op jit(solution)/shard_map/ppermute | solution.py:538
  95.1 7.3 %collective-permute-done.14 = bf16[4,128,128]{2,1,0:T(8,128)(2,1)S(1)} collective-permute-done((bf16[4,128,128]{2,1,0:T(8,128)(2,1)}, bf16[4,128,128]{2,1,0:T(8,128)(2,1)S(1)}, u32[]{:S(2)}, u32[]{:S(2)}) %collective-permute-start.14) | collective-permute-done | bytes 131104 | tf_op jit(solution)/shard_map/ppermute | solution.py:538
  104.7 4.2 collective-permute-done.15
  112.0 9.8 %collective-permute-done.19.refs_3_ = bf16[3,96,1120]{2,1,0:T(8,128)(2,1)S(1)} collective-permute-done((bf16[3,96,1120]{2,1,0:T(8,128)(2,1)}, bf16[3,96,1120]{2,1,0:T(8,128)(2,1)S(1)}, u32[]{:S(2)}, u32[]{:S(2)}) %collective-permute-start.19) | collective-permute-done | bytes 645152 | tf_op jit(solution)/shard_map/ppermute | solution.py:538
  125.5 8.6 %shard_map.189 = (bf16[4,2,64,384]{3,2,1,0:T(8,128)(2,1)S(1)}, f32[2,2,1,384]{3,2,1,0:T(1,128)S(1)}, bf16[2,2,2048,128]{3,2,1,0:T(8,128)(2,1)S(1)}) custom-call(s32[2,16]{1,0:T(2,128)S(1)} %copy-done.51, s32[6]{0:T(128)S(1)} %stack.95.place, bf16[4,2,64,384]{3,2,1,0:T(8,128)(2,1)S(1)} %bitcast.229, bf16[4,4,2,64,128]{4,3,2,1,0:T(8,128)(2,1)S(1)} %pad_maximum_fusion.14.a_own, ...), custom_call_target="tpu_custom_call" | custom-call | flops 1 | bytes 1 | tf_op jit(solution)/shard_map/pallas_call | solution.py:783
  135.4 10.4 %collective-permute-done.21 = bf16[2,96,1120]{2,1,0:T(8,128)(2,1)S(1)} collective-permute-done((bf16[2,96,1120]{2,1,0:T(8,128)(2,1)S(1)}, bf16[2,96,1120]{2,1,0:T(8,128)(2,1)S(1)}, u32[]{:S(2)}, u32[]{:S(2)}) %collective-permute-start.21) | collective-permute-done | bytes 430112 | tf_op jit(solution)/shard_map/ppermute | solution.py:538
  153.1 11.9 %collective-permute-done.26 = bf16[1,96,1120]{2,1,0:T(8,128)(2,1)S(1)} collective-permute-done((bf16[1,96,1120]{2,1,0:T(8,128)(2,1)S(1)}, bf16[1,96,1120]{2,1,0:T(8,128)(2,1)S(1)}, u32[]{:S(2)}, u32[]{:S(2)}) %collective-permute-start.26) | collective-permute-done | bytes 215072 | tf_op jit(solution)/shard_map/ppermute | solution.py:538
  169.8 7.3 %collective-permute-done.29 = bf16[128,1536]{1,0:T(8,128)(2,1)S(1)} collective-permute-done((bf16[128,1536]{1,0:T(8,128)(2,1)S(1)}, bf16[128,1536]{1,0:T(8,128)(2,1)S(1)}, u32[]{:S(2)}, u32[]{:S(2)}) %collective-permute-start.29) | collective-permute-done | bytes 393248 | tf_op jit(solution)/shard_map/ppermute | solution.py:544
  177.1 3.3 collective-permute-done.34
  180.7 3.7 collective-permute-done.30.refs_6_
  185.4 5.4 shard_map.192
  190.7 2.9 fusion.43
  194.3 3.2 collective-permute-done.37
  199.7 9.8 %collective-permute-done.38 = bf16[128,1536]{1,0:T(8,128)(2,1)S(1)} collective-permute-done((bf16[128,1536]{1,0:T(8,128)(2,1)S(1)}, bf16[128,1536]{1,0:T(8,128)(2,1)S(1)}, u32[]{:S(2)}, u32[]{:S(2)}) %collective-permute-start.38) | collective-permute-done | bytes 393248 | tf_op jit(solution)/shard_map/ppermute | solution.py:544
  209.6 5.5 collective-permute-done.48
  215.9 3.2 collective-permute-done.44
  221.1 2.7 fusion.36
  223.7 3.8 multiply_convert_fusion.3
  236.0 5.5 collective-permute-done.51
  244.5 2.6 multiply_convert_fusion.2
  258.0 2.6 multiply_convert_fusion.1
  268.6 2.6 multiply_convert_fusion
  280.4 9.5 %collective-permute-done.54 = bf16[128,1536]{1,0:T(8,128)(2,1)S(1)} collective-permute-done((bf16[128,1536]{1,0:T(8,128)(2,1)S(1)}, bf16[128,1536]{1,0:T(8,128)(2,1)S(1)}, u32[]{:S(2)}, u32[]{:S(2)}) %collective-permute-start.54) | collective-permute-done | bytes 393248 | tf_op jit(solution)/shard_map/ppermute | solution.py:544
  290.7 3.8 collective-permute-start.58
  301.1 8.4 %shard_map.193 = (bf16[4,1,96,1120]{3,2,1,0:T(8,128)(2,1)S(1)}, bf16[4,1,96,1120]{3,2,1,0:T(8,128)(2,1)S(1)}) custom-call(s32[6]{0:T(128)S(1)} %stack.95.place, bf16[512,1536]{1,0:T(8,128)(2,1)S(1)} %pad_maximum_fusion.refs_0_, bf16[512,1536]{1,0:T(8,128)(2,1)} %copy-done.70, bf16[512,1536]{1,0:T(8,128)(2,1)} %copy-done.71, bf16[512,1536]{1,0:T(8,128)(2,1)} %copy-done.67, ...), custom_call_target="tpu_custom_call" | custom-call | flops 1 | bytes 1 | tf_op jit(solution)/shard_map/pallas_call | solution.py:77
  312.3 2.4 collective-permute-start.60
  314.7 9.3 %shard_map.194 = (bf16[4,1,96,1120]{3,2,1,0:T(8,128)(2,1)S(1)}, bf16[4,1,96,1120]{3,2,1,0:T(8,128)(2,1)}) custom-call(s32[6]{0:T(128)S(1)} %stack.95.place, bf16[512,1536]{1,0:T(8,128)(2,1)S(1)} %pad_maximum_fusion.refs_0_, bf16[512,1536]{1,0:T(8,128)(2,1)} %copy-done.70, bf16[512,1536]{1,0:T(8,128)(2,1)} %copy-done.71, bf16[512,1536]{1,0:T(8,128)(2,1)} %copy-done.67, ...), custom_call_target="tpu_custom_call" | custom-call | flops 1 | bytes 1 | tf_op jit(solution)/shard_map/pallas_call | solution.py:77
  324.0 3.0 collective-permute-done.59
  327.4 2.8 collective-permute-done.62
  334.6 4.4 all-to-all-start.2
  344.7 9.3 %shard_map.195 = (bf16[4,1,96,1120]{3,2,1,0:T(8,128)(2,1)S(1)}, bf16[4,1,96,1120]{3,2,1,0:T(8,128)(2,1)}) custom-call(s32[6]{0:T(128)S(1)} %stack.95.place, bf16[512,1536]{1,0:T(8,128)(2,1)S(1)} %copy-done.16, bf16[512,1536]{1,0:T(8,128)(2,1)} %copy-done.81, bf16[512,1536]{1,0:T(8,128)(2,1)} %copy-done.79, bf16[512,1536]{1,0:T(8,128)(2,1)} %copy-done.80, ...), custom_call_target="tpu_custom_call" | custom-call | flops 1 | bytes 1 | tf_op jit(solution)/shard_map/pallas_call | solution.py:77
  360.5 2.5 add_convert_fusion.1
  363.1 4.7 all-to-all-start.3
  371.5 11.5 %shard_map.197 = (bf16[4,2,64,384]{3,2,1,0:T(8,128)(2,1)S(1)}, bf16[4,4,2,64,128]{4,3,2,1,0:T(8,128)(2,1)S(1)}, bf16[4,4,2,64,128]{4,3,2,1,0:T(8,128)(2,1)S(1)}, bf16[2,4,4,2,64,128]{5,4,3,2,1,0:T(8,128)(2,1)S(1)}) custom-call(s32[2,16]{1,0:T(2,128)S(1)} %copy-done.51, s32[6]{0:T(128)S(1)} %stack.95.place, bf16[4,2,64,384]{3,2,1,0:T(8,128)(2,1)S(1)} %bitcast.230, ...), custom_call_target="tpu_custom_call" | custom-call | flops 1 | bytes 1 | tf_op jit(solution)/shard_map/pallas_call | solution.py:924
  386.8 3.5 all-to-all-done.3.uppers
  390.3 2.5 add_convert_fusion.5
  393.4 2.4 convolution_convert_fusion
  400.9 8.4 %shard_map.201 = bf16[4,4,128,1536]{3,2,1,0:T(8,128)(2,1)} custom-call(s32[6]{0:T(128)S(1)} %stack.95.place, bf16[512,560]{1,0:T(8,128)(2,1)S(1)} %copy-done.8, bf16[512,560]{1,0:T(8,128)(2,1)S(1)} %copy-done.10, bf16[512,560]{1,0:T(8,128)(2,1)S(1)} %copy-done.12, bf16[512,560]{1,0:T(8,128)(2,1)S(1)} %copy-done.14, bf16[1536,560]{1,0:T(8,128)(2,1)S(1)} %bitcast.228), custom_call_target="tpu_custom_call" | custom-call | flops 1 | bytes 1 | tf_op jit(solution)/shard_map/pallas_call | solution.py:77
  409.3 8.1 %collective-permute-done.69 = bf16[4,4,2,64,128]{4,3,2,1,0:T(8,128)(2,1)} collective-permute-done((bf16[4,4,2,64,128]{4,3,2,1,0:T(8,128)(2,1)}, bf16[4,4,2,64,128]{4,3,2,1,0:T(8,128)(2,1)}, u32[]{:S(2)}, u32[]{:S(2)}) %collective-permute-start.69) | collective-permute-done | bytes 524320 | tf_op jit(solution)/shard_map/ppermute | solution.py:541
  422.2 5.1 collective-permute-start.71
  431.7 7.7 %collective-permute-done.72 = bf16[4,2,64,128]{3,2,1,0:T(8,128)(2,1)S(1)} collective-permute-done((bf16[4,2,64,128]{3,2,1,0:T(8,128)(2,1)}, bf16[4,2,64,128]{3,2,1,0:T(8,128)(2,1)S(1)}, u32[]{:S(2)}, u32[]{:S(2)}) %collective-permute-start.72) | collective-permute-done | bytes 131104 | tf_op jit(solution)/shard_map/ppermute | solution.py:538
  447.1 3.5 all-to-all-start.4
  452.5 2.6 shard_map.205
  455.1 4.3 collective-permute-done.78.got
  463.6 3.5 collective-permute-start.81
  469.0 3.3 collective-permute-done.80
  475.7 2.8 shard_map.208
  482.0 4.6 all-to-all-start.5
  487.7 4.1 collective-permute-done.76.refs_1_
  493.1 3.3 collective-permute-done.84.refs_4_
  498.3 3.7 collective-permute-start.90
  505.9 3.1 convert_add_fusion
  509.0 10.9 %all-to-all-done.5.downs = bf16[4,1,96,1120]{3,2,1,0:T(8,128)(2,1)} async-done(((bf16[4,1,96,1120]{3,2,1,0:T(8,128)(2,1)}), bf16[4,1,96,1120]{3,2,1,0:T(8,128)(2,1)}, u32[]{:S(2)}, u32[]{:S(2)}) %all-to-all-start.5) | async-done | bytes 860192 | tf_op jit(solution)/shard_map/all_to_all | solution.py:601
  519.9 6.2 %shard_map.210 = (f32[192,2240]{1,0:T(8,128)}, f32[192,2240]{1,0:T(8,128)}, f32[192,2240]{1,0:T(8,128)}, f32[192,1]{1,0:T(8,128)S(1)}) custom-call(bf16[4,1,96,1120]{3,2,1,0:T(8,128)(2,1)} %all-to-all-done.2.gates, bf16[4,1,96,1120]{3,2,1,0:T(8,128)(2,1)S(1)} %copy-done.4, bf16[4,1,96,1120]{3,2,1,0:T(8,128)(2,1)} %all-to-all-done.5.downs, ...), custom_call_target="tpu_custom_call" | custom-call | flops 1 | bytes 1 | tf_op jit(solution)/shard_map/pallas_call | solution.py:77
  529.8 11.3 %collective-permute-done.89 = bf16[1,48,1536]{2,1,0:T(8,128)(2,1)} collective-permute-done((bf16[1,48,1536]{2,1,0:T(8,128)(2,1)S(1)}, bf16[1,48,1536]{2,1,0:T(8,128)(2,1)}, u32[]{:S(2)}, u32[]{:S(2)}) %collective-permute-start.89) | collective-permute-done | bytes 147488 | tf_op jit(solution)/shard_map/ppermute | solution.py:538
  (547 shorter events, 200.0 us)
Async XLA Ops:
  16.1 18.3 %collective-permute-start.4 = (bf16[128,1536]{1,0:T(8,128)(2,1)S(1)}, bf16[128,1536]{1,0:T(8,128)(2,1)S(1)}, u32[]{:S(2)}, u32[]{:S(2)}) collective-permute-start(bf16[128,1536]{1,0:T(8,128)(2,1)S(1)} %fusion.9.own), channel_id=1, source_target_pairs={{0,2},{1,3},{2,0},{3,1},{4,6},{5,7},{6,4},{7,5},{8,10},{9,11},{10,... | collective-permute-start | bytes 1179656 | tf_op jit(solution)/shard_map/ppermute | solution.py:544
  26.2 15.9 %collective-permute-start.1 = (bf16[208,512]{1,0:T(8,128)(2,1)S(1)}, bf16[208,512]{1,0:T(8,128)(2,1)}, u32[]{:S(2)}, u32[]{:S(2)}) collective-permute-start(bf16[208,512]{1,0:T(8,128)(2,1)S(1)} %pad_maximum_fusion.23.rest_0_), channel_id=1, source_target_pairs={{0,16},{4,20},{8,24},{12,28},{16,0},{20,4},{24,8},{28,12},{1,17},{... | collective-permute-start | bytes 638984 | tf_op jit(solution)/shard_map/ppermute | solution.py:538
  28.8 13.3 %collective-permute-start.2 = (bf16[208,512]{1,0:T(8,128)(2,1)S(1)}, bf16[208,512]{1,0:T(8,128)(2,1)}, u32[]{:S(2)}, u32[]{:S(2)}) collective-permute-start(bf16[208,512]{1,0:T(8,128)(2,1)S(1)} %pad_maximum_fusion.23.rest_0_), channel_id=1, source_target_pairs={{0,24},{4,28},{8,0},{12,4},{16,8},{20,12},{24,16},{28,20},{1,25},{... | collective-permute-start | bytes 638984 | tf_op jit(solution)/shard_map/ppermute | solution.py:538
  49.9 36.6 %all-to-all-start.1 = ((bf16[4,48,1536]{2,1,0:T(8,128)(2,1)}), bf16[4,48,1536]{2,1,0:T(8,128)(2,1)S(1)}, u32[]{:S(2)}, u32[]{:S(2)}) async-start(bf16[4,48,1536]{2,1,0:T(8,128)(2,1)} %broadcast_in_dim.58), calls=%async_computation.1 | async-start | bytes 1179648 | tf_op jit(solution)/shard_map/all_to_all | solution.py:601
  58.2 17.4 %collective-permute-start.8 = (bf16[2,128,1536]{2,1,0:T(8,128)(2,1)}, bf16[2,128,1536]{2,1,0:T(8,128)(2,1)}, u32[]{:S(2)}, u32[]{:S(2)}) collective-permute-start(bf16[2,128,1536]{2,1,0:T(8,128)(2,1)} %pad_maximum_fusion.1), channel_id=1, source_target_pairs={{0,1},{1,0},{2,3},{3,2},{4,5},{5,4},{6,7},{7,6},{8,9},{9,8},{10,11... | collective-permute-start | bytes 2359304 | tf_op jit(solution)/shard_map/ppermute | solution.py:550
  60.4 15.2 %collective-permute-start.7 = (bf16[208,512]{1,0:T(8,128)(2,1)}, bf16[208,512]{1,0:T(8,128)(2,1)S(1)}, u32[]{:S(2)}, u32[]{:S(2)}) collective-permute-start(bf16[208,512]{1,0:T(8,128)(2,1)} %collective-permute-done.2.rest_3_), channel_id=1, source_target_pairs={{0,4},{4,0},{8,12},{12,8},{16,20},{20,16},{24,28},{28,24},{1,5},{5... | collective-permute-start | bytes 638984 | tf_op jit(solution)/shard_map/ppermute | solution.py:541
  62.9 47.0 %collective-permute-start.11 = (bf16[3,96,1120]{2,1,0:T(8,128)(2,1)}, bf16[3,96,1120]{2,1,0:T(8,128)(2,1)}, u32[]{:S(2)}, u32[]{:S(2)}) collective-permute-start(bf16[3,96,1120]{2,1,0:T(8,128)(2,1)} %copy-done.53), channel_id=1, source_target_pairs={{0,8},{4,12},{8,16},{12,20},{16,24},{20,28},{24,0},{28,4},{1,9},{5... | collective-permute-start | bytes 1935368 | tf_op jit(solution)/shard_map/ppermute | solution.py:538
  66.4 43.4 %collective-permute-start.12 = (bf16[3,96,1120]{2,1,0:T(8,128)(2,1)}, bf16[3,96,1120]{2,1,0:T(8,128)(2,1)}, u32[]{:S(2)}, u32[]{:S(2)}) collective-permute-start(bf16[3,96,1120]{2,1,0:T(8,128)(2,1)} %get-tuple-element.201.refs_0_), channel_id=1, source_target_pairs={{0,4},{4,0},{8,12},{12,8},{16,20},{20,16},{24,28},{28,24},{1,5},{5... | collective-permute-start | bytes 1935368 | tf_op jit(solution)/shard_map/ppermute | solution.py:541
  86.4 23.4 %collective-permute-start.9 = (bf16[4,48,1536]{2,1,0:T(8,128)(2,1)S(1)}, bf16[4,48,1536]{2,1,0:T(8,128)(2,1)S(1)}, u32[]{:S(2)}, u32[]{:S(2)}) collective-permute-start(bf16[4,48,1536]{2,1,0:T(8,128)(2,1)S(1)} %all-to-all-done.1.mine), channel_id=1, source_target_pairs={{0,4},{4,0},{8,12},{12,8},{16,20},{20,16},{24,28},{28,24},{1,5},{5... | collective-permute-start | bytes 1769480 | tf_op jit(solution)/shard_map/ppermute | solution.py:541
  88.0 21.9 %collective-permute-start.10 = (bf16[128,1536]{1,0:T(8,128)(2,1)}, bf16[128,1536]{1,0:T(8,128)(2,1)S(1)}, u32[]{:S(2)}, u32[]{:S(2)}) collective-permute-start(bf16[128,1536]{1,0:T(8,128)(2,1)} %bitcast.262), channel_id=1, source_target_pairs={{0,2},{1,3},{2,0},{3,1},{4,6},{5,7},{6,4},{7,5},{8,10},{9,11},{10,... | collective-permute-start | bytes 1179656 | tf_op jit(solution)/shard_map/ppermute | solution.py:544
  108.8 12.9 %collective-permute-start.19 = (bf16[3,96,1120]{2,1,0:T(8,128)(2,1)}, bf16[3,96,1120]{2,1,0:T(8,128)(2,1)S(1)}, u32[]{:S(2)}, u32[]{:S(2)}) collective-permute-start(bf16[3,96,1120]{2,1,0:T(8,128)(2,1)} %copy-done.52), channel_id=1, source_target_pairs={{0,24},{4,28},{8,0},{12,4},{16,8},{20,12},{24,16},{28,20},{1,25},{... | collective-permute-start | bytes 1935368 | tf_op jit(solution)/shard_map/ppermute | solution.py:538
  122.1 23.7 %collective-permute-start.20 = (bf16[3,96,1120]{2,1,0:T(8,128)(2,1)}, bf16[3,96,1120]{2,1,0:T(8,128)(2,1)S(1)}, u32[]{:S(2)}, u32[]{:S(2)}) collective-permute-start(bf16[3,96,1120]{2,1,0:T(8,128)(2,1)} %collective-permute-done.11.refs_1_), channel_id=1, source_target_pairs={{0,4},{4,0},{8,12},{12,8},{16,20},{20,16},{24,28},{28,24},{1,5},{5... | collective-permute-start | bytes 1935368 | tf_op jit(solution)/shard_map/ppermute | solution.py:541
  123.3 22.5 %collective-permute-start.21 = (bf16[2,96,1120]{2,1,0:T(8,128)(2,1)S(1)}, bf16[2,96,1120]{2,1,0:T(8,128)(2,1)S(1)}, u32[]{:S(2)}, u32[]{:S(2)}) collective-permute-start(bf16[2,96,1120]{2,1,0:T(8,128)(2,1)S(1)} %slice.172), channel_id=1, source_target_pairs={{0,16},{4,20},{8,24},{12,28},{16,0},{20,4},{24,8},{28,12},{1,17},{... | collective-permute-start | bytes 1290248 | tf_op jit(solution)/shard_map/ppermute | solution.py:538
  148.1 17.4 %collective-permute-start.27 = (bf16[3,96,1120]{2,1,0:T(8,128)(2,1)S(1)}, bf16[3,96,1120]{2,1,0:T(8,128)(2,1)S(1)}, u32[]{:S(2)}, u32[]{:S(2)}) collective-permute-start(bf16[3,96,1120]{2,1,0:T(8,128)(2,1)S(1)} %collective-permute-done.19.refs_3_), channel_id=1, source_target_pairs={{0,4},{4,0},{8,12},{12,8},{16,20},{20,16},{24,28},{28,24},{1,5},{5... | collective-permute-start | bytes 1935368 | tf_op jit(solution)/shard_map/ppermute | solution.py:541
  150.6 14.9 %collective-permute-start.25 = (bf16[128,1536]{1,0:T(8,128)(2,1)S(1)}, bf16[128,1536]{1,0:T(8,128)(2,1)S(1)}, u32[]{:S(2)}, u32[]{:S(2)}) collective-permute-start(bf16[128,1536]{1,0:T(8,128)(2,1)S(1)} %fusion.10), channel_id=1, source_target_pairs={{0,2},{1,3},{2,0},{3,1},{4,6},{5,7},{6,4},{7,5},{8,10},{9,11},{10,... | collective-permute-start | bytes 1179656 | tf_op jit(solution)/shard_map/ppermute | solution.py:544
  152.9 16.8 %collective-permute-start.28 = (bf16[256,1536]{1,0:T(8,128)(2,1)S(1)}, bf16[256,1536]{1,0:T(8,128)(2,1)S(1)}, u32[]{:S(2)}, u32[]{:S(2)}) collective-permute-start(bf16[256,1536]{1,0:T(8,128)(2,1)S(1)} %pad_maximum_fusion.2), channel_id=1, source_target_pairs={{0,1},{1,0},{2,3},{3,2},{4,5},{5,4},{6,7},{7,6},{8,9},{9,8},{10,11... | collective-permute-start | bytes 2359304 | tf_op jit(solution)/shard_map/ppermute | solution.py:550
  153.0 12.0 %collective-permute-start.26 = (bf16[1,96,1120]{2,1,0:T(8,128)(2,1)S(1)}, bf16[1,96,1120]{2,1,0:T(8,128)(2,1)S(1)}, u32[]{:S(2)}, u32[]{:S(2)}) collective-permute-start(bf16[1,96,1120]{2,1,0:T(8,128)(2,1)S(1)} %slice.173), channel_id=1, source_target_pairs={{0,16},{4,20},{8,24},{12,28},{16,0},{20,4},{24,8},{28,12},{1,17},{... | collective-permute-start | bytes 645128 | tf_op jit(solution)/shard_map/ppermute | solution.py:538
  168.1 12.2 %collective-permute-start.34 = (bf16[128,1536]{1,0:T(8,128)(2,1)S(1)}, bf16[128,1536]{1,0:T(8,128)(2,1)S(1)}, u32[]{:S(2)}, u32[]{:S(2)}) collective-permute-start(bf16[128,1536]{1,0:T(8,128)(2,1)S(1)} %multiply_convert_fusion.12), channel_id=1, source_target_pairs={{0,8},{4,12},{8,16},{12,20},{16,24},{20,28},{24,0},{28,4},{1,9},{5... | collective-permute-start | bytes 1179656 | tf_op jit(solution)/shard_map/ppermute | solution.py:538
  168.1 16.3 %collective-permute-start.30 = (bf16[3,96,1120]{2,1,0:T(8,128)(2,1)S(1)}, bf16[3,96,1120]{2,1,0:T(8,128)(2,1)S(1)}, u32[]{:S(2)}, u32[]{:S(2)}) collective-permute-start(bf16[3,96,1120]{2,1,0:T(8,128)(2,1)S(1)} %constant_dynamic-update-slice_fusion.3.refs_2_), channel_id=1, source_target_pairs={{0,4},{4,0},{8,12},{12,8},{16,20},{20,16},{24,28},{28,24},{1,5},{5... | collective-permute-start | bytes 1935368 | tf_op jit(solution)/shard_map/ppermute | solution.py:541
  177.1 21.8 %collective-permute-start.43 = (bf16[128,1536]{1,0:T(8,128)(2,1)S(1)}, bf16[128,1536]{1,0:T(8,128)(2,1)S(1)}, u32[]{:S(2)}, u32[]{:S(2)}) collective-permute-start(bf16[128,1536]{1,0:T(8,128)(2,1)S(1)} %bitcast.265), channel_id=1, source_target_pairs={{0,8},{4,12},{8,16},{12,20},{16,24},{20,28},{24,0},{28,4},{1,9},{5... | collective-permute-start | bytes 1179656 | tf_op jit(solution)/shard_map/ppermute | solution.py:538
  180.4 13.3 %collective-permute-start.35 = (bf16[128,1536]{1,0:T(8,128)(2,1)S(1)}, bf16[128,1536]{1,0:T(8,128)(2,1)S(1)}, u32[]{:S(2)}, u32[]{:S(2)}) collective-permute-start(bf16[128,1536]{1,0:T(8,128)(2,1)S(1)} %collective-permute-done.34), channel_id=1, source_target_pairs={{0,2},{1,3},{2,0},{3,1},{4,6},{5,7},{6,4},{7,5},{8,10},{9,11},{10,... | collective-permute-start | bytes 1179656 | tf_op jit(solution)/shard_map/ppermute | solution.py:544
  180.7 16.8 %collective-permute-start.37 = (bf16[128,1536]{1,0:T(8,128)(2,1)S(1)}, bf16[128,1536]{1,0:T(8,128)(2,1)S(1)}, u32[]{:S(2)}, u32[]{:S(2)}) collective-permute-start(bf16[128,1536]{1,0:T(8,128)(2,1)S(1)} %collective-permute-done.34), channel_id=1, source_target_pairs={{0,8},{4,12},{8,16},{12,20},{16,24},{20,28},{24,0},{28,4},{1,9},{5... | collective-permute-start | bytes 1179656 | tf_op jit(solution)/shard_map/ppermute | solution.py:538
  185.4 35.2 %collective-permute-start.31 = (bf16[256,1536]{1,0:T(8,128)(2,1)}, bf16[256,1536]{1,0:T(8,128)(2,1)}, u32[]{:S(2)}, u32[]{:S(2)}) collective-permute-start(bf16[256,1536]{1,0:T(8,128)(2,1)} %pad_maximum_fusion.3), channel_id=1, source_target_pairs={{0,1},{1,0},{2,3},{3,2},{4,5},{5,4},{6,7},{7,6},{8,9},{9,8},{10,11... | collective-permute-start | bytes 2359304 | tf_op jit(solution)/shard_map/ppermute | solution.py:550
  193.7 39.9 %collective-permute-start.36 = (bf16[256,1536]{1,0:T(8,128)(2,1)S(1)}, bf16[256,1536]{1,0:T(8,128)(2,1)S(1)}, u32[]{:S(2)}, u32[]{:S(2)}) collective-permute-start(bf16[256,1536]{1,0:T(8,128)(2,1)S(1)} %pad_maximum_fusion.4), channel_id=1, source_target_pairs={{0,1},{1,0},{2,3},{3,2},{4,5},{5,4},{6,7},{7,6},{8,9},{9,8},{10,11... | collective-permute-start | bytes 2359304 | tf_op jit(solution)/shard_map/ppermute | solution.py:550
  197.5 12.1 %collective-permute-start.38 = (bf16[128,1536]{1,0:T(8,128)(2,1)S(1)}, bf16[128,1536]{1,0:T(8,128)(2,1)S(1)}, u32[]{:S(2)}, u32[]{:S(2)}) collective-permute-start(bf16[128,1536]{1,0:T(8,128)(2,1)S(1)} %collective-permute-done.37), channel_id=1, source_target_pairs={{0,2},{1,3},{2,0},{3,1},{4,6},{5,7},{6,4},{7,5},{8,10},{9,11},{10,... | collective-permute-start | bytes 1179656 | tf_op jit(solution)/shard_map/ppermute | solution.py:544
  198.9 16.4 %collective-permute-start.40 = (bf16[128,1536]{1,0:T(8,128)(2,1)S(1)}, bf16[128,1536]{1,0:T(8,128)(2,1)S(1)}, u32[]{:S(2)}, u32[]{:S(2)}) collective-permute-start(bf16[128,1536]{1,0:T(8,128)(2,1)S(1)} %collective-permute-done.37), channel_id=1, source_target_pairs={{0,8},{4,12},{8,16},{12,20},{16,24},{20,28},{24,0},{28,4},{1,9},{5... | collective-permute-start | bytes 1179656 | tf_op jit(solution)/shard_map/ppermute | solution.py:538
  198.9 16.2 %collective-permute-start.48 = (bf16[128,1536]{1,0:T(8,128)(2,1)S(1)}, bf16[128,1536]{1,0:T(8,128)(2,1)S(1)}, u32[]{:S(2)}, u32[]{:S(2)}) collective-permute-start(bf16[128,1536]{1,0:T(8,128)(2,1)S(1)} %collective-permute-done.43), channel_id=1, source_target_pairs={{0,2},{1,3},{2,0},{3,1},{4,6},{5,7},{6,4},{7,5},{8,10},{9,11},{10,... | collective-permute-start | bytes 1179656 | tf_op jit(solution)/shard_map/ppermute | solution.py:544
  215.1 36.6 %collective-permute-start.39 = (bf16[256,1536]{1,0:T(8,128)(2,1)S(1)}, bf16[256,1536]{1,0:T(8,128)(2,1)S(1)}, u32[]{:S(2)}, u32[]{:S(2)}) collective-permute-start(bf16[256,1536]{1,0:T(8,128)(2,1)S(1)} %pad_maximum_fusion.5), channel_id=1, source_target_pairs={{0,1},{1,0},{2,3},{3,2},{4,5},{5,4},{6,7},{7,6},{8,9},{9,8},{10,11... | collective-permute-start | bytes 2359304 | tf_op jit(solution)/shard_map/ppermute | solution.py:550
  215.3 26.9 %collective-permute-start.49 = (bf16[256,1536]{1,0:T(8,128)(2,1)S(1)}, bf16[256,1536]{1,0:T(8,128)(2,1)S(1)}, u32[]{:S(2)}, u32[]{:S(2)}) collective-permute-start(bf16[256,1536]{1,0:T(8,128)(2,1)S(1)} %pad_maximum_fusion.8), channel_id=1, source_target_pairs={{0,1},{1,0},{2,3},{3,2},{4,5},{5,4},{6,7},{7,6},{8,9},{9,8},{10,11... | collective-permute-start | bytes 2359304 | tf_op jit(solution)/shard_map/ppermute | solution.py:550
  219.1 16.7 %collective-permute-start.41 = (bf16[128,1536]{1,0:T(8,128)(2,1)S(1)}, bf16[128,1536]{1,0:T(8,128)(2,1)S(1)}, u32[]{:S(2)}, u32[]{:S(2)}) collective-permute-start(bf16[128,1536]{1,0:T(8,128)(2,1)S(1)} %collective-permute-done.40), channel_id=1, source_target_pairs={{0,2},{1,3},{2,0},{3,1},{4,6},{5,7},{6,4},{7,5},{8,10},{9,11},{10,... | collective-permute-start | bytes 1179656 | tf_op jit(solution)/shard_map/ppermute | solution.py:544
  220.6 21.0 %collective-permute-start.45 = (bf16[128,1536]{1,0:T(8,128)(2,1)S(1)}, bf16[128,1536]{1,0:T(8,128)(2,1)S(1)}, u32[]{:S(2)}, u32[]{:S(2)}) collective-permute-start(bf16[128,1536]{1,0:T(8,128)(2,1)S(1)} %collective-permute-done.44), channel_id=1, source_target_pairs={{0,8},{4,12},{8,16},{12,20},{16,24},{20,28},{24,0},{28,4},{1,9},{5... | collective-permute-start | bytes 1179656 | tf_op jit(solution)/shard_map/ppermute | solution.py:538
  235.8 18.4 %collective-permute-start.32 = (bf16[2,128,1536]{2,1,0:T(8,128)(2,1)S(1)}, bf16[2,128,1536]{2,1,0:T(8,128)(2,1)S(1)}, u32[]{:S(2)}, u32[]{:S(2)}) collective-permute-start(bf16[2,128,1536]{2,1,0:T(8,128)(2,1)S(1)} %bitcast.275), channel_id=1, source_target_pairs={{0,1},{1,0},{2,3},{3,2},{4,5},{5,4},{6,7},{7,6},{8,9},{9,8},{10,11... | collective-permute-start | bytes 2359304 | tf_op jit(solution)/shard_map/ppermute | solution.py:550
  241.5 24.1 %collective-permute-start.42 = (bf16[256,1536]{1,0:T(8,128)(2,1)S(1)}, bf16[256,1536]{1,0:T(8,128)(2,1)S(1)}, u32[]{:S(2)}, u32[]{:S(2)}) collective-permute-start(bf16[256,1536]{1,0:T(8,128)(2,1)S(1)} %pad_maximum_fusion.6), channel_id=1, source_target_pairs={{0,1},{1,0},{2,3},{3,2},{4,5},{5,4},{6,7},{7,6},{8,9},{9,8},{10,11... | collective-permute-start | bytes 2359304 | tf_op jit(solution)/shard_map/ppermute | solution.py:550
  241.6 15.0 %collective-permute-start.52 = (bf16[256,1536]{1,0:T(8,128)(2,1)S(1)}, bf16[256,1536]{1,0:T(8,128)(2,1)S(1)}, u32[]{:S(2)}, u32[]{:S(2)}) collective-permute-start(bf16[256,1536]{1,0:T(8,128)(2,1)S(1)} %pad_maximum_fusion.9), channel_id=1, source_target_pairs={{0,1},{1,0},{2,3},{3,2},{4,5},{5,4},{6,7},{7,6},{8,9},{9,8},{10,11... | collective-permute-start | bytes 2359304 | tf_op jit(solution)/shard_map/ppermute | solution.py:550
  251.8 24.5 %collective-permute-start.50 = (bf16[2,128,1536]{2,1,0:T(8,128)(2,1)S(1)}, bf16[2,128,1536]{2,1,0:T(8,128)(2,1)S(1)}, u32[]{:S(2)}, u32[]{:S(2)}) collective-permute-start(bf16[2,128,1536]{2,1,0:T(8,128)(2,1)S(1)} %bitcast.274), channel_id=1, source_target_pairs={{0,1},{1,0},{2,3},{3,2},{4,5},{5,4},{6,7},{7,6},{8,9},{9,8},{10,11... | collective-permute-start | bytes 2359304 | tf_op jit(solution)/shard_map/ppermute | solution.py:550
  254.1 13.1 %collective-permute-start.47 = (bf16[256,1536]{1,0:T(8,128)(2,1)S(1)}, bf16[256,1536]{1,0:T(8,128)(2,1)S(1)}, u32[]{:S(2)}, u32[]{:S(2)}) collective-permute-start(bf16[256,1536]{1,0:T(8,128)(2,1)S(1)} %pad_maximum_fusion.7), channel_id=1, source_target_pairs={{0,1},{1,0},{2,3},{3,2},{4,5},{5,4},{6,7},{7,6},{8,9},{9,8},{10,11... | collective-permute-start | bytes 2359304 | tf_op jit(solution)/shard_map/ppermute | solution.py:550
  265.3 13.9 %collective-permute-start.53 = (bf16[2,128,1536]{2,1,0:T(8,128)(2,1)S(1)}, bf16[2,128,1536]{2,1,0:T(8,128)(2,1)S(1)}, u32[]{:S(2)}, u32[]{:S(2)}) collective-permute-start(bf16[2,128,1536]{2,1,0:T(8,128)(2,1)S(1)} %bitcast.276), channel_id=1, source_target_pairs={{0,1},{1,0},{2,3},{3,2},{4,5},{5,4},{6,7},{7,6},{8,9},{9,8},{10,11... | collective-permute-start | bytes 2359304 | tf_op jit(solution)/shard_map/ppermute | solution.py:550
  277.9 12.0 %collective-permute-start.54 = (bf16[128,1536]{1,0:T(8,128)(2,1)S(1)}, bf16[128,1536]{1,0:T(8,128)(2,1)S(1)}, u32[]{:S(2)}, u32[]{:S(2)}) collective-permute-start(bf16[128,1536]{1,0:T(8,128)(2,1)S(1)} %fusion.12), channel_id=1, source_target_pairs={{0,2},{1,3},{2,0},{3,1},{4,6},{5,7},{6,4},{7,5},{8,10},{9,11},{10,... | collective-permute-start | bytes 1179656 | tf_op jit(solution)/shard_map/ppermute | solution.py:544
  279.0 15.5 %collective-permute-start.56 = (bf16[2,128,1536]{2,1,0:T(8,128)(2,1)S(1)}, bf16[2,128,1536]{2,1,0:T(8,128)(2,1)S(1)}, u32[]{:S(2)}, u32[]{:S(2)}) collective-permute-start(bf16[2,128,1536]{2,1,0:T(8,128)(2,1)S(1)} %bitcast.277), channel_id=1, source_target_pairs={{0,1},{1,0},{2,3},{3,2},{4,5},{5,4},{6,7},{7,6},{8,9},{9,8},{10,11... | collective-permute-start | bytes 2359304 | tf_op jit(solution)/shard_map/ppermute | solution.py:550
  279.5 18.8 %collective-permute-start.55 = (bf16[128,1536]{1,0:T(8,128)(2,1)S(1)}, bf16[128,1536]{1,0:T(8,128)(2,1)S(1)}, u32[]{:S(2)}, u32[]{:S(2)}) collective-permute-start(bf16[128,1536]{1,0:T(8,128)(2,1)S(1)} %fusion.13), channel_id=1, source_target_pairs={{0,2},{1,3},{2,0},{3,1},{4,6},{5,7},{6,4},{7,5},{8,10},{9,11},{10,... | collective-permute-start | bytes 1179656 | tf_op jit(solution)/shard_map/ppermute | solution.py:544
  290.7 24.0 %collective-permute-start.58 = (bf16[128,1536]{1,0:T(8,128)(2,1)}, bf16[128,1536]{1,0:T(8,128)(2,1)S(1)}, u32[]{:S(2)}, u32[]{:S(2)}) collective-permute-start(bf16[128,1536]{1,0:T(8,128)(2,1)} %fusion.4), channel_id=1, source_target_pairs={{0,24},{4,28},{8,0},{12,4},{16,8},{20,12},{24,16},{28,20},{1,25},{... | collective-permute-start | bytes 1179656 | tf_op jit(solution)/shard_map/ppermute | solution.py:538
  294.8 16.3 %collective-permute-start.57 = (bf16[128,1536]{1,0:T(8,128)(2,1)S(1)}, bf16[128,1536]{1,0:T(8,128)(2,1)S(1)}, u32[]{:S(2)}, u32[]{:S(2)}) collective-permute-start(bf16[128,1536]{1,0:T(8,128)(2,1)S(1)} %fusion.14), channel_id=1, source_target_pairs={{0,2},{1,3},{2,0},{3,1},{4,6},{5,7},{6,4},{7,5},{8,10},{9,11},{10,... | collective-permute-start | bytes 1179656 | tf_op jit(solution)/shard_map/ppermute | solution.py:544
  299.1 27.9 %collective-permute-start.59 = (bf16[128,1536]{1,0:T(8,128)(2,1)}, bf16[128,1536]{1,0:T(8,128)(2,1)S(1)}, u32[]{:S(2)}, u32[]{:S(2)}) collective-permute-start(bf16[128,1536]{1,0:T(8,128)(2,1)} %fusion.3), channel_id=1, source_target_pairs={{0,16},{4,20},{8,24},{12,28},{16,0},{20,4},{24,8},{28,12},{1,17},{... | collective-permute-start | bytes 1179656 | tf_op jit(solution)/shard_map/ppermute | solution.py:538
  309.5 20.6 %collective-permute-start.62 = (bf16[4,1,96,1120]{3,2,1,0:T(8,128)(2,1)S(1)}, bf16[4,1,96,1120]{3,2,1,0:T(8,128)(2,1)S(1)}, u32[]{:S(2)}, u32[]{:S(2)}) collective-permute-start(bf16[4,1,96,1120]{3,2,1,0:T(8,128)(2,1)S(1)} %get-tuple-element.251), channel_id=1, source_target_pairs={{0,4},{4,0},{8,12},{12,8},{16,20},{20,16},{24,28},{28,24},{1,5},{5... | collective-permute-start | bytes 2580488 | tf_op jit(solution)/shard_map/ppermute | solution.py:541
  312.3 14.7 %collective-permute-start.60 = (bf16[128,1536]{1,0:T(8,128)(2,1)S(1)}, bf16[128,1536]{1,0:T(8,128)(2,1)S(1)}, u32[]{:S(2)}, u32[]{:S(2)}) collective-permute-start(bf16[128,1536]{1,0:T(8,128)(2,1)S(1)} %fusion.2), channel_id=1, source_target_pairs={{0,8},{4,12},{8,16},{12,20},{16,24},{20,28},{24,0},{28,4},{1,9},{5... | collective-permute-start | bytes 1179656 | tf_op jit(solution)/shard_map/ppermute | solution.py:538
  330.1 23.9 %collective-permute-start.63 = (bf16[4,1,96,1120]{3,2,1,0:T(8,128)(2,1)}, bf16[4,1,96,1120]{3,2,1,0:T(8,128)(2,1)}, u32[]{:S(2)}, u32[]{:S(2)}) collective-permute-start(bf16[4,1,96,1120]{3,2,1,0:T(8,128)(2,1)} %get-tuple-element.267), channel_id=1, source_target_pairs={{0,4},{4,0},{8,12},{12,8},{16,20},{20,16},{24,28},{28,24},{1,5},{5... | collective-permute-start | bytes 2580488 | tf_op jit(solution)/shard_map/ppermute | solution.py:541
  332.9 21.1 %collective-permute-start.61 = (bf16[128,1536]{1,0:T(8,128)(2,1)S(1)}, bf16[128,1536]{1,0:T(8,128)(2,1)S(1)}, u32[]{:S(2)}, u32[]{:S(2)}) collective-permute-start(bf16[128,1536]{1,0:T(8,128)(2,1)S(1)} %get-tuple-element.286.own), channel_id=1, source_target_pairs={{0,2},{1,3},{2,0},{3,1},{4,6},{5,7},{6,4},{7,5},{8,10},{9,11},{10,... | collective-permute-start | bytes 1179656 | tf_op jit(solution)/shard_map/ppermute | solution.py:544
  334.6 25.9 %all-to-all-start.2 = ((bf16[4,1,96,1120]{3,2,1,0:T(8,128)(2,1)}), bf16[4,1,96,1120]{3,2,1,0:T(8,128)(2,1)}, u32[]{:S(2)}, u32[]{:S(2)}) async-start(bf16[4,1,96,1120]{3,2,1,0:T(8,128)(2,1)} %add_convert_fusion.2), calls=%async_computation.2 | async-start | bytes 1769472 | tf_op jit(solution)/shard_map/all_to_all | solution.py:601
  363.1 27.2 %all-to-all-start.3 = ((bf16[4,1,96,1120]{3,2,1,0:T(8,128)(2,1)}), bf16[4,1,96,1120]{3,2,1,0:T(8,128)(2,1)S(1)}, u32[]{:S(2)}, u32[]{:S(2)}) async-start(bf16[4,1,96,1120]{3,2,1,0:T(8,128)(2,1)} %add_convert_fusion.1), calls=%async_computation.3 | async-start | bytes 1769472 | tf_op jit(solution)/shard_map/all_to_all | solution.py:601
  367.8 138.0 %reduce-scatter.3.cloned.1.call-start = ((), (), s32[]{:S(2)}) async-start(), calls=%async_computation.8 | async-start | bytes 7864320 | tf_op jit(solution)/shard_map/reduce_scatter | solution.py:977
  384.2 25.1 %collective-permute-start.70 = (bf16[4,1,96,1120]{3,2,1,0:T(8,128)(2,1)}, bf16[4,1,96,1120]{3,2,1,0:T(8,128)(2,1)}, u32[]{:S(2)}, u32[]{:S(2)}) collective-permute-start(bf16[4,1,96,1120]{3,2,1,0:T(8,128)(2,1)} %get-tuple-element.294), channel_id=1, source_target_pairs={{0,4},{4,0},{8,12},{12,8},{16,20},{20,16},{24,28},{28,24},{1,5},{5... | collective-permute-start | bytes 2580488 | tf_op jit(solution)/shard_map/ppermute | solution.py:541
  392.9 24.5 %collective-permute-start.69 = (bf16[4,4,2,64,128]{4,3,2,1,0:T(8,128)(2,1)}, bf16[4,4,2,64,128]{4,3,2,1,0:T(8,128)(2,1)}, u32[]{:S(2)}, u32[]{:S(2)}) collective-permute-start(bf16[4,4,2,64,128]{4,3,2,1,0:T(8,128)(2,1)} %add_convert_fusion.5), channel_id=1, source_target_pairs={{0,4},{4,0},{8,12},{12,8},{16,20},{20,16},{24,28},{28,24},{1,5},{5... | collective-permute-start | bytes 1572872 | tf_op jit(solution)/shard_map/ppermute | solution.py:541
  417.4 22.0 %collective-permute-start.74 = (bf16[2,2,48,1536]{3,2,1,0:T(8,128)(2,1)}, bf16[2,2,48,1536]{3,2,1,0:T(8,128)(2,1)S(1)}, u32[]{:S(2)}, u32[]{:S(2)}) collective-permute-start(bf16[2,2,48,1536]{3,2,1,0:T(8,128)(2,1)} %copy-done.55), channel_id=1, source_target_pairs={{0,2},{1,3},{2,0},{3,1},{4,6},{5,7},{6,4},{7,5},{8,10},{9,11},{10,... | collective-permute-start | bytes 1769480 | tf_op jit(solution)/shard_map/ppermute | solution.py:544
  418.9 20.4 %collective-permute-start.75 = (bf16[4,1,4,48,384]{4,3,2,1,0:T(8,128)(2,1)}, bf16[4,1,4,48,384]{4,3,2,1,0:T(8,128)(2,1)}, u32[]{:S(2)}, u32[]{:S(2)}) collective-permute-start(bf16[4,1,4,48,384]{4,3,2,1,0:T(8,128)(2,1)} %copy-done.54), channel_id=1, source_target_pairs={{0,4},{4,0},{8,12},{12,8},{16,20},{20,16},{24,28},{28,24},{1,5},{5... | collective-permute-start | bytes 1769480 | tf_op jit(solution)/shard_map/ppermute | solution.py:541
  447.1 26.1 %all-to-all-start.4 = ((bf16[4,1,4,48,384]{4,3,2,1,0:T(8,128)(2,1)}), bf16[4,1,4,48,384]{4,3,2,1,0:T(8,128)(2,1)S(1)}, u32[]{:S(2)}, u32[]{:S(2)}) async-start(bf16[4,1,4,48,384]{4,3,2,1,0:T(8,128)(2,1)} %add_convert_fusion.3), calls=%async_computation.6 | async-start | bytes 1179648 | tf_op jit(solution)/shard_map/all_to_all | solution.py:601
  459.4 14.9 %collective-permute-start.83 = (bf16[4,1,48,1536]{3,2,1,0:T(8,128)(2,1)}, bf16[4,1,48,1536]{3,2,1,0:T(8,128)(2,1)}, u32[]{:S(2)}, u32[]{:S(2)}) collective-permute-start(bf16[4,1,48,1536]{3,2,1,0:T(8,128)(2,1)} %get-tuple-element.322), channel_id=1, source_target_pairs={{0,4},{4,0},{8,12},{12,8},{16,20},{20,16},{24,28},{28,24},{1,5},{5... | collective-permute-start | bytes 1769480 | tf_op jit(solution)/shard_map/ppermute | solution.py:541
  479.7 26.2 %collective-permute-start.86 = (bf16[2,128,1536]{2,1,0:T(8,128)(2,1)}, bf16[2,128,1536]{2,1,0:T(8,128)(2,1)}, u32[]{:S(2)}, u32[]{:S(2)}) collective-permute-start(bf16[2,128,1536]{2,1,0:T(8,128)(2,1)} %get-tuple-element.331), channel_id=1, source_target_pairs={{0,1},{1,0},{2,3},{3,2},{4,5},{5,4},{6,7},{7,6},{8,9},{9,8},{10,11... | collective-permute-start | bytes 2359304 | tf_op jit(solution)/shard_map/ppermute | solution.py:550
  482.0 37.9 %all-to-all-start.5 = ((bf16[4,1,96,1120]{3,2,1,0:T(8,128)(2,1)}), bf16[4,1,96,1120]{3,2,1,0:T(8,128)(2,1)}, u32[]{:S(2)}, u32[]{:S(2)}) async-start(bf16[4,1,96,1120]{3,2,1,0:T(8,128)(2,1)} %add_convert_fusion), calls=%async_computation.7 | async-start | bytes 1769472 | tf_op jit(solution)/shard_map/all_to_all | solution.py:601
  486.5 60.5 %reduce-scatter.5.cloned.1.call-start = ((), (), s32[]{:S(2)}) async-start(), calls=%async_computation.9 | async-start | bytes 1966080 | tf_op jit(solution)/shard_map/reduce_scatter | solution.py:1007
  498.3 31.5 %collective-permute-start.90 = (bf16[1,48,1536]{2,1,0:T(8,128)(2,1)S(1)}, bf16[1,48,1536]{2,1,0:T(8,128)(2,1)}, u32[]{:S(2)}, u32[]{:S(2)}) collective-permute-start(bf16[1,48,1536]{2,1,0:T(8,128)(2,1)S(1)} %get-tuple-element.339), channel_id=1, source_target_pairs={{0,24},{4,28},{8,0},{12,4},{16,8},{20,12},{24,16},{28,20},{1,25},{... | collective-permute-start | bytes 442376 | tf_op jit(solution)/shard_map/ppermute | solution.py:538
  502.0 39.1 %collective-permute-start.89 = (bf16[1,48,1536]{2,1,0:T(8,128)(2,1)S(1)}, bf16[1,48,1536]{2,1,0:T(8,128)(2,1)}, u32[]{:S(2)}, u32[]{:S(2)}) collective-permute-start(bf16[1,48,1536]{2,1,0:T(8,128)(2,1)S(1)} %get-tuple-element.338), channel_id=1, source_target_pairs={{0,16},{4,20},{8,24},{12,28},{16,0},{20,4},{24,8},{28,12},{1,17},{... | collective-permute-start | bytes 442376 | tf_op jit(solution)/shard_map/ppermute | solution.py:538
  502.0 39.1 %collective-permute-start.88 = (bf16[1,48,1536]{2,1,0:T(8,128)(2,1)S(1)}, bf16[1,48,1536]{2,1,0:T(8,128)(2,1)}, u32[]{:S(2)}, u32[]{:S(2)}) collective-permute-start(bf16[1,48,1536]{2,1,0:T(8,128)(2,1)S(1)} %get-tuple-element.337), channel_id=1, source_target_pairs={{0,8},{4,12},{8,16},{12,20},{16,24},{20,28},{24,0},{28,4},{1,9},{5... | collective-permute-start | bytes 442376 | tf_op jit(solution)/shard_map/ppermute | solution.py:538
  527.6 15.9 %collective-permute-start.87 = (bf16[128,1536]{1,0:T(8,128)(2,1)S(1)}, bf16[128,1536]{1,0:T(8,128)(2,1)S(1)}, u32[]{:S(2)}, u32[]{:S(2)}) collective-permute-start(bf16[128,1536]{1,0:T(8,128)(2,1)S(1)} %fusion.15), channel_id=1, source_target_pairs={{0,2},{1,3},{2,0},{3,1},{4,6},{5,7},{6,4},{7,5},{8,10},{9,11},{10,... | collective-permute-start | bytes 1179656 | tf_op jit(solution)/shard_map/ppermute | solution.py:544
  527.7 15.3 %collective-permute-start.92 = (f32[48]{0:T(128)S(1)}, f32[48]{0:T(128)S(1)}, u32[]{:S(2)}, u32[]{:S(2)}) collective-permute-start(f32[48]{0:T(128)S(1)} %fusion.34), channel_id=1, source_target_pairs={{0,2},{1,3},{2,0},{3,1},{4,6},{5,7},{6,4},{7,5},{8,10},{9,11},{10,... | collective-permute-start | bytes 584 | tf_op jit(solution)/shard_map/ppermute | solution.py:544
  (138 other events, 1087.2 us)
Sparse Core Ops, SparseCore 0:
  417.5 60.5 reduce-scatter.2
  506.0 41.0 reduce-scatter.4
